TPU v7x, 256 devices: a whole 4x4x8 slice. The times are simulated.
256 devices in a mesh: blk: 32 (over x, z), tile: 8 (over y, core).
Axes of the slice: x: 4, y: 4, z: 8, core: 2. Of those that a mesh axis runs over, the one named last changes fastest.
Arguments:
- stream_in: bfloat16 [32, 64, 16, 2240], P('tile', 'blk'), may hold values from -6 to 6
- queries: bfloat16 [32, 64, 16, 2240], P('tile', 'blk'), may hold values from -12 to 12
- key_rows: bfloat16 [32, 64, 16, 2240], P('tile', 'blk'), may hold values from -12 to 12
- value_rows: bfloat16 [32, 64, 16, 2240], P('tile', 'blk'), may hold values from -12 to 12
- w_output: bfloat16 [2240, 2240], P('tile'), may hold values from -0.125 to 0.125
- w_inner: bfloat16 [2240, 2, 4096], P(None, None, 'tile'), may hold values from -0.125 to 0.125
- w_down: bfloat16 [4096, 2240], P('tile'), may hold values from -0.09375 to 0.09375
- spatial_taps: float32 [3, 3, 2, 4096], P(None, None, None, 'tile'), may hold values from -2 to 2
- temporal_taps: float32 [3, 2, 4096], P(None, None, 'tile'), may hold values from -3.5 to 3.5
Outputs:
- layer_out: bfloat16 [32, 64, 16, 2240], P('tile', 'blk')
All inputs are finite; a program needn't handle non-finite values.
Results may differ from a plain program's by a relative error of at most 0.009.
Values may be sent and summed in bfloat16 or wider, within the bound.
No kernel may reach another device: no remote copies, remote signals or barrier semaphores. Data moves between devices by JAX's collectives and lax.ppermute only.
A program may use at most 128 MiB of HBM per device.

v0:
```python
import jax
import jax.numpy as jnp
from jax import lax
from jax.sharding import PartitionSpec as P

HEADS = 20
HEAD_DIM = 112
TAPS = 3


EPS = 1e-06


def from_partner(value, axis, stride):
    mask = 2**stride
    pairs = [(source, source ^ mask) for source in range(lax.axis_size(axis))]
    return lax.ppermute(value, axis, pairs)


def carried_in(x, axis, combine, identity):
    peers, position = (lax.axis_size(axis), lax.axis_index(axis))
    everything = jax.tree.map(lambda part: lax.all_gather(part, axis), x)
    start = jax.tree.map(
        lambda part, zero: jnp.broadcast_to(jnp.asarray(zero, part.dtype), part.shape), x, identity
    )

    def step(k, before):
        reached = k < position
        new = combine(before, jax.tree.map(lambda part: part[k], everything))
        return jax.tree.map(lambda a, b: jnp.where(reached, a, b), new, before)

    return lax.fori_loop(0, peers, step, start)


def shifted(x, axis, by):
    peers = lax.axis_size(axis)
    pairs = [(i, i + by) for i in range(peers) if 0 <= i + by < peers]
    return lax.ppermute(x, axis, pairs)


def add_pair(earlier, later):
    return (earlier[0] + later[0], earlier[1] + later[1])


def prefix_state(state_parts):
    partner = from_partner((state_parts[0], state_parts[1]), "blk", 0)
    block_sum = add_pair(state_parts, partner)
    odd_side = (lax.axis_index("blk") % 2).astype(jnp.float32)
    keep_share = 1.0 - 0.5 * odd_side
    zero_state = (jnp.zeros_like(block_sum[0]), jnp.zeros_like(block_sum[1]))
    before = carried_in((block_sum[0] * 0.5, block_sum[1] * 0.5), "blk", add_pair, zero_state)
    return (before[0] + block_sum[0] * keep_share, before[1] + block_sum[1] * keep_share)


def spatial_conv(inner_act, spatial_taps):
    row_count = inner_act.shape[0]
    col_count = inner_act.shape[2]
    padded = jnp.pad(inner_act, ((1, 1), (0, 0), (1, 1), (0, 0), (0, 0)))
    running = jnp.zeros(inner_act.shape, jnp.float32)
    for tap_row in range(3):
        for tap_col in range(3):
            window = padded[tap_row : tap_row + row_count, :, tap_col : tap_col + col_count]
            running = running + window.astype(jnp.float32) * spatial_taps[tap_row, tap_col]
    return running


def on_device(
    stream_in, queries, key_rows, value_rows, w_output, w_inner, w_down, spatial_taps, temporal_taps
):
    row_count, frames, col_count, model_width = queries.shape
    tokens = row_count * frames * col_count
    highest = lax.Precision.HIGHEST
    key_pos = jax.nn.relu(key_rows).reshape(tokens, HEADS, HEAD_DIM)
    value_heads = value_rows.reshape(tokens, HEADS, HEAD_DIM)
    local_kv = jnp.einsum("thd,the->hde", key_pos, value_heads, preferred_element_type=jnp.float32)
    local_kv = local_kv.reshape(model_width, HEAD_DIM)
    local_z = jnp.sum(key_pos.astype(jnp.float32), axis=0).reshape(model_width)
    group_parts = lax.psum((local_kv, local_z), "tile")
    state, zsum = prefix_state(group_parts)
    state = state.reshape(HEADS, HEAD_DIM, HEAD_DIM)
    zsum = zsum.reshape(HEADS, HEAD_DIM)
    query_pos = jax.nn.relu(queries.astype(jnp.float32)).reshape(tokens, HEADS, HEAD_DIM)
    numerator = jnp.einsum("thd,hde->the", query_pos, state, precision=highest)
    denominator = jnp.einsum("thd,hd->th", query_pos, zsum, precision=highest) + EPS
    attended = (numerator / denominator[..., None]).astype(jnp.bfloat16)
    attended = attended.reshape(row_count, frames, col_count, model_width)
    by_feature = lax.all_to_all(attended, "tile", split_axis=3, concat_axis=0, tiled=True)
    portion = by_feature
    product = jnp.dot(
        portion.reshape(-1, portion.shape[3]), w_output, preferred_element_type=jnp.float32
    )
    attn_out = lax.psum_scatter(
        product.reshape(row_count * lax.axis_size("tile"), frames, col_count, model_width),
        "tile",
        scatter_dimension=0,
        tiled=True,
    )
    hidden = (stream_in.astype(jnp.float32) + attn_out).astype(jnp.bfloat16)
    chan_dev = w_inner.shape[2]
    w_flat = w_inner.reshape(model_width, 2 * chan_dev)
    portion = lax.all_gather(hidden, "tile", axis=0, tiled=True)
    product = jnp.dot(portion.reshape(-1, model_width), w_flat, preferred_element_type=jnp.float32)
    activated = jax.nn.silu(product).astype(jnp.bfloat16)
    inner_act = activated.reshape(portion.shape[0], frames, col_count, 2, chan_dev)
    spatial = spatial_conv(inner_act, spatial_taps).astype(jnp.bfloat16)
    earlier_frames = shifted(spatial, "blk", 1)
    extended = jnp.concatenate([earlier_frames, spatial], axis=1)
    temporal_mix = jnp.zeros(spatial.shape, jnp.float32)
    for lag in range(TAPS):
        window = extended[:, TAPS - 1 - lag : TAPS - 1 - lag + frames]
        temporal_mix = temporal_mix + window.astype(jnp.float32) * temporal_taps[lag]
    gated_out = (temporal_mix[..., 0, :] * jax.nn.silu(temporal_mix[..., 1, :])).astype(
        jnp.bfloat16
    )
    portion = gated_out
    product = jnp.dot(portion.reshape(-1, chan_dev), w_down, preferred_element_type=jnp.float32)
    ffn_out = lax.psum_scatter(
        product.reshape(lax.axis_size("tile") * row_count, frames, col_count, model_width).astype(
            jnp.bfloat16
        ),
        "tile",
        scatter_dimension=0,
        tiled=True,
    ).astype(jnp.float32)
    return (hidden.astype(jnp.float32) + ffn_out).astype(jnp.bfloat16)


def solution(mesh):
    in_specs = (
        P("tile", "blk", None, None),
        P("tile", "blk", None, None),
        P("tile", "blk", None, None),
        P("tile", "blk", None, None),
        P("tile", None),
        P(None, None, "tile"),
        P("tile", None),
        P(None, None, None, "tile"),
        P(None, None, "tile"),
    )
    out_specs = P("tile", "blk", None, None)
    return jax.shard_map(
        on_device, mesh=mesh, in_specs=in_specs, out_specs=out_specs, check_vma=False
    )
```

profile of v0, /device:TPU:2, one launch (start us, length us, event | category | flops | bytes accessed | tf_op | source)
XLA Modules:
  0.0 1003.1 jit_solution(15481732146756911971)
XLA Ops:
  11.5 2.7 reshape.59
  16.8 71.2 %all-reduce.5.cloned.1.call-done = f32[2240,112]{1,0:T(8,128)} async-done(((f32[2240,112]{1,0:T(8,128)}), f32[2240,112]{1,0:T(8,128)}) %all-reduce.5.cloned.1.call-update) | async-done | bytes 1003536 | tf_op jit(solution)/shard_map/psum | solution.py:78
  87.9 2.6 copy.39
  93.3 23.9 %psum.15 = f32[2240]{0:T(1024)S(1)} all-reduce(f32[2240]{0:T(1024)S(1)} %convert_reduce_fusion), channel_id=1, replica_groups=mesh['blk'=32,'tile'=8] {'tile'}, use_global_device_ids=true, to_apply=%region_2.3 | all-reduce | flops 2240 | bytes 17920 | tf_op jit(solution)/shard_map/psum | solution.py:78
  134.2 2.8 copy.44
  137.0 127.0 %all-reduce.7.cloned.1.call-done = f32[71680]{0:T(1024)} async-done(((f32[71680]{0:T(1024)}), f32[71680]{0:T(1024)}) %all-reduce.7.cloned.1.call-update) | async-done | bytes 286736
  265.8 228.1 %all-gather.8.cloned.1.call-done = f32[32,2240,112]{1,2,0:T(8,128)} async-done(((f32[1,2240,112]{1,2,0:T(8,128)}), f32[32,2240,112]{1,2,0:T(8,128)}) %all-gather.8.cloned.1.call-update) | async-done | bytes 32112656 | tf_op jit(solution)/shard_map/all_gather | solution.py:22
  493.9 230.8 %while.16 = (s32[]{:T(128)}, f32[2240,112]{1,0:T(8,128)}, f32[2240]{0:T(1024)S(1)}, s32[]{:T(128)}, f32[32,2240,112]{1,2,0:T(8,128)}, /*index=5*/f32[32,2240]{1,0:T(8,128)}, s32[]{:T(128)}, s32[]{:T(128)}) while((s32[]{:T(128)}, f32[2240,112]{1,0:T(8,128)}, f32[2240]{0:T(1024)S(1)}, s32[]{:T(128)}, f32[32,2240,112]{1,2,0:T(8,128)}, ...), condition=%wide.region_4.5_spmd.clone, body=%wide.region_3.4_spmd.clone.sunk | while | flops 759364 | bytes 7069555 | solution.py:32
  731.5 4.2 reshape.84
  735.7 6.1 reshape.86
  741.7 15.0 %all_to_all.15 = bf16[8,2,17920]{2,1,0:T(2,128)(2,1)S(1)} all-to-all(bf16[8,2,17920]{2,1,0:T(2,128)(2,1)S(1)} %reshape.86), channel_id=1, replica_groups=mesh['blk'=32,'tile'=8] {'tile'}, dimensions={0} | all-to-all | bytes 1146880 | tf_op jit(solution)/shard_map/all_to_all | solution.py:87
  756.7 4.4 reshape.87
  761.1 9.4 copy.47
  770.5 6.4 fusion.5
  777.0 56.6 %reduce-scatter.3.cloned.1.call-done = f32[4,2,16,2240]{3,2,1,0:T(8,128)} async-done(((f32[32,2,16,2240]{3,2,1,0:T(8,128)}), f32[4,2,16,2240]{3,2,1,0:T(8,128)}) %reduce-scatter.3.cloned.1.call-update) | async-done | bytes 1146896 | tf_op jit(solution)/shard_map/reduce_scatter | solution.py:92
  836.1 5.9 copy.56
  842.0 30.5 %all-gather.6.cloned.1.call-done = bf16[32,2,16,2240]{3,2,1,0:T(8,128)(2,1)} async-done(((bf16[4,2,16,2240]{3,2,1,0:T(8,128)(2,1)}), bf16[32,2,16,2240]{3,2,1,0:T(8,128)(2,1)}) %all-gather.6.cloned.1.call-update) | async-done | bytes 4587536 | tf_op jit(solution)/shard_map/all_gather | solution.py:101
  872.4 9.7 multiply_convert_fusion
  882.2 4.5 reshape.67
  888.7 6.5 add_convert_fusion
  895.2 3.5 collective-permute-start.2
  898.7 48.3 %collective-permute-done.2 = bf16[32,2,16,2,512]{4,2,1,0,3:T(8,128)(2,1)S(1)} collective-permute-done((bf16[32,2,16,2,512]{4,2,1,0,3:T(8,128)(2,1)S(1)}, bf16[32,2,16,2,512]{4,2,1,0,3:T(8,128)(2,1)S(1)}, u32[]{:S(2)}, u32[]{:S(2)}) %collective-permute-start.2) | collective-permute-done | bytes 2097184 | tf_op jit(solution)/shard_map/ppermute | solution.py:38
  948.5 4.6 convolution_convert_fusion
  953.1 40.8 %reduce-scatter.5.cloned.1.call-done = bf16[4,2,16,2240]{3,2,1,0:T(8,128)(2,1)} async-done(((bf16[32,2,16,2240]{3,2,1,0:T(8,128)(2,1)}), bf16[4,2,16,2240]{3,2,1,0:T(8,128)(2,1)}) %reduce-scatter.5.cloned.1.call-update) | async-done | bytes 573456 | tf_op jit(solution)/shard_map/reduce_scatter | solution.py:117
  (219 shorter events, 271.9 us)
Async XLA Ops:
  7.4 941.1 %copy-start = (bf16[512,2240]{0,1:T(8,128)(2,1)S(1)}, bf16[512,2240]{0,1:T(8,128)(2,1)}, u32[]{:S(2)}) copy-start(bf16[512,2240]{0,1:T(8,128)(2,1)} %param.17) | copy-start | bytes 6881284
  7.4 80.6 %all-reduce.5.cloned.1.call-start = ((), (), s32[]{:S(2)}) async-start(), calls=%async_computation.3 | async-start | bytes 2293760 | tf_op jit(solution)/shard_map/psum | solution.py:78
  16.7 101.2 %copy-start.7 = (u32[256]{0:T(256)S(1)}, u32[256]{0:T(256)}, u32[]{:S(2)}) copy-start(u32[256]{0:T(256)} %constant.72) | copy-start | bytes 3076
  16.7 247.3 %all-reduce.7.cloned.1.call-start = ((), (), s32[]{:S(2)}) async-start(), calls=%async_computation.7 | async-start | bytes 573440
  90.6 35.2 %copy-start.1 = (f32[2240,112]{1,0:T(8,128)S(1)}, f32[2240,112]{1,0:T(8,128)}, u32[]{:S(2)}) copy-start(f32[2240,112]{1,0:T(8,128)} %all-reduce.5.cloned.1.call-done) | copy-start | bytes 3010564
  90.6 32.6 %collective-permute-start = (f32[2240,112]{0,1:T(8,128)}, f32[2240,112]{0,1:T(8,128)}, u32[]{:S(2)}, u32[]{:S(2)}) collective-permute-start(f32[2240,112]{0,1:T(8,128)} %copy.39), channel_id=1, source_target_pairs={{0,8},{8,0},{16,24},{24,16},{32,40},{40,32},{48,56},{56,48},{64,72... | collective-permute-start | bytes 3010568 | tf_op jit(solution)/shard_map/ppermute | solution.py:17
  117.3 3.7 collective-permute-start.1
  123.1 370.8 %all-gather.8.cloned.1.call-start = ((), (), s32[]{:S(2)}) async-start(), calls=%async_computation.8 | async-start | bytes 34062336 | tf_op jit(solution)/shard_map/all_gather | solution.py:22
  130.8 702.7 %reduce-scatter.3.cloned.1.call-start = ((), (), s32[]{:S(2)}) async-start(), calls=%async_computation.4 | async-start | bytes 10616832 | tf_op jit(solution)/shard_map/reduce_scatter | solution.py:92
  727.1 2.3 copy-start.3
  776.9 56.7 %copy-start.4 = (bf16[4,2,16,2240]{3,2,1,0:T(8,128)(2,1)S(1)}, bf16[4,2,16,2240]{3,2,1,0:T(8,128)(2,1)}, u32[]{:S(2)}) copy-start(bf16[4,2,16,2240]{3,2,1,0:T(8,128)(2,1)} %param.11) | copy-start | bytes 1720324
  776.9 95.5 %all-gather.6.cloned.1.call-start = ((), (), s32[]{:S(2)}) async-start(), calls=%async_computation.5 | async-start | bytes 5308416 | tf_op jit(solution)/shard_map/all_gather | solution.py:101
  835.8 158.2 %reduce-scatter.5.cloned.1.call-start = ((), (), s32[]{:S(2)}) async-start(), calls=%async_computation.6 | async-start | bytes 5308416 | tf_op jit(solution)/shard_map/reduce_scatter | solution.py:117
  836.0 5.9 copy-start.5
  888.7 10.0 copy-start.6
  895.2 51.8 %collective-permute-start.2 = (bf16[32,2,16,2,512]{4,2,1,0,3:T(8,128)(2,1)S(1)}, bf16[32,2,16,2,512]{4,2,1,0,3:T(8,128)(2,1)S(1)}, u32[]{:S(2)}, u32[]{:S(2)}) collective-permute-start(bf16[32,2,16,2,512]{4,2,1,0,3:T(8,128)(2,1)S(1)} %add_convert_fusion), channel_id=1, source_target_pairs={{0,8},{8,16},{16,24},{24,32},{32,40},{40,48},{48,56},{56,64},{64,7... | collective-permute-start | bytes 6291464 | tf_op jit(solution)/shard_map/ppermute | solution.py:38
  953.1 40.9 %copy-start.2 = (bf16[4,2,16,2240]{3,2,1,0:T(8,128)(2,1)S(1)}, bf16[4,2,16,2240]{3,2,1,0:T(8,128)(2,1)}, u32[]{:S(2)}) copy-start(bf16[4,2,16,2240]{3,2,1,0:T(8,128)(2,1)} %add_convert_fusion.2) | copy-start | bytes 1720324
Sparse Core Ops, SparseCore 0:
  16.8 71.0 all-reduce.4
  777.0 56.4 reduce-scatter.2
  835.9 36.4 all-gather.5
  953.2 40.6 reduce-scatter.4
Sparse Core Ops, SparseCore 1:
  123.2 140.7 all-reduce.6
  266.4 227.4 all-gather.7
where the time goes:
time: 1010 us; the launch traced here: 1000 us
  waiting for transfers between devices  604 us (60%)
  local copies, waits for them, and re-layouts  211 us (21%)
  other arithmetic  98.3 us (10%)
  blocking collectives  38.9 us (4%)
  matrix products  27.6 us (3%)
  between operations  15.4 us (2%)
    all_gather x1, waiting for transfers between devices, carried_in(): everything = jax.tree.map(lambda part: lax.all_gather(part, axis), x)  228 us
    dynamic_slice x96, local copies, waits for them, and re-layouts, step(): new = combine(before, jax.tree.map(lambda part: part[k], everything))  154 us
    unnamed x7, waiting for transfers between devices  127 us
    select_n x64, other arithmetic, step(): return jax.tree.map(lambda a, b: jnp.where(reached, a, b), new, before)  75.7 us
    psum x1, waiting for transfers between devices, on_device(): group_parts = lax.psum((local_kv, local_z), 'tile')  71.2 us
    reduce_scatter x1, waiting for transfers between devices, on_device(): lax.psum_scatter(product.reshape(row_count * lax.axis_size('tile'), frame...  56.6 us
    ppermute x1, waiting for transfers between devices, shifted(): return lax.ppermute(x, axis, pairs)  48.3 us
    reduce_scatter x1, waiting for transfers between devices, on_device(): lax.psum_scatter(product.reshape(lax.axis_size('tile') * row_count, frame...  40.8 us
  transfers between devices with their start and end apart: 9, of which 8 were waited for; matrix products, arithmetic and copies ran while one was open for 3% of the time, Pallas kernels for 0%

commit v1 on v0

v1 whole, which is shorter than its diff:
```python
import functools

import jax
import jax.numpy as jnp
from jax import lax
from jax.experimental import pallas as pl
from jax.experimental.pallas import tpu as pltpu
from jax.sharding import PartitionSpec as P

HEADS = 20
HEAD_DIM = 112
D = 2240
TAPS = 3
EPS = 1e-6
LANES = 128
SLABS = 18
SUB = 14
PIECES = 256
BF = jnp.bfloat16
F32 = jnp.float32
MIB = 1 << 20


def slab_of(c):
    first = (LANES * c) // HEAD_DIM
    bound = HEAD_DIM * (first + 1) - LANES * c
    start = (HEAD_DIM * first) // LANES * LANES
    pair = 2 if first + 1 < HEADS else 1
    stop = min(-(-(HEAD_DIM * (first + pair)) // LANES) * LANES, D)
    return first, pair, bound, start, stop, HEAD_DIM * first - start


def kv_kernel(k_ref, v_ref, out_ref, last_ref):
    tokens = k_ref.shape[0]
    key_pos = jnp.maximum(k_ref[...], 0)
    last_ref[...] = jnp.ones((tokens, LANES), BF)
    last_ref[:, : D - LANES * (SLABS - 1)] = v_ref[:, LANES * (SLABS - 1) :]
    lane = lax.broadcasted_iota(jnp.int32, (HEAD_DIM, LANES), 1)
    over_tokens = (((0,), (0,)), ((), ()))
    for c in range(SLABS):
        first, pair, bound, start, stop, offset = slab_of(c)
        values = last_ref[...] if c == SLABS - 1 else v_ref[:, LANES * c : LANES * (c + 1)]
        product = lax.dot_general(
            key_pos[:, start:stop], values, over_tokens, preferred_element_type=F32
        )
        tile = product[offset : offset + HEAD_DIM]
        if pair == 2:
            tile = jnp.where(lane < bound, tile, product[offset + HEAD_DIM : offset + 2 * HEAD_DIM])
        if c == SLABS - 1:
            sums = lax.dot_general(
                key_pos, jnp.ones((tokens, LANES), BF), over_tokens, preferred_element_type=F32
            )
            tile = jnp.where(lane < bound, tile, 0.0)
            for h in range(HEADS):
                tile = jnp.where(
                    lane == bound + h, sums[HEAD_DIM * h : HEAD_DIM * (h + 1)], tile
                )
        out_ref[SUB * c : SUB * (c + 1)] = tile.reshape(SUB, 8, LANES).astype(BF)
    rest = PIECES - SUB * SLABS
    out_ref[SUB * SLABS :] = jnp.zeros((rest, 8, LANES), BF)


def prefix_kernel(in_ref, out_ref):
    per_block = 16

    def block(b, total):
        here = in_ref[pl.ds(b * per_block, per_block)].astype(F32)
        total = total + jnp.sum(here, axis=0)
        out_ref[pl.ds(b * per_block, per_block)] = jnp.broadcast_to(
            total.astype(BF)[None], (per_block, 8, LANES)
        )
        return total

    lax.fori_loop(0, PIECES // per_block, block, jnp.zeros((8, LANES), F32))


def hidden_kernel(q_ref, state_ref, stream_ref, w_hbm, hid0_ref, hid1_ref, w_ref, att_ref, sem):
    copy = pltpu.make_async_copy(w_hbm, w_ref, sem)
    copy.start()
    tokens = q_ref.shape[0]
    query_pos = jnp.maximum(q_ref[...], 0)
    lane = lax.broadcasted_iota(jnp.int32, (HEAD_DIM, LANES), 1)
    tile_of = lambda c: state_ref[SUB * c : SUB * (c + 1)].astype(F32).reshape(HEAD_DIM, LANES)
    sums = tile_of(SLABS - 1)
    z_lane = D - LANES * (SLABS - 1)
    for c in range(SLABS):
        first, pair, bound, start, stop, offset = slab_of(c)
        tile = tile_of(c)
        weights = []
        for which in range(2):
            rows = []
            if offset > 0:
                rows.append(jnp.zeros((offset, LANES), F32))
            for k in range(pair):
                if which == 0:
                    part = tile
                else:
                    h = z_lane + first + k
                    part = jnp.broadcast_to(sums[:, h : h + 1], (HEAD_DIM, LANES))
                inside = (lane < bound) if k == 0 else (lane >= bound)
                rows.append(jnp.where(inside, part, 0.0))
            left = stop - start - offset - pair * HEAD_DIM
            if left > 0:
                rows.append(jnp.zeros((left, LANES), F32))
            weights.append(jnp.concatenate(rows, axis=0))
        weight = jnp.concatenate(weights, axis=1).astype(BF)
        both = jnp.dot(query_pos[:, start:stop], weight, preferred_element_type=F32)
        attended = (both[:, :LANES] / (both[:, LANES:] + EPS)).astype(BF)
        width = min(LANES, D - LANES * c)
        att_ref[:, LANES * c : LANES * c + width] = attended[:, :width]
    copy.wait()
    step = 256
    for n in range(0, D, step):
        cols = slice(n, min(n + step, D))
        out = jnp.dot(att_ref[...], w_ref[:, cols], preferred_element_type=F32)
        out = (out + stream_ref[:, cols].astype(F32)).astype(BF)
        for r in range(tokens // 32):
            hid0_ref[16 * r : 16 * r + 16, cols] = out[32 * r : 32 * r + 16]
            hid1_ref[16 * r : 16 * r + 16, cols] = out[32 * r + 16 : 32 * r + 32]


def spatial_kernel(hid_ref, w_ref, taps_ref, out_ref, act_ref):
    tokens, cols = hid_ref.shape[0], 16
    width = w_ref.shape[1]
    product = jnp.dot(hid_ref[...], w_ref[...], preferred_element_type=F32)
    act = (product * jax.nn.sigmoid(product)).astype(BF).astype(F32)
    act_ref[:cols] = jnp.zeros((cols, width), F32)
    act_ref[cols + tokens :] = jnp.zeros((cols, width), F32)
    act_ref[cols : cols + tokens] = act
    taps = taps_ref[...]
    chunk = 32
    col = lax.broadcasted_iota(jnp.int32, (chunk, width), 0) % cols
    for r in range(0, tokens, chunk):
        rows = [act_ref[r + cols * a : r + cols * a + chunk] for a in range(3)]
        left, mid, right = (
            rows[0] * taps[b : b + 1] + rows[1] * taps[3 + b : 4 + b] + rows[2] * taps[6 + b : 7 + b]
            for b in range(3)
        )
        left = jnp.where(col == 0, 0.0, pltpu.roll(left, 1, 0))
        right = jnp.where(col == cols - 1, 0.0, pltpu.roll(right, chunk - 1, 0))
        out_ref[r : r + chunk] = (left + mid + right).astype(BF)


def point_kernel(place_ref, now_ref, one_ref, two_ref, taps_ref, w_ref, mine_ref, other_ref):
    half = w_ref.shape[0]
    taps = taps_ref[...]
    mix = now_ref[...].astype(F32) * taps[0:1]
    mix = mix + one_ref[...].astype(F32) * taps[1:2]
    mix = mix + two_ref[...].astype(F32) * taps[2:3]
    gate = mix[:, half:]
    gated = (mix[:, :half] * (gate * jax.nn.sigmoid(gate))).astype(BF)
    out = jnp.dot(gated, w_ref[...], preferred_element_type=F32).astype(BF)
    y, core = place_ref[0], place_ref[1]
    i = pl.program_id(0)
    rows = out.shape[0] // 4
    for k in range(4):
        target = 4 * i + k
        slot = (target // 2 - y + 4) % 4

        @pl.when(core == k % 2)
        def _():
            mine_ref[slot] = out[rows * k : rows * (k + 1)]

        @pl.when(core != k % 2)
        def _():
            other_ref[slot] = out[rows * k : rows * (k + 1)]


def params(mib):
    return pltpu.CompilerParams(vmem_limit_bytes=mib * MIB)


VMEM = pl.BlockSpec(memory_space=pltpu.VMEM)


def on_device(
    stream_in, queries, key_rows, value_rows, w_output, w_inner, w_down, spatial_taps, temporal_taps
):
    row_count, frames, col_count, width = queries.shape
    tokens = row_count * frames * col_count
    flat = lambda a: a.reshape(tokens, width)
    chan = w_inner.shape[2]
    peers = lax.axis_size("tile")
    place = lax.axis_index("tile")
    where_am_i = jnp.stack([place // 2, place % 2]).astype(jnp.int32)

    w_out_whole = lax.all_gather(w_output, "tile", axis=0, tiled=True)
    w_flat = w_inner.reshape(width, 2 * chan)
    taps_s = spatial_taps.reshape(9, 2 * chan)
    taps_t = temporal_taps.reshape(TAPS, 2 * chan)

    pieces = jax.ShapeDtypeStruct((PIECES, 8, LANES), BF)
    parts = pl.pallas_call(
        kv_kernel,
        out_shape=pieces,
        in_specs=[VMEM] * 2,
        out_specs=VMEM,
        scratch_shapes=[pltpu.VMEM((tokens, LANES), BF)],
        compiler_params=params(40),
    )(flat(key_rows), flat(value_rows))
    everyone = ("blk", "tile")
    parts = lax.all_to_all(parts, everyone, 0, 0, tiled=True)
    sums = pl.pallas_call(
        prefix_kernel, out_shape=pieces, in_specs=[VMEM], out_specs=VMEM, compiler_params=params(40)
    )(parts)
    state = lax.all_to_all(sums, everyone, 0, 0, tiled=True)

    frame_rows = row_count * col_count
    hidden = pl.pallas_call(
        hidden_kernel,
        out_shape=[jax.ShapeDtypeStruct((frame_rows, width), BF)] * 2,
        in_specs=[VMEM, VMEM, VMEM, pl.BlockSpec(memory_space=pl.ANY)],
        out_specs=[VMEM, VMEM],
        scratch_shapes=[
            pltpu.VMEM((width, width), BF),
            pltpu.VMEM((tokens, width), BF),
            pltpu.SemaphoreType.DMA,
        ],
        compiler_params=params(48),
    )(flat(queries), state, flat(stream_in), w_out_whole)

    whole_rows = peers * frame_rows
    block = 256
    spatial_call = pl.pallas_call(
        spatial_kernel,
        out_shape=jax.ShapeDtypeStruct((whole_rows, 2 * chan), BF),
        grid=(2 * chan // block,),
        in_specs=[
            pl.BlockSpec((whole_rows, width), lambda i: (0, 0)),
            pl.BlockSpec((width, block), lambda i: (0, i)),
            pl.BlockSpec((9, block), lambda i: (0, i)),
        ],
        out_specs=pl.BlockSpec((whole_rows, block), lambda i: (0, i)),
        scratch_shapes=[pltpu.VMEM((whole_rows + 2 * col_count, block), F32)],
        compiler_params=params(40),
    )
    row_block = 256
    point_call = pl.pallas_call(
        point_kernel,
        out_shape=[jax.ShapeDtypeStruct((4, frame_rows, width), BF)] * 2,
        grid=(whole_rows // row_block,),
        in_specs=[pl.BlockSpec(memory_space=pltpu.SMEM)]
        + [pl.BlockSpec((row_block, 2 * chan), lambda i: (i, 0))] * 3
        + [
            pl.BlockSpec((TAPS, 2 * chan), lambda i: (0, 0)),
            pl.BlockSpec((chan, width), lambda i: (0, 0)),
        ],
        out_specs=[pl.BlockSpec((4, frame_rows, width), lambda i: (0, 0, 0))] * 2,
        compiler_params=params(40),
    )

    blocks = lax.axis_size("blk")
    next_frames = [(i, i + 1) for i in range(blocks - 1)]
    other_core = [(i, i ^ 1) for i in range(peers)]
    spatial, halo = [None, None], [None, None]
    for f in (1, 0):
        whole = lax.all_gather(hidden[f], "tile", axis=0, tiled=True)
        spatial[f] = spatial_call(whole, w_flat, taps_s)
        halo[f] = lax.ppermute(spatial[f], "blk", next_frames)

    def reduced(f):
        now, one, two = (spatial[1], spatial[0], halo[1]) if f else (spatial[0], halo[1], halo[0])
        mine, other = point_call(where_am_i, now, one, two, taps_t, w_down)
        from_core = lax.ppermute(other, "tile", other_core)
        total = mine.astype(F32) + from_core.astype(F32)
        result = hidden[f].astype(F32) + total[0]
        for k in range(1, 4):
            pairs = [(i, (i + 2 * k) % peers) for i in range(peers)]
            result = result + lax.ppermute(total[k].astype(BF), "tile", pairs).astype(F32)
        return result.astype(BF).reshape(row_count, 1, col_count, width)

    late = reduced(1)
    early = reduced(0)
    return jnp.concatenate([early, late], axis=1)


def solution(mesh):
    in_specs = (
        P("tile", "blk", None, None),
        P("tile", "blk", None, None),
        P("tile", "blk", None, None),
        P("tile", "blk", None, None),
        P("tile", None),
        P(None, None, "tile"),
        P("tile", None),
        P(None, None, None, "tile"),
        P(None, None, "tile"),
    )
    out_specs = P("tile", "blk", None, None)
    return jax.shard_map(
        on_device, mesh=mesh, in_specs=in_specs, out_specs=out_specs, check_vma=False
    )
```

time: 1010 us -> 236 us (0.23)
  waiting for transfers between devices: 604 us -> 98.3 us
  local copies, waits for them, and re-layouts: 211 us -> 19 us
  other arithmetic: 98.3 us -> 3.91 us
  matrix products: 27.6 us -> 0 us
  Pallas kernels: 0 us -> 26 us
  blocking collectives: 38.9 us -> 59.6 us
    all_gather x2 -> x3, waiting for transfers between devices: 259 us -> 48.6 us  [the longest x2 35.4 us: on_device(): whole = lax.all_gather(hidden[f], 'tile', axis=0, tiled=True)]
    dynamic_slice x96 -> x0, local copies, waits for them, and re-layouts: 154 us -> none  [step(): new = combine(before, jax.tree.map(lambda part: part[k], everything))]
    unnamed x7 -> x3, waiting for transfers between devices: 127 us -> 1.41 us
    reduce_scatter x2 -> x0, waiting for transfers between devices: 97.4 us -> none  [the longest x1 56.6 us: on_device(): lax.psum_scatter(product.reshape(row_count * lax.axis_size('tile'), frame...]
    select_n x64 -> x0, other arithmetic: 75.7 us -> none  [step(): return jax.tree.map(lambda a, b: jnp.where(reached, a, b), new, before)]
    psum x1 -> x0, waiting for transfers between devices: 71.2 us -> none  [on_device(): group_parts = lax.psum((local_kv, local_z), 'tile')]
    all_to_all x1 -> x2, blocking collectives: 15 us -> 59.6 us  [the longest x1 33.6 us: on_device(): parts = lax.all_to_all(parts, everyone, 0, 0, tiled=True)]
    dot_general x6 -> x0, matrix products: 27.6 us -> none  [the longest x1 9.71 us: on_device(): jnp.dot(portion.reshape(-1, model_width), w_flat, preferred_element_type=...]
  transfers between devices with their start and end apart: 9 -> 13, of which waited for: 8 -> 9; matrix products, arithmetic and copies ran while one was open for 3% -> 5% of each run, Pallas kernels for 0% -> 7%
where the time goes in v1:
time: 236 us; the launch traced here: 235 us
  waiting for transfers between devices  98.3 us (42%)
  blocking collectives  59.6 us (25%)
  Pallas kernels  26 us (11%)
  local copies, waits for them, and re-layouts  19 us (8%)
  starting transfers between devices  15.1 us (6%)
  between operations  13.3 us (6%)
  other arithmetic  3.91 us (2%)
    all_gather x2, waiting for transfers between devices, on_device(): whole = lax.all_gather(hidden[f], 'tile', axis=0, tiled=True)  35.4 us
    all_to_all x1, blocking collectives, on_device(): parts = lax.all_to_all(parts, everyone, 0, 0, tiled=True)  33.6 us
    all_to_all x1, blocking collectives, on_device(): state = lax.all_to_all(sums, everyone, 0, 0, tiled=True)  26 us
    ppermute x2, waiting for transfers between devices, on_device(): halo[f] = lax.ppermute(spatial[f], 'blk', next_frames)  25.9 us
    ppermute x6, waiting for transfers between devices, reduced(): lax.ppermute(total[k].astype(BF), 'tile', pairs).astype(F32)  22.4 us
    unnamed x25, local copies, waits for them, and re-layouts  18.8 us
    all_gather x1, waiting for transfers between devices, on_device(): w_out_whole = lax.all_gather(w_output, 'tile', axis=0, tiled=True)  13.2 us
    pallas_call x2, Pallas kernels, on_device(): spatial[f] = spatial_call(whole, w_flat, taps_s)  10.8 us
  transfers between devices with their start and end apart: 13, of which 9 were waited for; matrix products, arithmetic and copies ran while one was open for 5% of the time, Pallas kernels for 7%

profile of v1, /device:TPU:2, one launch (start us, length us, event | category | flops | bytes accessed | tf_op | source)
XLA Modules:
  0.0 235.1 jit_solution(9067200185596393576)
XLA Ops:
  10.2 33.6 %all_to_all.10.in_ref = bf16[256,8,128]{2,1,0:T(8,128)(2,1)S(1)} all-to-all(bf16[256,8,128]{2,1,0:T(8,128)(2,1)S(1)} %shard_map.91), channel_id=1, replica_groups=mesh['blk'=32,'tile'=8] {'blk','tile'}, dimensions={0} | all-to-all | bytes 1048576 | tf_op jit(solution)/shard_map/all_to_all | solution.py:202
  44.1 26.0 %all_to_all.11.state_ref = bf16[256,8,128]{2,1,0:T(8,128)(2,1)S(1)} all-to-all(bf16[256,8,128]{2,1,0:T(8,128)(2,1)S(1)} %shard_map.92), channel_id=1, replica_groups=mesh['blk'=32,'tile'=8] {'blk','tile'}, dimensions={0} | all-to-all | bytes 1048576 | tf_op jit(solution)/shard_map/all_to_all | solution.py:206
  70.1 13.2 %all-gather.4.cloned.1.call-done.w_hbm = bf16[2240,2240]{1,0:T(8,128)(2,1)} async-done(((bf16[280,2240]{1,0:T(8,128)(2,1)}), bf16[2240,2240]{1,0:T(8,128)(2,1)}) %all-gather.4.cloned.1.call-update) | async-done | bytes 10035216 | tf_op jit(solution)/shard_map/all_gather | solution.py:187
  83.3 7.2 %shard_map.93 = (bf16[64,2240]{1,0:T(8,128)(2,1)}, bf16[64,2240]{1,0:T(8,128)(2,1)}) custom-call(bf16[128,2240]{1,0:T(8,128)(2,1)S(1)} %bitcast.60, bf16[256,8,128]{2,1,0:T(8,128)(2,1)S(1)} %all_to_all.11.state_ref, bf16[128,2240]{1,0:T(8,128)(2,1)S(1)} %bitcast.61, bf16[2240,2240]{1,0:T(8,128)(2,1)} %all-gather.4.cloned.1.call-done.w_hbm), custom_call_target="tpu_custom_call" | custom-call | tf_op jit(solution)/shard_map/pallas_call | solution.py:209
  91.3 5.9 %copy.14 = bf16[280,8,2,512]{3,1,2,0:T(8,128)(2,1)} copy(bf16[280,8,2,512]{3,2,1,0:T(2,128)(2,1)} %bitcast.66) | data formatting | bytes 9175040
  97.2 20.6 %all-gather.8.cloned.1.call-done.hid_ref = bf16[512,2240]{1,0:T(8,128)(2,1)} async-done(((bf16[64,2240]{1,0:T(8,128)(2,1)}), bf16[512,2240]{1,0:T(8,128)(2,1)}) %all-gather.8.cloned.1.call-update) | async-done | bytes 2293776 | tf_op jit(solution)/shard_map/all_gather | solution.py:257
  117.8 2.3 copy-done
  121.8 5.4 %shard_map.95.now_ref = bf16[512,1024]{1,0:T(8,128)(2,1)S(1)} custom-call(bf16[512,2240]{1,0:T(8,128)(2,1)S(1)} %copy-done.3, bf16[2240,1024]{1,0:T(8,128)(2,1)S(1)} %bitcast.56, f32[9,1024]{1,0:T(8,128)S(1)} %bitcast.58), custom_call_target="tpu_custom_call" | custom-call | tf_op jit(solution)/shard_map/pallas_call | solution.py:258
  127.2 3.5 %collective-permute-start = (bf16[512,1024]{1,0:T(8,128)(2,1)S(1)}, bf16[512,1024]{1,0:T(8,128)(2,1)}, u32[]{:S(2)}, u32[]{:S(2)}) collective-permute-start(bf16[512,1024]{1,0:T(8,128)(2,1)S(1)} %shard_map.95.now_ref), channel_id=1, source_target_pairs={{0,8},{8,16},{16,24},{24,32},{32,40},{40,48},{48,56},{56,64},{64,7... | collective-permute-start | bytes 3145736 | tf_op jit(solution)/shard_map/ppermute | solution.py:259
  130.7 2.9 %copy.10.w_ref = bf16[512,2240]{1,0:T(8,128)(2,1)S(1)} copy(bf16[512,2240]{0,1:T(8,128)(2,1)} %param.15) | data formatting | bytes 4587520 | tf_op args[6]
  133.7 14.8 %all-gather.6.cloned.1.call-done.hid_ref = bf16[512,2240]{1,0:T(8,128)(2,1)} async-done(((bf16[64,2240]{1,0:T(8,128)(2,1)}), bf16[512,2240]{1,0:T(8,128)(2,1)}) %all-gather.6.cloned.1.call-update) | async-done | bytes 2293776 | tf_op jit(solution)/shard_map/all_gather | solution.py:257
  148.4 2.3 copy-done.1
  152.4 5.4 %shard_map.94.now_ref.one_ref = bf16[512,1024]{1,0:T(8,128)(2,1)S(1)} custom-call(bf16[512,2240]{1,0:T(8,128)(2,1)S(1)} %copy-done.2, bf16[2240,1024]{1,0:T(8,128)(2,1)S(1)} %bitcast.57, f32[9,1024]{1,0:T(8,128)S(1)} %bitcast.59), custom_call_target="tpu_custom_call" | custom-call | tf_op jit(solution)/shard_map/pallas_call | solution.py:258
  157.8 3.5 %shard_map.97 = (bf16[4,64,2240]{2,1,0:T(8,128)(2,1)S(1)}, bf16[4,64,2240]{2,1,0:T(8,128)(2,1)S(1)}) custom-call(s32[2]{0:T(128)S(1)} %pad_add_fusion.place_ref, bf16[512,1024]{1,0:T(8,128)(2,1)S(1)} %shard_map.95.now_ref, bf16[512,1024]{1,0:T(8,128)(2,1)S(1)} %shard_map.94.now_ref.one_ref, bf16[512,1024]{1,0:T(8,128)(2,1)} %collective-permute-done.one_ref.two_ref, ...), custom_call_target="tpu_custom_call" | custom-call | tf_op jit(solution)/shard_map/pallas_call | solution.py:263
  161.8 3.4 %collective-permute-start.1 = (bf16[512,1024]{1,0:T(8,128)(2,1)S(1)}, bf16[512,1024]{1,0:T(8,128)(2,1)S(1)}, u32[]{:S(2)}, u32[]{:S(2)}) collective-permute-start(bf16[512,1024]{1,0:T(8,128)(2,1)S(1)} %shard_map.94.now_ref.one_ref), channel_id=1, source_target_pairs={{0,8},{8,16},{16,24},{24,32},{32,40},{40,48},{48,56},{56,64},{64,7... | collective-permute-start | bytes 3145736 | tf_op jit(solution)/shard_map/ppermute | solution.py:259
  165.3 25.9 %collective-permute-done.1.two_ref = bf16[512,1024]{1,0:T(8,128)(2,1)S(1)} collective-permute-done((bf16[512,1024]{1,0:T(8,128)(2,1)S(1)}, bf16[512,1024]{1,0:T(8,128)(2,1)S(1)}, u32[]{:S(2)}, u32[]{:S(2)}) %collective-permute-start.1) | collective-permute-done | bytes 1048608 | tf_op jit(solution)/shard_map/ppermute | solution.py:259
  191.1 3.5 %shard_map.96 = (bf16[4,64,2240]{2,1,0:T(8,128)(2,1)S(1)}, bf16[4,64,2240]{2,1,0:T(8,128)(2,1)S(1)}) custom-call(s32[2]{0:T(128)S(1)} %pad_add_fusion.place_ref, bf16[512,1024]{1,0:T(8,128)(2,1)S(1)} %shard_map.94.now_ref.one_ref, bf16[512,1024]{1,0:T(8,128)(2,1)} %collective-permute-done.one_ref.two_ref, ...), custom_call_target="tpu_custom_call" | custom-call | tf_op jit(solution)/shard_map/pallas_call | solution.py:263
  195.2 1.8 collective-permute-start.9
  199.4 2.3 collective-permute-start.5
  203.1 7.3 %collective-permute-done.9 = bf16[64,2240]{1,0:T(8,128)(2,1)S(1)} collective-permute-done((bf16[64,2240]{1,0:T(8,128)(2,1)S(1)}, bf16[64,2240]{1,0:T(8,128)(2,1)S(1)}, u32[]{:S(2)}, u32[]{:S(2)}) %collective-permute-start.9) | collective-permute-done | bytes 286752 | tf_op jit(solution)/shard_map/ppermute | solution.py:269
  210.4 4.4 %collective-permute-done.7 = bf16[64,2240]{1,0:T(8,128)(2,1)S(1)} collective-permute-done((bf16[64,2240]{1,0:T(8,128)(2,1)S(1)}, bf16[64,2240]{1,0:T(8,128)(2,1)S(1)}, u32[]{:S(2)}, u32[]{:S(2)}) %collective-permute-start.7) | collective-permute-done | bytes 286752 | tf_op jit(solution)/shard_map/ppermute | solution.py:269
  215.9 1.8 collective-permute-done.5
  217.7 3.3 %collective-permute-done.4 = bf16[64,2240]{1,0:T(8,128)(2,1)S(1)} collective-permute-done((bf16[64,2240]{1,0:T(8,128)(2,1)S(1)}, bf16[64,2240]{1,0:T(8,128)(2,1)S(1)}, u32[]{:S(2)}, u32[]{:S(2)}) %collective-permute-start.4) | collective-permute-done | bytes 286752 | tf_op jit(solution)/shard_map/ppermute | solution.py:269
  221.1 5.5 %collective-permute-done.3 = bf16[64,2240]{1,0:T(8,128)(2,1)S(1)} collective-permute-done((bf16[64,2240]{1,0:T(8,128)(2,1)S(1)}, bf16[64,2240]{1,0:T(8,128)(2,1)S(1)}, u32[]{:S(2)}, u32[]{:S(2)}) %collective-permute-start.3) | collective-permute-done | bytes 286752 | tf_op jit(solution)/shard_map/ppermute | solution.py:269
  (47 shorter events, 16.1 us)
Async XLA Ops:
  6.5 76.8 %all-gather.4.cloned.1.call-start = ((), (), s32[]{:S(2)}) async-start(), calls=%async_computation.2 | async-start | bytes 11612160 | tf_op jit(solution)/shard_map/all_gather | solution.py:187
  7.3 110.6 %all-gather.8.cloned.1.call-start = ((), (), s32[]{:S(2)}) async-start(), calls=%async_computation.4 | async-start | bytes 2654208 | tf_op jit(solution)/shard_map/all_gather | solution.py:257
  7.3 1.1 copy-start.6
  8.4 1.1 copy-start.7
  9.4 73.9 %copy-start.4 = (bf16[4,2,16,2240]{3,2,1,0:T(8,128)(2,1)S(1)}, bf16[4,2,16,2240]{3,2,1,0:T(8,128)(2,1)}, u32[]{:S(2)}) copy-start(bf16[4,2,16,2240]{3,2,1,0:T(8,128)(2,1)} %param.10) | copy-start | bytes 1720324
  9.4 73.9 %copy-start.5 = (bf16[4,2,16,2240]{3,2,1,0:T(8,128)(2,1)S(1)}, bf16[4,2,16,2240]{3,2,1,0:T(8,128)(2,1)}, u32[]{:S(2)}) copy-start(bf16[4,2,16,2240]{3,2,1,0:T(8,128)(2,1)} %param.9) | copy-start | bytes 1720324
  90.5 57.9 %all-gather.6.cloned.1.call-start = ((), (), s32[]{:S(2)}) async-start(), calls=%async_computation.3 | async-start | bytes 2654208 | tf_op jit(solution)/shard_map/all_gather | solution.py:257
  91.3 5.9 %copy-start.8 = (f32[3,3,2,512]{3,2,1,0:T(2,128)S(1)}, f32[3,3,2,512]{3,2,1,0:T(2,128)}, u32[]{:S(2)}) copy-start(f32[3,3,2,512]{3,2,1,0:T(2,128)} %param.16) | copy-start | bytes 110596
  117.8 2.3 copy-start
  120.1 1.7 copy-start.3
  121.8 8.9 %copy-start.9 = (f32[3,2,512]{2,1,0:T(2,128)S(1)}, f32[3,2,512]{2,1,0:T(2,128)}, u32[]{:S(2)}) copy-start(f32[3,2,512]{2,1,0:T(2,128)} %param.17) | copy-start | bytes 36868
  127.2 30.6 %collective-permute-start = (bf16[512,1024]{1,0:T(8,128)(2,1)S(1)}, bf16[512,1024]{1,0:T(8,128)(2,1)}, u32[]{:S(2)}, u32[]{:S(2)}) collective-permute-start(bf16[512,1024]{1,0:T(8,128)(2,1)S(1)} %shard_map.95.now_ref), channel_id=1, source_target_pairs={{0,8},{8,16},{16,24},{24,32},{32,40},{40,48},{48,56},{56,64},{64,7... | collective-permute-start | bytes 3145736 | tf_op jit(solution)/shard_map/ppermute | solution.py:259
  148.4 2.3 copy-start.1
  150.7 1.7 copy-start.2
  161.3 33.4 %collective-permute-start.6 = (bf16[4,64,2240]{2,1,0:T(8,128)(2,1)S(1)}, bf16[4,64,2240]{2,1,0:T(8,128)(2,1)S(1)}, u32[]{:S(2)}, u32[]{:S(2)}) collective-permute-start(bf16[4,64,2240]{2,1,0:T(8,128)(2,1)S(1)} %get-tuple-element.16), channel_id=1, source_target_pairs={{0,1},{1,0},{2,3},{3,2},{4,5},{5,4},{6,7},{7,6},{8,9},{9,8},{10,11... | collective-permute-start | bytes 3440648 | tf_op jit(solution)/shard_map/ppermute | solution.py:264
  161.8 29.3 %collective-permute-start.1 = (bf16[512,1024]{1,0:T(8,128)(2,1)S(1)}, bf16[512,1024]{1,0:T(8,128)(2,1)S(1)}, u32[]{:S(2)}, u32[]{:S(2)}) collective-permute-start(bf16[512,1024]{1,0:T(8,128)(2,1)S(1)} %shard_map.94.now_ref.one_ref), channel_id=1, source_target_pairs={{0,8},{8,16},{16,24},{24,32},{32,40},{40,48},{48,56},{56,64},{64,7... | collective-permute-start | bytes 3145736 | tf_op jit(solution)/shard_map/ppermute | solution.py:259
  194.6 4.3 %collective-permute-start.2 = (bf16[4,64,2240]{2,1,0:T(8,128)(2,1)S(1)}, bf16[4,64,2240]{2,1,0:T(8,128)(2,1)S(1)}, u32[]{:S(2)}, u32[]{:S(2)}) collective-permute-start(bf16[4,64,2240]{2,1,0:T(8,128)(2,1)S(1)} %get-tuple-element.14), channel_id=1, source_target_pairs={{0,1},{1,0},{2,3},{3,2},{4,5},{5,4},{6,7},{7,6},{8,9},{9,8},{10,11... | collective-permute-start | bytes 3440648 | tf_op jit(solution)/shard_map/ppermute | solution.py:264
  195.2 15.2 %collective-permute-start.9 = (bf16[64,2240]{1,0:T(8,128)(2,1)S(1)}, bf16[64,2240]{1,0:T(8,128)(2,1)S(1)}, u32[]{:S(2)}, u32[]{:S(2)}) collective-permute-start(bf16[64,2240]{1,0:T(8,128)(2,1)S(1)} %get-tuple-element.25), channel_id=1, source_target_pairs={{0,6},{1,7},{2,0},{3,1},{4,2},{5,3},{6,4},{7,5},{8,14},{9,15},{10,... | collective-permute-start | bytes 860168 | tf_op jit(solution)/shard_map/ppermute | solution.py:269
  197.0 13.4 %collective-permute-start.8 = (bf16[64,2240]{1,0:T(8,128)(2,1)S(1)}, bf16[64,2240]{1,0:T(8,128)(2,1)S(1)}, u32[]{:S(2)}, u32[]{:S(2)}) collective-permute-start(bf16[64,2240]{1,0:T(8,128)(2,1)S(1)} %get-tuple-element.26), channel_id=1, source_target_pairs={{0,4},{1,5},{2,6},{3,7},{4,0},{5,1},{6,2},{7,3},{8,12},{9,13},{10,... | collective-permute-start | bytes 860168 | tf_op jit(solution)/shard_map/ppermute | solution.py:269
  197.9 16.9 %collective-permute-start.7 = (bf16[64,2240]{1,0:T(8,128)(2,1)S(1)}, bf16[64,2240]{1,0:T(8,128)(2,1)S(1)}, u32[]{:S(2)}, u32[]{:S(2)}) collective-permute-start(bf16[64,2240]{1,0:T(8,128)(2,1)S(1)} %get-tuple-element.24), channel_id=1, source_target_pairs={{0,2},{1,3},{2,4},{3,5},{4,6},{5,7},{6,0},{7,1},{8,10},{9,11},{10,... | collective-permute-start | bytes 860168 | tf_op jit(solution)/shard_map/ppermute | solution.py:269
  199.4 18.4 %collective-permute-start.5 = (bf16[64,2240]{1,0:T(8,128)(2,1)S(1)}, bf16[64,2240]{1,0:T(8,128)(2,1)S(1)}, u32[]{:S(2)}, u32[]{:S(2)}) collective-permute-start(bf16[64,2240]{1,0:T(8,128)(2,1)S(1)} %get-tuple-element.22), channel_id=1, source_target_pairs={{0,6},{1,7},{2,0},{3,1},{4,2},{5,3},{6,4},{7,5},{8,14},{9,15},{10,... | collective-permute-start | bytes 860168 | tf_op jit(solution)/shard_map/ppermute | solution.py:269
  201.6 19.4 %collective-permute-start.4 = (bf16[64,2240]{1,0:T(8,128)(2,1)S(1)}, bf16[64,2240]{1,0:T(8,128)(2,1)S(1)}, u32[]{:S(2)}, u32[]{:S(2)}) collective-permute-start(bf16[64,2240]{1,0:T(8,128)(2,1)S(1)} %get-tuple-element.23), channel_id=1, source_target_pairs={{0,4},{1,5},{2,6},{3,7},{4,0},{5,1},{6,2},{7,3},{8,12},{9,13},{10,... | collective-permute-start | bytes 860168 | tf_op jit(solution)/shard_map/ppermute | solution.py:269
  210.4 16.2 %collective-permute-start.3 = (bf16[64,2240]{1,0:T(8,128)(2,1)S(1)}, bf16[64,2240]{1,0:T(8,128)(2,1)S(1)}, u32[]{:S(2)}, u32[]{:S(2)}) collective-permute-start(bf16[64,2240]{1,0:T(8,128)(2,1)S(1)} %get-tuple-element.21), channel_id=1, source_target_pairs={{0,2},{1,3},{2,4},{3,5},{4,6},{5,7},{6,0},{7,1},{8,10},{9,11},{10,... | collective-permute-start | bytes 860168 | tf_op jit(solution)/shard_map/ppermute | solution.py:269
Sparse Core Ops, SparseCore 0:
  9.2 74.1 all-gather.3
  90.7 27.1 all-gather.7
  119.7 28.7 all-gather.5

commit v2 on v1

--- a/solution.py
+++ b/solution.py
@@ -74,10 +74,7 @@
     lax.fori_loop(0, PIECES // per_block, block, jnp.zeros((8, LANES), F32))
 
 
-def hidden_kernel(q_ref, state_ref, stream_ref, w_hbm, hid0_ref, hid1_ref, w_ref, att_ref, sem):
-    copy = pltpu.make_async_copy(w_hbm, w_ref, sem)
-    copy.start()
-    tokens = q_ref.shape[0]
+def attend_kernel(q_ref, state_ref, att_ref):
     query_pos = jnp.maximum(q_ref[...], 0)
     lane = lax.broadcasted_iota(jnp.int32, (HEAD_DIM, LANES), 1)
     tile_of = lambda c: state_ref[SUB * c : SUB * (c + 1)].astype(F32).reshape(HEAD_DIM, LANES)
@@ -108,21 +105,36 @@
         attended = (both[:, :LANES] / (both[:, LANES:] + EPS)).astype(BF)
         width = min(LANES, D - LANES * c)
         att_ref[:, LANES * c : LANES * c + width] = attended[:, :width]
-    copy.wait()
-    step = 256
-    for n in range(0, D, step):
-        cols = slice(n, min(n + step, D))
+
+
+def hidden_kernel(att_ref, stream_ref, w_hbm, both_ref, early_ref, w_ref, sems):
+    tokens = att_ref.shape[0]
+    step = 384
+    spans = [(n, min(n + step, D)) for n in range(0, D, step)]
+    copies = []
+    for i, (n, stop) in enumerate(spans):
+        span = pl.ds(n, stop - n)
+        copies.append(pltpu.make_async_copy(w_hbm.at[:, span], w_ref.at[:, span], sems.at[i]))
+    for copy in copies:
+        copy.start()
+    for copy, (n, stop) in zip(copies, spans):
+        cols = slice(n, stop)
+        copy.wait()
         out = jnp.dot(att_ref[...], w_ref[:, cols], preferred_element_type=F32)
         out = (out + stream_ref[:, cols].astype(F32)).astype(BF)
         for r in range(tokens // 32):
-            hid0_ref[16 * r : 16 * r + 16, cols] = out[32 * r : 32 * r + 16]
-            hid1_ref[16 * r : 16 * r + 16, cols] = out[32 * r + 16 : 32 * r + 32]
+            rows = slice(16 * r, 16 * r + 16)
+            both_ref[0, rows, cols] = out[32 * r : 32 * r + 16]
+            early_ref[rows, cols] = out[32 * r : 32 * r + 16]
+            both_ref[1, rows, cols] = out[32 * r + 16 : 32 * r + 32]
 
 
 def spatial_kernel(hid_ref, w_ref, taps_ref, out_ref, act_ref):
-    tokens, cols = hid_ref.shape[0], 16
+    groups, rows, model = hid_ref.shape
+    tokens, cols = groups * rows, 16
     width = w_ref.shape[1]
-    product = jnp.dot(hid_ref[...], w_ref[...], preferred_element_type=F32)
+    hid = hid_ref[...].reshape(tokens, model)
+    product = jnp.dot(hid, w_ref[...], preferred_element_type=F32)
     act = (product * jax.nn.sigmoid(product)).astype(BF).astype(F32)
     act_ref[:cols] = jnp.zeros((cols, width), F32)
     act_ref[cols + tokens :] = jnp.zeros((cols, width), F32)
@@ -131,9 +143,9 @@
     chunk = 32
     col = lax.broadcasted_iota(jnp.int32, (chunk, width), 0) % cols
     for r in range(0, tokens, chunk):
-        rows = [act_ref[r + cols * a : r + cols * a + chunk] for a in range(3)]
+        near = [act_ref[r + cols * a : r + cols * a + chunk] for a in range(3)]
         left, mid, right = (
-            rows[0] * taps[b : b + 1] + rows[1] * taps[3 + b : 4 + b] + rows[2] * taps[6 + b : 7 + b]
+            near[0] * taps[b : b + 1] + near[1] * taps[3 + b : 4 + b] + near[2] * taps[6 + b : 7 + b]
             for b in range(3)
         )
         left = jnp.where(col == 0, 0.0, pltpu.roll(left, 1, 0))
@@ -166,6 +178,25 @@
             other_ref[slot] = out[rows * k : rows * (k + 1)]
 
 
+def sum_kernel(count, mine_ref, other_ref, hidden_ref, *refs):
+    kept_ref, *sends = refs[count:]
+    total = lambda k: mine_ref[k].astype(F32) + other_ref[k].astype(F32)
+    kept_ref[...] = hidden_ref[...].astype(F32) + total(0)
+    for k, send in enumerate(sends):
+        send[...] = total(k + 1).astype(BF)
+
+
+def final_kernel(early_ref, late_ref, *refs):
+    pieces, out_ref = refs[:6], refs[6]
+    for f, kept in enumerate((early_ref, late_ref)):
+        total = kept[...]
+        for piece in pieces[3 * f : 3 * f + 3]:
+            total = total + piece[...].astype(F32)
+        out = total.astype(BF)
+        for r in range(out_ref.shape[0]):
+            out_ref[r, f] = out[16 * r : 16 * r + 16]
+
+
 def params(mib):
     return pltpu.CompilerParams(vmem_limit_bytes=mib * MIB)
 
@@ -205,35 +236,43 @@
     )(parts)
     state = lax.all_to_all(sums, everyone, 0, 0, tiled=True)
 
+    anywhere = pl.BlockSpec(memory_space=pl.ANY)
     frame_rows = row_count * col_count
-    hidden = pl.pallas_call(
+    attended = pl.pallas_call(
+        attend_kernel,
+        out_shape=jax.ShapeDtypeStruct((tokens, width), BF),
+        in_specs=[VMEM, VMEM],
+        out_specs=VMEM,
+        compiler_params=params(40),
+    )(flat(queries), state)
+    one_frame = jax.ShapeDtypeStruct((frame_rows, width), BF)
+    hidden, early = pl.pallas_call(
         hidden_kernel,
-        out_shape=[jax.ShapeDtypeStruct((frame_rows, width), BF)] * 2,
-        in_specs=[VMEM, VMEM, VMEM, pl.BlockSpec(memory_space=pl.ANY)],
+        out_shape=[jax.ShapeDtypeStruct((2, frame_rows, width), BF), one_frame],
+        in_specs=[VMEM, VMEM, anywhere],
         out_specs=[VMEM, VMEM],
-        scratch_shapes=[
-            pltpu.VMEM((width, width), BF),
-            pltpu.VMEM((tokens, width), BF),
-            pltpu.SemaphoreType.DMA,
-        ],
-        compiler_params=params(48),
-    )(flat(queries), state, flat(stream_in), w_out_whole)
+        scratch_shapes=[pltpu.VMEM((width, width), BF), pltpu.SemaphoreType.DMA((6,))],
+        compiler_params=params(52),
+    )(attended, flat(stream_in), w_out_whole)
 
     whole_rows = peers * frame_rows
     block = 256
-    spatial_call = pl.pallas_call(
-        spatial_kernel,
-        out_shape=jax.ShapeDtypeStruct((whole_rows, 2 * chan), BF),
-        grid=(2 * chan // block,),
-        in_specs=[
-            pl.BlockSpec((whole_rows, width), lambda i: (0, 0)),
-            pl.BlockSpec((width, block), lambda i: (0, i)),
-            pl.BlockSpec((9, block), lambda i: (0, i)),
-        ],
-        out_specs=pl.BlockSpec((whole_rows, block), lambda i: (0, i)),
-        scratch_shapes=[pltpu.VMEM((whole_rows + 2 * col_count, block), F32)],
-        compiler_params=params(40),
-    )
+
+    def spatial_call(whole, f):
+        return pl.pallas_call(
+            spatial_kernel,
+            out_shape=jax.ShapeDtypeStruct((whole_rows, 2 * chan), BF),
+            grid=(2 * chan // block,),
+            in_specs=[
+                pl.BlockSpec((peers, None, frame_rows, width), lambda i: (0, f, 0, 0)),
+                pl.BlockSpec((width, block), lambda i: (0, i)),
+                pl.BlockSpec((9, block), lambda i: (0, i)),
+            ],
+            out_specs=pl.BlockSpec((whole_rows, block), lambda i: (0, i)),
+            scratch_shapes=[pltpu.VMEM((whole_rows + 2 * col_count, block), F32)],
+            compiler_params=params(52),
+        )(whole, w_flat, taps_s)
+
     row_block = 256
     point_call = pl.pallas_call(
         point_kernel,
@@ -252,26 +291,40 @@
     blocks = lax.axis_size("blk")
     next_frames = [(i, i + 1) for i in range(blocks - 1)]
     other_core = [(i, i ^ 1) for i in range(peers)]
-    spatial, halo = [None, None], [None, None]
-    for f in (1, 0):
-        whole = lax.all_gather(hidden[f], "tile", axis=0, tiled=True)
-        spatial[f] = spatial_call(whole, w_flat, taps_s)
-        halo[f] = lax.ppermute(spatial[f], "blk", next_frames)
-
-    def reduced(f):
-        now, one, two = (spatial[1], spatial[0], halo[1]) if f else (spatial[0], halo[1], halo[0])
+    ahead = [[(i, (i + 2 * k) % peers) for i in range(peers)] for k in range(4)]
+
+    before_early = lax.ppermute(early, "blk", next_frames)
+    whole = lax.all_gather(hidden, "tile", axis=0)
+    before_whole = lax.all_gather(before_early[None], "tile", axis=0)
+    late_sp = spatial_call(whole, 1)
+    before_late_sp = lax.ppermute(late_sp, "blk", next_frames)
+    early_sp = spatial_call(whole, 0)
+    before_early_sp = spatial_call(before_whole, 0)
+
+    def reduced(f, now, one, two, needed):
         mine, other = point_call(where_am_i, now, one, two, taps_t, w_down)
         from_core = lax.ppermute(other, "tile", other_core)
-        total = mine.astype(F32) + from_core.astype(F32)
-        result = hidden[f].astype(F32) + total[0]
-        for k in range(1, 4):
-            pairs = [(i, (i + 2 * k) % peers) for i in range(peers)]
-            result = result + lax.ppermute(total[k].astype(BF), "tile", pairs).astype(F32)
-        return result.astype(BF).reshape(row_count, 1, col_count, width)
-
-    late = reduced(1)
-    early = reduced(0)
-    return jnp.concatenate([early, late], axis=1)
+        kept, *sends = pl.pallas_call(
+            functools.partial(sum_kernel, len(needed)),
+            out_shape=[jax.ShapeDtypeStruct((frame_rows, width), F32)] + [one_frame] * 3,
+            grid=(1,),
+            in_specs=[pl.BlockSpec((4, frame_rows, width), lambda i: (0, 0, 0))] * 2
+            + [pl.BlockSpec((None, frame_rows, width), lambda i: (f, 0, 0))]
+            + [anywhere] * len(needed),
+            out_specs=[pl.BlockSpec((frame_rows, width), lambda i: (0, 0))] * 4,
+            compiler_params=params(20),
+        )(mine, from_core, hidden, *needed)
+        return kept, [lax.ppermute(part, "tile", ahead[k + 1]) for k, part in enumerate(sends)]
+
+    late_kept, late_back = reduced(1, late_sp, early_sp, before_late_sp, [])
+    early_kept, early_back = reduced(0, early_sp, before_late_sp, before_early_sp, late_back[:1])
+    return pl.pallas_call(
+        final_kernel,
+        out_shape=jax.ShapeDtypeStruct(stream_in.shape, BF),
+        in_specs=[VMEM] * 8,
+        out_specs=VMEM,
+        compiler_params=params(20),
+    )(early_kept, late_kept, *early_back, *late_back)
 
 
 def solution(mesh):

time: 236 us -> 220 us (0.932)
  waiting for transfers between devices: 98.3 us -> 76.5 us
  Pallas kernels: 26 us -> 42.2 us
  local copies, waits for them, and re-layouts: 19 us -> 12.7 us
  other arithmetic: 3.91 us -> 0.08 us
    all_gather x2, waiting for transfers between devices: 35.4 us -> 16.1 us  [the longest x1 16.1 us: on_device(): whole = lax.all_gather(hidden, 'tile', axis=0)]
    pallas_call x3 -> x8, Pallas kernels: 17.9 us -> 32.8 us  [the longest x3 21.6 us: spatial_call(): pl.pallas_call(spatial_kernel, out_shape=jax.ShapeDtypeStruct((whole_rows...]
    unnamed x25 -> x21, local copies, waits for them, and re-layouts: 18.8 us -> 12.7 us
  transfers between devices with their start and end apart: 13 -> 13, of which waited for: 9 -> 7; matrix products, arithmetic and copies ran while one was open for 5% -> 4% of each run, Pallas kernels for 7% -> 16%
where the time goes in v2:
time: 220 us
  waiting for transfers between devices  76.5 us (35%)
  blocking collectives  59.6 us (27%)
  Pallas kernels  42.2 us (19%)
  starting transfers between devices  15.3 us (7%)
  between operations  13.3 us (6%)
  local copies, waits for them, and re-layouts  12.7 us (6%)
    all_to_all x1, blocking collectives, on_device(): parts = lax.all_to_all(parts, everyone, 0, 0, tiled=True)  33.6 us
    all_to_all x1, blocking collectives, on_device(): state = lax.all_to_all(sums, everyone, 0, 0, tiled=True)  26 us
    pallas_call x3, Pallas kernels, spatial_call(): pl.pallas_call(spatial_kernel, out_shape=jax.ShapeDtypeStruct((whole_rows...  21.6 us
    ppermute x6, waiting for transfers between devices, reduced(): lax.ppermute(part, 'tile', ahead[k + 1])  21.3 us
    all_gather x1, waiting for transfers between devices, on_device(): whole = lax.all_gather(hidden, 'tile', axis=0)  16.1 us
    ppermute x1, waiting for transfers between devices, on_device(): before_late_sp = lax.ppermute(late_sp, 'blk', next_frames)  15.9 us
    unnamed x21, local copies, waits for them, and re-layouts  12.7 us
    all_gather x1, waiting for transfers between devices, on_device(): w_out_whole = lax.all_gather(w_output, 'tile', axis=0, tiled=True)  12.5 us
  transfers between devices with their start and end apart: 13, of which 7 were waited for; matrix products, arithmetic and copies ran while one was open for 4% of the time, Pallas kernels for 16%

profile of v2, /device:TPU:2, one launch (start us, length us, event | category | flops | bytes accessed | tf_op | source)
XLA Modules:
  0.0 219.5 jit_solution(15271038842891226263)
XLA Ops:
  10.2 33.6 %all_to_all.10.in_ref = bf16[256,8,128]{2,1,0:T(8,128)(2,1)S(1)} all-to-all(bf16[256,8,128]{2,1,0:T(8,128)(2,1)S(1)} %shard_map.91), channel_id=1, replica_groups=mesh['blk'=32,'tile'=8] {'blk','tile'}, dimensions={0} | all-to-all | bytes 1048576 | tf_op jit(solution)/shard_map/all_to_all | solution.py:233
  44.1 26.0 %all_to_all.11.state_ref = bf16[256,8,128]{2,1,0:T(8,128)(2,1)S(1)} all-to-all(bf16[256,8,128]{2,1,0:T(8,128)(2,1)S(1)} %shard_map.92), channel_id=1, replica_groups=mesh['blk'=32,'tile'=8] {'blk','tile'}, dimensions={0} | all-to-all | bytes 1048576 | tf_op jit(solution)/shard_map/all_to_all | solution.py:237
  70.9 12.5 %all-gather.6.cloned.1.call-done.w_hbm = bf16[2240,2240]{1,0:T(8,128)(2,1)} async-done(((bf16[280,2240]{1,0:T(8,128)(2,1)}), bf16[2240,2240]{1,0:T(8,128)(2,1)}) %all-gather.6.cloned.1.call-update) | async-done | bytes 10035216 | tf_op jit(solution)/shard_map/all_gather | solution.py:218
  83.3 6.5 %shard_map.94 = (bf16[2,64,2240]{2,1,0:T(8,128)(2,1)}, bf16[64,2240]{1,0:T(8,128)(2,1)S(1)}) custom-call(bf16[128,2240]{1,0:T(8,128)(2,1)S(1)} %shard_map.93.att_ref, bf16[128,2240]{1,0:T(8,128)(2,1)} %bitcast.31, bf16[2240,2240]{1,0:T(8,128)(2,1)} %all-gather.6.cloned.1.call-done.w_hbm), custom_call_target="tpu_custom_call" | custom-call | tf_op jit(solution)/shard_map/pallas_call | solution.py:249
  89.9 3.3 %collective-permute-start.1 = (bf16[64,2240]{1,0:T(8,128)(2,1)S(1)}, bf16[64,2240]{1,0:T(8,128)(2,1)S(1)}, u32[]{:S(2)}, u32[]{:S(2)}) collective-permute-start(bf16[64,2240]{1,0:T(8,128)(2,1)S(1)} %get-tuple-element.20), channel_id=1, source_target_pairs={{0,8},{8,16},{16,24},{24,32},{32,40},{40,48},{48,56},{56,64},{64,7... | collective-permute-start | bytes 860168 | tf_op jit(solution)/shard_map/ppermute | solution.py:296
  93.2 9.9 %collective-permute-done.1 = bf16[64,2240]{1,0:T(8,128)(2,1)S(1)} collective-permute-done((bf16[64,2240]{1,0:T(8,128)(2,1)S(1)}, bf16[64,2240]{1,0:T(8,128)(2,1)S(1)}, u32[]{:S(2)}, u32[]{:S(2)}) %collective-permute-start.1) | collective-permute-done | bytes 286752 | tf_op jit(solution)/shard_map/ppermute | solution.py:296
  103.8 5.9 %copy.14 = bf16[280,8,2,512]{3,1,2,0:T(8,128)(2,1)} copy(bf16[280,8,2,512]{3,2,1,0:T(2,128)(2,1)} %bitcast.29) | data formatting | bytes 9175040
  109.8 16.1 %all-gather.8.cloned.1.call-done = bf16[16,64,2240]{2,1,0:T(8,128)(2,1)} async-done(((bf16[2,64,2240]{2,1,0:T(8,128)(2,1)}), bf16[16,64,2240]{2,1,0:T(8,128)(2,1)}) %all-gather.8.cloned.1.call-update) | async-done | bytes 4587536 | tf_op jit(solution)/shard_map/all_gather | solution.py:297
  125.8 7.7 %shard_map.96.now_ref = bf16[512,1024]{1,0:T(8,128)(2,1)} custom-call(bf16[8,2,64,2240]{3,2,1,0:T(8,128)(2,1)} %bitcast.27, bf16[2240,1024]{1,0:T(8,128)(2,1)} %bitcast.24, f32[9,1024]{1,0:T(8,128)S(1)} %bitcast.16), custom_call_target="tpu_custom_call" | custom-call | tf_op jit(solution)/shard_map/pallas_call | solution.py:262
  133.5 3.6 %collective-permute-start = (bf16[512,1024]{1,0:T(8,128)(2,1)}, bf16[512,1024]{1,0:T(8,128)(2,1)}, u32[]{:S(2)}, u32[]{:S(2)}) collective-permute-start(bf16[512,1024]{1,0:T(8,128)(2,1)} %shard_map.96.now_ref), channel_id=1, source_target_pairs={{0,8},{8,16},{16,24},{24,32},{32,40},{40,48},{48,56},{56,64},{64,7... | collective-permute-start | bytes 3145736 | tf_op jit(solution)/shard_map/ppermute | solution.py:300
  137.2 2.9 %copy.12.w_ref = bf16[512,2240]{1,0:T(8,128)(2,1)S(1)} copy(bf16[512,2240]{0,1:T(8,128)(2,1)} %param.15) | data formatting | bytes 4587520 | tf_op args[6]
  140.1 7.0 %shard_map.95.now_ref.one_ref = bf16[512,1024]{1,0:T(8,128)(2,1)S(1)} custom-call(bf16[8,2,64,2240]{3,2,1,0:T(8,128)(2,1)} %bitcast.28, bf16[2240,1024]{1,0:T(8,128)(2,1)} %bitcast.25, f32[9,1024]{1,0:T(8,128)S(1)} %bitcast.17), custom_call_target="tpu_custom_call" | custom-call | tf_op jit(solution)/shard_map/pallas_call | solution.py:262
  147.2 15.9 %collective-permute-done.one_ref.two_ref = bf16[512,1024]{1,0:T(8,128)(2,1)} collective-permute-done((bf16[512,1024]{1,0:T(8,128)(2,1)}, bf16[512,1024]{1,0:T(8,128)(2,1)}, u32[]{:S(2)}, u32[]{:S(2)}) %collective-permute-start) | collective-permute-done | bytes 1048608 | tf_op jit(solution)/shard_map/ppermute | solution.py:300
  163.1 4.7 %shard_map.99 = (bf16[4,64,2240]{2,1,0:T(8,128)(2,1)S(1)}, bf16[4,64,2240]{2,1,0:T(8,128)(2,1)}) custom-call(s32[2]{0:T(128)S(1)} %pad_add_fusion.place_ref, bf16[512,1024]{1,0:T(8,128)(2,1)} %shard_map.96.now_ref, bf16[512,1024]{1,0:T(8,128)(2,1)S(1)} %shard_map.95.now_ref.one_ref, bf16[512,1024]{1,0:T(8,128)(2,1)} %collective-permute-done.one_ref.two_ref, ...), custom_call_target="tpu_custom_call" | custom-call | tf_op jit(solution)/shard_map/pallas_call | solution.py:305
  168.8 6.9 %shard_map.97.two_ref = bf16[512,1024]{1,0:T(8,128)(2,1)S(1)} custom-call(bf16[8,1,64,2240]{3,2,1,0:T(8,128)(2,1)} %bitcast.30, bf16[2240,1024]{1,0:T(8,128)(2,1)} %bitcast.26, f32[9,1024]{1,0:T(8,128)S(1)} %bitcast.18), custom_call_target="tpu_custom_call" | custom-call | tf_op jit(solution)/shard_map/pallas_call | solution.py:262
  175.8 3.6 %shard_map.98 = (bf16[4,64,2240]{2,1,0:T(8,128)(2,1)S(1)}, bf16[4,64,2240]{2,1,0:T(8,128)(2,1)S(1)}) custom-call(s32[2]{0:T(128)S(1)} %pad_add_fusion.place_ref, bf16[512,1024]{1,0:T(8,128)(2,1)S(1)} %shard_map.95.now_ref.one_ref, bf16[512,1024]{1,0:T(8,128)(2,1)} %collective-permute-done.one_ref.two_ref, bf16[512,1024]{1,0:T(8,128)(2,1)S(1)} %shard_map.97.two_ref, ...), custom_call_target="tpu_custom_call" | custom-call | tf_op jit(solution)/shard_map/pallas_call | solution.py:305
  180.0 1.6 shard_map.100
  182.1 1.8 collective-permute-start.8
  184.0 2.0 collective-permute-start.9
  186.0 12.6 %collective-permute-done.4.refs_0_.refs_3_ = bf16[64,2240]{1,0:T(8,128)(2,1)S(1)} collective-permute-done((bf16[64,2240]{1,0:T(8,128)(2,1)S(1)}, bf16[64,2240]{1,0:T(8,128)(2,1)S(1)}, u32[]{:S(2)}, u32[]{:S(2)}) %collective-permute-start.4) | collective-permute-done | bytes 286752 | tf_op jit(solution)/shard_map/ppermute | solution.py:317
  198.6 1.3 shard_map.101
  200.8 2.4 %collective-permute-start.7 = (bf16[64,2240]{1,0:T(8,128)(2,1)S(1)}, bf16[64,2240]{1,0:T(8,128)(2,1)S(1)}, u32[]{:S(2)}, u32[]{:S(2)}) collective-permute-start(bf16[64,2240]{1,0:T(8,128)(2,1)S(1)} %get-tuple-element.30), channel_id=1, source_target_pairs={{0,6},{1,7},{2,0},{3,1},{4,2},{5,3},{6,4},{7,5},{8,14},{9,15},{10,... | collective-permute-start | bytes 860168 | tf_op jit(solution)/shard_map/ppermute | solution.py:317
  203.2 7.9 %collective-permute-done.5.refs_0_ = bf16[64,2240]{1,0:T(8,128)(2,1)S(1)} collective-permute-done((bf16[64,2240]{1,0:T(8,128)(2,1)S(1)}, bf16[64,2240]{1,0:T(8,128)(2,1)S(1)}, u32[]{:S(2)}, u32[]{:S(2)}) %collective-permute-start.5) | collective-permute-done | bytes 286752 | tf_op jit(solution)/shard_map/ppermute | solution.py:317
  211.9 1.1 shard_map.102
  (41 shorter events, 9.6 us)
Async XLA Ops:
  6.5 76.8 %all-gather.6.cloned.1.call-start = ((), (), s32[]{:S(2)}) async-start(), calls=%async_computation.2 | async-start | bytes 11612160 | tf_op jit(solution)/shard_map/all_gather | solution.py:218
  7.3 118.6 %all-gather.8.cloned.1.call-start = ((), (), s32[]{:S(2)}) async-start(), calls=%async_computation.3 | async-start | bytes 5308416 | tf_op jit(solution)/shard_map/all_gather | solution.py:297
  7.3 1.1 copy-start.2
  8.4 1.1 copy-start.3
  9.4 60.7 %copy-start.4 = (bf16[4,2,16,2240]{3,2,1,0:T(8,128)(2,1)S(1)}, bf16[4,2,16,2240]{3,2,1,0:T(8,128)(2,1)}, u32[]{:S(2)}) copy-start(bf16[4,2,16,2240]{3,2,1,0:T(8,128)(2,1)} %param.10) | copy-start | bytes 1720324
  89.9 79.0 %all-gather.10.cloned.1.call-start = ((), (), s32[]{:S(2)}) async-start(), calls=%async_computation.4 | async-start | bytes 2654208 | tf_op jit(solution)/shard_map/all_gather | solution.py:298
  89.9 13.2 %collective-permute-start.1 = (bf16[64,2240]{1,0:T(8,128)(2,1)S(1)}, bf16[64,2240]{1,0:T(8,128)(2,1)S(1)}, u32[]{:S(2)}, u32[]{:S(2)}) collective-permute-start(bf16[64,2240]{1,0:T(8,128)(2,1)S(1)} %get-tuple-element.20), channel_id=1, source_target_pairs={{0,8},{8,16},{16,24},{24,32},{32,40},{40,48},{48,56},{56,64},{64,7... | collective-permute-start | bytes 860168 | tf_op jit(solution)/shard_map/ppermute | solution.py:296
  103.1 0.7 copy-start.5
  103.8 5.9 %copy-start.6 = (f32[3,3,2,512]{3,2,1,0:T(2,128)S(1)}, f32[3,3,2,512]{3,2,1,0:T(2,128)}, u32[]{:S(2)}) copy-start(f32[3,3,2,512]{3,2,1,0:T(2,128)} %param.16) | copy-start | bytes 110596
  125.8 11.3 %copy-start.7 = (f32[3,2,512]{2,1,0:T(2,128)S(1)}, f32[3,2,512]{2,1,0:T(2,128)}, u32[]{:S(2)}) copy-start(f32[3,2,512]{2,1,0:T(2,128)} %param.17) | copy-start | bytes 36868
  133.5 29.6 %collective-permute-start = (bf16[512,1024]{1,0:T(8,128)(2,1)}, bf16[512,1024]{1,0:T(8,128)(2,1)}, u32[]{:S(2)}, u32[]{:S(2)}) collective-permute-start(bf16[512,1024]{1,0:T(8,128)(2,1)} %shard_map.96.now_ref), channel_id=1, source_target_pairs={{0,8},{8,16},{16,24},{24,32},{32,40},{40,48},{48,56},{56,64},{64,7... | collective-permute-start | bytes 3145736 | tf_op jit(solution)/shard_map/ppermute | solution.py:300
  167.8 1.0 copy-start
  168.8 11.1 %collective-permute-start.3 = (bf16[4,64,2240]{2,1,0:T(8,128)(2,1)}, bf16[4,64,2240]{2,1,0:T(8,128)(2,1)}, u32[]{:S(2)}, u32[]{:S(2)}) collective-permute-start(bf16[4,64,2240]{2,1,0:T(8,128)(2,1)} %get-tuple-element.24), channel_id=1, source_target_pairs={{0,1},{1,0},{2,3},{3,2},{4,5},{5,4},{6,7},{7,6},{8,9},{9,8},{10,11... | collective-permute-start | bytes 3440648 | tf_op jit(solution)/shard_map/ppermute | solution.py:306
  175.7 4.2 %copy-start.1 = (bf16[4,64,2240]{2,1,0:T(8,128)(2,1)S(1)}, bf16[4,64,2240]{2,1,0:T(8,128)(2,1)}, u32[]{:S(2)}) copy-start(bf16[4,64,2240]{2,1,0:T(8,128)(2,1)} %copy-done) | copy-start | bytes 3440644
  179.4 6.6 %collective-permute-start.2 = (bf16[4,64,2240]{2,1,0:T(8,128)(2,1)S(1)}, bf16[4,64,2240]{2,1,0:T(8,128)(2,1)S(1)}, u32[]{:S(2)}, u32[]{:S(2)}) collective-permute-start(bf16[4,64,2240]{2,1,0:T(8,128)(2,1)S(1)} %get-tuple-element.22), channel_id=1, source_target_pairs={{0,1},{1,0},{2,3},{3,2},{4,5},{5,4},{6,7},{7,6},{8,9},{9,8},{10,11... | collective-permute-start | bytes 3440648 | tf_op jit(solution)/shard_map/ppermute | solution.py:306
  181.6 17.0 %collective-permute-start.4 = (bf16[64,2240]{1,0:T(8,128)(2,1)S(1)}, bf16[64,2240]{1,0:T(8,128)(2,1)S(1)}, u32[]{:S(2)}, u32[]{:S(2)}) collective-permute-start(bf16[64,2240]{1,0:T(8,128)(2,1)S(1)} %get-tuple-element.25), channel_id=1, source_target_pairs={{0,2},{1,3},{2,4},{3,5},{4,6},{5,7},{6,0},{7,1},{8,10},{9,11},{10,... | collective-permute-start | bytes 860168 | tf_op jit(solution)/shard_map/ppermute | solution.py:317
  182.1 21.0 %collective-permute-start.8 = (bf16[64,2240]{1,0:T(8,128)(2,1)S(1)}, bf16[64,2240]{1,0:T(8,128)(2,1)S(1)}, u32[]{:S(2)}, u32[]{:S(2)}) collective-permute-start(bf16[64,2240]{1,0:T(8,128)(2,1)S(1)} %get-tuple-element.31), channel_id=1, source_target_pairs={{0,4},{1,5},{2,6},{3,7},{4,0},{5,1},{6,2},{7,3},{8,12},{9,13},{10,... | collective-permute-start | bytes 860168 | tf_op jit(solution)/shard_map/ppermute | solution.py:317
  184.0 19.2 %collective-permute-start.9 = (bf16[64,2240]{1,0:T(8,128)(2,1)S(1)}, bf16[64,2240]{1,0:T(8,128)(2,1)S(1)}, u32[]{:S(2)}, u32[]{:S(2)}) collective-permute-start(bf16[64,2240]{1,0:T(8,128)(2,1)S(1)} %get-tuple-element.32), channel_id=1, source_target_pairs={{0,6},{1,7},{2,0},{3,1},{4,2},{5,3},{6,4},{7,5},{8,14},{9,15},{10,... | collective-permute-start | bytes 860168 | tf_op jit(solution)/shard_map/ppermute | solution.py:317
  199.8 11.2 %collective-permute-start.5 = (bf16[64,2240]{1,0:T(8,128)(2,1)S(1)}, bf16[64,2240]{1,0:T(8,128)(2,1)S(1)}, u32[]{:S(2)}, u32[]{:S(2)}) collective-permute-start(bf16[64,2240]{1,0:T(8,128)(2,1)S(1)} %get-tuple-element.28), channel_id=1, source_target_pairs={{0,2},{1,3},{2,4},{3,5},{4,6},{5,7},{6,0},{7,1},{8,10},{9,11},{10,... | collective-permute-start | bytes 860168 | tf_op jit(solution)/shard_map/ppermute | solution.py:317
  199.9 11.1 %collective-permute-start.6 = (bf16[64,2240]{1,0:T(8,128)(2,1)S(1)}, bf16[64,2240]{1,0:T(8,128)(2,1)S(1)}, u32[]{:S(2)}, u32[]{:S(2)}) collective-permute-start(bf16[64,2240]{1,0:T(8,128)(2,1)S(1)} %get-tuple-element.29), channel_id=1, source_target_pairs={{0,4},{1,5},{2,6},{3,7},{4,0},{5,1},{6,2},{7,3},{8,12},{9,13},{10,... | collective-permute-start | bytes 860168 | tf_op jit(solution)/shard_map/ppermute | solution.py:317
  200.8 11.1 %collective-permute-start.7 = (bf16[64,2240]{1,0:T(8,128)(2,1)S(1)}, bf16[64,2240]{1,0:T(8,128)(2,1)S(1)}, u32[]{:S(2)}, u32[]{:S(2)}) collective-permute-start(bf16[64,2240]{1,0:T(8,128)(2,1)S(1)} %get-tuple-element.30), channel_id=1, source_target_pairs={{0,6},{1,7},{2,0},{3,1},{4,2},{5,3},{6,4},{7,5},{8,14},{9,15},{10,... | collective-permute-start | bytes 860168 | tf_op jit(solution)/shard_map/ppermute | solution.py:317
Sparse Core Ops, SparseCore 0:
  9.2 74.1 all-gather.5
  90.0 35.8 all-gather.7
  127.7 28.3 all-gather.9

commit v3 on v2

--- a/solution.py
+++ b/solution.py
@@ -107,7 +107,7 @@
         att_ref[:, LANES * c : LANES * c + width] = attended[:, :width]
 
 
-def hidden_kernel(att_ref, stream_ref, w_hbm, both_ref, early_ref, w_ref, sems):
+def hidden_kernel(att_ref, stream_ref, w_hbm, early_ref, late_ref, w_ref, sems):
     tokens = att_ref.shape[0]
     step = 384
     spans = [(n, min(n + step, D)) for n in range(0, D, step)]
@@ -124,16 +124,13 @@
         out = (out + stream_ref[:, cols].astype(F32)).astype(BF)
         for r in range(tokens // 32):
             rows = slice(16 * r, 16 * r + 16)
-            both_ref[0, rows, cols] = out[32 * r : 32 * r + 16]
             early_ref[rows, cols] = out[32 * r : 32 * r + 16]
-            both_ref[1, rows, cols] = out[32 * r + 16 : 32 * r + 32]
-
-
-def spatial_kernel(hid_ref, w_ref, taps_ref, out_ref, act_ref):
-    groups, rows, model = hid_ref.shape
-    tokens, cols = groups * rows, 16
+            late_ref[rows, cols] = out[32 * r + 16 : 32 * r + 32]
+
+
+def depthwise(hid, w_ref, taps_ref, out_ref, act_ref):
+    tokens, cols = hid.shape[0], 16
     width = w_ref.shape[1]
-    hid = hid_ref[...].reshape(tokens, model)
     product = jnp.dot(hid, w_ref[...], preferred_element_type=F32)
     act = (product * jax.nn.sigmoid(product)).astype(BF).astype(F32)
     act_ref[:cols] = jnp.zeros((cols, width), F32)
@@ -153,7 +150,28 @@
         out_ref[r : r + chunk] = (left + mid + right).astype(BF)
 
 
-def point_kernel(place_ref, now_ref, one_ref, two_ref, taps_ref, w_ref, mine_ref, other_ref):
+def spatial_kernel(hid_ref, w_ref, taps_ref, needed_ref, out_ref, act_ref):
+    groups, rows, model = hid_ref.shape
+    depthwise(hid_ref[...].reshape(groups * rows, model), w_ref, taps_ref, out_ref, act_ref)
+
+
+def pieces_kernel(place_ref, *refs):
+    peers = 8
+    pieces, (w_ref, taps_ref, out_ref, act_ref, hid_ref) = refs[:peers], refs[peers:]
+    rows = pieces[0].shape[0]
+
+    @pl.when(pl.program_id(0) == 0)
+    def _():
+        for p, piece in enumerate(pieces):
+            source = 2 * ((place_ref[0] + 4 - p // 2) % 4) + (place_ref[1] + p % 2) % 2
+            hid_ref[pl.ds(pl.multiple_of(source * rows, rows), rows)] = piece[...]
+
+    depthwise(hid_ref[...], w_ref, taps_ref, out_ref, act_ref)
+
+
+def point_kernel(
+    place_ref, now_ref, one_ref, two_ref, taps_ref, w_ref, needed_ref, mine_ref, other_ref
+):
     half = w_ref.shape[0]
     taps = taps_ref[...]
     mix = now_ref[...].astype(F32) * taps[0:1]
@@ -178,12 +196,16 @@
             other_ref[slot] = out[rows * k : rows * (k + 1)]
 
 
-def sum_kernel(count, mine_ref, other_ref, hidden_ref, *refs):
-    kept_ref, *sends = refs[count:]
+def sum_kernel(mine_ref, other_ref, hidden_ref, kept_ref, *sends):
     total = lambda k: mine_ref[k].astype(F32) + other_ref[k].astype(F32)
     kept_ref[...] = hidden_ref[...].astype(F32) + total(0)
     for k, send in enumerate(sends):
         send[...] = total(k + 1).astype(BF)
+
+
+def stack_kernel(one_ref, two_ref, needed_ref, out_ref):
+    out_ref[0] = one_ref[...]
+    out_ref[1] = two_ref[...]
 
 
 def final_kernel(early_ref, late_ref, *refs):
@@ -246,9 +268,9 @@
         compiler_params=params(40),
     )(flat(queries), state)
     one_frame = jax.ShapeDtypeStruct((frame_rows, width), BF)
-    hidden, early = pl.pallas_call(
+    early, late = pl.pallas_call(
         hidden_kernel,
-        out_shape=[jax.ShapeDtypeStruct((2, frame_rows, width), BF), one_frame],
+        out_shape=[one_frame] * 2,
         in_specs=[VMEM, VMEM, anywhere],
         out_specs=[VMEM, VMEM],
         scratch_shapes=[pltpu.VMEM((width, width), BF), pltpu.SemaphoreType.DMA((6,))],
@@ -258,20 +280,37 @@
     whole_rows = peers * frame_rows
     block = 256
 
-    def spatial_call(whole, f):
+    spatial_out = dict(
+        out_shape=jax.ShapeDtypeStruct((whole_rows, 2 * chan), BF),
+        grid=(2 * chan // block,),
+        out_specs=pl.BlockSpec((whole_rows, block), lambda i: (0, i)),
+        compiler_params=params(52),
+    )
+    weight_specs = [
+        pl.BlockSpec((width, block), lambda i: (0, i)),
+        pl.BlockSpec((9, block), lambda i: (0, i)),
+    ]
+    act_scratch = pltpu.VMEM((whole_rows + 2 * col_count, block), F32)
+
+    def spatial_call(whole, f, needed):
         return pl.pallas_call(
             spatial_kernel,
-            out_shape=jax.ShapeDtypeStruct((whole_rows, 2 * chan), BF),
-            grid=(2 * chan // block,),
-            in_specs=[
-                pl.BlockSpec((peers, None, frame_rows, width), lambda i: (0, f, 0, 0)),
-                pl.BlockSpec((width, block), lambda i: (0, i)),
-                pl.BlockSpec((9, block), lambda i: (0, i)),
-            ],
-            out_specs=pl.BlockSpec((whole_rows, block), lambda i: (0, i)),
-            scratch_shapes=[pltpu.VMEM((whole_rows + 2 * col_count, block), F32)],
-            compiler_params=params(52),
-        )(whole, w_flat, taps_s)
+            in_specs=[pl.BlockSpec((peers, None, frame_rows, width), lambda i: (0, f, 0, 0))]
+            + weight_specs
+            + [anywhere],
+            scratch_shapes=[act_scratch],
+            **spatial_out,
+        )(whole, w_flat, taps_s, needed)
+
+    def pieces_call(pieces):
+        return pl.pallas_call(
+            pieces_kernel,
+            in_specs=[pl.BlockSpec(memory_space=pltpu.SMEM)]
+            + [pl.BlockSpec((frame_rows, width), lambda i: (0, 0))] * peers
+            + weight_specs,
+            scratch_shapes=[act_scratch, pltpu.VMEM((whole_rows, width), BF)],
+            **spatial_out,
+        )(where_am_i, *pieces, w_flat, taps_s)
 
     row_block = 256
     point_call = pl.pallas_call(
@@ -283,6 +322,7 @@
         + [
             pl.BlockSpec((TAPS, 2 * chan), lambda i: (0, 0)),
             pl.BlockSpec((chan, width), lambda i: (0, 0)),
+            anywhere,
         ],
         out_specs=[pl.BlockSpec((4, frame_rows, width), lambda i: (0, 0, 0))] * 2,
         compiler_params=params(40),
@@ -293,31 +333,42 @@
     other_core = [(i, i ^ 1) for i in range(peers)]
     ahead = [[(i, (i + 2 * k) % peers) for i in range(peers)] for k in range(4)]
 
+    late_along = [late] + [lax.ppermute(late, "tile", ahead[k]) for k in (1, 2, 3)]
     before_early = lax.ppermute(early, "blk", next_frames)
-    whole = lax.all_gather(hidden, "tile", axis=0)
-    before_whole = lax.all_gather(before_early[None], "tile", axis=0)
-    late_sp = spatial_call(whole, 1)
+    pieces = []
+    for part in late_along:
+        pieces += [part, lax.ppermute(part, "tile", other_core)]
+    stacked = pl.pallas_call(
+        stack_kernel,
+        out_shape=jax.ShapeDtypeStruct((2, frame_rows, width), BF),
+        in_specs=[VMEM, VMEM, anywhere],
+        out_specs=VMEM,
+        compiler_params=params(20),
+    )(early, before_early, late_along[1])
+    whole = lax.all_gather(stacked, "tile", axis=0)
+    late_sp = pieces_call(pieces)
     before_late_sp = lax.ppermute(late_sp, "blk", next_frames)
-    early_sp = spatial_call(whole, 0)
-    before_early_sp = spatial_call(before_whole, 0)
-
-    def reduced(f, now, one, two, needed):
-        mine, other = point_call(where_am_i, now, one, two, taps_t, w_down)
-        from_core = lax.ppermute(other, "tile", other_core)
+    early_sp = spatial_call(whole, 0, late_sp)
+    before_early_sp = spatial_call(whole, 1, early_sp)
+
+    def core_shares(now, one, two, needed):
+        mine, other = point_call(where_am_i, now, one, two, taps_t, w_down, needed)
+        return mine, lax.ppermute(other, "tile", other_core)
+
+    def sums(mine, from_core, rows):
         kept, *sends = pl.pallas_call(
-            functools.partial(sum_kernel, len(needed)),
+            sum_kernel,
             out_shape=[jax.ShapeDtypeStruct((frame_rows, width), F32)] + [one_frame] * 3,
-            grid=(1,),
-            in_specs=[pl.BlockSpec((4, frame_rows, width), lambda i: (0, 0, 0))] * 2
-            + [pl.BlockSpec((None, frame_rows, width), lambda i: (f, 0, 0))]
-            + [anywhere] * len(needed),
-            out_specs=[pl.BlockSpec((frame_rows, width), lambda i: (0, 0))] * 4,
+            in_specs=[VMEM] * 3,
+            out_specs=[VMEM] * 4,
             compiler_params=params(20),
-        )(mine, from_core, hidden, *needed)
+        )(mine, from_core, rows)
         return kept, [lax.ppermute(part, "tile", ahead[k + 1]) for k, part in enumerate(sends)]
 
-    late_kept, late_back = reduced(1, late_sp, early_sp, before_late_sp, [])
-    early_kept, early_back = reduced(0, early_sp, before_late_sp, before_early_sp, late_back[:1])
+    late_shares = core_shares(late_sp, early_sp, before_late_sp, before_early_sp)
+    early_shares = core_shares(early_sp, before_late_sp, before_early_sp, late_shares[0])
+    late_kept, late_back = sums(*late_shares, late)
+    early_kept, early_back = sums(*early_shares, early)
     return pl.pallas_call(
         final_kernel,
         out_shape=jax.ShapeDtypeStruct(stream_in.shape, BF),

time: 220 us -> 212 us (0.964)
  Pallas kernels: 42.2 us -> 36.2 us
  waiting for transfers between devices: 76.5 us -> 72.1 us
    ppermute x8 -> x15, waiting for transfers between devices: 21.3 us -> 44.8 us  [the longest x6 23.2 us: sums(): lax.ppermute(part, 'tile', ahead[k + 1])]
    all_gather x2 -> x1, waiting for transfers between devices: 16.1 us -> 0.02 us  [on_device(): whole = lax.all_gather(stacked, 'tile', axis=0)]
    ppermute x1, waiting for transfers between devices: 9.9 us -> 3.04 us  [on_device(): before_early = lax.ppermute(early, 'blk', next_frames)]
    ppermute x1, waiting for transfers between devices: 15.9 us -> 9.92 us  [on_device(): before_late_sp = lax.ppermute(late_sp, 'blk', next_frames)]
    pallas_call x8 -> x9, Pallas kernels: 39.3 us -> 33.3 us  [the longest x2 13.9 us: spatial_call(): pl.pallas_call(spatial_kernel, in_specs=[pl.BlockSpec((peers, None, frame...]
    ppermute x8 -> x15, starting transfers between devices: 8.31 us -> 12.1 us  [the longest x6 6.4 us: sums(): lax.ppermute(part, 'tile', ahead[k + 1])]
    unnamed x21 -> x37, local copies, waits for them, and re-layouts: 12.7 us -> 13.1 us
  transfers between devices with their start and end apart: 13 -> 19, of which waited for: 7 -> 12; matrix products, arithmetic and copies ran while one was open for 4% -> 4% of each run, Pallas kernels for 16% -> 13%
where the time goes in v3:
time: 212 us
  waiting for transfers between devices  72.1 us (34%)
  blocking collectives  59.6 us (28%)
  Pallas kernels  36.2 us (17%)
  starting transfers between devices  17.2 us (8%)
  between operations  13.7 us (6%)
  local copies, waits for them, and re-layouts  13.1 us (6%)
    all_to_all x1, blocking collectives, on_device(): parts = lax.all_to_all(parts, everyone, 0, 0, tiled=True)  33.6 us
    all_to_all x1, blocking collectives, on_device(): state = lax.all_to_all(sums, everyone, 0, 0, tiled=True)  26 us
    ppermute x6, waiting for transfers between devices, sums(): lax.ppermute(part, 'tile', ahead[k + 1])  23.2 us
    ppermute x3, waiting for transfers between devices, on_device(): lax.ppermute(late, 'tile', ahead[k])  21.6 us
    pallas_call x2, Pallas kernels, spatial_call(): pl.pallas_call(spatial_kernel, in_specs=[pl.BlockSpec((peers, None, frame...  13.9 us
    all_gather x1, waiting for transfers between devices, on_device(): w_out_whole = lax.all_gather(w_output, 'tile', axis=0, tiled=True)  13.6 us
    unnamed x37, local copies, waits for them, and re-layouts  13.1 us
    ppermute x1, waiting for transfers between devices, on_device(): before_late_sp = lax.ppermute(late_sp, 'blk', next_frames)  9.92 us
  transfers between devices with their start and end apart: 19, of which 12 were waited for; matrix products, arithmetic and copies ran while one was open for 4% of the time, Pallas kernels for 13%

profile of v3, /device:TPU:2, one launch (start us, length us, event | category | flops | bytes accessed | tf_op | source)
XLA Modules:
  0.0 211.9 jit_solution(1475827408562467892)
XLA Ops:
  8.5 33.6 %all_to_all.10.in_ref = bf16[256,8,128]{2,1,0:T(8,128)(2,1)S(1)} all-to-all(bf16[256,8,128]{2,1,0:T(8,128)(2,1)S(1)} %shard_map.91), channel_id=1, replica_groups=mesh['blk'=32,'tile'=8] {'blk','tile'}, dimensions={0} | all-to-all | bytes 1048576 | tf_op jit(solution)/shard_map/all_to_all | solution.py:255
  42.5 26.0 %all_to_all.11.state_ref = bf16[256,8,128]{2,1,0:T(8,128)(2,1)S(1)} all-to-all(bf16[256,8,128]{2,1,0:T(8,128)(2,1)S(1)} %shard_map.92), channel_id=1, replica_groups=mesh['blk'=32,'tile'=8] {'blk','tile'}, dimensions={0} | all-to-all | bytes 1048576 | tf_op jit(solution)/shard_map/all_to_all | solution.py:259
  69.2 13.6 %all-gather.4.cloned.1.call-done.w_hbm = bf16[2240,2240]{1,0:T(8,128)(2,1)} async-done(((bf16[280,2240]{1,0:T(8,128)(2,1)}), bf16[2240,2240]{1,0:T(8,128)(2,1)}) %all-gather.4.cloned.1.call-update) | async-done | bytes 10035216 | tf_op jit(solution)/shard_map/all_gather | solution.py:240
  82.8 4.6 %shard_map.94 = (bf16[64,2240]{1,0:T(8,128)(2,1)S(1)}, bf16[64,2240]{1,0:T(8,128)(2,1)S(1)}) custom-call(bf16[128,2240]{1,0:T(8,128)(2,1)S(1)} %shard_map.93.att_ref, bf16[128,2240]{1,0:T(8,128)(2,1)S(1)} %bitcast.18, bf16[2240,2240]{1,0:T(8,128)(2,1)} %all-gather.4.cloned.1.call-done.w_hbm), custom_call_target="tpu_custom_call" | custom-call | tf_op jit(solution)/shard_map/pallas_call | solution.py:271
  88.1 3.1 %collective-permute-start = (bf16[64,2240]{1,0:T(8,128)(2,1)S(1)}, bf16[64,2240]{1,0:T(8,128)(2,1)S(1)}, u32[]{:S(2)}, u32[]{:S(2)}) collective-permute-start(bf16[64,2240]{1,0:T(8,128)(2,1)S(1)} %get-tuple-element.19.one_ref.hidden_ref), channel_id=1, source_target_pairs={{0,8},{8,16},{16,24},{24,32},{32,40},{40,48},{48,56},{56,64},{64,7... | collective-permute-start | bytes 860168 | tf_op jit(solution)/shard_map/ppermute | solution.py:337
  91.1 6.8 %collective-permute-done.1.needed_ref.refs_2_ = bf16[64,2240]{1,0:T(8,128)(2,1)S(1)} collective-permute-done((bf16[64,2240]{1,0:T(8,128)(2,1)S(1)}, bf16[64,2240]{1,0:T(8,128)(2,1)S(1)}, u32[]{:S(2)}, u32[]{:S(2)}) %collective-permute-start.1) | collective-permute-done | bytes 286752 | tf_op jit(solution)/shard_map/ppermute | solution.py:336
  97.9 3.0 %collective-permute-done.two_ref = bf16[64,2240]{1,0:T(8,128)(2,1)S(1)} collective-permute-done((bf16[64,2240]{1,0:T(8,128)(2,1)S(1)}, bf16[64,2240]{1,0:T(8,128)(2,1)S(1)}, u32[]{:S(2)}, u32[]{:S(2)}) %collective-permute-start) | collective-permute-done | bytes 286752 | tf_op jit(solution)/shard_map/ppermute | solution.py:337
  104.4 2.0 collective-permute-start.6
  106.9 5.2 %collective-permute-done.4.refs_4_ = bf16[64,2240]{1,0:T(8,128)(2,1)S(1)} collective-permute-done((bf16[64,2240]{1,0:T(8,128)(2,1)S(1)}, bf16[64,2240]{1,0:T(8,128)(2,1)S(1)}, u32[]{:S(2)}, u32[]{:S(2)}) %collective-permute-start.4) | collective-permute-done | bytes 286752 | tf_op jit(solution)/shard_map/ppermute | solution.py:336
  112.1 9.6 %collective-permute-done.6.refs_6_ = bf16[64,2240]{1,0:T(8,128)(2,1)S(1)} collective-permute-done((bf16[64,2240]{1,0:T(8,128)(2,1)S(1)}, bf16[64,2240]{1,0:T(8,128)(2,1)S(1)}, u32[]{:S(2)}, u32[]{:S(2)}) %collective-permute-start.6) | collective-permute-done | bytes 286752 | tf_op jit(solution)/shard_map/ppermute | solution.py:336
  121.8 6.1 %copy.14 = bf16[280,8,2,512]{3,1,2,0:T(8,128)(2,1)} copy(bf16[280,8,2,512]{3,2,1,0:T(2,128)(2,1)} %bitcast.29) | data formatting | bytes 9175040
  128.8 7.3 %shard_map.96.needed_ref.now_ref = bf16[512,1024]{1,0:T(8,128)(2,1)} custom-call(s32[2]{0:T(128)S(1)} %pad_add_fusion.place_ref, bf16[64,2240]{1,0:T(8,128)(2,1)S(1)} %get-tuple-element.20.refs_0_.hidden_ref, bf16[64,2240]{1,0:T(8,128)(2,1)S(1)} %collective-permute-done.2.refs_1_, bf16[64,2240]{1,0:T(8,128)(2,1)S(1)} %collective-permute-done.1.needed_ref.refs_2_, ...), custom_call_target="tpu_custom_call" | custom-call | tf_op jit(solution)/shard_map/pallas_call | solution.py:306
  136.2 2.0 collective-permute-start.8
  138.2 2.8 %copy.13.w_ref = bf16[512,2240]{1,0:T(8,128)(2,1)S(1)} copy(bf16[512,2240]{0,1:T(8,128)(2,1)} %param.15) | data formatting | bytes 4587520 | tf_op args[6]
  141.1 6.9 %shard_map.97.needed_ref.one_ref.now_ref = bf16[512,1024]{1,0:T(8,128)(2,1)S(1)} custom-call(bf16[8,2,64,2240]{3,2,1,0:T(8,128)(2,1)} %bitcast.27, bf16[2240,1024]{1,0:T(8,128)(2,1)} %bitcast.25, f32[9,1024]{1,0:T(8,128)S(1)} %bitcast.16, bf16[512,1024]{1,0:T(8,128)(2,1)} %shard_map.96.needed_ref.now_ref), custom_call_target="tpu_custom_call" | custom-call | tf_op jit(solution)/shard_map/pallas_call | solution.py:296
  149.0 7.0 %shard_map.98.needed_ref.two_ref = bf16[512,1024]{1,0:T(8,128)(2,1)S(1)} custom-call(bf16[8,2,64,2240]{3,2,1,0:T(8,128)(2,1)} %bitcast.28, bf16[2240,1024]{1,0:T(8,128)(2,1)} %bitcast.26, f32[9,1024]{1,0:T(8,128)S(1)} %bitcast.17, bf16[512,1024]{1,0:T(8,128)(2,1)} %copy-done), custom_call_target="tpu_custom_call" | custom-call | tf_op jit(solution)/shard_map/pallas_call | solution.py:296
  156.0 9.9 %collective-permute-done.8.two_ref.one_ref = bf16[512,1024]{1,0:T(8,128)(2,1)S(1)} collective-permute-done((bf16[512,1024]{1,0:T(8,128)(2,1)}, bf16[512,1024]{1,0:T(8,128)(2,1)S(1)}, u32[]{:S(2)}, u32[]{:S(2)}) %collective-permute-start.8) | collective-permute-done | bytes 1048608 | tf_op jit(solution)/shard_map/ppermute | solution.py:350
  167.2 3.0 %shard_map.99 = (bf16[4,64,2240]{2,1,0:T(8,128)(2,1)S(1)}, bf16[4,64,2240]{2,1,0:T(8,128)(2,1)S(1)}) custom-call(s32[2]{0:T(128)S(1)} %pad_add_fusion.place_ref, bf16[512,1024]{1,0:T(8,128)(2,1)S(1)} %copy-done.3, bf16[512,1024]{1,0:T(8,128)(2,1)S(1)} %copy-done.1, bf16[512,1024]{1,0:T(8,128)(2,1)S(1)} %collective-permute-done.8.two_ref.one_ref, ...), custom_call_target="tpu_custom_call" | custom-call | tf_op jit(solution)/shard_map/pallas_call | solution.py:355
  170.3 3.0 %shard_map.100 = (bf16[4,64,2240]{2,1,0:T(8,128)(2,1)S(1)}, bf16[4,64,2240]{2,1,0:T(8,128)(2,1)S(1)}) custom-call(s32[2]{0:T(128)S(1)} %pad_add_fusion.place_ref, bf16[512,1024]{1,0:T(8,128)(2,1)S(1)} %copy-done.2, bf16[512,1024]{1,0:T(8,128)(2,1)S(1)} %collective-permute-done.8.two_ref.one_ref, bf16[512,1024]{1,0:T(8,128)(2,1)S(1)} %shard_map.98.needed_ref.two_ref, ...), custom_call_target="tpu_custom_call" | custom-call | tf_op jit(solution)/shard_map/pallas_call | solution.py:355
  174.2 3.5 %collective-permute-start.15 = (bf16[64,2240]{1,0:T(8,128)(2,1)S(1)}, bf16[64,2240]{1,0:T(8,128)(2,1)S(1)}, u32[]{:S(2)}, u32[]{:S(2)}) collective-permute-start(bf16[64,2240]{1,0:T(8,128)(2,1)S(1)} %get-tuple-element.31), channel_id=1, source_target_pairs={{0,4},{1,5},{2,6},{3,7},{4,0},{5,1},{6,2},{7,3},{8,12},{9,13},{10,... | collective-permute-start | bytes 860168 | tf_op jit(solution)/shard_map/ppermute | solution.py:366
  178.0 2.1 collective-permute-start.11
  180.8 10.5 %collective-permute-done.14.refs_3_ = bf16[64,2240]{1,0:T(8,128)(2,1)S(1)} collective-permute-done((bf16[64,2240]{1,0:T(8,128)(2,1)S(1)}, bf16[64,2240]{1,0:T(8,128)(2,1)S(1)}, u32[]{:S(2)}, u32[]{:S(2)}) %collective-permute-start.14) | collective-permute-done | bytes 286752 | tf_op jit(solution)/shard_map/ppermute | solution.py:366
  192.5 5.1 %collective-permute-done.11.refs_0_ = bf16[64,2240]{1,0:T(8,128)(2,1)S(1)} collective-permute-done((bf16[64,2240]{1,0:T(8,128)(2,1)S(1)}, bf16[64,2240]{1,0:T(8,128)(2,1)S(1)}, u32[]{:S(2)}, u32[]{:S(2)}) %collective-permute-start.11) | collective-permute-done | bytes 286752 | tf_op jit(solution)/shard_map/ppermute | solution.py:366
  197.6 6.0 %collective-permute-done.12.refs_1_ = bf16[64,2240]{1,0:T(8,128)(2,1)S(1)} collective-permute-done((bf16[64,2240]{1,0:T(8,128)(2,1)S(1)}, bf16[64,2240]{1,0:T(8,128)(2,1)S(1)}, u32[]{:S(2)}, u32[]{:S(2)}) %collective-permute-start.12) | collective-permute-done | bytes 286752 | tf_op jit(solution)/shard_map/ppermute | solution.py:366
  (69 shorter events, 15.4 us)
Async XLA Ops:
  6.5 76.3 %all-gather.4.cloned.1.call-start = ((), (), s32[]{:S(2)}) async-start(), calls=%async_computation.2 | async-start | bytes 11612160 | tf_op jit(solution)/shard_map/all_gather | solution.py:240
  7.3 133.8 %all-gather.6.cloned.1.call-start = ((), (), s32[]{:S(2)}) async-start(), calls=%async_computation.3 | async-start | bytes 5308416 | tf_op jit(solution)/shard_map/all_gather | solution.py:348
  42.1 26.4 %copy-start.11 = (bf16[4,2,16,2240]{3,2,1,0:T(8,128)(2,1)S(1)}, bf16[4,2,16,2240]{3,2,1,0:T(8,128)(2,1)}, u32[]{:S(2)}) copy-start(bf16[4,2,16,2240]{3,2,1,0:T(8,128)(2,1)} %param.10) | copy-start | bytes 1720324
  42.4 40.4 %copy-start.8 = (bf16[4,2,16,2240]{3,2,1,0:T(8,128)(2,1)S(1)}, bf16[4,2,16,2240]{3,2,1,0:T(8,128)(2,1)}, u32[]{:S(2)}) copy-start(bf16[4,2,16,2240]{3,2,1,0:T(8,128)(2,1)} %param.9) | copy-start | bytes 1720324
  87.4 40.7 %copy-start.4 = (bf16[64,2240]{1,0:T(8,128)(2,1)}, bf16[64,2240]{1,0:T(8,128)(2,1)S(1)}, u32[]{:S(2)}) copy-start(bf16[64,2240]{1,0:T(8,128)(2,1)S(1)} %get-tuple-element.20.refs_0_.hidden_ref) | copy-start | bytes 860164
  87.4 10.5 %collective-permute-start.1 = (bf16[64,2240]{1,0:T(8,128)(2,1)S(1)}, bf16[64,2240]{1,0:T(8,128)(2,1)S(1)}, u32[]{:S(2)}, u32[]{:S(2)}) collective-permute-start(bf16[64,2240]{1,0:T(8,128)(2,1)S(1)} %get-tuple-element.20.refs_0_.hidden_ref), channel_id=1, source_target_pairs={{0,2},{1,3},{2,4},{3,5},{4,6},{5,7},{6,0},{7,1},{8,10},{9,11},{10,... | collective-permute-start | bytes 860168 | tf_op jit(solution)/shard_map/ppermute | solution.py:336
  88.1 12.9 %collective-permute-start = (bf16[64,2240]{1,0:T(8,128)(2,1)S(1)}, bf16[64,2240]{1,0:T(8,128)(2,1)S(1)}, u32[]{:S(2)}, u32[]{:S(2)}) collective-permute-start(bf16[64,2240]{1,0:T(8,128)(2,1)S(1)} %get-tuple-element.19.one_ref.hidden_ref), channel_id=1, source_target_pairs={{0,8},{8,16},{16,24},{24,32},{32,40},{40,48},{48,56},{56,64},{64,7... | collective-permute-start | bytes 860168 | tf_op jit(solution)/shard_map/ppermute | solution.py:337
  102.5 9.6 %collective-permute-start.4 = (bf16[64,2240]{1,0:T(8,128)(2,1)S(1)}, bf16[64,2240]{1,0:T(8,128)(2,1)S(1)}, u32[]{:S(2)}, u32[]{:S(2)}) collective-permute-start(bf16[64,2240]{1,0:T(8,128)(2,1)S(1)} %get-tuple-element.20.refs_0_.hidden_ref), channel_id=1, source_target_pairs={{0,4},{1,5},{2,6},{3,7},{4,0},{5,1},{6,2},{7,3},{8,12},{9,13},{10,... | collective-permute-start | bytes 860168 | tf_op jit(solution)/shard_map/ppermute | solution.py:336
  104.4 17.4 %collective-permute-start.6 = (bf16[64,2240]{1,0:T(8,128)(2,1)S(1)}, bf16[64,2240]{1,0:T(8,128)(2,1)S(1)}, u32[]{:S(2)}, u32[]{:S(2)}) collective-permute-start(bf16[64,2240]{1,0:T(8,128)(2,1)S(1)} %get-tuple-element.20.refs_0_.hidden_ref), channel_id=1, source_target_pairs={{0,6},{1,7},{2,0},{3,1},{4,2},{5,3},{6,4},{7,5},{8,14},{9,15},{10,... | collective-permute-start | bytes 860168 | tf_op jit(solution)/shard_map/ppermute | solution.py:336
  106.4 21.7 %collective-permute-start.2 = (bf16[64,2240]{1,0:T(8,128)(2,1)S(1)}, bf16[64,2240]{1,0:T(8,128)(2,1)S(1)}, u32[]{:S(2)}, u32[]{:S(2)}) collective-permute-start(bf16[64,2240]{1,0:T(8,128)(2,1)S(1)} %get-tuple-element.20.refs_0_.hidden_ref), channel_id=1, source_target_pairs={{0,1},{1,0},{2,3},{3,2},{4,5},{5,4},{6,7},{7,6},{8,9},{9,8},{10,11... | collective-permute-start | bytes 860168 | tf_op jit(solution)/shard_map/ppermute | solution.py:340
  106.4 21.7 %collective-permute-start.3 = (bf16[64,2240]{1,0:T(8,128)(2,1)S(1)}, bf16[64,2240]{1,0:T(8,128)(2,1)S(1)}, u32[]{:S(2)}, u32[]{:S(2)}) collective-permute-start(bf16[64,2240]{1,0:T(8,128)(2,1)S(1)} %collective-permute-done.1.needed_ref.refs_2_), channel_id=1, source_target_pairs={{0,1},{1,0},{2,3},{3,2},{4,5},{5,4},{6,7},{7,6},{8,9},{9,8},{10,11... | collective-permute-start | bytes 860168 | tf_op jit(solution)/shard_map/ppermute | solution.py:340
  112.1 15.9 %collective-permute-start.5 = (bf16[64,2240]{1,0:T(8,128)(2,1)S(1)}, bf16[64,2240]{1,0:T(8,128)(2,1)S(1)}, u32[]{:S(2)}, u32[]{:S(2)}) collective-permute-start(bf16[64,2240]{1,0:T(8,128)(2,1)S(1)} %collective-permute-done.4.refs_4_), channel_id=1, source_target_pairs={{0,1},{1,0},{2,3},{3,2},{4,5},{5,4},{6,7},{7,6},{8,9},{9,8},{10,11... | collective-permute-start | bytes 860168 | tf_op jit(solution)/shard_map/ppermute | solution.py:340
  121.8 6.1 %copy-start.12 = (bf16[64,2240]{1,0:T(8,128)(2,1)}, bf16[64,2240]{1,0:T(8,128)(2,1)S(1)}, u32[]{:S(2)}) copy-start(bf16[64,2240]{1,0:T(8,128)(2,1)S(1)} %collective-permute-done.6.refs_6_) | copy-start | bytes 860164
  121.8 6.3 %collective-permute-start.7 = (bf16[64,2240]{1,0:T(8,128)(2,1)S(1)}, bf16[64,2240]{1,0:T(8,128)(2,1)S(1)}, u32[]{:S(2)}, u32[]{:S(2)}) collective-permute-start(bf16[64,2240]{1,0:T(8,128)(2,1)S(1)} %collective-permute-done.6.refs_6_), channel_id=1, source_target_pairs={{0,1},{1,0},{2,3},{3,2},{4,5},{5,4},{6,7},{7,6},{8,9},{9,8},{10,11... | collective-permute-start | bytes 860168 | tf_op jit(solution)/shard_map/ppermute | solution.py:340
  136.2 29.8 %collective-permute-start.8 = (bf16[512,1024]{1,0:T(8,128)(2,1)}, bf16[512,1024]{1,0:T(8,128)(2,1)S(1)}, u32[]{:S(2)}, u32[]{:S(2)}) collective-permute-start(bf16[512,1024]{1,0:T(8,128)(2,1)} %shard_map.96.needed_ref.now_ref), channel_id=1, source_target_pairs={{0,8},{8,16},{16,24},{24,32},{32,40},{40,48},{48,56},{56,64},{64,7... | collective-permute-start | bytes 3145736 | tf_op jit(solution)/shard_map/ppermute | solution.py:350
  149.0 16.9 %copy-start.3 = (bf16[512,1024]{1,0:T(8,128)(2,1)S(1)}, bf16[512,1024]{1,0:T(8,128)(2,1)}, u32[]{:S(2)}) copy-start(bf16[512,1024]{1,0:T(8,128)(2,1)} %shard_map.96.needed_ref.now_ref) | copy-start | bytes 3145732
  170.1 3.7 %collective-permute-start.10 = (bf16[4,64,2240]{2,1,0:T(8,128)(2,1)S(1)}, bf16[4,64,2240]{2,1,0:T(8,128)(2,1)S(1)}, u32[]{:S(2)}, u32[]{:S(2)}) collective-permute-start(bf16[4,64,2240]{2,1,0:T(8,128)(2,1)S(1)} %get-tuple-element.25), channel_id=1, source_target_pairs={{0,1},{1,0},{2,3},{3,2},{4,5},{5,4},{6,7},{7,6},{8,9},{9,8},{10,11... | collective-permute-start | bytes 3440648 | tf_op jit(solution)/shard_map/ppermute | solution.py:356
  173.3 4.4 %collective-permute-start.9 = (bf16[4,64,2240]{2,1,0:T(8,128)(2,1)S(1)}, bf16[4,64,2240]{2,1,0:T(8,128)(2,1)S(1)}, u32[]{:S(2)}, u32[]{:S(2)}) collective-permute-start(bf16[4,64,2240]{2,1,0:T(8,128)(2,1)S(1)} %get-tuple-element.23), channel_id=1, source_target_pairs={{0,1},{1,0},{2,3},{3,2},{4,5},{5,4},{6,7},{7,6},{8,9},{9,8},{10,11... | collective-permute-start | bytes 3440648 | tf_op jit(solution)/shard_map/ppermute | solution.py:356
  174.1 17.2 %collective-permute-start.14 = (bf16[64,2240]{1,0:T(8,128)(2,1)S(1)}, bf16[64,2240]{1,0:T(8,128)(2,1)S(1)}, u32[]{:S(2)}, u32[]{:S(2)}) collective-permute-start(bf16[64,2240]{1,0:T(8,128)(2,1)S(1)} %get-tuple-element.30), channel_id=1, source_target_pairs={{0,2},{1,3},{2,4},{3,5},{4,6},{5,7},{6,0},{7,1},{8,10},{9,11},{10,... | collective-permute-start | bytes 860168 | tf_op jit(solution)/shard_map/ppermute | solution.py:366
  174.2 17.7 %collective-permute-start.15 = (bf16[64,2240]{1,0:T(8,128)(2,1)S(1)}, bf16[64,2240]{1,0:T(8,128)(2,1)S(1)}, u32[]{:S(2)}, u32[]{:S(2)}) collective-permute-start(bf16[64,2240]{1,0:T(8,128)(2,1)S(1)} %get-tuple-element.31), channel_id=1, source_target_pairs={{0,4},{1,5},{2,6},{3,7},{4,0},{5,1},{6,2},{7,3},{8,12},{9,13},{10,... | collective-permute-start | bytes 860168 | tf_op jit(solution)/shard_map/ppermute | solution.py:366
  177.7 14.8 %collective-permute-start.16 = (bf16[64,2240]{1,0:T(8,128)(2,1)S(1)}, bf16[64,2240]{1,0:T(8,128)(2,1)S(1)}, u32[]{:S(2)}, u32[]{:S(2)}) collective-permute-start(bf16[64,2240]{1,0:T(8,128)(2,1)S(1)} %get-tuple-element.32), channel_id=1, source_target_pairs={{0,6},{1,7},{2,0},{3,1},{4,2},{5,3},{6,4},{7,5},{8,14},{9,15},{10,... | collective-permute-start | bytes 860168 | tf_op jit(solution)/shard_map/ppermute | solution.py:366
  178.0 19.6 %collective-permute-start.11 = (bf16[64,2240]{1,0:T(8,128)(2,1)S(1)}, bf16[64,2240]{1,0:T(8,128)(2,1)S(1)}, u32[]{:S(2)}, u32[]{:S(2)}) collective-permute-start(bf16[64,2240]{1,0:T(8,128)(2,1)S(1)} %get-tuple-element.27), channel_id=1, source_target_pairs={{0,2},{1,3},{2,4},{3,5},{4,6},{5,7},{6,0},{7,1},{8,10},{9,11},{10,... | collective-permute-start | bytes 860168 | tf_op jit(solution)/shard_map/ppermute | solution.py:366
  180.1 23.5 %collective-permute-start.12 = (bf16[64,2240]{1,0:T(8,128)(2,1)S(1)}, bf16[64,2240]{1,0:T(8,128)(2,1)S(1)}, u32[]{:S(2)}, u32[]{:S(2)}) collective-permute-start(bf16[64,2240]{1,0:T(8,128)(2,1)S(1)} %get-tuple-element.28), channel_id=1, source_target_pairs={{0,4},{1,5},{2,6},{3,7},{4,0},{5,1},{6,2},{7,3},{8,12},{9,13},{10,... | collective-permute-start | bytes 860168 | tf_op jit(solution)/shard_map/ppermute | solution.py:366
  191.3 12.7 %collective-permute-start.13 = (bf16[64,2240]{1,0:T(8,128)(2,1)S(1)}, bf16[64,2240]{1,0:T(8,128)(2,1)S(1)}, u32[]{:S(2)}, u32[]{:S(2)}) collective-permute-start(bf16[64,2240]{1,0:T(8,128)(2,1)S(1)} %get-tuple-element.29), channel_id=1, source_target_pairs={{0,6},{1,7},{2,0},{3,1},{4,2},{5,3},{6,4},{7,5},{8,14},{9,15},{10,... | collective-permute-start | bytes 860168 | tf_op jit(solution)/shard_map/ppermute | solution.py:366
  (11 other events, 28.0 us)
Sparse Core Ops, SparseCore 0:
  9.2 73.5 all-gather.3
  102.6 36.4 all-gather.5

commit v4 on v3

--- a/solution.py
+++ b/solution.py
@@ -107,7 +107,7 @@
         att_ref[:, LANES * c : LANES * c + width] = attended[:, :width]
 
 
-def hidden_kernel(att_ref, stream_ref, w_hbm, early_ref, late_ref, w_ref, sems):
+def hidden_kernel(att_ref, stream_ref, w_hbm, needed_ref, early_ref, late_ref, w_ref, sems):
     tokens = att_ref.shape[0]
     step = 384
     spans = [(n, min(n + step, D)) for n in range(0, D, step)]
@@ -203,7 +203,8 @@
         send[...] = total(k + 1).astype(BF)
 
 
-def stack_kernel(one_ref, two_ref, needed_ref, out_ref):
+def stack_kernel(one_ref, two_ref, *refs):
+    out_ref = refs[-1]
     out_ref[0] = one_ref[...]
     out_ref[1] = two_ref[...]
 
@@ -271,11 +272,11 @@
     early, late = pl.pallas_call(
         hidden_kernel,
         out_shape=[one_frame] * 2,
-        in_specs=[VMEM, VMEM, anywhere],
+        in_specs=[VMEM, VMEM, anywhere, anywhere],
         out_specs=[VMEM, VMEM],
         scratch_shapes=[pltpu.VMEM((width, width), BF), pltpu.SemaphoreType.DMA((6,))],
         compiler_params=params(52),
-    )(attended, flat(stream_in), w_out_whole)
+    )(attended, flat(stream_in), w_out_whole, w_flat)
 
     whole_rows = peers * frame_rows
     block = 256
@@ -341,15 +342,14 @@
     stacked = pl.pallas_call(
         stack_kernel,
         out_shape=jax.ShapeDtypeStruct((2, frame_rows, width), BF),
-        in_specs=[VMEM, VMEM, anywhere],
+        in_specs=[VMEM, VMEM] + [anywhere] * 3,
         out_specs=VMEM,
         compiler_params=params(20),
-    )(early, before_early, late_along[1])
+    )(early, before_early, *late_along[1:])
     whole = lax.all_gather(stacked, "tile", axis=0)
     late_sp = pieces_call(pieces)
     before_late_sp = lax.ppermute(late_sp, "blk", next_frames)
     early_sp = spatial_call(whole, 0, late_sp)
-    before_early_sp = spatial_call(whole, 1, early_sp)
 
     def core_shares(now, one, two, needed):
         mine, other = point_call(where_am_i, now, one, two, taps_t, w_down, needed)
@@ -365,9 +365,10 @@
         )(mine, from_core, rows)
         return kept, [lax.ppermute(part, "tile", ahead[k + 1]) for k, part in enumerate(sends)]
 
-    late_shares = core_shares(late_sp, early_sp, before_late_sp, before_early_sp)
-    early_shares = core_shares(early_sp, before_late_sp, before_early_sp, late_shares[0])
+    late_shares = core_shares(late_sp, early_sp, before_late_sp, early_sp)
+    before_early_sp = spatial_call(whole, 1, late_shares[0])
     late_kept, late_back = sums(*late_shares, late)
+    early_shares = core_shares(early_sp, before_late_sp, before_early_sp, late_kept)
     early_kept, early_back = sums(*early_shares, early)
     return pl.pallas_call(
         final_kernel,

time: 212 us -> 206 us (0.972)
  blocking collectives: 59.6 us -> 33.6 us
  waiting for transfers between devices: 72.1 us -> 83.2 us
  starting transfers between devices: 17.2 us -> 26 us
    all_to_all x1 -> x0, blocking collectives: 26 us -> none  [on_device(): state = lax.all_to_all(sums, everyone, 0, 0, tiled=True)]
    all_gather x1, waiting for transfers between devices: 0.02 us -> 19.2 us  [on_device(): whole = lax.all_gather(stacked, 'tile', axis=0)]
    ppermute x3, waiting for transfers between devices: 21.6 us -> 7.06 us  [on_device(): lax.ppermute(late, 'tile', ahead[k])]
    all_to_all x0 -> x1, waiting for transfers between devices: none -> 12.9 us  [on_device(): state = lax.all_to_all(sums, everyone, 0, 0, tiled=True)]
    ppermute x1, waiting for transfers between devices: 9.92 us -> 0.01 us  [on_device(): before_late_sp = lax.ppermute(late_sp, 'blk', next_frames)]
    all_to_all x0 -> x1, starting transfers between devices: none -> 7.13 us  [on_device(): state = lax.all_to_all(sums, everyone, 0, 0, tiled=True)]
    ppermute x1, waiting for transfers between devices: 3.04 us -> 5.71 us  [on_device(): before_early = lax.ppermute(early, 'blk', next_frames)]
    unnamed x37 -> x35, local copies, waits for them, and re-layouts: 13.1 us -> 12 us
  transfers between devices with their start and end apart: 19 -> 20, of which waited for: 12 -> 14; matrix products, arithmetic and copies ran while one was open for 4% -> 4% of each run, Pallas kernels for 13% -> 12%
where the time goes in v4:
time: 206 us
  waiting for transfers between devices  83.2 us (40%)
  Pallas kernels  37.1 us (18%)
  blocking collectives  33.6 us (16%)
  starting transfers between devices  26 us (13%)
  between operations  13.7 us (7%)
  local copies, waits for them, and re-layouts  12 us (6%)
    all_to_all x1, blocking collectives, on_device(): parts = lax.all_to_all(parts, everyone, 0, 0, tiled=True)  33.6 us
    ppermute x6, waiting for transfers between devices, sums(): lax.ppermute(part, 'tile', ahead[k + 1])  23.3 us
    all_gather x1, waiting for transfers between devices, on_device(): whole = lax.all_gather(stacked, 'tile', axis=0)  19.2 us
    pallas_call x2, Pallas kernels, spatial_call(): pl.pallas_call(spatial_kernel, in_specs=[pl.BlockSpec((peers, None, frame...  14 us
    all_to_all x1, waiting for transfers between devices, on_device(): state = lax.all_to_all(sums, everyone, 0, 0, tiled=True)  12.9 us
    all_gather x1, waiting for transfers between devices, on_device(): w_out_whole = lax.all_gather(w_output, 'tile', axis=0, tiled=True)  12.6 us
    unnamed x35, local copies, waits for them, and re-layouts  12 us
    pallas_call x1, Pallas kernels, pieces_call(): pl.pallas_call(pieces_kernel, in_specs=[pl.BlockSpec(memory_space=pltpu.S...  7.29 us
  transfers between devices with their start and end apart: 20, of which 14 were waited for; matrix products, arithmetic and copies ran while one was open for 4% of the time, Pallas kernels for 12%

profile of v4, /device:TPU:2, one launch (start us, length us, event | category | flops | bytes accessed | tf_op | source)
XLA Modules:
  0.0 205.6 jit_solution(9180671827344068545)
XLA Ops:
  8.5 33.6 %all_to_all.10.in_ref = bf16[256,8,128]{2,1,0:T(8,128)(2,1)S(1)} all-to-all(bf16[256,8,128]{2,1,0:T(8,128)(2,1)S(1)} %shard_map.91), channel_id=1, replica_groups=mesh['blk'=32,'tile'=8] {'blk','tile'}, dimensions={0} | all-to-all | bytes 1048576 | tf_op jit(solution)/shard_map/all_to_all | solution.py:256
  43.2 7.1 %all-to-all-start.1 = ((bf16[256,8,128]{2,1,0:T(8,128)(2,1)}), bf16[256,8,128]{2,1,0:T(8,128)(2,1)S(1)}, u32[]{:S(2)}, u32[]{:S(2)}) async-start(bf16[256,8,128]{2,1,0:T(8,128)(2,1)} %shard_map.92), calls=%async_computation.1 | async-start | bytes 1048576 | tf_op jit(solution)/shard_map/all_to_all | solution.py:260
  50.4 6.1 %copy.14 = bf16[280,8,2,512]{3,1,2,0:T(8,128)(2,1)} copy(bf16[280,8,2,512]{3,2,1,0:T(2,128)(2,1)} %bitcast.30) | data formatting | bytes 9175040
  56.6 12.9 %all-to-all-done.1.state_ref = bf16[256,8,128]{2,1,0:T(8,128)(2,1)S(1)} async-done(((bf16[256,8,128]{2,1,0:T(8,128)(2,1)}), bf16[256,8,128]{2,1,0:T(8,128)(2,1)S(1)}, u32[]{:S(2)}, u32[]{:S(2)}) %all-to-all-start.1) | async-done | bytes 524320 | tf_op jit(solution)/shard_map/all_to_all | solution.py:260
  70.2 12.6 %all-gather.4.cloned.1.call-done.w_hbm = bf16[2240,2240]{1,0:T(8,128)(2,1)} async-done(((bf16[280,2240]{1,0:T(8,128)(2,1)}), bf16[2240,2240]{1,0:T(8,128)(2,1)}) %all-gather.4.cloned.1.call-update) | async-done | bytes 10035216 | tf_op jit(solution)/shard_map/all_gather | solution.py:241
  82.8 4.6 %shard_map.94 = (bf16[64,2240]{1,0:T(8,128)(2,1)S(1)}, bf16[64,2240]{1,0:T(8,128)(2,1)S(1)}) custom-call(bf16[128,2240]{1,0:T(8,128)(2,1)S(1)} %shard_map.93.att_ref, bf16[128,2240]{1,0:T(8,128)(2,1)S(1)} %bitcast.18, bf16[2240,2240]{1,0:T(8,128)(2,1)} %all-gather.4.cloned.1.call-done.w_hbm, bf16[2240,1024]{1,0:T(8,128)(2,1)} %bitcast.24), custom_call_target="tpu_custom_call" | custom-call | tf_op jit(solution)/shard_map/pallas_call | solution.py:272
  87.4 3.1 %collective-permute-start = (bf16[64,2240]{1,0:T(8,128)(2,1)S(1)}, bf16[64,2240]{1,0:T(8,128)(2,1)S(1)}, u32[]{:S(2)}, u32[]{:S(2)}) collective-permute-start(bf16[64,2240]{1,0:T(8,128)(2,1)S(1)} %get-tuple-element.19.one_ref.hidden_ref), channel_id=1, source_target_pairs={{0,8},{8,16},{16,24},{24,32},{32,40},{40,48},{48,56},{56,64},{64,7... | collective-permute-start | bytes 860168 | tf_op jit(solution)/shard_map/ppermute | solution.py:338
  91.2 1.8 collective-permute-start.2
  92.9 2.0 collective-permute-start.3
  94.9 5.7 %collective-permute-done.two_ref = bf16[64,2240]{1,0:T(8,128)(2,1)S(1)} collective-permute-done((bf16[64,2240]{1,0:T(8,128)(2,1)S(1)}, bf16[64,2240]{1,0:T(8,128)(2,1)S(1)}, u32[]{:S(2)}, u32[]{:S(2)}) %collective-permute-start) | collective-permute-done | bytes 286752 | tf_op jit(solution)/shard_map/ppermute | solution.py:338
  100.6 6.4 %collective-permute-done.1.refs_0_.refs_2_ = bf16[64,2240]{1,0:T(8,128)(2,1)S(1)} collective-permute-done((bf16[64,2240]{1,0:T(8,128)(2,1)S(1)}, bf16[64,2240]{1,0:T(8,128)(2,1)S(1)}, u32[]{:S(2)}, u32[]{:S(2)}) %collective-permute-start.1) | collective-permute-done | bytes 286752 | tf_op jit(solution)/shard_map/ppermute | solution.py:337
  113.0 7.3 %shard_map.96.needed_ref.now_ref = bf16[512,1024]{1,0:T(8,128)(2,1)} custom-call(s32[2]{0:T(128)S(1)} %pad_add_fusion.place_ref, bf16[64,2240]{1,0:T(8,128)(2,1)S(1)} %get-tuple-element.20.refs_0_.hidden_ref, bf16[64,2240]{1,0:T(8,128)(2,1)S(1)} %collective-permute-done.4.refs_1_, bf16[64,2240]{1,0:T(8,128)(2,1)S(1)} %collective-permute-done.1.refs_0_.refs_2_, ...), custom_call_target="tpu_custom_call" | custom-call | tf_op jit(solution)/shard_map/pallas_call | solution.py:307
  120.2 3.4 %collective-permute-start.8 = (bf16[512,1024]{1,0:T(8,128)(2,1)}, bf16[512,1024]{1,0:T(8,128)(2,1)S(1)}, u32[]{:S(2)}, u32[]{:S(2)}) collective-permute-start(bf16[512,1024]{1,0:T(8,128)(2,1)} %shard_map.96.needed_ref.now_ref), channel_id=1, source_target_pairs={{0,8},{8,16},{16,24},{24,32},{32,40},{40,48},{48,56},{56,64},{64,7... | collective-permute-start | bytes 3145736 | tf_op jit(solution)/shard_map/ppermute | solution.py:351
  123.7 2.8 %copy.12.w_ref = bf16[512,2240]{1,0:T(8,128)(2,1)S(1)} copy(bf16[512,2240]{0,1:T(8,128)(2,1)} %param.15) | data formatting | bytes 4587520 | tf_op args[6]
  126.5 19.2 %all-gather.6.cloned.1.call-done = bf16[16,64,2240]{2,1,0:T(8,128)(2,1)} async-done(((bf16[2,64,2240]{2,1,0:T(8,128)(2,1)}), bf16[16,64,2240]{2,1,0:T(8,128)(2,1)}) %all-gather.6.cloned.1.call-update) | async-done | bytes 4587536 | tf_op jit(solution)/shard_map/all_gather | solution.py:349
  145.7 7.0 %shard_map.97.one_ref.needed_ref.now_ref = bf16[512,1024]{1,0:T(8,128)(2,1)S(1)} custom-call(bf16[8,2,64,2240]{3,2,1,0:T(8,128)(2,1)} %bitcast.28, bf16[2240,1024]{1,0:T(8,128)(2,1)} %bitcast.26, f32[9,1024]{1,0:T(8,128)S(1)} %bitcast.16, bf16[512,1024]{1,0:T(8,128)(2,1)} %shard_map.96.needed_ref.now_ref), custom_call_target="tpu_custom_call" | custom-call | tf_op jit(solution)/shard_map/pallas_call | solution.py:297
  152.7 3.0 %shard_map.98 = (bf16[4,64,2240]{2,1,0:T(8,128)(2,1)S(1)}, bf16[4,64,2240]{2,1,0:T(8,128)(2,1)S(1)}) custom-call(s32[2]{0:T(128)S(1)} %pad_add_fusion.place_ref, bf16[512,1024]{1,0:T(8,128)(2,1)S(1)} %copy-done, bf16[512,1024]{1,0:T(8,128)(2,1)S(1)} %shard_map.97.one_ref.needed_ref.now_ref, bf16[512,1024]{1,0:T(8,128)(2,1)S(1)} %collective-permute-done.8.two_ref.one_ref, ...), custom_call_target="tpu_custom_call" | custom-call | tf_op jit(solution)/shard_map/pallas_call | solution.py:355
  157.0 7.0 %shard_map.99.two_ref = bf16[512,1024]{1,0:T(8,128)(2,1)S(1)} custom-call(bf16[8,2,64,2240]{3,2,1,0:T(8,128)(2,1)} %bitcast.29, bf16[2240,1024]{1,0:T(8,128)(2,1)} %bitcast.27, f32[9,1024]{1,0:T(8,128)S(1)} %bitcast.17, bf16[4,64,2240]{2,1,0:T(8,128)(2,1)} %copy-done.1), custom_call_target="tpu_custom_call" | custom-call | tf_op jit(solution)/shard_map/pallas_call | solution.py:297
  164.4 3.0 %shard_map.101 = (bf16[4,64,2240]{2,1,0:T(8,128)(2,1)S(1)}, bf16[4,64,2240]{2,1,0:T(8,128)(2,1)S(1)}) custom-call(s32[2]{0:T(128)S(1)} %pad_add_fusion.place_ref, bf16[512,1024]{1,0:T(8,128)(2,1)S(1)} %shard_map.97.one_ref.needed_ref.now_ref, bf16[512,1024]{1,0:T(8,128)(2,1)S(1)} %collective-permute-done.8.two_ref.one_ref, ...), custom_call_target="tpu_custom_call" | custom-call | tf_op jit(solution)/shard_map/pallas_call | solution.py:355
  168.2 1.8 collective-permute-start.15
  170.0 2.1 collective-permute-start.16
  172.5 1.9 collective-permute-start.12
  174.4 10.7 %collective-permute-done.14.refs_3_ = bf16[64,2240]{1,0:T(8,128)(2,1)S(1)} collective-permute-done((bf16[64,2240]{1,0:T(8,128)(2,1)S(1)}, bf16[64,2240]{1,0:T(8,128)(2,1)S(1)}, u32[]{:S(2)}, u32[]{:S(2)}) %collective-permute-start.14) | collective-permute-done | bytes 286752 | tf_op jit(solution)/shard_map/ppermute | solution.py:366
  186.0 11.0 %collective-permute-done.11.refs_0_ = bf16[64,2240]{1,0:T(8,128)(2,1)S(1)} collective-permute-done((bf16[64,2240]{1,0:T(8,128)(2,1)S(1)}, bf16[64,2240]{1,0:T(8,128)(2,1)S(1)}, u32[]{:S(2)}, u32[]{:S(2)}) %collective-permute-start.11) | collective-permute-done | bytes 286752 | tf_op jit(solution)/shard_map/ppermute | solution.py:366
  (68 shorter events, 15.9 us)
Async XLA Ops:
  6.5 76.3 %all-gather.4.cloned.1.call-start = ((), (), s32[]{:S(2)}) async-start(), calls=%async_computation.2 | async-start | bytes 11612160 | tf_op jit(solution)/shard_map/all_gather | solution.py:241
  43.2 26.2 %all-to-all-start.1 = ((bf16[256,8,128]{2,1,0:T(8,128)(2,1)}), bf16[256,8,128]{2,1,0:T(8,128)(2,1)S(1)}, u32[]{:S(2)}, u32[]{:S(2)}) async-start(bf16[256,8,128]{2,1,0:T(8,128)(2,1)} %shard_map.92), calls=%async_computation.1 | async-start | bytes 1048576 | tf_op jit(solution)/shard_map/all_to_all | solution.py:260
  50.4 95.3 %all-gather.6.cloned.1.call-start = ((), (), s32[]{:S(2)}) async-start(), calls=%async_computation.3 | async-start | bytes 5308416 | tf_op jit(solution)/shard_map/all_gather | solution.py:349
  50.4 19.0 %copy-start.11 = (bf16[4,2,16,2240]{3,2,1,0:T(8,128)(2,1)S(1)}, bf16[4,2,16,2240]{3,2,1,0:T(8,128)(2,1)}, u32[]{:S(2)}) copy-start(bf16[4,2,16,2240]{3,2,1,0:T(8,128)(2,1)} %param.10) | copy-start | bytes 1720324
  56.6 26.2 %copy-start.8 = (bf16[4,2,16,2240]{3,2,1,0:T(8,128)(2,1)S(1)}, bf16[4,2,16,2240]{3,2,1,0:T(8,128)(2,1)}, u32[]{:S(2)}) copy-start(bf16[4,2,16,2240]{3,2,1,0:T(8,128)(2,1)} %param.9) | copy-start | bytes 1720324
  87.4 24.8 %copy-start.3 = (bf16[64,2240]{1,0:T(8,128)(2,1)}, bf16[64,2240]{1,0:T(8,128)(2,1)S(1)}, u32[]{:S(2)}) copy-start(bf16[64,2240]{1,0:T(8,128)(2,1)S(1)} %get-tuple-element.20.refs_0_.hidden_ref) | copy-start | bytes 860164
  87.4 13.2 %collective-permute-start = (bf16[64,2240]{1,0:T(8,128)(2,1)S(1)}, bf16[64,2240]{1,0:T(8,128)(2,1)S(1)}, u32[]{:S(2)}, u32[]{:S(2)}) collective-permute-start(bf16[64,2240]{1,0:T(8,128)(2,1)S(1)} %get-tuple-element.19.one_ref.hidden_ref), channel_id=1, source_target_pairs={{0,8},{8,16},{16,24},{24,32},{32,40},{40,48},{48,56},{56,64},{64,7... | collective-permute-start | bytes 860168 | tf_op jit(solution)/shard_map/ppermute | solution.py:338
  90.5 19.9 %copy-start.13 = (f32[3,3,2,512]{3,2,1,0:T(2,128)S(1)}, f32[3,3,2,512]{3,2,1,0:T(2,128)}, u32[]{:S(2)}) copy-start(f32[3,3,2,512]{3,2,1,0:T(2,128)} %param.16) | copy-start | bytes 110596
  90.5 16.5 %collective-permute-start.1 = (bf16[64,2240]{1,0:T(8,128)(2,1)S(1)}, bf16[64,2240]{1,0:T(8,128)(2,1)S(1)}, u32[]{:S(2)}, u32[]{:S(2)}) collective-permute-start(bf16[64,2240]{1,0:T(8,128)(2,1)S(1)} %get-tuple-element.20.refs_0_.hidden_ref), channel_id=1, source_target_pairs={{0,2},{1,3},{2,4},{3,5},{4,6},{5,7},{6,0},{7,1},{8,10},{9,11},{10,... | collective-permute-start | bytes 860168 | tf_op jit(solution)/shard_map/ppermute | solution.py:337
  91.2 15.9 %collective-permute-start.2 = (bf16[64,2240]{1,0:T(8,128)(2,1)S(1)}, bf16[64,2240]{1,0:T(8,128)(2,1)S(1)}, u32[]{:S(2)}, u32[]{:S(2)}) collective-permute-start(bf16[64,2240]{1,0:T(8,128)(2,1)S(1)} %get-tuple-element.20.refs_0_.hidden_ref), channel_id=1, source_target_pairs={{0,4},{1,5},{2,6},{3,7},{4,0},{5,1},{6,2},{7,3},{8,12},{9,13},{10,... | collective-permute-start | bytes 860168 | tf_op jit(solution)/shard_map/ppermute | solution.py:337
  92.9 14.7 %collective-permute-start.3 = (bf16[64,2240]{1,0:T(8,128)(2,1)S(1)}, bf16[64,2240]{1,0:T(8,128)(2,1)S(1)}, u32[]{:S(2)}, u32[]{:S(2)}) collective-permute-start(bf16[64,2240]{1,0:T(8,128)(2,1)S(1)} %get-tuple-element.20.refs_0_.hidden_ref), channel_id=1, source_target_pairs={{0,6},{1,7},{2,0},{3,1},{4,2},{5,3},{6,4},{7,5},{8,14},{9,15},{10,... | collective-permute-start | bytes 860168 | tf_op jit(solution)/shard_map/ppermute | solution.py:337
  109.3 1.7 collective-permute-start.4
  109.4 2.0 collective-permute-start.5
  109.9 1.9 collective-permute-start.6
  110.0 2.2 %collective-permute-start.7 = (bf16[64,2240]{1,0:T(8,128)(2,1)S(1)}, bf16[64,2240]{1,0:T(8,128)(2,1)S(1)}, u32[]{:S(2)}, u32[]{:S(2)}) collective-permute-start(bf16[64,2240]{1,0:T(8,128)(2,1)S(1)} %collective-permute-done.3.refs_2_.refs_6_), channel_id=1, source_target_pairs={{0,1},{1,0},{2,3},{3,2},{4,5},{5,4},{6,7},{7,6},{8,9},{9,8},{10,11... | collective-permute-start | bytes 860168 | tf_op jit(solution)/shard_map/ppermute | solution.py:341
  120.2 32.5 %collective-permute-start.8 = (bf16[512,1024]{1,0:T(8,128)(2,1)}, bf16[512,1024]{1,0:T(8,128)(2,1)S(1)}, u32[]{:S(2)}, u32[]{:S(2)}) collective-permute-start(bf16[512,1024]{1,0:T(8,128)(2,1)} %shard_map.96.needed_ref.now_ref), channel_id=1, source_target_pairs={{0,8},{8,16},{16,24},{24,32},{32,40},{40,48},{48,56},{56,64},{64,7... | collective-permute-start | bytes 3145736 | tf_op jit(solution)/shard_map/ppermute | solution.py:351
  156.8 7.3 %collective-permute-start.9 = (bf16[4,64,2240]{2,1,0:T(8,128)(2,1)S(1)}, bf16[4,64,2240]{2,1,0:T(8,128)(2,1)S(1)}, u32[]{:S(2)}, u32[]{:S(2)}) collective-permute-start(bf16[4,64,2240]{2,1,0:T(8,128)(2,1)S(1)} %get-tuple-element.22), channel_id=1, source_target_pairs={{0,1},{1,0},{2,3},{3,2},{4,5},{5,4},{6,7},{7,6},{8,9},{9,8},{10,11... | collective-permute-start | bytes 3440648 | tf_op jit(solution)/shard_map/ppermute | solution.py:356
  167.4 4.7 %collective-permute-start.10 = (bf16[4,64,2240]{2,1,0:T(8,128)(2,1)S(1)}, bf16[4,64,2240]{2,1,0:T(8,128)(2,1)S(1)}, u32[]{:S(2)}, u32[]{:S(2)}) collective-permute-start(bf16[4,64,2240]{2,1,0:T(8,128)(2,1)S(1)} %get-tuple-element.25), channel_id=1, source_target_pairs={{0,1},{1,0},{2,3},{3,2},{4,5},{5,4},{6,7},{7,6},{8,9},{9,8},{10,11... | collective-permute-start | bytes 3440648 | tf_op jit(solution)/shard_map/ppermute | solution.py:356
  167.7 17.4 %collective-permute-start.14 = (bf16[64,2240]{1,0:T(8,128)(2,1)S(1)}, bf16[64,2240]{1,0:T(8,128)(2,1)S(1)}, u32[]{:S(2)}, u32[]{:S(2)}) collective-permute-start(bf16[64,2240]{1,0:T(8,128)(2,1)S(1)} %get-tuple-element.30), channel_id=1, source_target_pairs={{0,2},{1,3},{2,4},{3,5},{4,6},{5,7},{6,0},{7,1},{8,10},{9,11},{10,... | collective-permute-start | bytes 860168 | tf_op jit(solution)/shard_map/ppermute | solution.py:366
  168.2 16.9 %collective-permute-start.15 = (bf16[64,2240]{1,0:T(8,128)(2,1)S(1)}, bf16[64,2240]{1,0:T(8,128)(2,1)S(1)}, u32[]{:S(2)}, u32[]{:S(2)}) collective-permute-start(bf16[64,2240]{1,0:T(8,128)(2,1)S(1)} %get-tuple-element.31), channel_id=1, source_target_pairs={{0,4},{1,5},{2,6},{3,7},{4,0},{5,1},{6,2},{7,3},{8,12},{9,13},{10,... | collective-permute-start | bytes 860168 | tf_op jit(solution)/shard_map/ppermute | solution.py:366
  170.0 16.0 %collective-permute-start.16 = (bf16[64,2240]{1,0:T(8,128)(2,1)S(1)}, bf16[64,2240]{1,0:T(8,128)(2,1)S(1)}, u32[]{:S(2)}, u32[]{:S(2)}) collective-permute-start(bf16[64,2240]{1,0:T(8,128)(2,1)S(1)} %get-tuple-element.32), channel_id=1, source_target_pairs={{0,6},{1,7},{2,0},{3,1},{4,2},{5,3},{6,4},{7,5},{8,14},{9,15},{10,... | collective-permute-start | bytes 860168 | tf_op jit(solution)/shard_map/ppermute | solution.py:366
  172.4 24.7 %collective-permute-start.11 = (bf16[64,2240]{1,0:T(8,128)(2,1)S(1)}, bf16[64,2240]{1,0:T(8,128)(2,1)S(1)}, u32[]{:S(2)}, u32[]{:S(2)}) collective-permute-start(bf16[64,2240]{1,0:T(8,128)(2,1)S(1)} %get-tuple-element.27), channel_id=1, source_target_pairs={{0,2},{1,3},{2,4},{3,5},{4,6},{5,7},{6,0},{7,1},{8,10},{9,11},{10,... | collective-permute-start | bytes 860168 | tf_op jit(solution)/shard_map/ppermute | solution.py:366
  172.5 24.6 %collective-permute-start.12 = (bf16[64,2240]{1,0:T(8,128)(2,1)S(1)}, bf16[64,2240]{1,0:T(8,128)(2,1)S(1)}, u32[]{:S(2)}, u32[]{:S(2)}) collective-permute-start(bf16[64,2240]{1,0:T(8,128)(2,1)S(1)} %get-tuple-element.28), channel_id=1, source_target_pairs={{0,4},{1,5},{2,6},{3,7},{4,0},{5,1},{6,2},{7,3},{8,12},{9,13},{10,... | collective-permute-start | bytes 860168 | tf_op jit(solution)/shard_map/ppermute | solution.py:366
  185.1 12.6 %collective-permute-start.13 = (bf16[64,2240]{1,0:T(8,128)(2,1)S(1)}, bf16[64,2240]{1,0:T(8,128)(2,1)S(1)}, u32[]{:S(2)}, u32[]{:S(2)}) collective-permute-start(bf16[64,2240]{1,0:T(8,128)(2,1)S(1)} %get-tuple-element.29), channel_id=1, source_target_pairs={{0,6},{1,7},{2,0},{3,1},{4,2},{5,3},{6,4},{7,5},{8,14},{9,15},{10,... | collective-permute-start | bytes 860168 | tf_op jit(solution)/shard_map/ppermute | solution.py:366
  (11 other events, 46.7 us)
Sparse Core Ops, SparseCore 0:
  9.2 73.5 all-gather.3
  109.4 36.2 all-gather.5

commit v5 on v4

--- a/solution.py
+++ b/solution.py
@@ -150,14 +150,9 @@
         out_ref[r : r + chunk] = (left + mid + right).astype(BF)
 
 
-def spatial_kernel(hid_ref, w_ref, taps_ref, needed_ref, out_ref, act_ref):
-    groups, rows, model = hid_ref.shape
-    depthwise(hid_ref[...].reshape(groups * rows, model), w_ref, taps_ref, out_ref, act_ref)
-
-
 def pieces_kernel(place_ref, *refs):
     peers = 8
-    pieces, (w_ref, taps_ref, out_ref, act_ref, hid_ref) = refs[:peers], refs[peers:]
+    pieces, (w_ref, taps_ref, _, out_ref, act_ref, hid_ref) = refs[:peers], refs[peers:]
     rows = pieces[0].shape[0]
 
     @pl.when(pl.program_id(0) == 0)
@@ -203,8 +198,8 @@
         send[...] = total(k + 1).astype(BF)
 
 
-def stack_kernel(one_ref, two_ref, *refs):
-    out_ref = refs[-1]
+def stack_kernel(*refs):
+    one_ref, two_ref, out_ref = refs[-3:]
     out_ref[0] = one_ref[...]
     out_ref[1] = two_ref[...]
 
@@ -293,25 +288,16 @@
     ]
     act_scratch = pltpu.VMEM((whole_rows + 2 * col_count, block), F32)
 
-    def spatial_call(whole, f, needed):
-        return pl.pallas_call(
-            spatial_kernel,
-            in_specs=[pl.BlockSpec((peers, None, frame_rows, width), lambda i: (0, f, 0, 0))]
-            + weight_specs
-            + [anywhere],
-            scratch_shapes=[act_scratch],
-            **spatial_out,
-        )(whole, w_flat, taps_s, needed)
-
-    def pieces_call(pieces):
+    def pieces_call(pieces, f, needed):
         return pl.pallas_call(
             pieces_kernel,
             in_specs=[pl.BlockSpec(memory_space=pltpu.SMEM)]
-            + [pl.BlockSpec((frame_rows, width), lambda i: (0, 0))] * peers
-            + weight_specs,
+            + [pl.BlockSpec((None, frame_rows, width), lambda i: (f, 0, 0))] * peers
+            + weight_specs
+            + [anywhere],
             scratch_shapes=[act_scratch, pltpu.VMEM((whole_rows, width), BF)],
             **spatial_out,
-        )(where_am_i, *pieces, w_flat, taps_s)
+        )(where_am_i, *pieces, w_flat, taps_s, needed)
 
     row_block = 256
     point_call = pl.pallas_call(
@@ -334,22 +320,29 @@
     other_core = [(i, i ^ 1) for i in range(peers)]
     ahead = [[(i, (i + 2 * k) % peers) for i in range(peers)] for k in range(4)]
 
-    late_along = [late] + [lax.ppermute(late, "tile", ahead[k]) for k in (1, 2, 3)]
+    def along_of(rows):
+        return [rows] + [lax.ppermute(rows, "tile", ahead[k]) for k in (1, 2, 3)]
+
+    late_along = along_of(late[None])
     before_early = lax.ppermute(early, "blk", next_frames)
+    others = pl.pallas_call(
+        stack_kernel,
+        out_shape=jax.ShapeDtypeStruct((2, frame_rows, width), BF),
+        in_specs=[anywhere] * 3 + [VMEM] * 2,
+        out_specs=VMEM,
+        compiler_params=params(20),
+    )(*late_along[1:], early, before_early)
+    others_along = along_of(others)
     pieces = []
     for part in late_along:
         pieces += [part, lax.ppermute(part, "tile", other_core)]
-    stacked = pl.pallas_call(
-        stack_kernel,
-        out_shape=jax.ShapeDtypeStruct((2, frame_rows, width), BF),
-        in_specs=[VMEM, VMEM] + [anywhere] * 3,
-        out_specs=VMEM,
-        compiler_params=params(20),
-    )(early, before_early, *late_along[1:])
-    whole = lax.all_gather(stacked, "tile", axis=0)
-    late_sp = pieces_call(pieces)
+    late_sp = pieces_call(pieces, 0, taps_t)
     before_late_sp = lax.ppermute(late_sp, "blk", next_frames)
-    early_sp = spatial_call(whole, 0, late_sp)
+    both = []
+    for part in others_along:
+        both += [part, lax.ppermute(part, "tile", other_core)]
+    early_sp = pieces_call(both, 0, late_sp)
+    before_early_sp = pieces_call(both, 1, early_sp)
 
     def core_shares(now, one, two, needed):
         mine, other = point_call(where_am_i, now, one, two, taps_t, w_down, needed)
@@ -365,10 +358,9 @@
         )(mine, from_core, rows)
         return kept, [lax.ppermute(part, "tile", ahead[k + 1]) for k, part in enumerate(sends)]
 
-    late_shares = core_shares(late_sp, early_sp, before_late_sp, early_sp)
-    before_early_sp = spatial_call(whole, 1, late_shares[0])
+    late_shares = core_shares(late_sp, early_sp, before_late_sp, before_early_sp)
     late_kept, late_back = sums(*late_shares, late)
-    early_shares = core_shares(early_sp, before_late_sp, before_early_sp, late_kept)
+    early_shares = core_shares(early_sp, before_late_sp, before_early_sp, late_shares[0])
     early_kept, early_back = sums(*early_shares, early)
     return pl.pallas_call(
         final_kernel,

time: 206 us -> 206 us (level)
  waiting for transfers between devices: 83.2 us -> 75.8 us
  starting transfers between devices: 26 us -> 30.4 us
    ppermute x3 -> x10, waiting for transfers between devices: 7.06 us -> 26.4 us  [the longest x6 26.4 us: along_of(): return [rows] + [lax.ppermute(rows, 'tile', ahead[k]) for k in (1, 2, 3)]]
    all_gather x1 -> x0, waiting for transfers between devices: 19.2 us -> none  [on_device(): whole = lax.all_gather(stacked, 'tile', axis=0)]
    pallas_call x1 -> x3, Pallas kernels: 7.29 us -> 22.9 us  [pieces_call(): pl.pallas_call(pieces_kernel, in_specs=[pl.BlockSpec(memory_space=pltpu.S...]
    pallas_call x2 -> x0, Pallas kernels: 14 us -> none  [spatial_call(): pl.pallas_call(spatial_kernel, in_specs=[pl.BlockSpec((peers, None, frame...]
    ppermute x1, waiting for transfers between devices: 5.71 us -> 0.01 us  [on_device(): before_early = lax.ppermute(early, 'blk', next_frames)]
    ppermute x3 -> x10, starting transfers between devices: 4.35 us -> 9.31 us  [the longest x6 8.7 us: along_of(): return [rows] + [lax.ppermute(rows, 'tile', ahead[k]) for k in (1, 2, 3)]]
    unnamed x35 -> x47, local copies, waits for them, and re-layouts: 12 us -> 12.3 us
  transfers between devices with their start and end apart: 20 -> 26, of which waited for: 14 -> 10; matrix products, arithmetic and copies ran while one was open for 4% -> 4% of each run, Pallas kernels for 12% -> 15%
where the time goes in v5:
time: 206 us; the launch traced here: 205 us
  waiting for transfers between devices  75.8 us (37%)
  Pallas kernels  39 us (19%)
  blocking collectives  33.6 us (16%)
  starting transfers between devices  30.4 us (15%)
  between operations  13.8 us (7%)
  local copies, waits for them, and re-layouts  12.3 us (6%)
    all_to_all x1, blocking collectives, on_device(): parts = lax.all_to_all(parts, everyone, 0, 0, tiled=True)  33.6 us
    ppermute x6, waiting for transfers between devices, along_of(): return [rows] + [lax.ppermute(rows, 'tile', ahead[k]) for k in (1, 2, 3)]  26.4 us
    ppermute x6, waiting for transfers between devices, sums(): lax.ppermute(part, 'tile', ahead[k + 1])  23.1 us
    pallas_call x3, Pallas kernels, pieces_call(): pl.pallas_call(pieces_kernel, in_specs=[pl.BlockSpec(memory_space=pltpu.S...  22.9 us
    all_to_all x1, waiting for transfers between devices, on_device(): state = lax.all_to_all(sums, everyone, 0, 0, tiled=True)  12.9 us
    all_gather x1, waiting for transfers between devices, on_device(): w_out_whole = lax.all_gather(w_output, 'tile', axis=0, tiled=True)  12.6 us
    unnamed x47, local copies, waits for them, and re-layouts  12.3 us
    ppermute x6, starting transfers between devices, along_of(): return [rows] + [lax.ppermute(rows, 'tile', ahead[k]) for k in (1, 2, 3)]  8.7 us
  transfers between devices with their start and end apart: 26, of which 10 were waited for; matrix products, arithmetic and copies ran while one was open for 4% of the time, Pallas kernels for 15%

profile of v5, /device:TPU:2, one launch (start us, length us, event | category | flops | bytes accessed | tf_op | source)
XLA Modules:
  0.0 204.9 jit_solution(17466022521747946791)
XLA Ops:
  8.5 33.6 %all_to_all.10.in_ref = bf16[256,8,128]{2,1,0:T(8,128)(2,1)S(1)} all-to-all(bf16[256,8,128]{2,1,0:T(8,128)(2,1)S(1)} %shard_map.91), channel_id=1, replica_groups=mesh['blk'=32,'tile'=8] {'blk','tile'}, dimensions={0} | all-to-all | bytes 1048576 | tf_op jit(solution)/shard_map/all_to_all | solution.py:251
  43.2 7.1 %all-to-all-start.1 = ((bf16[256,8,128]{2,1,0:T(8,128)(2,1)}), bf16[256,8,128]{2,1,0:T(8,128)(2,1)S(1)}, u32[]{:S(2)}, u32[]{:S(2)}) async-start(bf16[256,8,128]{2,1,0:T(8,128)(2,1)} %shard_map.92), calls=%async_computation.1 | async-start | bytes 1048576 | tf_op jit(solution)/shard_map/all_to_all | solution.py:255
  50.4 6.1 %copy.12 = bf16[280,8,2,512]{3,1,2,0:T(8,128)(2,1)} copy(bf16[280,8,2,512]{3,2,1,0:T(2,128)(2,1)} %bitcast.34) | data formatting | bytes 9175040
  56.5 12.9 %all-to-all-done.1.state_ref = bf16[256,8,128]{2,1,0:T(8,128)(2,1)S(1)} async-done(((bf16[256,8,128]{2,1,0:T(8,128)(2,1)}), bf16[256,8,128]{2,1,0:T(8,128)(2,1)S(1)}, u32[]{:S(2)}, u32[]{:S(2)}) %all-to-all-start.1) | async-done | bytes 524320 | tf_op jit(solution)/shard_map/all_to_all | solution.py:255
  70.2 12.6 %all-gather.2.cloned.1.call-done.w_hbm = bf16[2240,2240]{1,0:T(8,128)(2,1)} async-done(((bf16[280,2240]{1,0:T(8,128)(2,1)}), bf16[2240,2240]{1,0:T(8,128)(2,1)}) %all-gather.2.cloned.1.call-update) | async-done | bytes 10035216 | tf_op jit(solution)/shard_map/all_gather | solution.py:236
  82.8 4.6 %shard_map.94 = (bf16[64,2240]{1,0:T(8,128)(2,1)S(1)}, bf16[64,2240]{1,0:T(8,128)(2,1)S(1)}) custom-call(bf16[128,2240]{1,0:T(8,128)(2,1)S(1)} %shard_map.93.att_ref, bf16[128,2240]{1,0:T(8,128)(2,1)S(1)} %bitcast.23, bf16[2240,2240]{1,0:T(8,128)(2,1)} %all-gather.2.cloned.1.call-done.w_hbm, bf16[2240,1024]{1,0:T(8,128)(2,1)} %bitcast.30), custom_call_target="tpu_custom_call" | custom-call | tf_op jit(solution)/shard_map/pallas_call | solution.py:267
  88.1 1.8 collective-permute-start.1
  89.8 2.0 collective-permute-start.2
  91.9 3.0 %collective-permute-start.3 = (bf16[64,2240]{1,0:T(8,128)(2,1)S(1)}, bf16[64,2240]{1,0:T(8,128)(2,1)S(1)}, u32[]{:S(2)}, u32[]{:S(2)}) collective-permute-start(bf16[64,2240]{1,0:T(8,128)(2,1)S(1)} %get-tuple-element.20.refs_3_.hidden_ref), channel_id=1, source_target_pairs={{0,8},{8,16},{16,24},{24,32},{32,40},{40,48},{48,56},{56,64},{64,7... | collective-permute-start | bytes 860168 | tf_op jit(solution)/shard_map/ppermute | solution.py:327
  95.0 9.2 %collective-permute-done.refs_0_.refs_2_ = bf16[1,64,2240]{2,1,0:T(8,128)(2,1)S(1)} collective-permute-done((bf16[1,64,2240]{2,1,0:T(8,128)(2,1)S(1)}, bf16[1,64,2240]{2,1,0:T(8,128)(2,1)S(1)}, u32[]{:S(2)}, u32[]{:S(2)}) %collective-permute-start) | collective-permute-done | bytes 286752 | tf_op jit(solution)/shard_map/ppermute | solution.py:324
  105.0 2.7 %collective-permute-start.9 = (bf16[2,64,2240]{2,1,0:T(8,128)(2,1)S(1)}, bf16[2,64,2240]{2,1,0:T(8,128)(2,1)}, u32[]{:S(2)}, u32[]{:S(2)}) collective-permute-start(bf16[2,64,2240]{2,1,0:T(8,128)(2,1)S(1)} %shard_map.95.refs_0_), channel_id=1, source_target_pairs={{0,6},{1,7},{2,0},{3,1},{4,2},{5,3},{6,4},{7,5},{8,14},{9,15},{10,... | collective-permute-start | bytes 1720328 | tf_op jit(solution)/shard_map/ppermute | solution.py:324
  109.4 7.4 %shard_map.96.refs_10_.now_ref = bf16[512,1024]{1,0:T(8,128)(2,1)} custom-call(s32[2]{0:T(128)S(1)} %pad_add_fusion.place_ref, bf16[1,64,2240]{2,1,0:T(8,128)(2,1)S(1)} %bitcast.19, bf16[1,64,2240]{2,1,0:T(8,128)(2,1)S(1)} %collective-permute-done.11.refs_1_, bf16[1,64,2240]{2,1,0:T(8,128)(2,1)S(1)} %collective-permute-done.refs_0_.refs_2_, ...), custom_call_target="tpu_custom_call" | custom-call | tf_op jit(solution)/shard_map/pallas_call | solution.py:292
  116.8 3.1 %collective-permute-start.15 = (bf16[512,1024]{1,0:T(8,128)(2,1)}, bf16[512,1024]{1,0:T(8,128)(2,1)}, u32[]{:S(2)}, u32[]{:S(2)}) collective-permute-start(bf16[512,1024]{1,0:T(8,128)(2,1)} %shard_map.96.refs_10_.now_ref), channel_id=1, source_target_pairs={{0,8},{8,16},{16,24},{24,32},{32,40},{40,48},{48,56},{56,64},{64,7... | collective-permute-start | bytes 3145736 | tf_op jit(solution)/shard_map/ppermute | solution.py:340
  120.0 13.6 %collective-permute-done.9.refs_6_ = bf16[2,64,2240]{2,1,0:T(8,128)(2,1)} collective-permute-done((bf16[2,64,2240]{2,1,0:T(8,128)(2,1)S(1)}, bf16[2,64,2240]{2,1,0:T(8,128)(2,1)}, u32[]{:S(2)}, u32[]{:S(2)}) %collective-permute-start.9) | collective-permute-done | bytes 573472 | tf_op jit(solution)/shard_map/ppermute | solution.py:324
  133.7 3.4 %collective-permute-done.5.refs_2_ = bf16[2,64,2240]{2,1,0:T(8,128)(2,1)S(1)} collective-permute-done((bf16[2,64,2240]{2,1,0:T(8,128)(2,1)S(1)}, bf16[2,64,2240]{2,1,0:T(8,128)(2,1)S(1)}, u32[]{:S(2)}, u32[]{:S(2)}) %collective-permute-start.5) | collective-permute-done | bytes 573472 | tf_op jit(solution)/shard_map/ppermute | solution.py:324
  137.6 2.8 %copy.11.w_ref = bf16[512,2240]{1,0:T(8,128)(2,1)S(1)} copy(bf16[512,2240]{0,1:T(8,128)(2,1)} %param.15) | data formatting | bytes 4587520 | tf_op args[6]
  141.9 7.7 %shard_map.97.refs_10_.one_ref.now_ref = bf16[512,1024]{1,0:T(8,128)(2,1)} custom-call(s32[2]{0:T(128)S(1)} %copy-done.17, bf16[2,64,2240]{2,1,0:T(8,128)(2,1)S(1)} %shard_map.95.refs_0_, bf16[2,64,2240]{2,1,0:T(8,128)(2,1)} %collective-permute-done.4.refs_1_, bf16[2,64,2240]{2,1,0:T(8,128)(2,1)S(1)} %collective-permute-done.5.refs_2_, ...), custom_call_target="tpu_custom_call" | custom-call | tf_op jit(solution)/shard_map/pallas_call | solution.py:292
  149.6 7.8 %shard_map.98.needed_ref.two_ref = bf16[512,1024]{1,0:T(8,128)(2,1)} custom-call(s32[2]{0:T(128)S(1)} %copy-done.18, bf16[2,64,2240]{2,1,0:T(8,128)(2,1)S(1)} %shard_map.95.refs_0_, bf16[2,64,2240]{2,1,0:T(8,128)(2,1)} %collective-permute-done.4.refs_1_, bf16[2,64,2240]{2,1,0:T(8,128)(2,1)S(1)} %collective-permute-done.5.refs_2_, ...), custom_call_target="tpu_custom_call" | custom-call | tf_op jit(solution)/shard_map/pallas_call | solution.py:292
  158.7 3.6 %shard_map.99 = (bf16[4,64,2240]{2,1,0:T(8,128)(2,1)S(1)}, bf16[4,64,2240]{2,1,0:T(8,128)(2,1)S(1)}) custom-call(s32[2]{0:T(128)S(1)} %copy-done.18, bf16[512,1024]{1,0:T(8,128)(2,1)S(1)} %copy-done.1, bf16[512,1024]{1,0:T(8,128)(2,1)S(1)} %copy-done, bf16[512,1024]{1,0:T(8,128)(2,1)} %collective-permute-done.15.two_ref.one_ref, f32[3,1024]{1,0:T(4,128)S(1)} %bitcast.28, ...), custom_call_target="tpu_custom_call" | custom-call | tf_op jit(solution)/shard_map/pallas_call | solution.py:348
  162.4 3.6 %shard_map.100 = (bf16[4,64,2240]{2,1,0:T(8,128)(2,1)S(1)}, bf16[4,64,2240]{2,1,0:T(8,128)(2,1)S(1)}) custom-call(s32[2]{0:T(128)S(1)} %copy-done.18, bf16[512,1024]{1,0:T(8,128)(2,1)S(1)} %copy-done, bf16[512,1024]{1,0:T(8,128)(2,1)} %collective-permute-done.15.two_ref.one_ref, bf16[512,1024]{1,0:T(8,128)(2,1)S(1)} %copy-done.3, f32[3,1024]{1,0:T(4,128)S(1)} %bitcast.29, ...), custom_call_target="tpu_custom_call" | custom-call | tf_op jit(solution)/shard_map/pallas_call | solution.py:348
  167.2 2.5 %collective-permute-start.22 = (bf16[64,2240]{1,0:T(8,128)(2,1)S(1)}, bf16[64,2240]{1,0:T(8,128)(2,1)S(1)}, u32[]{:S(2)}, u32[]{:S(2)}) collective-permute-start(bf16[64,2240]{1,0:T(8,128)(2,1)S(1)} %get-tuple-element.31), channel_id=1, source_target_pairs={{0,4},{1,5},{2,6},{3,7},{4,0},{5,1},{6,2},{7,3},{8,12},{9,13},{10,... | collective-permute-start | bytes 860168 | tf_op jit(solution)/shard_map/ppermute | solution.py:359
  172.1 1.7 collective-permute-start.19
  173.8 10.8 %collective-permute-done.21.refs_3_ = bf16[64,2240]{1,0:T(8,128)(2,1)S(1)} collective-permute-done((bf16[64,2240]{1,0:T(8,128)(2,1)S(1)}, bf16[64,2240]{1,0:T(8,128)(2,1)S(1)}, u32[]{:S(2)}, u32[]{:S(2)}) %collective-permute-start.21) | collective-permute-done | bytes 286752 | tf_op jit(solution)/shard_map/ppermute | solution.py:359
  185.5 10.8 %collective-permute-done.18.refs_0_ = bf16[64,2240]{1,0:T(8,128)(2,1)S(1)} collective-permute-done((bf16[64,2240]{1,0:T(8,128)(2,1)S(1)}, bf16[64,2240]{1,0:T(8,128)(2,1)S(1)}, u32[]{:S(2)}, u32[]{:S(2)}) %collective-permute-start.18) | collective-permute-done | bytes 286752 | tf_op jit(solution)/shard_map/ppermute | solution.py:359
  (91 shorter events, 16.6 us)
Async XLA Ops:
  6.5 76.3 %all-gather.2.cloned.1.call-start = ((), (), s32[]{:S(2)}) async-start(), calls=%async_computation.2 | async-start | bytes 11612160 | tf_op jit(solution)/shard_map/all_gather | solution.py:236
  43.2 26.2 %all-to-all-start.1 = ((bf16[256,8,128]{2,1,0:T(8,128)(2,1)}), bf16[256,8,128]{2,1,0:T(8,128)(2,1)S(1)}, u32[]{:S(2)}, u32[]{:S(2)}) async-start(bf16[256,8,128]{2,1,0:T(8,128)(2,1)} %shard_map.92), calls=%async_computation.1 | async-start | bytes 1048576 | tf_op jit(solution)/shard_map/all_to_all | solution.py:255
  87.4 16.8 %collective-permute-start = (bf16[1,64,2240]{2,1,0:T(8,128)(2,1)S(1)}, bf16[1,64,2240]{2,1,0:T(8,128)(2,1)S(1)}, u32[]{:S(2)}, u32[]{:S(2)}) collective-permute-start(bf16[1,64,2240]{2,1,0:T(8,128)(2,1)S(1)} %bitcast.15), channel_id=1, source_target_pairs={{0,2},{1,3},{2,4},{3,5},{4,6},{5,7},{6,0},{7,1},{8,10},{9,11},{10,... | collective-permute-start | bytes 860168 | tf_op jit(solution)/shard_map/ppermute | solution.py:324
  88.1 16.2 %collective-permute-start.1 = (bf16[1,64,2240]{2,1,0:T(8,128)(2,1)S(1)}, bf16[1,64,2240]{2,1,0:T(8,128)(2,1)S(1)}, u32[]{:S(2)}, u32[]{:S(2)}) collective-permute-start(bf16[1,64,2240]{2,1,0:T(8,128)(2,1)S(1)} %bitcast.16), channel_id=1, source_target_pairs={{0,4},{1,5},{2,6},{3,7},{4,0},{5,1},{6,2},{7,3},{8,12},{9,13},{10,... | collective-permute-start | bytes 860168 | tf_op jit(solution)/shard_map/ppermute | solution.py:324
  89.8 15.0 %collective-permute-start.2 = (bf16[1,64,2240]{2,1,0:T(8,128)(2,1)S(1)}, bf16[1,64,2240]{2,1,0:T(8,128)(2,1)S(1)}, u32[]{:S(2)}, u32[]{:S(2)}) collective-permute-start(bf16[1,64,2240]{2,1,0:T(8,128)(2,1)S(1)} %bitcast.17), channel_id=1, source_target_pairs={{0,6},{1,7},{2,0},{3,1},{4,2},{5,3},{6,4},{7,5},{8,14},{9,15},{10,... | collective-permute-start | bytes 860168 | tf_op jit(solution)/shard_map/ppermute | solution.py:324
  91.9 13.1 %collective-permute-start.3 = (bf16[64,2240]{1,0:T(8,128)(2,1)S(1)}, bf16[64,2240]{1,0:T(8,128)(2,1)S(1)}, u32[]{:S(2)}, u32[]{:S(2)}) collective-permute-start(bf16[64,2240]{1,0:T(8,128)(2,1)S(1)} %get-tuple-element.20.refs_3_.hidden_ref), channel_id=1, source_target_pairs={{0,8},{8,16},{16,24},{24,32},{32,40},{40,48},{48,56},{56,64},{64,7... | collective-permute-start | bytes 860168 | tf_op jit(solution)/shard_map/ppermute | solution.py:327
  94.9 12.9 %collective-permute-start.11 = (bf16[1,64,2240]{2,1,0:T(8,128)(2,1)S(1)}, bf16[1,64,2240]{2,1,0:T(8,128)(2,1)S(1)}, u32[]{:S(2)}, u32[]{:S(2)}) collective-permute-start(bf16[1,64,2240]{2,1,0:T(8,128)(2,1)S(1)} %bitcast.18), channel_id=1, source_target_pairs={{0,1},{1,0},{2,3},{3,2},{4,5},{5,4},{6,7},{7,6},{8,9},{9,8},{10,11... | collective-permute-start | bytes 860168 | tf_op jit(solution)/shard_map/ppermute | solution.py:338
  104.2 3.5 %collective-permute-start.12 = (bf16[1,64,2240]{2,1,0:T(8,128)(2,1)S(1)}, bf16[1,64,2240]{2,1,0:T(8,128)(2,1)S(1)}, u32[]{:S(2)}, u32[]{:S(2)}) collective-permute-start(bf16[1,64,2240]{2,1,0:T(8,128)(2,1)S(1)} %collective-permute-done.refs_0_.refs_2_), channel_id=1, source_target_pairs={{0,1},{1,0},{2,3},{3,2},{4,5},{5,4},{6,7},{7,6},{8,9},{9,8},{10,11... | collective-permute-start | bytes 860168 | tf_op jit(solution)/shard_map/ppermute | solution.py:338
  104.2 5.1 %collective-permute-start.13 = (bf16[1,64,2240]{2,1,0:T(8,128)(2,1)S(1)}, bf16[1,64,2240]{2,1,0:T(8,128)(2,1)}, u32[]{:S(2)}, u32[]{:S(2)}) collective-permute-start(bf16[1,64,2240]{2,1,0:T(8,128)(2,1)S(1)} %collective-permute-done.1.refs_1_.refs_4_), channel_id=1, source_target_pairs={{0,1},{1,0},{2,3},{3,2},{4,5},{5,4},{6,7},{7,6},{8,9},{9,8},{10,11... | collective-permute-start | bytes 860168 | tf_op jit(solution)/shard_map/ppermute | solution.py:338
  104.9 4.5 %collective-permute-start.14 = (bf16[1,64,2240]{2,1,0:T(8,128)(2,1)S(1)}, bf16[1,64,2240]{2,1,0:T(8,128)(2,1)}, u32[]{:S(2)}, u32[]{:S(2)}) collective-permute-start(bf16[1,64,2240]{2,1,0:T(8,128)(2,1)S(1)} %collective-permute-done.2.refs_2_.refs_6_), channel_id=1, source_target_pairs={{0,1},{1,0},{2,3},{3,2},{4,5},{5,4},{6,7},{7,6},{8,9},{9,8},{10,11... | collective-permute-start | bytes 860168 | tf_op jit(solution)/shard_map/ppermute | solution.py:338
  105.0 28.6 %collective-permute-start.9 = (bf16[2,64,2240]{2,1,0:T(8,128)(2,1)S(1)}, bf16[2,64,2240]{2,1,0:T(8,128)(2,1)}, u32[]{:S(2)}, u32[]{:S(2)}) collective-permute-start(bf16[2,64,2240]{2,1,0:T(8,128)(2,1)S(1)} %shard_map.95.refs_0_), channel_id=1, source_target_pairs={{0,6},{1,7},{2,0},{3,1},{4,2},{5,3},{6,4},{7,5},{8,14},{9,15},{10,... | collective-permute-start | bytes 1720328 | tf_op jit(solution)/shard_map/ppermute | solution.py:324
  107.7 29.3 %collective-permute-start.5 = (bf16[2,64,2240]{2,1,0:T(8,128)(2,1)S(1)}, bf16[2,64,2240]{2,1,0:T(8,128)(2,1)S(1)}, u32[]{:S(2)}, u32[]{:S(2)}) collective-permute-start(bf16[2,64,2240]{2,1,0:T(8,128)(2,1)S(1)} %shard_map.95.refs_0_), channel_id=1, source_target_pairs={{0,2},{1,3},{2,4},{3,5},{4,6},{5,7},{6,0},{7,1},{8,10},{9,11},{10,... | collective-permute-start | bytes 1720328 | tf_op jit(solution)/shard_map/ppermute | solution.py:324
  107.8 29.3 %collective-permute-start.7 = (bf16[2,64,2240]{2,1,0:T(8,128)(2,1)S(1)}, bf16[2,64,2240]{2,1,0:T(8,128)(2,1)}, u32[]{:S(2)}, u32[]{:S(2)}) collective-permute-start(bf16[2,64,2240]{2,1,0:T(8,128)(2,1)S(1)} %shard_map.95.refs_0_), channel_id=1, source_target_pairs={{0,4},{1,5},{2,6},{3,7},{4,0},{5,1},{6,2},{7,3},{8,12},{9,13},{10,... | collective-permute-start | bytes 1720328 | tf_op jit(solution)/shard_map/ppermute | solution.py:324
  116.8 40.7 %collective-permute-start.15 = (bf16[512,1024]{1,0:T(8,128)(2,1)}, bf16[512,1024]{1,0:T(8,128)(2,1)}, u32[]{:S(2)}, u32[]{:S(2)}) collective-permute-start(bf16[512,1024]{1,0:T(8,128)(2,1)} %shard_map.96.refs_10_.now_ref), channel_id=1, source_target_pairs={{0,8},{8,16},{16,24},{24,32},{32,40},{40,48},{48,56},{56,64},{64,7... | collective-permute-start | bytes 3145736 | tf_op jit(solution)/shard_map/ppermute | solution.py:340
  119.9 20.5 %collective-permute-start.4 = (bf16[2,64,2240]{2,1,0:T(8,128)(2,1)S(1)}, bf16[2,64,2240]{2,1,0:T(8,128)(2,1)}, u32[]{:S(2)}, u32[]{:S(2)}) collective-permute-start(bf16[2,64,2240]{2,1,0:T(8,128)(2,1)S(1)} %shard_map.95.refs_0_), channel_id=1, source_target_pairs={{0,1},{1,0},{2,3},{3,2},{4,5},{5,4},{6,7},{7,6},{8,9},{9,8},{10,11... | collective-permute-start | bytes 1720328 | tf_op jit(solution)/shard_map/ppermute | solution.py:343
  133.7 6.7 %collective-permute-start.10 = (bf16[2,64,2240]{2,1,0:T(8,128)(2,1)}, bf16[2,64,2240]{2,1,0:T(8,128)(2,1)}, u32[]{:S(2)}, u32[]{:S(2)}) collective-permute-start(bf16[2,64,2240]{2,1,0:T(8,128)(2,1)} %collective-permute-done.9.refs_6_), channel_id=1, source_target_pairs={{0,1},{1,0},{2,3},{3,2},{4,5},{5,4},{6,7},{7,6},{8,9},{9,8},{10,11... | collective-permute-start | bytes 1720328 | tf_op jit(solution)/shard_map/ppermute | solution.py:343
  162.3 4.5 %collective-permute-start.17 = (bf16[4,64,2240]{2,1,0:T(8,128)(2,1)S(1)}, bf16[4,64,2240]{2,1,0:T(8,128)(2,1)S(1)}, u32[]{:S(2)}, u32[]{:S(2)}) collective-permute-start(bf16[4,64,2240]{2,1,0:T(8,128)(2,1)S(1)} %get-tuple-element.25), channel_id=1, source_target_pairs={{0,1},{1,0},{2,3},{3,2},{4,5},{5,4},{6,7},{7,6},{8,9},{9,8},{10,11... | collective-permute-start | bytes 3440648 | tf_op jit(solution)/shard_map/ppermute | solution.py:349
  166.0 4.4 %collective-permute-start.16 = (bf16[4,64,2240]{2,1,0:T(8,128)(2,1)S(1)}, bf16[4,64,2240]{2,1,0:T(8,128)(2,1)S(1)}, u32[]{:S(2)}, u32[]{:S(2)}) collective-permute-start(bf16[4,64,2240]{2,1,0:T(8,128)(2,1)S(1)} %get-tuple-element.23), channel_id=1, source_target_pairs={{0,1},{1,0},{2,3},{3,2},{4,5},{5,4},{6,7},{7,6},{8,9},{9,8},{10,11... | collective-permute-start | bytes 3440648 | tf_op jit(solution)/shard_map/ppermute | solution.py:349
  167.1 17.5 %collective-permute-start.21 = (bf16[64,2240]{1,0:T(8,128)(2,1)S(1)}, bf16[64,2240]{1,0:T(8,128)(2,1)S(1)}, u32[]{:S(2)}, u32[]{:S(2)}) collective-permute-start(bf16[64,2240]{1,0:T(8,128)(2,1)S(1)} %get-tuple-element.30), channel_id=1, source_target_pairs={{0,2},{1,3},{2,4},{3,5},{4,6},{5,7},{6,0},{7,1},{8,10},{9,11},{10,... | collective-permute-start | bytes 860168 | tf_op jit(solution)/shard_map/ppermute | solution.py:359
  167.2 17.4 %collective-permute-start.22 = (bf16[64,2240]{1,0:T(8,128)(2,1)S(1)}, bf16[64,2240]{1,0:T(8,128)(2,1)S(1)}, u32[]{:S(2)}, u32[]{:S(2)}) collective-permute-start(bf16[64,2240]{1,0:T(8,128)(2,1)S(1)} %get-tuple-element.31), channel_id=1, source_target_pairs={{0,4},{1,5},{2,6},{3,7},{4,0},{5,1},{6,2},{7,3},{8,12},{9,13},{10,... | collective-permute-start | bytes 860168 | tf_op jit(solution)/shard_map/ppermute | solution.py:359
  169.7 15.8 %collective-permute-start.23 = (bf16[64,2240]{1,0:T(8,128)(2,1)S(1)}, bf16[64,2240]{1,0:T(8,128)(2,1)S(1)}, u32[]{:S(2)}, u32[]{:S(2)}) collective-permute-start(bf16[64,2240]{1,0:T(8,128)(2,1)S(1)} %get-tuple-element.32), channel_id=1, source_target_pairs={{0,6},{1,7},{2,0},{3,1},{4,2},{5,3},{6,4},{7,5},{8,14},{9,15},{10,... | collective-permute-start | bytes 860168 | tf_op jit(solution)/shard_map/ppermute | solution.py:359
  170.7 25.6 %collective-permute-start.18 = (bf16[64,2240]{1,0:T(8,128)(2,1)S(1)}, bf16[64,2240]{1,0:T(8,128)(2,1)S(1)}, u32[]{:S(2)}, u32[]{:S(2)}) collective-permute-start(bf16[64,2240]{1,0:T(8,128)(2,1)S(1)} %get-tuple-element.27), channel_id=1, source_target_pairs={{0,2},{1,3},{2,4},{3,5},{4,6},{5,7},{6,0},{7,1},{8,10},{9,11},{10,... | collective-permute-start | bytes 860168 | tf_op jit(solution)/shard_map/ppermute | solution.py:359
  172.1 24.2 %collective-permute-start.19 = (bf16[64,2240]{1,0:T(8,128)(2,1)S(1)}, bf16[64,2240]{1,0:T(8,128)(2,1)S(1)}, u32[]{:S(2)}, u32[]{:S(2)}) collective-permute-start(bf16[64,2240]{1,0:T(8,128)(2,1)S(1)} %get-tuple-element.28), channel_id=1, source_target_pairs={{0,4},{1,5},{2,6},{3,7},{4,0},{5,1},{6,2},{7,3},{8,12},{9,13},{10,... | collective-permute-start | bytes 860168 | tf_op jit(solution)/shard_map/ppermute | solution.py:359
  184.6 12.4 %collective-permute-start.20 = (bf16[64,2240]{1,0:T(8,128)(2,1)S(1)}, bf16[64,2240]{1,0:T(8,128)(2,1)S(1)}, u32[]{:S(2)}, u32[]{:S(2)}) collective-permute-start(bf16[64,2240]{1,0:T(8,128)(2,1)S(1)} %get-tuple-element.29), channel_id=1, source_target_pairs={{0,6},{1,7},{2,0},{3,1},{4,2},{5,3},{6,4},{7,5},{8,14},{9,15},{10,... | collective-permute-start | bytes 860168 | tf_op jit(solution)/shard_map/ppermute | solution.py:359
  (23 other events, 227.5 us)
Sparse Core Ops, SparseCore 0:
  9.2 73.5 all-gather.1

commit v6 on v5

--- a/solution.py
+++ b/solution.py
@@ -164,16 +164,55 @@
     depthwise(hid_ref[...], w_ref, taps_ref, out_ref, act_ref)
 
 
+def both_kernel(place_ref, *refs):
+    peers, frames = 8, 2
+    pieces = refs[:peers]
+    w_ref, taps_ref, _, one_ref, two_ref, act_ref, hid_ref = refs[peers:]
+    rows = pieces[0].shape[1]
+
+    @pl.when(pl.program_id(0) == 0)
+    def _():
+        for p, piece in enumerate(pieces):
+            source = 2 * ((place_ref[0] + 4 - p // 2) % 4) + (place_ref[1] + p % 2) % 2
+            target = pl.ds(pl.multiple_of(source * rows, rows), rows)
+            for f in range(frames):
+                hid_ref[f, target] = piece[f]
+
+    for f, out_ref in enumerate((one_ref, two_ref)):
+        depthwise(hid_ref[f], w_ref, taps_ref, out_ref, act_ref.at[f])
+
+
 def point_kernel(
-    place_ref, now_ref, one_ref, two_ref, taps_ref, w_ref, needed_ref, mine_ref, other_ref
+    place_ref,
+    now_ref,
+    one_ref,
+    two_ref,
+    taps_ref,
+    w_hbm,
+    needed_ref,
+    mine_ref,
+    other_ref,
+    w_ref,
+    sem,
 ):
     half = w_ref.shape[0]
+    copy = pltpu.make_async_copy(w_hbm, w_ref, sem)
+
+    @pl.when(pl.program_id(0) == 0)
+    def _():
+        copy.start()
+
     taps = taps_ref[...]
     mix = now_ref[...].astype(F32) * taps[0:1]
     mix = mix + one_ref[...].astype(F32) * taps[1:2]
     mix = mix + two_ref[...].astype(F32) * taps[2:3]
     gate = mix[:, half:]
     gated = (mix[:, :half] * (gate * jax.nn.sigmoid(gate))).astype(BF)
+
+    @pl.when(pl.program_id(0) == 0)
+    def _():
+        copy.wait()
+
     out = jnp.dot(gated, w_ref[...], preferred_element_type=F32).astype(BF)
     y, core = place_ref[0], place_ref[1]
     i = pl.program_id(0)
@@ -276,27 +315,29 @@
     whole_rows = peers * frame_rows
     block = 256
 
-    spatial_out = dict(
-        out_shape=jax.ShapeDtypeStruct((whole_rows, 2 * chan), BF),
-        grid=(2 * chan // block,),
-        out_specs=pl.BlockSpec((whole_rows, block), lambda i: (0, i)),
-        compiler_params=params(52),
-    )
+    spatial_out = jax.ShapeDtypeStruct((whole_rows, 2 * chan), BF)
     weight_specs = [
         pl.BlockSpec((width, block), lambda i: (0, i)),
         pl.BlockSpec((9, block), lambda i: (0, i)),
     ]
-    act_scratch = pltpu.VMEM((whole_rows + 2 * col_count, block), F32)
-
-    def pieces_call(pieces, f, needed):
+
+    def pieces_call(kernel, frames, pieces, needed):
+        outs = 1 if frames is None else frames
+        lead = () if frames is None else (frames,)
         return pl.pallas_call(
-            pieces_kernel,
+            kernel,
+            out_shape=[spatial_out] * outs,
+            grid=(2 * chan // block,),
             in_specs=[pl.BlockSpec(memory_space=pltpu.SMEM)]
-            + [pl.BlockSpec((None, frame_rows, width), lambda i: (f, 0, 0))] * peers
+            + [pl.BlockSpec(part.shape, lambda i, n=part.ndim: (0,) * n) for part in pieces]
             + weight_specs
             + [anywhere],
-            scratch_shapes=[act_scratch, pltpu.VMEM((whole_rows, width), BF)],
-            **spatial_out,
+            out_specs=[pl.BlockSpec((whole_rows, block), lambda i: (0, i))] * outs,
+            scratch_shapes=[
+                pltpu.VMEM(lead + (whole_rows + 2 * col_count, block), F32),
+                pltpu.VMEM(lead + (whole_rows, width), BF),
+            ],
+            compiler_params=params(52),
         )(where_am_i, *pieces, w_flat, taps_s, needed)
 
     row_block = 256
@@ -308,13 +349,15 @@
         + [pl.BlockSpec((row_block, 2 * chan), lambda i: (i, 0))] * 3
         + [
             pl.BlockSpec((TAPS, 2 * chan), lambda i: (0, 0)),
-            pl.BlockSpec((chan, width), lambda i: (0, 0)),
+            anywhere,
             anywhere,
         ],
         out_specs=[pl.BlockSpec((4, frame_rows, width), lambda i: (0, 0, 0))] * 2,
+        scratch_shapes=[pltpu.VMEM((chan, width), BF), pltpu.SemaphoreType.DMA],
         compiler_params=params(40),
     )
 
+    w_down_far = pltpu.with_memory_space_constraint(w_down, pltpu.HBM)
     blocks = lax.axis_size("blk")
     next_frames = [(i, i + 1) for i in range(blocks - 1)]
     other_core = [(i, i ^ 1) for i in range(peers)]
@@ -323,7 +366,7 @@
     def along_of(rows):
         return [rows] + [lax.ppermute(rows, "tile", ahead[k]) for k in (1, 2, 3)]
 
-    late_along = along_of(late[None])
+    late_along = along_of(late)
     before_early = lax.ppermute(early, "blk", next_frames)
     others = pl.pallas_call(
         stack_kernel,
@@ -336,16 +379,17 @@
     pieces = []
     for part in late_along:
         pieces += [part, lax.ppermute(part, "tile", other_core)]
-    late_sp = pieces_call(pieces, 0, taps_t)
+    (late_sp,) = pieces_call(pieces_kernel, None, pieces, taps_t)
     before_late_sp = lax.ppermute(late_sp, "blk", next_frames)
     both = []
     for part in others_along:
         both += [part, lax.ppermute(part, "tile", other_core)]
-    early_sp = pieces_call(both, 0, late_sp)
-    before_early_sp = pieces_call(both, 1, early_sp)
+    early_sp, before_early_sp = pieces_call(both_kernel, 2, both, late_sp)
 
     def core_shares(now, one, two, needed):
-        mine, other = point_call(where_am_i, now, one, two, taps_t, w_down, needed)
+        mine, other = point_call(
+            where_am_i, now, one, two, taps_t, w_down_far, needed
+        )
         return mine, lax.ppermute(other, "tile", other_core)
 
     def sums(mine, from_core, rows):

time: 206 us -> 206 us (level)
    unnamed x47 -> x29, local copies, waits for them, and re-layouts: 12.3 us -> 13.4 us
    pallas_call x5 -> x4, Pallas kernels: 30 us -> 29.5 us  [the longest x2 20 us: pieces_call(): pl.pallas_call(kernel, out_shape=[spatial_out] * outs, grid=(2 * chan //...]
  transfers between devices with their start and end apart: 26 -> 26, of which waited for: 10 -> 10; matrix products, arithmetic and copies ran while one was open for 4% -> 5% of each run, Pallas kernels for 15% -> 14%
where the time goes in v6:
time: 206 us; the launch traced here: 205 us
  waiting for transfers between devices  75.8 us (37%)
  Pallas kernels  38.5 us (19%)
  blocking collectives  33.6 us (16%)
  starting transfers between devices  30.4 us (15%)
  between operations  13.6 us (7%)
  local copies, waits for them, and re-layouts  13.4 us (7%)
    all_to_all x1, blocking collectives, on_device(): parts = lax.all_to_all(parts, everyone, 0, 0, tiled=True)  33.6 us
    ppermute x6, waiting for transfers between devices, along_of(): return [rows] + [lax.ppermute(rows, 'tile', ahead[k]) for k in (1, 2, 3)]  26.4 us
    ppermute x6, waiting for transfers between devices, sums(): lax.ppermute(part, 'tile', ahead[k + 1])  23.2 us
    pallas_call x2, Pallas kernels, pieces_call(): pl.pallas_call(kernel, out_shape=[spatial_out] * outs, grid=(2 * chan //...  20 us
    unnamed x29, local copies, waits for them, and re-layouts  13.4 us
    all_to_all x1, waiting for transfers between devices, on_device(): state = lax.all_to_all(sums, everyone, 0, 0, tiled=True)  12.9 us
    all_gather x1, waiting for transfers between devices, on_device(): w_out_whole = lax.all_gather(w_output, 'tile', axis=0, tiled=True)  12.6 us
    pallas_call x2, Pallas kernels, core_shares(): point_call(where_am_i, now, one, two, taps_t, w_down_far, needed)  9.54 us
  transfers between devices with their start and end apart: 26, of which 10 were waited for; matrix products, arithmetic and copies ran while one was open for 5% of the time, Pallas kernels for 14%

profile of v6, /device:TPU:2, one launch (start us, length us, event | category | flops | bytes accessed | tf_op | source)
XLA Modules:
  0.0 205.4 jit_solution(809554820276047418)
XLA Ops:
  8.5 33.6 %all_to_all.10.in_ref = bf16[256,8,128]{2,1,0:T(8,128)(2,1)S(1)} all-to-all(bf16[256,8,128]{2,1,0:T(8,128)(2,1)S(1)} %shard_map.91), channel_id=1, replica_groups=mesh['blk'=32,'tile'=8] {'blk','tile'}, dimensions={0} | all-to-all | bytes 1048576 | tf_op jit(solution)/shard_map/all_to_all | solution.py:290
  43.2 7.1 %all-to-all-start.1 = ((bf16[256,8,128]{2,1,0:T(8,128)(2,1)}), bf16[256,8,128]{2,1,0:T(8,128)(2,1)S(1)}, u32[]{:S(2)}, u32[]{:S(2)}) async-start(bf16[256,8,128]{2,1,0:T(8,128)(2,1)} %shard_map.92), calls=%async_computation.1 | async-start | bytes 1048576 | tf_op jit(solution)/shard_map/all_to_all | solution.py:294
  50.4 6.1 %copy.12 = bf16[280,8,2,512]{3,1,2,0:T(8,128)(2,1)} copy(bf16[280,8,2,512]{3,2,1,0:T(2,128)(2,1)} %bitcast.26) | data formatting | bytes 9175040
  56.5 12.9 %all-to-all-done.1.state_ref = bf16[256,8,128]{2,1,0:T(8,128)(2,1)S(1)} async-done(((bf16[256,8,128]{2,1,0:T(8,128)(2,1)}), bf16[256,8,128]{2,1,0:T(8,128)(2,1)S(1)}, u32[]{:S(2)}, u32[]{:S(2)}) %all-to-all-start.1) | async-done | bytes 524320 | tf_op jit(solution)/shard_map/all_to_all | solution.py:294
  70.2 12.6 %all-gather.2.cloned.1.call-done.w_hbm = bf16[2240,2240]{1,0:T(8,128)(2,1)} async-done(((bf16[280,2240]{1,0:T(8,128)(2,1)}), bf16[2240,2240]{1,0:T(8,128)(2,1)}) %all-gather.2.cloned.1.call-update) | async-done | bytes 10035216 | tf_op jit(solution)/shard_map/all_gather | solution.py:275
  82.8 4.6 %shard_map.94 = (bf16[64,2240]{1,0:T(8,128)(2,1)S(1)}, bf16[64,2240]{1,0:T(8,128)(2,1)S(1)}) custom-call(bf16[128,2240]{1,0:T(8,128)(2,1)S(1)} %shard_map.93.att_ref, bf16[128,2240]{1,0:T(8,128)(2,1)S(1)} %bitcast.16, bf16[2240,2240]{1,0:T(8,128)(2,1)} %all-gather.2.cloned.1.call-done.w_hbm, bf16[2240,1024]{1,0:T(8,128)(2,1)} %bitcast.23), custom_call_target="tpu_custom_call" | custom-call | tf_op jit(solution)/shard_map/pallas_call | solution.py:306
  88.1 1.8 collective-permute-start.1
  89.8 2.0 collective-permute-start.2
  91.9 3.0 %collective-permute-start.3 = (bf16[64,2240]{1,0:T(8,128)(2,1)S(1)}, bf16[64,2240]{1,0:T(8,128)(2,1)S(1)}, u32[]{:S(2)}, u32[]{:S(2)}) collective-permute-start(bf16[64,2240]{1,0:T(8,128)(2,1)S(1)} %get-tuple-element.22.refs_3_.hidden_ref), channel_id=1, source_target_pairs={{0,8},{8,16},{16,24},{24,32},{32,40},{40,48},{48,56},{56,64},{64,7... | collective-permute-start | bytes 860168 | tf_op jit(solution)/shard_map/ppermute | solution.py:370
  95.0 9.2 %collective-permute-done.refs_0_.refs_2_ = bf16[64,2240]{1,0:T(8,128)(2,1)S(1)} collective-permute-done((bf16[64,2240]{1,0:T(8,128)(2,1)S(1)}, bf16[64,2240]{1,0:T(8,128)(2,1)S(1)}, u32[]{:S(2)}, u32[]{:S(2)}) %collective-permute-start) | collective-permute-done | bytes 286752 | tf_op jit(solution)/shard_map/ppermute | solution.py:367
  105.0 2.7 %collective-permute-start.9 = (bf16[2,64,2240]{2,1,0:T(8,128)(2,1)S(1)}, bf16[2,64,2240]{2,1,0:T(8,128)(2,1)}, u32[]{:S(2)}, u32[]{:S(2)}) collective-permute-start(bf16[2,64,2240]{2,1,0:T(8,128)(2,1)S(1)} %shard_map.95.refs_0_), channel_id=1, source_target_pairs={{0,6},{1,7},{2,0},{3,1},{4,2},{5,3},{6,4},{7,5},{8,14},{9,15},{10,... | collective-permute-start | bytes 1720328 | tf_op jit(solution)/shard_map/ppermute | solution.py:367
  107.7 1.6 collective-permute-start.7
  109.4 7.4 %shard_map.96.refs_10_.now_ref = bf16[512,1024]{1,0:T(8,128)(2,1)} custom-call(s32[2]{0:T(128)S(1)} %pad_add_fusion.place_ref, bf16[64,2240]{1,0:T(8,128)(2,1)S(1)} %get-tuple-element.21.refs_0_.hidden_ref, bf16[64,2240]{1,0:T(8,128)(2,1)S(1)} %collective-permute-done.11.refs_1_, bf16[64,2240]{1,0:T(8,128)(2,1)S(1)} %collective-permute-done.refs_0_.refs_2_, ...), custom_call_target="tpu_custom_call" | custom-call | tf_op jit(solution)/shard_map/pallas_call | solution.py:327
  116.7 3.1 %collective-permute-start.15 = (bf16[512,1024]{1,0:T(8,128)(2,1)}, bf16[512,1024]{1,0:T(8,128)(2,1)S(1)}, u32[]{:S(2)}, u32[]{:S(2)}) collective-permute-start(bf16[512,1024]{1,0:T(8,128)(2,1)} %shard_map.96.refs_10_.now_ref), channel_id=1, source_target_pairs={{0,8},{8,16},{16,24},{24,32},{32,40},{40,48},{48,56},{56,64},{64,7... | collective-permute-start | bytes 3145736 | tf_op jit(solution)/shard_map/ppermute | solution.py:383
  119.9 13.7 %collective-permute-done.9.refs_6_ = bf16[2,64,2240]{2,1,0:T(8,128)(2,1)} collective-permute-done((bf16[2,64,2240]{2,1,0:T(8,128)(2,1)S(1)}, bf16[2,64,2240]{2,1,0:T(8,128)(2,1)}, u32[]{:S(2)}, u32[]{:S(2)}) %collective-permute-start.9) | collective-permute-done | bytes 573472 | tf_op jit(solution)/shard_map/ppermute | solution.py:367
  133.6 3.4 %collective-permute-done.5.refs_2_ = bf16[2,64,2240]{2,1,0:T(8,128)(2,1)S(1)} collective-permute-done((bf16[2,64,2240]{2,1,0:T(8,128)(2,1)S(1)}, bf16[2,64,2240]{2,1,0:T(8,128)(2,1)S(1)}, u32[]{:S(2)}, u32[]{:S(2)}) %collective-permute-start.5) | collective-permute-done | bytes 573472 | tf_op jit(solution)/shard_map/ppermute | solution.py:367
  137.5 4.2 %copy.11.w_hbm = bf16[512,2240]{1,0:T(8,128)(2,1)} copy(bf16[512,2240]{0,1:T(8,128)(2,1)} %param.15) | data formatting | bytes 4587520 | tf_op args[6]
  141.8 12.6 %shard_map.97 = (bf16[512,1024]{1,0:T(8,128)(2,1)}, bf16[512,1024]{1,0:T(8,128)(2,1)}) custom-call(s32[2]{0:T(128)S(1)} %pad_add_fusion.place_ref, bf16[2,64,2240]{2,1,0:T(8,128)(2,1)S(1)} %shard_map.95.refs_0_, bf16[2,64,2240]{2,1,0:T(8,128)(2,1)S(1)} %collective-permute-done.4.refs_1_, bf16[2,64,2240]{2,1,0:T(8,128)(2,1)S(1)} %collective-permute-done.5.refs_2_, ...), custom_call_target="tpu_custom_call" | custom-call | tf_op jit(solution)/shard_map/pallas_call | solution.py:327
  156.9 4.8 %shard_map.98 = (bf16[4,64,2240]{2,1,0:T(8,128)(2,1)S(1)}, bf16[4,64,2240]{2,1,0:T(8,128)(2,1)S(1)}) custom-call(s32[2]{0:T(128)S(1)} %pad_add_fusion.place_ref, bf16[512,1024]{1,0:T(8,128)(2,1)S(1)} %copy-done, bf16[512,1024]{1,0:T(8,128)(2,1)S(1)} %copy-done.1, bf16[512,1024]{1,0:T(8,128)(2,1)S(1)} %collective-permute-done.15.two_ref.one_ref, ...), custom_call_target="tpu_custom_call" | custom-call | tf_op jit(solution)/shard_map/pallas_call | solution.py:390
  162.0 4.7 %shard_map.99 = (bf16[4,64,2240]{2,1,0:T(8,128)(2,1)S(1)}, bf16[4,64,2240]{2,1,0:T(8,128)(2,1)S(1)}) custom-call(s32[2]{0:T(128)S(1)} %pad_add_fusion.place_ref, bf16[512,1024]{1,0:T(8,128)(2,1)S(1)} %copy-done.2, bf16[512,1024]{1,0:T(8,128)(2,1)S(1)} %collective-permute-done.15.two_ref.one_ref, bf16[512,1024]{1,0:T(8,128)(2,1)S(1)} %copy-done.4, ...), custom_call_target="tpu_custom_call" | custom-call | tf_op jit(solution)/shard_map/pallas_call | solution.py:390
  167.7 1.9 collective-permute-start.22
  172.2 2.2 %collective-permute-start.19 = (bf16[64,2240]{1,0:T(8,128)(2,1)S(1)}, bf16[64,2240]{1,0:T(8,128)(2,1)S(1)}, u32[]{:S(2)}, u32[]{:S(2)}) collective-permute-start(bf16[64,2240]{1,0:T(8,128)(2,1)S(1)} %get-tuple-element.32), channel_id=1, source_target_pairs={{0,4},{1,5},{2,6},{3,7},{4,0},{5,1},{6,2},{7,3},{8,12},{9,13},{10,... | collective-permute-start | bytes 860168 | tf_op jit(solution)/shard_map/ppermute | solution.py:403
  174.3 10.8 %collective-permute-done.21.refs_3_ = bf16[64,2240]{1,0:T(8,128)(2,1)S(1)} collective-permute-done((bf16[64,2240]{1,0:T(8,128)(2,1)S(1)}, bf16[64,2240]{1,0:T(8,128)(2,1)S(1)}, u32[]{:S(2)}, u32[]{:S(2)}) %collective-permute-start.21) | collective-permute-done | bytes 286752 | tf_op jit(solution)/shard_map/ppermute | solution.py:403
  186.0 10.8 %collective-permute-done.18.refs_0_ = bf16[64,2240]{1,0:T(8,128)(2,1)S(1)} collective-permute-done((bf16[64,2240]{1,0:T(8,128)(2,1)S(1)}, bf16[64,2240]{1,0:T(8,128)(2,1)S(1)}, u32[]{:S(2)}, u32[]{:S(2)}) %collective-permute-start.18) | collective-permute-done | bytes 286752 | tf_op jit(solution)/shard_map/ppermute | solution.py:403
  (72 shorter events, 14.9 us)
Async XLA Ops:
  6.5 76.3 %all-gather.2.cloned.1.call-start = ((), (), s32[]{:S(2)}) async-start(), calls=%async_computation.2 | async-start | bytes 11612160 | tf_op jit(solution)/shard_map/all_gather | solution.py:275
  43.2 26.2 %all-to-all-start.1 = ((bf16[256,8,128]{2,1,0:T(8,128)(2,1)}), bf16[256,8,128]{2,1,0:T(8,128)(2,1)S(1)}, u32[]{:S(2)}, u32[]{:S(2)}) async-start(bf16[256,8,128]{2,1,0:T(8,128)(2,1)} %shard_map.92), calls=%async_computation.1 | async-start | bytes 1048576 | tf_op jit(solution)/shard_map/all_to_all | solution.py:294
  87.4 16.8 %collective-permute-start = (bf16[64,2240]{1,0:T(8,128)(2,1)S(1)}, bf16[64,2240]{1,0:T(8,128)(2,1)S(1)}, u32[]{:S(2)}, u32[]{:S(2)}) collective-permute-start(bf16[64,2240]{1,0:T(8,128)(2,1)S(1)} %get-tuple-element.21.refs_0_.hidden_ref), channel_id=1, source_target_pairs={{0,2},{1,3},{2,4},{3,5},{4,6},{5,7},{6,0},{7,1},{8,10},{9,11},{10,... | collective-permute-start | bytes 860168 | tf_op jit(solution)/shard_map/ppermute | solution.py:367
  88.1 16.2 %collective-permute-start.1 = (bf16[64,2240]{1,0:T(8,128)(2,1)S(1)}, bf16[64,2240]{1,0:T(8,128)(2,1)S(1)}, u32[]{:S(2)}, u32[]{:S(2)}) collective-permute-start(bf16[64,2240]{1,0:T(8,128)(2,1)S(1)} %get-tuple-element.21.refs_0_.hidden_ref), channel_id=1, source_target_pairs={{0,4},{1,5},{2,6},{3,7},{4,0},{5,1},{6,2},{7,3},{8,12},{9,13},{10,... | collective-permute-start | bytes 860168 | tf_op jit(solution)/shard_map/ppermute | solution.py:367
  89.8 15.0 %collective-permute-start.2 = (bf16[64,2240]{1,0:T(8,128)(2,1)S(1)}, bf16[64,2240]{1,0:T(8,128)(2,1)S(1)}, u32[]{:S(2)}, u32[]{:S(2)}) collective-permute-start(bf16[64,2240]{1,0:T(8,128)(2,1)S(1)} %get-tuple-element.21.refs_0_.hidden_ref), channel_id=1, source_target_pairs={{0,6},{1,7},{2,0},{3,1},{4,2},{5,3},{6,4},{7,5},{8,14},{9,15},{10,... | collective-permute-start | bytes 860168 | tf_op jit(solution)/shard_map/ppermute | solution.py:367
  91.9 13.1 %collective-permute-start.3 = (bf16[64,2240]{1,0:T(8,128)(2,1)S(1)}, bf16[64,2240]{1,0:T(8,128)(2,1)S(1)}, u32[]{:S(2)}, u32[]{:S(2)}) collective-permute-start(bf16[64,2240]{1,0:T(8,128)(2,1)S(1)} %get-tuple-element.22.refs_3_.hidden_ref), channel_id=1, source_target_pairs={{0,8},{8,16},{16,24},{24,32},{32,40},{40,48},{48,56},{56,64},{64,7... | collective-permute-start | bytes 860168 | tf_op jit(solution)/shard_map/ppermute | solution.py:370
  94.9 12.8 %collective-permute-start.11 = (bf16[64,2240]{1,0:T(8,128)(2,1)S(1)}, bf16[64,2240]{1,0:T(8,128)(2,1)S(1)}, u32[]{:S(2)}, u32[]{:S(2)}) collective-permute-start(bf16[64,2240]{1,0:T(8,128)(2,1)S(1)} %get-tuple-element.21.refs_0_.hidden_ref), channel_id=1, source_target_pairs={{0,1},{1,0},{2,3},{3,2},{4,5},{5,4},{6,7},{7,6},{8,9},{9,8},{10,11... | collective-permute-start | bytes 860168 | tf_op jit(solution)/shard_map/ppermute | solution.py:381
  104.2 5.1 %collective-permute-start.13 = (bf16[64,2240]{1,0:T(8,128)(2,1)S(1)}, bf16[64,2240]{1,0:T(8,128)(2,1)}, u32[]{:S(2)}, u32[]{:S(2)}) collective-permute-start(bf16[64,2240]{1,0:T(8,128)(2,1)S(1)} %collective-permute-done.1.refs_1_.refs_4_), channel_id=1, source_target_pairs={{0,1},{1,0},{2,3},{3,2},{4,5},{5,4},{6,7},{7,6},{8,9},{9,8},{10,11... | collective-permute-start | bytes 860168 | tf_op jit(solution)/shard_map/ppermute | solution.py:381
  104.8 4.5 %collective-permute-start.14 = (bf16[64,2240]{1,0:T(8,128)(2,1)S(1)}, bf16[64,2240]{1,0:T(8,128)(2,1)}, u32[]{:S(2)}, u32[]{:S(2)}) collective-permute-start(bf16[64,2240]{1,0:T(8,128)(2,1)S(1)} %collective-permute-done.2.refs_2_.refs_6_), channel_id=1, source_target_pairs={{0,1},{1,0},{2,3},{3,2},{4,5},{5,4},{6,7},{7,6},{8,9},{9,8},{10,11... | collective-permute-start | bytes 860168 | tf_op jit(solution)/shard_map/ppermute | solution.py:381
  105.0 28.6 %collective-permute-start.9 = (bf16[2,64,2240]{2,1,0:T(8,128)(2,1)S(1)}, bf16[2,64,2240]{2,1,0:T(8,128)(2,1)}, u32[]{:S(2)}, u32[]{:S(2)}) collective-permute-start(bf16[2,64,2240]{2,1,0:T(8,128)(2,1)S(1)} %shard_map.95.refs_0_), channel_id=1, source_target_pairs={{0,6},{1,7},{2,0},{3,1},{4,2},{5,3},{6,4},{7,5},{8,14},{9,15},{10,... | collective-permute-start | bytes 1720328 | tf_op jit(solution)/shard_map/ppermute | solution.py:367
  107.7 29.3 %collective-permute-start.5 = (bf16[2,64,2240]{2,1,0:T(8,128)(2,1)S(1)}, bf16[2,64,2240]{2,1,0:T(8,128)(2,1)S(1)}, u32[]{:S(2)}, u32[]{:S(2)}) collective-permute-start(bf16[2,64,2240]{2,1,0:T(8,128)(2,1)S(1)} %shard_map.95.refs_0_), channel_id=1, source_target_pairs={{0,2},{1,3},{2,4},{3,5},{4,6},{5,7},{6,0},{7,1},{8,10},{9,11},{10,... | collective-permute-start | bytes 1720328 | tf_op jit(solution)/shard_map/ppermute | solution.py:367
  107.7 29.3 %collective-permute-start.7 = (bf16[2,64,2240]{2,1,0:T(8,128)(2,1)S(1)}, bf16[2,64,2240]{2,1,0:T(8,128)(2,1)}, u32[]{:S(2)}, u32[]{:S(2)}) collective-permute-start(bf16[2,64,2240]{2,1,0:T(8,128)(2,1)S(1)} %shard_map.95.refs_0_), channel_id=1, source_target_pairs={{0,4},{1,5},{2,6},{3,7},{4,0},{5,1},{6,2},{7,3},{8,12},{9,13},{10,... | collective-permute-start | bytes 1720328 | tf_op jit(solution)/shard_map/ppermute | solution.py:367
  116.7 37.7 %collective-permute-start.15 = (bf16[512,1024]{1,0:T(8,128)(2,1)}, bf16[512,1024]{1,0:T(8,128)(2,1)S(1)}, u32[]{:S(2)}, u32[]{:S(2)}) collective-permute-start(bf16[512,1024]{1,0:T(8,128)(2,1)} %shard_map.96.refs_10_.now_ref), channel_id=1, source_target_pairs={{0,8},{8,16},{16,24},{24,32},{32,40},{40,48},{48,56},{56,64},{64,7... | collective-permute-start | bytes 3145736 | tf_op jit(solution)/shard_map/ppermute | solution.py:383
  119.8 21.9 %collective-permute-start.4 = (bf16[2,64,2240]{2,1,0:T(8,128)(2,1)S(1)}, bf16[2,64,2240]{2,1,0:T(8,128)(2,1)S(1)}, u32[]{:S(2)}, u32[]{:S(2)}) collective-permute-start(bf16[2,64,2240]{2,1,0:T(8,128)(2,1)S(1)} %shard_map.95.refs_0_), channel_id=1, source_target_pairs={{0,1},{1,0},{2,3},{3,2},{4,5},{5,4},{6,7},{7,6},{8,9},{9,8},{10,11... | collective-permute-start | bytes 1720328 | tf_op jit(solution)/shard_map/ppermute | solution.py:386
  133.6 8.1 %collective-permute-start.10 = (bf16[2,64,2240]{2,1,0:T(8,128)(2,1)}, bf16[2,64,2240]{2,1,0:T(8,128)(2,1)}, u32[]{:S(2)}, u32[]{:S(2)}) collective-permute-start(bf16[2,64,2240]{2,1,0:T(8,128)(2,1)} %collective-permute-done.9.refs_6_), channel_id=1, source_target_pairs={{0,1},{1,0},{2,3},{3,2},{4,5},{5,4},{6,7},{7,6},{8,9},{9,8},{10,11... | collective-permute-start | bytes 1720328 | tf_op jit(solution)/shard_map/ppermute | solution.py:386
  137.0 4.8 %collective-permute-start.6 = (bf16[2,64,2240]{2,1,0:T(8,128)(2,1)S(1)}, bf16[2,64,2240]{2,1,0:T(8,128)(2,1)}, u32[]{:S(2)}, u32[]{:S(2)}) collective-permute-start(bf16[2,64,2240]{2,1,0:T(8,128)(2,1)S(1)} %collective-permute-done.5.refs_2_), channel_id=1, source_target_pairs={{0,1},{1,0},{2,3},{3,2},{4,5},{5,4},{6,7},{7,6},{8,9},{9,8},{10,11... | collective-permute-start | bytes 1720328 | tf_op jit(solution)/shard_map/ppermute | solution.py:386
  137.0 4.8 %collective-permute-start.8 = (bf16[2,64,2240]{2,1,0:T(8,128)(2,1)}, bf16[2,64,2240]{2,1,0:T(8,128)(2,1)}, u32[]{:S(2)}, u32[]{:S(2)}) collective-permute-start(bf16[2,64,2240]{2,1,0:T(8,128)(2,1)} %collective-permute-done.7.refs_4_), channel_id=1, source_target_pairs={{0,1},{1,0},{2,3},{3,2},{4,5},{5,4},{6,7},{7,6},{8,9},{9,8},{10,11... | collective-permute-start | bytes 1720328 | tf_op jit(solution)/shard_map/ppermute | solution.py:386
  161.7 5.6 %collective-permute-start.17 = (bf16[4,64,2240]{2,1,0:T(8,128)(2,1)S(1)}, bf16[4,64,2240]{2,1,0:T(8,128)(2,1)S(1)}, u32[]{:S(2)}, u32[]{:S(2)}) collective-permute-start(bf16[4,64,2240]{2,1,0:T(8,128)(2,1)S(1)} %get-tuple-element.29), channel_id=1, source_target_pairs={{0,1},{1,0},{2,3},{3,2},{4,5},{5,4},{6,7},{7,6},{8,9},{9,8},{10,11... | collective-permute-start | bytes 3440648 | tf_op jit(solution)/shard_map/ppermute | solution.py:393
  167.6 17.5 %collective-permute-start.21 = (bf16[64,2240]{1,0:T(8,128)(2,1)S(1)}, bf16[64,2240]{1,0:T(8,128)(2,1)S(1)}, u32[]{:S(2)}, u32[]{:S(2)}) collective-permute-start(bf16[64,2240]{1,0:T(8,128)(2,1)S(1)} %get-tuple-element.34), channel_id=1, source_target_pairs={{0,2},{1,3},{2,4},{3,5},{4,6},{5,7},{6,0},{7,1},{8,10},{9,11},{10,... | collective-permute-start | bytes 860168 | tf_op jit(solution)/shard_map/ppermute | solution.py:403
  167.7 17.4 %collective-permute-start.22 = (bf16[64,2240]{1,0:T(8,128)(2,1)S(1)}, bf16[64,2240]{1,0:T(8,128)(2,1)S(1)}, u32[]{:S(2)}, u32[]{:S(2)}) collective-permute-start(bf16[64,2240]{1,0:T(8,128)(2,1)S(1)} %get-tuple-element.35), channel_id=1, source_target_pairs={{0,4},{1,5},{2,6},{3,7},{4,0},{5,1},{6,2},{7,3},{8,12},{9,13},{10,... | collective-permute-start | bytes 860168 | tf_op jit(solution)/shard_map/ppermute | solution.py:403
  169.6 16.4 %collective-permute-start.23 = (bf16[64,2240]{1,0:T(8,128)(2,1)S(1)}, bf16[64,2240]{1,0:T(8,128)(2,1)S(1)}, u32[]{:S(2)}, u32[]{:S(2)}) collective-permute-start(bf16[64,2240]{1,0:T(8,128)(2,1)S(1)} %get-tuple-element.36), channel_id=1, source_target_pairs={{0,6},{1,7},{2,0},{3,1},{4,2},{5,3},{6,4},{7,5},{8,14},{9,15},{10,... | collective-permute-start | bytes 860168 | tf_op jit(solution)/shard_map/ppermute | solution.py:403
  171.2 25.6 %collective-permute-start.18 = (bf16[64,2240]{1,0:T(8,128)(2,1)S(1)}, bf16[64,2240]{1,0:T(8,128)(2,1)S(1)}, u32[]{:S(2)}, u32[]{:S(2)}) collective-permute-start(bf16[64,2240]{1,0:T(8,128)(2,1)S(1)} %get-tuple-element.31), channel_id=1, source_target_pairs={{0,2},{1,3},{2,4},{3,5},{4,6},{5,7},{6,0},{7,1},{8,10},{9,11},{10,... | collective-permute-start | bytes 860168 | tf_op jit(solution)/shard_map/ppermute | solution.py:403
  172.2 24.7 %collective-permute-start.19 = (bf16[64,2240]{1,0:T(8,128)(2,1)S(1)}, bf16[64,2240]{1,0:T(8,128)(2,1)S(1)}, u32[]{:S(2)}, u32[]{:S(2)}) collective-permute-start(bf16[64,2240]{1,0:T(8,128)(2,1)S(1)} %get-tuple-element.32), channel_id=1, source_target_pairs={{0,4},{1,5},{2,6},{3,7},{4,0},{5,1},{6,2},{7,3},{8,12},{9,13},{10,... | collective-permute-start | bytes 860168 | tf_op jit(solution)/shard_map/ppermute | solution.py:403
  185.1 12.4 %collective-permute-start.20 = (bf16[64,2240]{1,0:T(8,128)(2,1)S(1)}, bf16[64,2240]{1,0:T(8,128)(2,1)S(1)}, u32[]{:S(2)}, u32[]{:S(2)}) collective-permute-start(bf16[64,2240]{1,0:T(8,128)(2,1)S(1)} %get-tuple-element.33), channel_id=1, source_target_pairs={{0,6},{1,7},{2,0},{3,1},{4,2},{5,3},{6,4},{7,5},{8,14},{9,15},{10,... | collective-permute-start | bytes 860168 | tf_op jit(solution)/shard_map/ppermute | solution.py:403
  (14 other events, 129.3 us)
Sparse Core Ops, SparseCore 0:
  9.2 73.5 all-gather.1

commit v7 on v6

--- a/solution.py
+++ b/solution.py
@@ -183,37 +183,17 @@
 
 
 def point_kernel(
-    place_ref,
-    now_ref,
-    one_ref,
-    two_ref,
-    taps_ref,
-    w_hbm,
-    needed_ref,
-    mine_ref,
-    other_ref,
-    w_ref,
-    sem,
+    place_ref, now_ref, one_ref, two_ref, taps_ref, w_ref, needed_ref, mine_ref, other_ref
 ):
-    half = w_ref.shape[0]
-    copy = pltpu.make_async_copy(w_hbm, w_ref, sem)
-
-    @pl.when(pl.program_id(0) == 0)
-    def _():
-        copy.start()
-
+    half = w_ref.shape[1]
     taps = taps_ref[...]
     mix = now_ref[...].astype(F32) * taps[0:1]
     mix = mix + one_ref[...].astype(F32) * taps[1:2]
     mix = mix + two_ref[...].astype(F32) * taps[2:3]
     gate = mix[:, half:]
     gated = (mix[:, :half] * (gate * jax.nn.sigmoid(gate))).astype(BF)
-
-    @pl.when(pl.program_id(0) == 0)
-    def _():
-        copy.wait()
-
-    out = jnp.dot(gated, w_ref[...], preferred_element_type=F32).astype(BF)
+    over_channels = (((1,), (1,)), ((), ()))
+    out = lax.dot_general(gated, w_ref[...], over_channels, preferred_element_type=F32).astype(BF)
     y, core = place_ref[0], place_ref[1]
     i = pl.program_id(0)
     rows = out.shape[0] // 4
@@ -349,15 +329,14 @@
         + [pl.BlockSpec((row_block, 2 * chan), lambda i: (i, 0))] * 3
         + [
             pl.BlockSpec((TAPS, 2 * chan), lambda i: (0, 0)),
-            anywhere,
+            pl.BlockSpec((width, chan), lambda i: (0, 0)),
             anywhere,
         ],
         out_specs=[pl.BlockSpec((4, frame_rows, width), lambda i: (0, 0, 0))] * 2,
-        scratch_shapes=[pltpu.VMEM((chan, width), BF), pltpu.SemaphoreType.DMA],
         compiler_params=params(40),
     )
 
-    w_down_far = pltpu.with_memory_space_constraint(w_down, pltpu.HBM)
+    w_point = w_down.T
     blocks = lax.axis_size("blk")
     next_frames = [(i, i + 1) for i in range(blocks - 1)]
     other_core = [(i, i ^ 1) for i in range(peers)]
@@ -387,9 +366,7 @@
     early_sp, before_early_sp = pieces_call(both_kernel, 2, both, late_sp)
 
     def core_shares(now, one, two, needed):
-        mine, other = point_call(
-            where_am_i, now, one, two, taps_t, w_down_far, needed
-        )
+        mine, other = point_call(where_am_i, now, one, two, taps_t, w_point, needed)
         return mine, lax.ppermute(other, "tile", other_core)
 
     def sums(mine, from_core, rows):

time: 206 us -> 201 us (0.976)
  Pallas kernels: 38.5 us -> 34.8 us
  local copies, waits for them, and re-layouts: 13.4 us -> 11.3 us
    pallas_call x2, Pallas kernels: 9.54 us -> 5.96 us  [core_shares(): mine, other = point_call(where_am_i, now, one, two, taps_t, w_point, needed)]
    ppermute x4, waiting for transfers between devices: 0.01 us -> 2.32 us  [on_device(): both += [part, lax.ppermute(part, 'tile', other_core)]]
    unnamed x29 -> x40, local copies, waits for them, and re-layouts: 13.4 us -> 11.3 us
  transfers between devices with their start and end apart: 26 -> 26, of which waited for: 10 -> 12; matrix products, arithmetic and copies ran while one was open for 5% -> 3% of each run, Pallas kernels for 14% -> 13%
where the time goes in v7:
time: 201 us
  waiting for transfers between devices  77.1 us (38%)
  Pallas kernels  34.8 us (17%)
  blocking collectives  33.6 us (17%)
  starting transfers between devices  30.4 us (15%)
  between operations  13.6 us (7%)
  local copies, waits for them, and re-layouts  11.3 us (6%)
    all_to_all x1, blocking collectives, on_device(): parts = lax.all_to_all(parts, everyone, 0, 0, tiled=True)  33.6 us
    ppermute x6, waiting for transfers between devices, along_of(): return [rows] + [lax.ppermute(rows, 'tile', ahead[k]) for k in (1, 2, 3)]  25.3 us
    ppermute x6, waiting for transfers between devices, sums(): lax.ppermute(part, 'tile', ahead[k + 1])  23.2 us
    pallas_call x2, Pallas kernels, pieces_call(): pl.pallas_call(kernel, out_shape=[spatial_out] * outs, grid=(2 * chan //...  19.9 us
    all_to_all x1, waiting for transfers between devices, on_device(): state = lax.all_to_all(sums, everyone, 0, 0, tiled=True)  12.9 us
    all_gather x1, waiting for transfers between devices, on_device(): w_out_whole = lax.all_gather(w_output, 'tile', axis=0, tiled=True)  12.6 us
    unnamed x40, local copies, waits for them, and re-layouts  11.3 us
    ppermute x6, starting transfers between devices, along_of(): return [rows] + [lax.ppermute(rows, 'tile', ahead[k]) for k in (1, 2, 3)]  8.52 us
  transfers between devices with their start and end apart: 26, of which 12 were waited for; matrix products, arithmetic and copies ran while one was open for 3% of the time, Pallas kernels for 13%

profile of v7, /device:TPU:2, one launch (start us, length us, event | category | flops | bytes accessed | tf_op | source)
XLA Modules:
  0.0 200.9 jit_solution(6554488601567503788)
XLA Ops:
  8.5 33.6 %all_to_all.10.in_ref = bf16[256,8,128]{2,1,0:T(8,128)(2,1)S(1)} all-to-all(bf16[256,8,128]{2,1,0:T(8,128)(2,1)S(1)} %shard_map.91), channel_id=1, replica_groups=mesh['blk'=32,'tile'=8] {'blk','tile'}, dimensions={0} | all-to-all | bytes 1048576 | tf_op jit(solution)/shard_map/all_to_all | solution.py:270
  43.2 7.1 %all-to-all-start.1 = ((bf16[256,8,128]{2,1,0:T(8,128)(2,1)}), bf16[256,8,128]{2,1,0:T(8,128)(2,1)S(1)}, u32[]{:S(2)}, u32[]{:S(2)}) async-start(bf16[256,8,128]{2,1,0:T(8,128)(2,1)} %shard_map.92), calls=%async_computation.1 | async-start | bytes 1048576 | tf_op jit(solution)/shard_map/all_to_all | solution.py:274
  50.4 6.1 %copy.10 = bf16[280,8,2,512]{3,1,2,0:T(8,128)(2,1)} copy(bf16[280,8,2,512]{3,2,1,0:T(2,128)(2,1)} %bitcast.29) | data formatting | bytes 9175040
  56.5 12.9 %all-to-all-done.1.state_ref = bf16[256,8,128]{2,1,0:T(8,128)(2,1)S(1)} async-done(((bf16[256,8,128]{2,1,0:T(8,128)(2,1)}), bf16[256,8,128]{2,1,0:T(8,128)(2,1)S(1)}, u32[]{:S(2)}, u32[]{:S(2)}) %all-to-all-start.1) | async-done | bytes 524320 | tf_op jit(solution)/shard_map/all_to_all | solution.py:274
  70.2 12.6 %all-gather.2.cloned.1.call-done.w_hbm = bf16[2240,2240]{1,0:T(8,128)(2,1)} async-done(((bf16[280,2240]{1,0:T(8,128)(2,1)}), bf16[2240,2240]{1,0:T(8,128)(2,1)}) %all-gather.2.cloned.1.call-update) | async-done | bytes 10035216 | tf_op jit(solution)/shard_map/all_gather | solution.py:255
  82.8 4.6 %shard_map.94 = (bf16[64,2240]{1,0:T(8,128)(2,1)S(1)}, bf16[64,2240]{1,0:T(8,128)(2,1)S(1)}) custom-call(bf16[128,2240]{1,0:T(8,128)(2,1)S(1)} %shard_map.93.att_ref, bf16[128,2240]{1,0:T(8,128)(2,1)S(1)} %bitcast.19, bf16[2240,2240]{1,0:T(8,128)(2,1)} %all-gather.2.cloned.1.call-done.w_hbm, bf16[2240,1024]{1,0:T(8,128)(2,1)} %bitcast.26), custom_call_target="tpu_custom_call" | custom-call | tf_op jit(solution)/shard_map/pallas_call | solution.py:286
  88.1 1.8 collective-permute-start.1
  89.8 2.0 %collective-permute-start.2 = (bf16[64,2240]{1,0:T(8,128)(2,1)S(1)}, bf16[64,2240]{1,0:T(8,128)(2,1)S(1)}, u32[]{:S(2)}, u32[]{:S(2)}) collective-permute-start(bf16[64,2240]{1,0:T(8,128)(2,1)S(1)} %get-tuple-element.21.refs_0_.hidden_ref), channel_id=1, source_target_pairs={{0,6},{1,7},{2,0},{3,1},{4,2},{5,3},{6,4},{7,5},{8,14},{9,15},{10,... | collective-permute-start | bytes 860168 | tf_op jit(solution)/shard_map/ppermute | solution.py:346
  91.9 3.0 %collective-permute-start.3 = (bf16[64,2240]{1,0:T(8,128)(2,1)S(1)}, bf16[64,2240]{1,0:T(8,128)(2,1)S(1)}, u32[]{:S(2)}, u32[]{:S(2)}) collective-permute-start(bf16[64,2240]{1,0:T(8,128)(2,1)S(1)} %get-tuple-element.22.refs_3_.hidden_ref), channel_id=1, source_target_pairs={{0,8},{8,16},{16,24},{24,32},{32,40},{40,48},{48,56},{56,64},{64,7... | collective-permute-start | bytes 860168 | tf_op jit(solution)/shard_map/ppermute | solution.py:349
  95.0 9.2 %collective-permute-done.refs_0_.refs_2_ = bf16[64,2240]{1,0:T(8,128)(2,1)S(1)} collective-permute-done((bf16[64,2240]{1,0:T(8,128)(2,1)S(1)}, bf16[64,2240]{1,0:T(8,128)(2,1)S(1)}, u32[]{:S(2)}, u32[]{:S(2)}) %collective-permute-start) | collective-permute-done | bytes 286752 | tf_op jit(solution)/shard_map/ppermute | solution.py:346
  105.5 2.6 %collective-permute-start.9 = (bf16[2,64,2240]{2,1,0:T(8,128)(2,1)S(1)}, bf16[2,64,2240]{2,1,0:T(8,128)(2,1)S(1)}, u32[]{:S(2)}, u32[]{:S(2)}) collective-permute-start(bf16[2,64,2240]{2,1,0:T(8,128)(2,1)S(1)} %shard_map.95.refs_0_), channel_id=1, source_target_pairs={{0,6},{1,7},{2,0},{3,1},{4,2},{5,3},{6,4},{7,5},{8,14},{9,15},{10,... | collective-permute-start | bytes 1720328 | tf_op jit(solution)/shard_map/ppermute | solution.py:346
  108.2 1.5 collective-permute-start.7
  110.5 7.3 %shard_map.96.refs_10_.now_ref = bf16[512,1024]{1,0:T(8,128)(2,1)} custom-call(s32[2]{0:T(128)S(1)} %pad_add_fusion.place_ref, bf16[64,2240]{1,0:T(8,128)(2,1)S(1)} %get-tuple-element.21.refs_0_.hidden_ref, bf16[64,2240]{1,0:T(8,128)(2,1)S(1)} %collective-permute-done.11.refs_1_, bf16[64,2240]{1,0:T(8,128)(2,1)S(1)} %collective-permute-done.refs_0_.refs_2_, ...), custom_call_target="tpu_custom_call" | custom-call | tf_op jit(solution)/shard_map/pallas_call | solution.py:307
  117.7 3.2 %collective-permute-start.15 = (bf16[512,1024]{1,0:T(8,128)(2,1)}, bf16[512,1024]{1,0:T(8,128)(2,1)S(1)}, u32[]{:S(2)}, u32[]{:S(2)}) collective-permute-start(bf16[512,1024]{1,0:T(8,128)(2,1)} %shard_map.96.refs_10_.now_ref), channel_id=1, source_target_pairs={{0,8},{8,16},{16,24},{24,32},{32,40},{40,48},{48,56},{56,64},{64,7... | collective-permute-start | bytes 3145736 | tf_op jit(solution)/shard_map/ppermute | solution.py:362
  121.1 12.6 %collective-permute-done.9.refs_6_ = bf16[2,64,2240]{2,1,0:T(8,128)(2,1)S(1)} collective-permute-done((bf16[2,64,2240]{2,1,0:T(8,128)(2,1)S(1)}, bf16[2,64,2240]{2,1,0:T(8,128)(2,1)S(1)}, u32[]{:S(2)}, u32[]{:S(2)}) %collective-permute-start.9) | collective-permute-done | bytes 573472 | tf_op jit(solution)/shard_map/ppermute | solution.py:346
  133.6 3.4 %collective-permute-done.5.refs_2_ = bf16[2,64,2240]{2,1,0:T(8,128)(2,1)S(1)} collective-permute-done((bf16[2,64,2240]{2,1,0:T(8,128)(2,1)S(1)}, bf16[2,64,2240]{2,1,0:T(8,128)(2,1)S(1)}, u32[]{:S(2)}, u32[]{:S(2)}) %collective-permute-start.5) | collective-permute-done | bytes 573472 | tf_op jit(solution)/shard_map/ppermute | solution.py:346
  137.5 1.5 collective-permute-done.6.refs_3_
  140.7 12.6 %shard_map.97 = (bf16[512,1024]{1,0:T(8,128)(2,1)}, bf16[512,1024]{1,0:T(8,128)(2,1)}) custom-call(s32[2]{0:T(128)S(1)} %pad_add_fusion.place_ref, bf16[2,64,2240]{2,1,0:T(8,128)(2,1)S(1)} %shard_map.95.refs_0_, bf16[2,64,2240]{2,1,0:T(8,128)(2,1)S(1)} %collective-permute-done.4.refs_1_, bf16[2,64,2240]{2,1,0:T(8,128)(2,1)S(1)} %collective-permute-done.5.refs_2_, ...), custom_call_target="tpu_custom_call" | custom-call | tf_op jit(solution)/shard_map/pallas_call | solution.py:307
  155.8 3.0 %shard_map.98 = (bf16[4,64,2240]{2,1,0:T(8,128)(2,1)S(1)}, bf16[4,64,2240]{2,1,0:T(8,128)(2,1)S(1)}) custom-call(s32[2]{0:T(128)S(1)} %pad_add_fusion.place_ref, bf16[512,1024]{1,0:T(8,128)(2,1)S(1)} %copy-done, bf16[512,1024]{1,0:T(8,128)(2,1)S(1)} %copy-done.2, bf16[512,1024]{1,0:T(8,128)(2,1)S(1)} %collective-permute-done.15.two_ref.one_ref, ...), custom_call_target="tpu_custom_call" | custom-call | tf_op jit(solution)/shard_map/pallas_call | solution.py:369
  159.0 3.0 %shard_map.99 = (bf16[4,64,2240]{2,1,0:T(8,128)(2,1)S(1)}, bf16[4,64,2240]{2,1,0:T(8,128)(2,1)S(1)}) custom-call(s32[2]{0:T(128)S(1)} %pad_add_fusion.place_ref, bf16[512,1024]{1,0:T(8,128)(2,1)S(1)} %copy-done.3, bf16[512,1024]{1,0:T(8,128)(2,1)S(1)} %collective-permute-done.15.two_ref.one_ref, bf16[512,1024]{1,0:T(8,128)(2,1)S(1)} %copy-done.4, ...), custom_call_target="tpu_custom_call" | custom-call | tf_op jit(solution)/shard_map/pallas_call | solution.py:369
  163.1 2.6 %collective-permute-start.22 = (bf16[64,2240]{1,0:T(8,128)(2,1)S(1)}, bf16[64,2240]{1,0:T(8,128)(2,1)S(1)}, u32[]{:S(2)}, u32[]{:S(2)}) collective-permute-start(bf16[64,2240]{1,0:T(8,128)(2,1)S(1)} %get-tuple-element.35), channel_id=1, source_target_pairs={{0,4},{1,5},{2,6},{3,7},{4,0},{5,1},{6,2},{7,3},{8,12},{9,13},{10,... | collective-permute-start | bytes 860168 | tf_op jit(solution)/shard_map/ppermute | solution.py:380
  168.1 1.7 collective-permute-start.19
  169.7 10.7 %collective-permute-done.21.refs_3_ = bf16[64,2240]{1,0:T(8,128)(2,1)S(1)} collective-permute-done((bf16[64,2240]{1,0:T(8,128)(2,1)S(1)}, bf16[64,2240]{1,0:T(8,128)(2,1)S(1)}, u32[]{:S(2)}, u32[]{:S(2)}) %collective-permute-start.21) | collective-permute-done | bytes 286752 | tf_op jit(solution)/shard_map/ppermute | solution.py:380
  181.4 10.9 %collective-permute-done.18.refs_0_ = bf16[64,2240]{1,0:T(8,128)(2,1)S(1)} collective-permute-done((bf16[64,2240]{1,0:T(8,128)(2,1)S(1)}, bf16[64,2240]{1,0:T(8,128)(2,1)S(1)}, u32[]{:S(2)}, u32[]{:S(2)}) %collective-permute-start.18) | collective-permute-done | bytes 286752 | tf_op jit(solution)/shard_map/ppermute | solution.py:380
  (83 shorter events, 17.7 us)
Async XLA Ops:
  6.5 76.3 %all-gather.2.cloned.1.call-start = ((), (), s32[]{:S(2)}) async-start(), calls=%async_computation.2 | async-start | bytes 11612160 | tf_op jit(solution)/shard_map/all_gather | solution.py:255
  43.2 26.2 %all-to-all-start.1 = ((bf16[256,8,128]{2,1,0:T(8,128)(2,1)}), bf16[256,8,128]{2,1,0:T(8,128)(2,1)S(1)}, u32[]{:S(2)}, u32[]{:S(2)}) async-start(bf16[256,8,128]{2,1,0:T(8,128)(2,1)} %shard_map.92), calls=%async_computation.1 | async-start | bytes 1048576 | tf_op jit(solution)/shard_map/all_to_all | solution.py:274
  87.4 16.8 %collective-permute-start = (bf16[64,2240]{1,0:T(8,128)(2,1)S(1)}, bf16[64,2240]{1,0:T(8,128)(2,1)S(1)}, u32[]{:S(2)}, u32[]{:S(2)}) collective-permute-start(bf16[64,2240]{1,0:T(8,128)(2,1)S(1)} %get-tuple-element.21.refs_0_.hidden_ref), channel_id=1, source_target_pairs={{0,2},{1,3},{2,4},{3,5},{4,6},{5,7},{6,0},{7,1},{8,10},{9,11},{10,... | collective-permute-start | bytes 860168 | tf_op jit(solution)/shard_map/ppermute | solution.py:346
  88.1 16.2 %collective-permute-start.1 = (bf16[64,2240]{1,0:T(8,128)(2,1)S(1)}, bf16[64,2240]{1,0:T(8,128)(2,1)S(1)}, u32[]{:S(2)}, u32[]{:S(2)}) collective-permute-start(bf16[64,2240]{1,0:T(8,128)(2,1)S(1)} %get-tuple-element.21.refs_0_.hidden_ref), channel_id=1, source_target_pairs={{0,4},{1,5},{2,6},{3,7},{4,0},{5,1},{6,2},{7,3},{8,12},{9,13},{10,... | collective-permute-start | bytes 860168 | tf_op jit(solution)/shard_map/ppermute | solution.py:346
  89.8 15.0 %collective-permute-start.2 = (bf16[64,2240]{1,0:T(8,128)(2,1)S(1)}, bf16[64,2240]{1,0:T(8,128)(2,1)S(1)}, u32[]{:S(2)}, u32[]{:S(2)}) collective-permute-start(bf16[64,2240]{1,0:T(8,128)(2,1)S(1)} %get-tuple-element.21.refs_0_.hidden_ref), channel_id=1, source_target_pairs={{0,6},{1,7},{2,0},{3,1},{4,2},{5,3},{6,4},{7,5},{8,14},{9,15},{10,... | collective-permute-start | bytes 860168 | tf_op jit(solution)/shard_map/ppermute | solution.py:346
  91.9 13.1 %collective-permute-start.3 = (bf16[64,2240]{1,0:T(8,128)(2,1)S(1)}, bf16[64,2240]{1,0:T(8,128)(2,1)S(1)}, u32[]{:S(2)}, u32[]{:S(2)}) collective-permute-start(bf16[64,2240]{1,0:T(8,128)(2,1)S(1)} %get-tuple-element.22.refs_3_.hidden_ref), channel_id=1, source_target_pairs={{0,8},{8,16},{16,24},{24,32},{32,40},{40,48},{48,56},{56,64},{64,7... | collective-permute-start | bytes 860168 | tf_op jit(solution)/shard_map/ppermute | solution.py:349
  94.9 13.3 %collective-permute-start.11 = (bf16[64,2240]{1,0:T(8,128)(2,1)S(1)}, bf16[64,2240]{1,0:T(8,128)(2,1)S(1)}, u32[]{:S(2)}, u32[]{:S(2)}) collective-permute-start(bf16[64,2240]{1,0:T(8,128)(2,1)S(1)} %get-tuple-element.21.refs_0_.hidden_ref), channel_id=1, source_target_pairs={{0,1},{1,0},{2,3},{3,2},{4,5},{5,4},{6,7},{7,6},{8,9},{9,8},{10,11... | collective-permute-start | bytes 860168 | tf_op jit(solution)/shard_map/ppermute | solution.py:360
  104.2 4.0 %collective-permute-start.12 = (bf16[64,2240]{1,0:T(8,128)(2,1)S(1)}, bf16[64,2240]{1,0:T(8,128)(2,1)S(1)}, u32[]{:S(2)}, u32[]{:S(2)}) collective-permute-start(bf16[64,2240]{1,0:T(8,128)(2,1)S(1)} %collective-permute-done.refs_0_.refs_2_), channel_id=1, source_target_pairs={{0,1},{1,0},{2,3},{3,2},{4,5},{5,4},{6,7},{7,6},{8,9},{9,8},{10,11... | collective-permute-start | bytes 860168 | tf_op jit(solution)/shard_map/ppermute | solution.py:360
  104.2 5.5 %collective-permute-start.13 = (bf16[64,2240]{1,0:T(8,128)(2,1)S(1)}, bf16[64,2240]{1,0:T(8,128)(2,1)S(1)}, u32[]{:S(2)}, u32[]{:S(2)}) collective-permute-start(bf16[64,2240]{1,0:T(8,128)(2,1)S(1)} %collective-permute-done.1.refs_1_.refs_4_), channel_id=1, source_target_pairs={{0,1},{1,0},{2,3},{3,2},{4,5},{5,4},{6,7},{7,6},{8,9},{9,8},{10,11... | collective-permute-start | bytes 860168 | tf_op jit(solution)/shard_map/ppermute | solution.py:360
  104.8 4.9 %collective-permute-start.14 = (bf16[64,2240]{1,0:T(8,128)(2,1)S(1)}, bf16[64,2240]{1,0:T(8,128)(2,1)S(1)}, u32[]{:S(2)}, u32[]{:S(2)}) collective-permute-start(bf16[64,2240]{1,0:T(8,128)(2,1)S(1)} %collective-permute-done.2.refs_2_.refs_6_), channel_id=1, source_target_pairs={{0,1},{1,0},{2,3},{3,2},{4,5},{5,4},{6,7},{7,6},{8,9},{9,8},{10,11... | collective-permute-start | bytes 860168 | tf_op jit(solution)/shard_map/ppermute | solution.py:360
  105.5 28.1 %collective-permute-start.9 = (bf16[2,64,2240]{2,1,0:T(8,128)(2,1)S(1)}, bf16[2,64,2240]{2,1,0:T(8,128)(2,1)S(1)}, u32[]{:S(2)}, u32[]{:S(2)}) collective-permute-start(bf16[2,64,2240]{2,1,0:T(8,128)(2,1)S(1)} %shard_map.95.refs_0_), channel_id=1, source_target_pairs={{0,6},{1,7},{2,0},{3,1},{4,2},{5,3},{6,4},{7,5},{8,14},{9,15},{10,... | collective-permute-start | bytes 1720328 | tf_op jit(solution)/shard_map/ppermute | solution.py:346
  108.2 28.8 %collective-permute-start.5 = (bf16[2,64,2240]{2,1,0:T(8,128)(2,1)S(1)}, bf16[2,64,2240]{2,1,0:T(8,128)(2,1)S(1)}, u32[]{:S(2)}, u32[]{:S(2)}) collective-permute-start(bf16[2,64,2240]{2,1,0:T(8,128)(2,1)S(1)} %shard_map.95.refs_0_), channel_id=1, source_target_pairs={{0,2},{1,3},{2,4},{3,5},{4,6},{5,7},{6,0},{7,1},{8,10},{9,11},{10,... | collective-permute-start | bytes 1720328 | tf_op jit(solution)/shard_map/ppermute | solution.py:346
  108.2 28.8 %collective-permute-start.7 = (bf16[2,64,2240]{2,1,0:T(8,128)(2,1)S(1)}, bf16[2,64,2240]{2,1,0:T(8,128)(2,1)S(1)}, u32[]{:S(2)}, u32[]{:S(2)}) collective-permute-start(bf16[2,64,2240]{2,1,0:T(8,128)(2,1)S(1)} %shard_map.95.refs_0_), channel_id=1, source_target_pairs={{0,4},{1,5},{2,6},{3,7},{4,0},{5,1},{6,2},{7,3},{8,12},{9,13},{10,... | collective-permute-start | bytes 1720328 | tf_op jit(solution)/shard_map/ppermute | solution.py:346
  117.7 35.6 %collective-permute-start.15 = (bf16[512,1024]{1,0:T(8,128)(2,1)}, bf16[512,1024]{1,0:T(8,128)(2,1)S(1)}, u32[]{:S(2)}, u32[]{:S(2)}) collective-permute-start(bf16[512,1024]{1,0:T(8,128)(2,1)} %shard_map.96.refs_10_.now_ref), channel_id=1, source_target_pairs={{0,8},{8,16},{16,24},{24,32},{32,40},{40,48},{48,56},{56,64},{64,7... | collective-permute-start | bytes 3145736 | tf_op jit(solution)/shard_map/ppermute | solution.py:362
  121.0 16.6 %collective-permute-start.4 = (bf16[2,64,2240]{2,1,0:T(8,128)(2,1)S(1)}, bf16[2,64,2240]{2,1,0:T(8,128)(2,1)S(1)}, u32[]{:S(2)}, u32[]{:S(2)}) collective-permute-start(bf16[2,64,2240]{2,1,0:T(8,128)(2,1)S(1)} %shard_map.95.refs_0_), channel_id=1, source_target_pairs={{0,1},{1,0},{2,3},{3,2},{4,5},{5,4},{6,7},{7,6},{8,9},{9,8},{10,11... | collective-permute-start | bytes 1720328 | tf_op jit(solution)/shard_map/ppermute | solution.py:365
  133.6 3.9 %collective-permute-start.10 = (bf16[2,64,2240]{2,1,0:T(8,128)(2,1)S(1)}, bf16[2,64,2240]{2,1,0:T(8,128)(2,1)S(1)}, u32[]{:S(2)}, u32[]{:S(2)}) collective-permute-start(bf16[2,64,2240]{2,1,0:T(8,128)(2,1)S(1)} %collective-permute-done.9.refs_6_), channel_id=1, source_target_pairs={{0,1},{1,0},{2,3},{3,2},{4,5},{5,4},{6,7},{7,6},{8,9},{9,8},{10,11... | collective-permute-start | bytes 1720328 | tf_op jit(solution)/shard_map/ppermute | solution.py:365
  158.8 3.9 %collective-permute-start.17 = (bf16[4,64,2240]{2,1,0:T(8,128)(2,1)S(1)}, bf16[4,64,2240]{2,1,0:T(8,128)(2,1)S(1)}, u32[]{:S(2)}, u32[]{:S(2)}) collective-permute-start(bf16[4,64,2240]{2,1,0:T(8,128)(2,1)S(1)} %get-tuple-element.29), channel_id=1, source_target_pairs={{0,1},{1,0},{2,3},{3,2},{4,5},{5,4},{6,7},{7,6},{8,9},{9,8},{10,11... | collective-permute-start | bytes 3440648 | tf_op jit(solution)/shard_map/ppermute | solution.py:370
  162.0 4.3 %collective-permute-start.16 = (bf16[4,64,2240]{2,1,0:T(8,128)(2,1)S(1)}, bf16[4,64,2240]{2,1,0:T(8,128)(2,1)S(1)}, u32[]{:S(2)}, u32[]{:S(2)}) collective-permute-start(bf16[4,64,2240]{2,1,0:T(8,128)(2,1)S(1)} %get-tuple-element.27), channel_id=1, source_target_pairs={{0,1},{1,0},{2,3},{3,2},{4,5},{5,4},{6,7},{7,6},{8,9},{9,8},{10,11... | collective-permute-start | bytes 3440648 | tf_op jit(solution)/shard_map/ppermute | solution.py:370
  163.0 17.5 %collective-permute-start.21 = (bf16[64,2240]{1,0:T(8,128)(2,1)S(1)}, bf16[64,2240]{1,0:T(8,128)(2,1)S(1)}, u32[]{:S(2)}, u32[]{:S(2)}) collective-permute-start(bf16[64,2240]{1,0:T(8,128)(2,1)S(1)} %get-tuple-element.34), channel_id=1, source_target_pairs={{0,2},{1,3},{2,4},{3,5},{4,6},{5,7},{6,0},{7,1},{8,10},{9,11},{10,... | collective-permute-start | bytes 860168 | tf_op jit(solution)/shard_map/ppermute | solution.py:380
  163.1 17.4 %collective-permute-start.22 = (bf16[64,2240]{1,0:T(8,128)(2,1)S(1)}, bf16[64,2240]{1,0:T(8,128)(2,1)S(1)}, u32[]{:S(2)}, u32[]{:S(2)}) collective-permute-start(bf16[64,2240]{1,0:T(8,128)(2,1)S(1)} %get-tuple-element.35), channel_id=1, source_target_pairs={{0,4},{1,5},{2,6},{3,7},{4,0},{5,1},{6,2},{7,3},{8,12},{9,13},{10,... | collective-permute-start | bytes 860168 | tf_op jit(solution)/shard_map/ppermute | solution.py:380
  165.7 15.7 %collective-permute-start.23 = (bf16[64,2240]{1,0:T(8,128)(2,1)S(1)}, bf16[64,2240]{1,0:T(8,128)(2,1)S(1)}, u32[]{:S(2)}, u32[]{:S(2)}) collective-permute-start(bf16[64,2240]{1,0:T(8,128)(2,1)S(1)} %get-tuple-element.36), channel_id=1, source_target_pairs={{0,6},{1,7},{2,0},{3,1},{4,2},{5,3},{6,4},{7,5},{8,14},{9,15},{10,... | collective-permute-start | bytes 860168 | tf_op jit(solution)/shard_map/ppermute | solution.py:380
  166.6 25.7 %collective-permute-start.18 = (bf16[64,2240]{1,0:T(8,128)(2,1)S(1)}, bf16[64,2240]{1,0:T(8,128)(2,1)S(1)}, u32[]{:S(2)}, u32[]{:S(2)}) collective-permute-start(bf16[64,2240]{1,0:T(8,128)(2,1)S(1)} %get-tuple-element.31), channel_id=1, source_target_pairs={{0,2},{1,3},{2,4},{3,5},{4,6},{5,7},{6,0},{7,1},{8,10},{9,11},{10,... | collective-permute-start | bytes 860168 | tf_op jit(solution)/shard_map/ppermute | solution.py:380
  168.1 24.2 %collective-permute-start.19 = (bf16[64,2240]{1,0:T(8,128)(2,1)S(1)}, bf16[64,2240]{1,0:T(8,128)(2,1)S(1)}, u32[]{:S(2)}, u32[]{:S(2)}) collective-permute-start(bf16[64,2240]{1,0:T(8,128)(2,1)S(1)} %get-tuple-element.32), channel_id=1, source_target_pairs={{0,4},{1,5},{2,6},{3,7},{4,0},{5,1},{6,2},{7,3},{8,12},{9,13},{10,... | collective-permute-start | bytes 860168 | tf_op jit(solution)/shard_map/ppermute | solution.py:380
  180.5 12.5 %collective-permute-start.20 = (bf16[64,2240]{1,0:T(8,128)(2,1)S(1)}, bf16[64,2240]{1,0:T(8,128)(2,1)S(1)}, u32[]{:S(2)}, u32[]{:S(2)}) collective-permute-start(bf16[64,2240]{1,0:T(8,128)(2,1)S(1)} %get-tuple-element.33), channel_id=1, source_target_pairs={{0,6},{1,7},{2,0},{3,1},{4,2},{5,3},{6,4},{7,5},{8,14},{9,15},{10,... | collective-permute-start | bytes 860168 | tf_op jit(solution)/shard_map/ppermute | solution.py:380
  (20 other events, 165.1 us)
Sparse Core Ops, SparseCore 0:
  9.2 73.5 all-gather.1

commit v8 on v7

--- a/solution.py
+++ b/solution.py
@@ -19,6 +19,7 @@
 BF = jnp.bfloat16
 F32 = jnp.float32
 MIB = 1 << 20
+PIECES_MIB = 24
 
 
 def slab_of(c):
@@ -152,7 +153,9 @@
 
 def pieces_kernel(place_ref, *refs):
     peers = 8
-    pieces, (w_ref, taps_ref, _, out_ref, act_ref, hid_ref) = refs[:peers], refs[peers:]
+    pieces = refs[:peers]
+    w_ref, taps_ref, _, out_ref, token_ref, act_ref, hid_ref = refs[peers:]
+    token_ref[...] = jnp.zeros(token_ref.shape, F32)
     rows = pieces[0].shape[0]
 
     @pl.when(pl.program_id(0) == 0)
@@ -162,24 +165,6 @@
             hid_ref[pl.ds(pl.multiple_of(source * rows, rows), rows)] = piece[...]
 
     depthwise(hid_ref[...], w_ref, taps_ref, out_ref, act_ref)
-
-
-def both_kernel(place_ref, *refs):
-    peers, frames = 8, 2
-    pieces = refs[:peers]
-    w_ref, taps_ref, _, one_ref, two_ref, act_ref, hid_ref = refs[peers:]
-    rows = pieces[0].shape[1]
-
-    @pl.when(pl.program_id(0) == 0)
-    def _():
-        for p, piece in enumerate(pieces):
-            source = 2 * ((place_ref[0] + 4 - p // 2) % 4) + (place_ref[1] + p % 2) % 2
-            target = pl.ds(pl.multiple_of(source * rows, rows), rows)
-            for f in range(frames):
-                hid_ref[f, target] = piece[f]
-
-    for f, out_ref in enumerate((one_ref, two_ref)):
-        depthwise(hid_ref[f], w_ref, taps_ref, out_ref, act_ref.at[f])
 
 
 def point_kernel(
@@ -217,10 +202,9 @@
         send[...] = total(k + 1).astype(BF)
 
 
-def stack_kernel(*refs):
-    one_ref, two_ref, out_ref = refs[-3:]
-    out_ref[0] = one_ref[...]
-    out_ref[1] = two_ref[...]
+def follow_kernel(count, *refs):
+    for rows_ref, out_ref in zip(refs[:count], refs[-count:]):
+        out_ref[...] = rows_ref[...]
 
 
 def final_kernel(early_ref, late_ref, *refs):
@@ -301,23 +285,24 @@
         pl.BlockSpec((9, block), lambda i: (0, i)),
     ]
 
-    def pieces_call(kernel, frames, pieces, needed):
-        outs = 1 if frames is None else frames
-        lead = () if frames is None else (frames,)
+    def pieces_call(pieces, needed):
         return pl.pallas_call(
-            kernel,
-            out_shape=[spatial_out] * outs,
+            pieces_kernel,
+            out_shape=[spatial_out, jax.ShapeDtypeStruct((8, LANES), F32)],
             grid=(2 * chan // block,),
             in_specs=[pl.BlockSpec(memory_space=pltpu.SMEM)]
-            + [pl.BlockSpec(part.shape, lambda i, n=part.ndim: (0,) * n) for part in pieces]
+            + [pl.BlockSpec((frame_rows, width), lambda i: (0, 0))] * peers
             + weight_specs
             + [anywhere],
-            out_specs=[pl.BlockSpec((whole_rows, block), lambda i: (0, i))] * outs,
+            out_specs=[
+                pl.BlockSpec((whole_rows, block), lambda i: (0, i)),
+                pl.BlockSpec((8, LANES), lambda i: (0, 0)),
+            ],
             scratch_shapes=[
-                pltpu.VMEM(lead + (whole_rows + 2 * col_count, block), F32),
-                pltpu.VMEM(lead + (whole_rows, width), BF),
+                pltpu.VMEM((whole_rows + 2 * col_count, block), F32),
+                pltpu.VMEM((whole_rows, width), BF),
             ],
-            compiler_params=params(52),
+            compiler_params=params(PIECES_MIB),
         )(where_am_i, *pieces, w_flat, taps_s, needed)
 
     row_block = 256
@@ -345,25 +330,30 @@
     def along_of(rows):
         return [rows] + [lax.ppermute(rows, "tile", ahead[k]) for k in (1, 2, 3)]
 
+    def after(rows, needed):
+        return pl.pallas_call(
+            functools.partial(follow_kernel, len(rows)),
+            out_shape=[one_frame] * len(rows),
+            in_specs=[VMEM] * len(rows) + [anywhere] * len(needed),
+            out_specs=[VMEM] * len(rows),
+            compiler_params=params(20),
+        )(*rows, *needed)
+
+    def spatial_of(along, needed):
+        pieces = []
+        for part in along:
+            pieces += [part, lax.ppermute(part, "tile", other_core)]
+        return pieces_call(pieces, needed)
+
     late_along = along_of(late)
     before_early = lax.ppermute(early, "blk", next_frames)
-    others = pl.pallas_call(
-        stack_kernel,
-        out_shape=jax.ShapeDtypeStruct((2, frame_rows, width), BF),
-        in_specs=[anywhere] * 3 + [VMEM] * 2,
-        out_specs=VMEM,
-        compiler_params=params(20),
-    )(*late_along[1:], early, before_early)
-    others_along = along_of(others)
-    pieces = []
-    for part in late_along:
-        pieces += [part, lax.ppermute(part, "tile", other_core)]
-    (late_sp,) = pieces_call(pieces_kernel, None, pieces, taps_t)
+    early_along = along_of(*after([early], late_along[1:]))
+    late_sp, late_token = spatial_of(late_along, taps_t)
     before_late_sp = lax.ppermute(late_sp, "blk", next_frames)
-    both = []
-    for part in others_along:
-        both += [part, lax.ppermute(part, "tile", other_core)]
-    early_sp, before_early_sp = pieces_call(both_kernel, 2, both, late_sp)
+    before_early_along = along_of(*after([before_early], early_along[1:] + [late_token]))
+    early_sp, early_token = spatial_of(early_along, late_token)
+    before_early_along[1:] = after(before_early_along[1:], [early_token])
+    before_early_sp, last_token = spatial_of(before_early_along, early_token)
 
     def core_shares(now, one, two, needed):
         mine, other = point_call(where_am_i, now, one, two, taps_t, w_point, needed)
@@ -379,7 +369,7 @@
         )(mine, from_core, rows)
         return kept, [lax.ppermute(part, "tile", ahead[k + 1]) for k, part in enumerate(sends)]
 
-    late_shares = core_shares(late_sp, early_sp, before_late_sp, before_early_sp)
+    late_shares = core_shares(late_sp, early_sp, before_late_sp, last_token)
     late_kept, late_back = sums(*late_shares, late)
     early_shares = core_shares(early_sp, before_late_sp, before_early_sp, late_shares[0])
     early_kept, early_back = sums(*early_shares, early)

time: 201 us -> 205 us (1.020)
  starting transfers between devices: 30.4 us -> 34.6 us
  waiting for transfers between devices: 77.1 us -> 79.7 us
  local copies, waits for them, and re-layouts: 11.3 us -> 8.99 us
    ppermute x6 -> x9, starting transfers between devices: 8.52 us -> 12.2 us  [along_of(): return [rows] + [lax.ppermute(rows, 'tile', ahead[k]) for k in (1, 2, 3)]]
    ppermute x6 -> x9, waiting for transfers between devices: 25.3 us -> 28.3 us  [along_of(): return [rows] + [lax.ppermute(rows, 'tile', ahead[k]) for k in (1, 2, 3)]]
    unnamed x40 -> x20, local copies, waits for them, and re-layouts: 11.3 us -> 8.99 us
    pallas_call x3 -> x6, Pallas kernels: 20 us -> 18.2 us  [the longest x3 18.1 us: pieces_call(): pl.pallas_call(pieces_kernel, out_shape=[spatial_out, jax.ShapeDtypeStruc...]
  transfers between devices with their start and end apart: 26 -> 33, of which waited for: 12 -> 16; matrix products, arithmetic and copies ran while one was open for 3% -> 3% of each run, Pallas kernels for 13% -> 12%
where the time goes in v8:
time: 205 us; the launch traced here: 204 us
  waiting for transfers between devices  79.7 us (39%)
  starting transfers between devices  34.6 us (17%)
  blocking collectives  33.6 us (16%)
  Pallas kernels  33.2 us (16%)
  between operations  13.7 us (7%)
  local copies, waits for them, and re-layouts  8.99 us (4%)
    all_to_all x1, blocking collectives, on_device(): parts = lax.all_to_all(parts, everyone, 0, 0, tiled=True)  33.6 us
    ppermute x9, waiting for transfers between devices, along_of(): return [rows] + [lax.ppermute(rows, 'tile', ahead[k]) for k in (1, 2, 3)]  28.3 us
    ppermute x6, waiting for transfers between devices, sums(): lax.ppermute(part, 'tile', ahead[k + 1])  23.3 us
    pallas_call x3, Pallas kernels, pieces_call(): pl.pallas_call(pieces_kernel, out_shape=[spatial_out, jax.ShapeDtypeStruc...  18.1 us
    all_to_all x1, waiting for transfers between devices, on_device(): state = lax.all_to_all(sums, everyone, 0, 0, tiled=True)  12.9 us
    all_gather x1, waiting for transfers between devices, on_device(): w_out_whole = lax.all_gather(w_output, 'tile', axis=0, tiled=True)  12.6 us
    ppermute x9, starting transfers between devices, along_of(): return [rows] + [lax.ppermute(rows, 'tile', ahead[k]) for k in (1, 2, 3)]  12.2 us
    unnamed x20, local copies, waits for them, and re-layouts  8.99 us
  transfers between devices with their start and end apart: 33, of which 16 were waited for; matrix products, arithmetic and copies ran while one was open for 3% of the time, Pallas kernels for 12%

profile of v8, /device:TPU:2, one launch (start us, length us, event | category | flops | bytes accessed | tf_op | source)
XLA Modules:
  0.0 203.8 jit_solution(2505543253547244805)
XLA Ops:
  8.5 33.6 %all_to_all.10.in_ref = bf16[256,8,128]{2,1,0:T(8,128)(2,1)S(1)} all-to-all(bf16[256,8,128]{2,1,0:T(8,128)(2,1)S(1)} %shard_map.91), channel_id=1, replica_groups=mesh['blk'=32,'tile'=8] {'blk','tile'}, dimensions={0} | all-to-all | bytes 1048576 | tf_op jit(solution)/shard_map/all_to_all | solution.py:254
  43.2 7.1 %all-to-all-start.1 = ((bf16[256,8,128]{2,1,0:T(8,128)(2,1)}), bf16[256,8,128]{2,1,0:T(8,128)(2,1)S(1)}, u32[]{:S(2)}, u32[]{:S(2)}) async-start(bf16[256,8,128]{2,1,0:T(8,128)(2,1)} %shard_map.92), calls=%async_computation.1 | async-start | bytes 1048576 | tf_op jit(solution)/shard_map/all_to_all | solution.py:258
  50.4 6.1 %copy.10 = bf16[280,8,2,512]{3,1,2,0:T(8,128)(2,1)} copy(bf16[280,8,2,512]{3,2,1,0:T(2,128)(2,1)} %bitcast.31) | data formatting | bytes 9175040
  56.5 12.9 %all-to-all-done.1.state_ref = bf16[256,8,128]{2,1,0:T(8,128)(2,1)S(1)} async-done(((bf16[256,8,128]{2,1,0:T(8,128)(2,1)}), bf16[256,8,128]{2,1,0:T(8,128)(2,1)S(1)}, u32[]{:S(2)}, u32[]{:S(2)}) %all-to-all-start.1) | async-done | bytes 524320 | tf_op jit(solution)/shard_map/all_to_all | solution.py:258
  70.2 12.6 %all-gather.2.cloned.1.call-done.w_hbm = bf16[2240,2240]{1,0:T(8,128)(2,1)} async-done(((bf16[280,2240]{1,0:T(8,128)(2,1)}), bf16[2240,2240]{1,0:T(8,128)(2,1)}) %all-gather.2.cloned.1.call-update) | async-done | bytes 10035216 | tf_op jit(solution)/shard_map/all_gather | solution.py:239
  82.8 4.6 %shard_map.94 = (bf16[64,2240]{1,0:T(8,128)(2,1)S(1)}, bf16[64,2240]{1,0:T(8,128)(2,1)S(1)}) custom-call(bf16[128,2240]{1,0:T(8,128)(2,1)S(1)} %shard_map.93.att_ref, bf16[128,2240]{1,0:T(8,128)(2,1)S(1)} %bitcast.24, bf16[2240,2240]{1,0:T(8,128)(2,1)} %all-gather.2.cloned.1.call-done.w_hbm, bf16[2240,1024]{1,0:T(8,128)(2,1)} %bitcast.15), custom_call_target="tpu_custom_call" | custom-call | tf_op jit(solution)/shard_map/pallas_call | solution.py:270
  91.9 12.3 %collective-permute-done.refs_1_.refs_2_ = bf16[64,2240]{1,0:T(8,128)(2,1)S(1)} collective-permute-done((bf16[64,2240]{1,0:T(8,128)(2,1)S(1)}, bf16[64,2240]{1,0:T(8,128)(2,1)S(1)}, u32[]{:S(2)}, u32[]{:S(2)}) %collective-permute-start) | collective-permute-done | bytes 286752 | tf_op jit(solution)/shard_map/ppermute | solution.py:331
  104.9 3.1 %collective-permute-start.15 = (bf16[64,2240]{1,0:T(8,128)(2,1)S(1)}, bf16[64,2240]{1,0:T(8,128)(2,1)S(1)}, u32[]{:S(2)}, u32[]{:S(2)}) collective-permute-start(bf16[64,2240]{1,0:T(8,128)(2,1)S(1)} %get-tuple-element.28.refs_0_.hidden_ref), channel_id=1, source_target_pairs={{0,8},{8,16},{16,24},{24,32},{32,40},{40,48},{48,56},{56,64},{64,7... | collective-permute-start | bytes 860168 | tf_op jit(solution)/shard_map/ppermute | solution.py:349
  109.1 3.1 %collective-permute-start.6 = (bf16[64,2240]{1,0:T(8,128)(2,1)S(1)}, bf16[64,2240]{1,0:T(8,128)(2,1)S(1)}, u32[]{:S(2)}, u32[]{:S(2)}) collective-permute-start(bf16[64,2240]{1,0:T(8,128)(2,1)S(1)} %shard_map.95.refs_0_), channel_id=1, source_target_pairs={{0,4},{1,5},{2,6},{3,7},{4,0},{5,1},{6,2},{7,3},{8,12},{9,13},{10,... | collective-permute-start | bytes 860168 | tf_op jit(solution)/shard_map/ppermute | solution.py:331
  112.3 2.3 %copy-done = bf16[280,8,2,512]{3,1,2,0:T(8,128)(2,1)S(1)} copy-done((bf16[280,8,2,512]{3,1,2,0:T(8,128)(2,1)S(1)}, bf16[280,8,2,512]{3,1,2,0:T(8,128)(2,1)}, u32[]{:S(2)}) %copy-start) | copy-done | bytes 4587544
  114.6 6.0 %shard_map.96 = (bf16[512,1024]{1,0:T(8,128)(2,1)S(1)}, f32[8,128]{1,0:T(8,128)S(1)}) custom-call(s32[2]{0:T(128)S(1)} %pad_add_fusion.place_ref, bf16[64,2240]{1,0:T(8,128)(2,1)S(1)} %get-tuple-element.29.refs_0_.hidden_ref, bf16[64,2240]{1,0:T(8,128)(2,1)S(1)} %collective-permute-done.10.refs_1_, ...), custom_call_target="tpu_custom_call" | custom-call | tf_op jit(solution)/shard_map/pallas_call | solution.py:289
  120.7 3.4 %collective-permute-start.14 = (bf16[512,1024]{1,0:T(8,128)(2,1)S(1)}, bf16[512,1024]{1,0:T(8,128)(2,1)S(1)}, u32[]{:S(2)}, u32[]{:S(2)}) collective-permute-start(bf16[512,1024]{1,0:T(8,128)(2,1)S(1)} %get-tuple-element.32.now_ref), channel_id=1, source_target_pairs={{0,8},{8,16},{16,24},{24,32},{32,40},{40,48},{48,56},{56,64},{64,7... | collective-permute-start | bytes 3145736 | tf_op jit(solution)/shard_map/ppermute | solution.py:352
  125.7 6.8 %collective-permute-done.8.refs_6_.refs_3_ = bf16[64,2240]{1,0:T(8,128)(2,1)S(1)} collective-permute-done((bf16[64,2240]{1,0:T(8,128)(2,1)S(1)}, bf16[64,2240]{1,0:T(8,128)(2,1)S(1)}, u32[]{:S(2)}, u32[]{:S(2)}) %collective-permute-start.8) | collective-permute-done | bytes 286752 | tf_op jit(solution)/shard_map/ppermute | solution.py:331
  132.6 2.9 %collective-permute-start.18 = (bf16[64,2240]{1,0:T(8,128)(2,1)S(1)}, bf16[64,2240]{1,0:T(8,128)(2,1)S(1)}, u32[]{:S(2)}, u32[]{:S(2)}) collective-permute-start(bf16[64,2240]{1,0:T(8,128)(2,1)S(1)} %shard_map.98.refs_0_), channel_id=1, source_target_pairs={{0,4},{1,5},{2,6},{3,7},{4,0},{5,1},{6,2},{7,3},{8,12},{9,13},{10,... | collective-permute-start | bytes 860168 | tf_op jit(solution)/shard_map/ppermute | solution.py:331
  135.9 6.0 %shard_map.97 = (bf16[512,1024]{1,0:T(8,128)(2,1)S(1)}, f32[8,128]{1,0:T(8,128)S(1)}) custom-call(s32[2]{0:T(128)S(1)} %pad_add_fusion.place_ref, bf16[64,2240]{1,0:T(8,128)(2,1)S(1)} %shard_map.95.refs_0_, bf16[64,2240]{1,0:T(8,128)(2,1)S(1)} %collective-permute-done.3.refs_1_, bf16[64,2240]{1,0:T(8,128)(2,1)S(1)} %collective-permute-done.4.refs_2_.refs_1_, ...), custom_call_target="tpu_custom_call" | custom-call | tf_op jit(solution)/shard_map/pallas_call | solution.py:289
  141.9 7.6 %collective-permute-done.17.refs_0_ = bf16[64,2240]{1,0:T(8,128)(2,1)S(1)} collective-permute-done((bf16[64,2240]{1,0:T(8,128)(2,1)S(1)}, bf16[64,2240]{1,0:T(8,128)(2,1)S(1)}, u32[]{:S(2)}, u32[]{:S(2)}) %collective-permute-start.17) | collective-permute-done | bytes 286752 | tf_op jit(solution)/shard_map/ppermute | solution.py:331
  152.7 6.0 %shard_map.100 = (bf16[512,1024]{1,0:T(8,128)(2,1)S(1)}, f32[8,128]{1,0:T(8,128)S(1)}) custom-call(s32[2]{0:T(128)S(1)} %pad_add_fusion.place_ref, bf16[64,2240]{1,0:T(8,128)(2,1)S(1)} %shard_map.98.refs_0_, bf16[64,2240]{1,0:T(8,128)(2,1)S(1)} %collective-permute-done.16.refs_1_, bf16[64,2240]{1,0:T(8,128)(2,1)S(1)} %get-tuple-element.34.refs_2_, ...), custom_call_target="tpu_custom_call" | custom-call | tf_op jit(solution)/shard_map/pallas_call | solution.py:289
  158.8 3.1 %shard_map.101 = (bf16[4,64,2240]{2,1,0:T(8,128)(2,1)S(1)}, bf16[4,64,2240]{2,1,0:T(8,128)(2,1)S(1)}) custom-call(s32[2]{0:T(128)S(1)} %pad_add_fusion.place_ref, bf16[512,1024]{1,0:T(8,128)(2,1)S(1)} %get-tuple-element.32.now_ref, bf16[512,1024]{1,0:T(8,128)(2,1)S(1)} %get-tuple-element.31.one_ref.now_ref, ...), custom_call_target="tpu_custom_call" | custom-call | tf_op jit(solution)/shard_map/pallas_call | solution.py:359
  162.1 3.0 %shard_map.102 = (bf16[4,64,2240]{2,1,0:T(8,128)(2,1)S(1)}, bf16[4,64,2240]{2,1,0:T(8,128)(2,1)S(1)}) custom-call(s32[2]{0:T(128)S(1)} %pad_add_fusion.place_ref, bf16[512,1024]{1,0:T(8,128)(2,1)S(1)} %get-tuple-element.31.one_ref.now_ref, bf16[512,1024]{1,0:T(8,128)(2,1)S(1)} %collective-permute-done.14.two_ref.one_ref, ...), custom_call_target="tpu_custom_call" | custom-call | tf_op jit(solution)/shard_map/pallas_call | solution.py:359
  166.2 3.6 %collective-permute-start.29 = (bf16[64,2240]{1,0:T(8,128)(2,1)S(1)}, bf16[64,2240]{1,0:T(8,128)(2,1)S(1)}, u32[]{:S(2)}, u32[]{:S(2)}) collective-permute-start(bf16[64,2240]{1,0:T(8,128)(2,1)S(1)} %get-tuple-element.49), channel_id=1, source_target_pairs={{0,4},{1,5},{2,6},{3,7},{4,0},{5,1},{6,2},{7,3},{8,12},{9,13},{10,... | collective-permute-start | bytes 860168 | tf_op jit(solution)/shard_map/ppermute | solution.py:370
  170.1 2.1 %collective-permute-start.25 = (bf16[64,2240]{1,0:T(8,128)(2,1)S(1)}, bf16[64,2240]{1,0:T(8,128)(2,1)S(1)}, u32[]{:S(2)}, u32[]{:S(2)}) collective-permute-start(bf16[64,2240]{1,0:T(8,128)(2,1)S(1)} %get-tuple-element.45), channel_id=1, source_target_pairs={{0,2},{1,3},{2,4},{3,5},{4,6},{5,7},{6,0},{7,1},{8,10},{9,11},{10,... | collective-permute-start | bytes 860168 | tf_op jit(solution)/shard_map/ppermute | solution.py:370
  172.6 10.0 %collective-permute-done.28.refs_3_ = bf16[64,2240]{1,0:T(8,128)(2,1)S(1)} collective-permute-done((bf16[64,2240]{1,0:T(8,128)(2,1)S(1)}, bf16[64,2240]{1,0:T(8,128)(2,1)S(1)}, u32[]{:S(2)}, u32[]{:S(2)}) %collective-permute-start.28) | collective-permute-done | bytes 286752 | tf_op jit(solution)/shard_map/ppermute | solution.py:370
  184.3 4.7 %collective-permute-done.25.refs_0_ = bf16[64,2240]{1,0:T(8,128)(2,1)S(1)} collective-permute-done((bf16[64,2240]{1,0:T(8,128)(2,1)S(1)}, bf16[64,2240]{1,0:T(8,128)(2,1)S(1)}, u32[]{:S(2)}, u32[]{:S(2)}) %collective-permute-start.25) | collective-permute-done | bytes 286752 | tf_op jit(solution)/shard_map/ppermute | solution.py:370
  188.9 6.9 %collective-permute-done.26.refs_1_ = bf16[64,2240]{1,0:T(8,128)(2,1)S(1)} collective-permute-done((bf16[64,2240]{1,0:T(8,128)(2,1)S(1)}, bf16[64,2240]{1,0:T(8,128)(2,1)S(1)}, u32[]{:S(2)}, u32[]{:S(2)}) %collective-permute-start.26) | collective-permute-done | bytes 286752 | tf_op jit(solution)/shard_map/ppermute | solution.py:370
  (80 shorter events, 20.1 us)
Async XLA Ops:
  6.5 76.3 %all-gather.2.cloned.1.call-start = ((), (), s32[]{:S(2)}) async-start(), calls=%async_computation.2 | async-start | bytes 11612160 | tf_op jit(solution)/shard_map/all_gather | solution.py:239
  43.2 26.2 %all-to-all-start.1 = ((bf16[256,8,128]{2,1,0:T(8,128)(2,1)}), bf16[256,8,128]{2,1,0:T(8,128)(2,1)S(1)}, u32[]{:S(2)}, u32[]{:S(2)}) async-start(bf16[256,8,128]{2,1,0:T(8,128)(2,1)} %shard_map.92), calls=%async_computation.1 | async-start | bytes 1048576 | tf_op jit(solution)/shard_map/all_to_all | solution.py:258
  87.4 16.8 %collective-permute-start = (bf16[64,2240]{1,0:T(8,128)(2,1)S(1)}, bf16[64,2240]{1,0:T(8,128)(2,1)S(1)}, u32[]{:S(2)}, u32[]{:S(2)}) collective-permute-start(bf16[64,2240]{1,0:T(8,128)(2,1)S(1)} %get-tuple-element.29.refs_0_.hidden_ref), channel_id=1, source_target_pairs={{0,2},{1,3},{2,4},{3,5},{4,6},{5,7},{6,0},{7,1},{8,10},{9,11},{10,... | collective-permute-start | bytes 860168 | tf_op jit(solution)/shard_map/ppermute | solution.py:331
  88.1 16.2 %collective-permute-start.1 = (bf16[64,2240]{1,0:T(8,128)(2,1)S(1)}, bf16[64,2240]{1,0:T(8,128)(2,1)S(1)}, u32[]{:S(2)}, u32[]{:S(2)}) collective-permute-start(bf16[64,2240]{1,0:T(8,128)(2,1)S(1)} %get-tuple-element.29.refs_0_.hidden_ref), channel_id=1, source_target_pairs={{0,4},{1,5},{2,6},{3,7},{4,0},{5,1},{6,2},{7,3},{8,12},{9,13},{10,... | collective-permute-start | bytes 860168 | tf_op jit(solution)/shard_map/ppermute | solution.py:331
  89.8 15.0 %collective-permute-start.2 = (bf16[64,2240]{1,0:T(8,128)(2,1)S(1)}, bf16[64,2240]{1,0:T(8,128)(2,1)S(1)}, u32[]{:S(2)}, u32[]{:S(2)}) collective-permute-start(bf16[64,2240]{1,0:T(8,128)(2,1)S(1)} %get-tuple-element.29.refs_0_.hidden_ref), channel_id=1, source_target_pairs={{0,6},{1,7},{2,0},{3,1},{4,2},{5,3},{6,4},{7,5},{8,14},{9,15},{10,... | collective-permute-start | bytes 860168 | tf_op jit(solution)/shard_map/ppermute | solution.py:331
  91.9 16.2 %collective-permute-start.10 = (bf16[64,2240]{1,0:T(8,128)(2,1)S(1)}, bf16[64,2240]{1,0:T(8,128)(2,1)S(1)}, u32[]{:S(2)}, u32[]{:S(2)}) collective-permute-start(bf16[64,2240]{1,0:T(8,128)(2,1)S(1)} %get-tuple-element.29.refs_0_.hidden_ref), channel_id=1, source_target_pairs={{0,1},{1,0},{2,3},{3,2},{4,5},{5,4},{6,7},{7,6},{8,9},{9,8},{10,11... | collective-permute-start | bytes 860168 | tf_op jit(solution)/shard_map/ppermute | solution.py:345
  104.9 19.3 %collective-permute-start.15 = (bf16[64,2240]{1,0:T(8,128)(2,1)S(1)}, bf16[64,2240]{1,0:T(8,128)(2,1)S(1)}, u32[]{:S(2)}, u32[]{:S(2)}) collective-permute-start(bf16[64,2240]{1,0:T(8,128)(2,1)S(1)} %get-tuple-element.28.refs_0_.hidden_ref), channel_id=1, source_target_pairs={{0,8},{8,16},{16,24},{24,32},{32,40},{40,48},{48,56},{56,64},{64,7... | collective-permute-start | bytes 860168 | tf_op jit(solution)/shard_map/ppermute | solution.py:349
  108.1 16.2 %collective-permute-start.4 = (bf16[64,2240]{1,0:T(8,128)(2,1)S(1)}, bf16[64,2240]{1,0:T(8,128)(2,1)S(1)}, u32[]{:S(2)}, u32[]{:S(2)}) collective-permute-start(bf16[64,2240]{1,0:T(8,128)(2,1)S(1)} %shard_map.95.refs_0_), channel_id=1, source_target_pairs={{0,2},{1,3},{2,4},{3,5},{4,6},{5,7},{6,0},{7,1},{8,10},{9,11},{10,... | collective-permute-start | bytes 860168 | tf_op jit(solution)/shard_map/ppermute | solution.py:331
  109.1 16.5 %collective-permute-start.6 = (bf16[64,2240]{1,0:T(8,128)(2,1)S(1)}, bf16[64,2240]{1,0:T(8,128)(2,1)S(1)}, u32[]{:S(2)}, u32[]{:S(2)}) collective-permute-start(bf16[64,2240]{1,0:T(8,128)(2,1)S(1)} %shard_map.95.refs_0_), channel_id=1, source_target_pairs={{0,4},{1,5},{2,6},{3,7},{4,0},{5,1},{6,2},{7,3},{8,12},{9,13},{10,... | collective-permute-start | bytes 860168 | tf_op jit(solution)/shard_map/ppermute | solution.py:331
  120.7 38.1 %collective-permute-start.14 = (bf16[512,1024]{1,0:T(8,128)(2,1)S(1)}, bf16[512,1024]{1,0:T(8,128)(2,1)S(1)}, u32[]{:S(2)}, u32[]{:S(2)}) collective-permute-start(bf16[512,1024]{1,0:T(8,128)(2,1)S(1)} %get-tuple-element.32.now_ref), channel_id=1, source_target_pairs={{0,8},{8,16},{16,24},{24,32},{32,40},{40,48},{48,56},{56,64},{64,7... | collective-permute-start | bytes 3145736 | tf_op jit(solution)/shard_map/ppermute | solution.py:352
  124.1 8.4 %collective-permute-start.8 = (bf16[64,2240]{1,0:T(8,128)(2,1)S(1)}, bf16[64,2240]{1,0:T(8,128)(2,1)S(1)}, u32[]{:S(2)}, u32[]{:S(2)}) collective-permute-start(bf16[64,2240]{1,0:T(8,128)(2,1)S(1)} %shard_map.95.refs_0_), channel_id=1, source_target_pairs={{0,6},{1,7},{2,0},{3,1},{4,2},{5,3},{6,4},{7,5},{8,14},{9,15},{10,... | collective-permute-start | bytes 860168 | tf_op jit(solution)/shard_map/ppermute | solution.py:331
  124.3 8.2 %collective-permute-start.3 = (bf16[64,2240]{1,0:T(8,128)(2,1)S(1)}, bf16[64,2240]{1,0:T(8,128)(2,1)S(1)}, u32[]{:S(2)}, u32[]{:S(2)}) collective-permute-start(bf16[64,2240]{1,0:T(8,128)(2,1)S(1)} %shard_map.95.refs_0_), channel_id=1, source_target_pairs={{0,1},{1,0},{2,3},{3,2},{4,5},{5,4},{6,7},{7,6},{8,9},{9,8},{10,11... | collective-permute-start | bytes 860168 | tf_op jit(solution)/shard_map/ppermute | solution.py:345
  124.3 8.3 %collective-permute-start.5 = (bf16[64,2240]{1,0:T(8,128)(2,1)S(1)}, bf16[64,2240]{1,0:T(8,128)(2,1)S(1)}, u32[]{:S(2)}, u32[]{:S(2)}) collective-permute-start(bf16[64,2240]{1,0:T(8,128)(2,1)S(1)} %collective-permute-done.4.refs_2_.refs_1_), channel_id=1, source_target_pairs={{0,1},{1,0},{2,3},{3,2},{4,5},{5,4},{6,7},{7,6},{8,9},{9,8},{10,11... | collective-permute-start | bytes 860168 | tf_op jit(solution)/shard_map/ppermute | solution.py:345
  125.7 9.9 %collective-permute-start.7 = (bf16[64,2240]{1,0:T(8,128)(2,1)S(1)}, bf16[64,2240]{1,0:T(8,128)(2,1)S(1)}, u32[]{:S(2)}, u32[]{:S(2)}) collective-permute-start(bf16[64,2240]{1,0:T(8,128)(2,1)S(1)} %collective-permute-done.6.refs_4_.refs_2_), channel_id=1, source_target_pairs={{0,1},{1,0},{2,3},{3,2},{4,5},{5,4},{6,7},{7,6},{8,9},{9,8},{10,11... | collective-permute-start | bytes 860168 | tf_op jit(solution)/shard_map/ppermute | solution.py:345
  132.5 17.0 %collective-permute-start.17 = (bf16[64,2240]{1,0:T(8,128)(2,1)S(1)}, bf16[64,2240]{1,0:T(8,128)(2,1)S(1)}, u32[]{:S(2)}, u32[]{:S(2)}) collective-permute-start(bf16[64,2240]{1,0:T(8,128)(2,1)S(1)} %shard_map.98.refs_0_), channel_id=1, source_target_pairs={{0,2},{1,3},{2,4},{3,5},{4,6},{5,7},{6,0},{7,1},{8,10},{9,11},{10,... | collective-permute-start | bytes 860168 | tf_op jit(solution)/shard_map/ppermute | solution.py:331
  132.6 16.9 %collective-permute-start.18 = (bf16[64,2240]{1,0:T(8,128)(2,1)S(1)}, bf16[64,2240]{1,0:T(8,128)(2,1)S(1)}, u32[]{:S(2)}, u32[]{:S(2)}) collective-permute-start(bf16[64,2240]{1,0:T(8,128)(2,1)S(1)} %shard_map.98.refs_0_), channel_id=1, source_target_pairs={{0,4},{1,5},{2,6},{3,7},{4,0},{5,1},{6,2},{7,3},{8,12},{9,13},{10,... | collective-permute-start | bytes 860168 | tf_op jit(solution)/shard_map/ppermute | solution.py:331
  135.5 14.6 %collective-permute-start.19 = (bf16[64,2240]{1,0:T(8,128)(2,1)S(1)}, bf16[64,2240]{1,0:T(8,128)(2,1)S(1)}, u32[]{:S(2)}, u32[]{:S(2)}) collective-permute-start(bf16[64,2240]{1,0:T(8,128)(2,1)S(1)} %shard_map.98.refs_0_), channel_id=1, source_target_pairs={{0,6},{1,7},{2,0},{3,1},{4,2},{5,3},{6,4},{7,5},{8,14},{9,15},{10,... | collective-permute-start | bytes 860168 | tf_op jit(solution)/shard_map/ppermute | solution.py:331
  135.9 15.0 %collective-permute-start.16 = (bf16[64,2240]{1,0:T(8,128)(2,1)S(1)}, bf16[64,2240]{1,0:T(8,128)(2,1)S(1)}, u32[]{:S(2)}, u32[]{:S(2)}) collective-permute-start(bf16[64,2240]{1,0:T(8,128)(2,1)S(1)} %shard_map.98.refs_0_), channel_id=1, source_target_pairs={{0,1},{1,0},{2,3},{3,2},{4,5},{5,4},{6,7},{7,6},{8,9},{9,8},{10,11... | collective-permute-start | bytes 860168 | tf_op jit(solution)/shard_map/ppermute | solution.py:345
  165.9 16.8 %collective-permute-start.28 = (bf16[64,2240]{1,0:T(8,128)(2,1)S(1)}, bf16[64,2240]{1,0:T(8,128)(2,1)S(1)}, u32[]{:S(2)}, u32[]{:S(2)}) collective-permute-start(bf16[64,2240]{1,0:T(8,128)(2,1)S(1)} %get-tuple-element.48), channel_id=1, source_target_pairs={{0,2},{1,3},{2,4},{3,5},{4,6},{5,7},{6,0},{7,1},{8,10},{9,11},{10,... | collective-permute-start | bytes 860168 | tf_op jit(solution)/shard_map/ppermute | solution.py:370
  166.2 17.8 %collective-permute-start.29 = (bf16[64,2240]{1,0:T(8,128)(2,1)S(1)}, bf16[64,2240]{1,0:T(8,128)(2,1)S(1)}, u32[]{:S(2)}, u32[]{:S(2)}) collective-permute-start(bf16[64,2240]{1,0:T(8,128)(2,1)S(1)} %get-tuple-element.49), channel_id=1, source_target_pairs={{0,4},{1,5},{2,6},{3,7},{4,0},{5,1},{6,2},{7,3},{8,12},{9,13},{10,... | collective-permute-start | bytes 860168 | tf_op jit(solution)/shard_map/ppermute | solution.py:370
  169.8 14.4 %collective-permute-start.30 = (bf16[64,2240]{1,0:T(8,128)(2,1)S(1)}, bf16[64,2240]{1,0:T(8,128)(2,1)S(1)}, u32[]{:S(2)}, u32[]{:S(2)}) collective-permute-start(bf16[64,2240]{1,0:T(8,128)(2,1)S(1)} %get-tuple-element.50), channel_id=1, source_target_pairs={{0,6},{1,7},{2,0},{3,1},{4,2},{5,3},{6,4},{7,5},{8,14},{9,15},{10,... | collective-permute-start | bytes 860168 | tf_op jit(solution)/shard_map/ppermute | solution.py:370
  170.1 18.8 %collective-permute-start.25 = (bf16[64,2240]{1,0:T(8,128)(2,1)S(1)}, bf16[64,2240]{1,0:T(8,128)(2,1)S(1)}, u32[]{:S(2)}, u32[]{:S(2)}) collective-permute-start(bf16[64,2240]{1,0:T(8,128)(2,1)S(1)} %get-tuple-element.45), channel_id=1, source_target_pairs={{0,2},{1,3},{2,4},{3,5},{4,6},{5,7},{6,0},{7,1},{8,10},{9,11},{10,... | collective-permute-start | bytes 860168 | tf_op jit(solution)/shard_map/ppermute | solution.py:370
  172.2 23.6 %collective-permute-start.26 = (bf16[64,2240]{1,0:T(8,128)(2,1)S(1)}, bf16[64,2240]{1,0:T(8,128)(2,1)S(1)}, u32[]{:S(2)}, u32[]{:S(2)}) collective-permute-start(bf16[64,2240]{1,0:T(8,128)(2,1)S(1)} %get-tuple-element.46), channel_id=1, source_target_pairs={{0,4},{1,5},{2,6},{3,7},{4,0},{5,1},{6,2},{7,3},{8,12},{9,13},{10,... | collective-permute-start | bytes 860168 | tf_op jit(solution)/shard_map/ppermute | solution.py:370
  182.6 13.2 %collective-permute-start.27 = (bf16[64,2240]{1,0:T(8,128)(2,1)S(1)}, bf16[64,2240]{1,0:T(8,128)(2,1)S(1)}, u32[]{:S(2)}, u32[]{:S(2)}) collective-permute-start(bf16[64,2240]{1,0:T(8,128)(2,1)S(1)} %get-tuple-element.47), channel_id=1, source_target_pairs={{0,6},{1,7},{2,0},{3,1},{4,2},{5,3},{6,4},{7,5},{8,14},{9,15},{10,... | collective-permute-start | bytes 860168 | tf_op jit(solution)/shard_map/ppermute | solution.py:370
  (17 other events, 138.1 us)
Sparse Core Ops, SparseCore 0:
  9.2 73.5 all-gather.1

commit v9 on v7

--- a/solution.py
+++ b/solution.py
@@ -317,7 +317,7 @@
                 pltpu.VMEM(lead + (whole_rows + 2 * col_count, block), F32),
                 pltpu.VMEM(lead + (whole_rows, width), BF),
             ],
-            compiler_params=params(52),
+            compiler_params=params(24 if frames is None else 32),
         )(where_am_i, *pieces, w_flat, taps_s, needed)
 
     row_block = 256

time: 201 us -> 197 us (0.980)
  Pallas kernels: 34.8 us -> 31.8 us
    pallas_call x2, Pallas kernels: 19.9 us -> 16.7 us  [pieces_call(): pl.pallas_call(kernel, out_shape=[spatial_out] * outs, grid=(2 * chan //...]
    unnamed x40 -> x22, local copies, waits for them, and re-layouts: 11.3 us -> 9.81 us
  transfers between devices with their start and end apart: 26 -> 26, of which waited for: 12 -> 12; matrix products, arithmetic and copies ran while one was open for 3% -> 4% of each run, Pallas kernels for 13% -> 12%
where the time goes in v9:
time: 197 us
  waiting for transfers between devices  77.3 us (39%)
  blocking collectives  33.6 us (17%)
  Pallas kernels  31.8 us (16%)
  starting transfers between devices  30.4 us (15%)
  between operations  13.6 us (7%)
  local copies, waits for them, and re-layouts  9.81 us (5%)
    all_to_all x1, blocking collectives, on_device(): parts = lax.all_to_all(parts, everyone, 0, 0, tiled=True)  33.6 us
    ppermute x6, waiting for transfers between devices, along_of(): return [rows] + [lax.ppermute(rows, 'tile', ahead[k]) for k in (1, 2, 3)]  25.5 us
    ppermute x6, waiting for transfers between devices, sums(): lax.ppermute(part, 'tile', ahead[k + 1])  23.2 us
    pallas_call x2, Pallas kernels, pieces_call(): pl.pallas_call(kernel, out_shape=[spatial_out] * outs, grid=(2 * chan //...  16.7 us
    all_to_all x1, waiting for transfers between devices, on_device(): state = lax.all_to_all(sums, everyone, 0, 0, tiled=True)  12.9 us
    all_gather x1, waiting for transfers between devices, on_device(): w_out_whole = lax.all_gather(w_output, 'tile', axis=0, tiled=True)  12.6 us
    unnamed x22, local copies, waits for them, and re-layouts  9.81 us
    ppermute x6, starting transfers between devices, along_of(): return [rows] + [lax.ppermute(rows, 'tile', ahead[k]) for k in (1, 2, 3)]  8.7 us
  transfers between devices with their start and end apart: 26, of which 12 were waited for; matrix products, arithmetic and copies ran while one was open for 4% of the time, Pallas kernels for 12%

profile of v9, /device:TPU:2, one launch (start us, length us, event | category | flops | bytes accessed | tf_op | source)
XLA Modules:
  0.0 196.6 jit_solution(8322997669562365535)
XLA Ops:
  8.5 33.6 %all_to_all.10.in_ref = bf16[256,8,128]{2,1,0:T(8,128)(2,1)S(1)} all-to-all(bf16[256,8,128]{2,1,0:T(8,128)(2,1)S(1)} %shard_map.91), channel_id=1, replica_groups=mesh['blk'=32,'tile'=8] {'blk','tile'}, dimensions={0} | all-to-all | bytes 1048576 | tf_op jit(solution)/shard_map/all_to_all | solution.py:270
  43.2 7.1 %all-to-all-start.1 = ((bf16[256,8,128]{2,1,0:T(8,128)(2,1)}), bf16[256,8,128]{2,1,0:T(8,128)(2,1)S(1)}, u32[]{:S(2)}, u32[]{:S(2)}) async-start(bf16[256,8,128]{2,1,0:T(8,128)(2,1)} %shard_map.92), calls=%async_computation.1 | async-start | bytes 1048576 | tf_op jit(solution)/shard_map/all_to_all | solution.py:274
  50.4 6.1 %copy.10 = bf16[280,8,2,512]{3,1,2,0:T(8,128)(2,1)} copy(bf16[280,8,2,512]{3,2,1,0:T(2,128)(2,1)} %bitcast.31) | data formatting | bytes 9175040
  56.5 12.9 %all-to-all-done.1.state_ref = bf16[256,8,128]{2,1,0:T(8,128)(2,1)S(1)} async-done(((bf16[256,8,128]{2,1,0:T(8,128)(2,1)}), bf16[256,8,128]{2,1,0:T(8,128)(2,1)S(1)}, u32[]{:S(2)}, u32[]{:S(2)}) %all-to-all-start.1) | async-done | bytes 524320 | tf_op jit(solution)/shard_map/all_to_all | solution.py:274
  70.2 12.6 %all-gather.2.cloned.1.call-done.w_hbm = bf16[2240,2240]{1,0:T(8,128)(2,1)} async-done(((bf16[280,2240]{1,0:T(8,128)(2,1)}), bf16[2240,2240]{1,0:T(8,128)(2,1)}) %all-gather.2.cloned.1.call-update) | async-done | bytes 10035216 | tf_op jit(solution)/shard_map/all_gather | solution.py:255
  82.8 4.6 %shard_map.94 = (bf16[64,2240]{1,0:T(8,128)(2,1)S(1)}, bf16[64,2240]{1,0:T(8,128)(2,1)S(1)}) custom-call(bf16[128,2240]{1,0:T(8,128)(2,1)S(1)} %shard_map.93.att_ref, bf16[128,2240]{1,0:T(8,128)(2,1)S(1)} %bitcast.24, bf16[2240,2240]{1,0:T(8,128)(2,1)} %all-gather.2.cloned.1.call-done.w_hbm, bf16[2240,1024]{1,0:T(8,128)(2,1)} %bitcast.15), custom_call_target="tpu_custom_call" | custom-call | tf_op jit(solution)/shard_map/pallas_call | solution.py:286
  88.1 1.8 collective-permute-start.1
  89.8 2.0 %collective-permute-start.2 = (bf16[64,2240]{1,0:T(8,128)(2,1)S(1)}, bf16[64,2240]{1,0:T(8,128)(2,1)S(1)}, u32[]{:S(2)}, u32[]{:S(2)}) collective-permute-start(bf16[64,2240]{1,0:T(8,128)(2,1)S(1)} %get-tuple-element.21.refs_0_.hidden_ref), channel_id=1, source_target_pairs={{0,6},{1,7},{2,0},{3,1},{4,2},{5,3},{6,4},{7,5},{8,14},{9,15},{10,... | collective-permute-start | bytes 860168 | tf_op jit(solution)/shard_map/ppermute | solution.py:346
  91.9 3.0 %collective-permute-start.3 = (bf16[64,2240]{1,0:T(8,128)(2,1)S(1)}, bf16[64,2240]{1,0:T(8,128)(2,1)S(1)}, u32[]{:S(2)}, u32[]{:S(2)}) collective-permute-start(bf16[64,2240]{1,0:T(8,128)(2,1)S(1)} %get-tuple-element.22.refs_3_.hidden_ref), channel_id=1, source_target_pairs={{0,8},{8,16},{16,24},{24,32},{32,40},{40,48},{48,56},{56,64},{64,7... | collective-permute-start | bytes 860168 | tf_op jit(solution)/shard_map/ppermute | solution.py:349
  95.0 9.2 %collective-permute-done.refs_0_.refs_2_ = bf16[64,2240]{1,0:T(8,128)(2,1)S(1)} collective-permute-done((bf16[64,2240]{1,0:T(8,128)(2,1)S(1)}, bf16[64,2240]{1,0:T(8,128)(2,1)S(1)}, u32[]{:S(2)}, u32[]{:S(2)}) %collective-permute-start) | collective-permute-done | bytes 286752 | tf_op jit(solution)/shard_map/ppermute | solution.py:346
  105.8 2.7 %collective-permute-start.9 = (bf16[2,64,2240]{2,1,0:T(8,128)(2,1)S(1)}, bf16[2,64,2240]{2,1,0:T(8,128)(2,1)S(1)}, u32[]{:S(2)}, u32[]{:S(2)}) collective-permute-start(bf16[2,64,2240]{2,1,0:T(8,128)(2,1)S(1)} %shard_map.95.refs_0_), channel_id=1, source_target_pairs={{0,6},{1,7},{2,0},{3,1},{4,2},{5,3},{6,4},{7,5},{8,14},{9,15},{10,... | collective-permute-start | bytes 1720328 | tf_op jit(solution)/shard_map/ppermute | solution.py:346
  108.5 1.6 collective-permute-start.7
  110.2 2.3 %copy-done = bf16[280,8,2,512]{3,1,2,0:T(8,128)(2,1)S(1)} copy-done((bf16[280,8,2,512]{3,1,2,0:T(8,128)(2,1)S(1)}, bf16[280,8,2,512]{3,1,2,0:T(8,128)(2,1)}, u32[]{:S(2)}) %copy-start) | copy-done | bytes 4587544
  112.5 6.0 %shard_map.96.refs_10_.now_ref = bf16[512,1024]{1,0:T(8,128)(2,1)S(1)} custom-call(s32[2]{0:T(128)S(1)} %pad_add_fusion.place_ref, bf16[64,2240]{1,0:T(8,128)(2,1)S(1)} %get-tuple-element.21.refs_0_.hidden_ref, bf16[64,2240]{1,0:T(8,128)(2,1)S(1)} %collective-permute-done.11.refs_1_, bf16[64,2240]{1,0:T(8,128)(2,1)S(1)} %collective-permute-done.refs_0_.refs_2_, ...), custom_call_target="tpu_custom_call" | custom-call | tf_op jit(solution)/shard_map/pallas_call | solution.py:307
  118.5 3.1 %collective-permute-start.15 = (bf16[512,1024]{1,0:T(8,128)(2,1)S(1)}, bf16[512,1024]{1,0:T(8,128)(2,1)S(1)}, u32[]{:S(2)}, u32[]{:S(2)}) collective-permute-start(bf16[512,1024]{1,0:T(8,128)(2,1)S(1)} %shard_map.96.refs_10_.now_ref), channel_id=1, source_target_pairs={{0,8},{8,16},{16,24},{24,32},{32,40},{40,48},{48,56},{56,64},{64,7... | collective-permute-start | bytes 3145736 | tf_op jit(solution)/shard_map/ppermute | solution.py:362
  121.7 12.7 %collective-permute-done.9.refs_6_ = bf16[2,64,2240]{2,1,0:T(8,128)(2,1)S(1)} collective-permute-done((bf16[2,64,2240]{2,1,0:T(8,128)(2,1)S(1)}, bf16[2,64,2240]{2,1,0:T(8,128)(2,1)S(1)}, u32[]{:S(2)}, u32[]{:S(2)}) %collective-permute-start.9) | collective-permute-done | bytes 573472 | tf_op jit(solution)/shard_map/ppermute | solution.py:346
  134.4 3.4 %collective-permute-done.5.refs_2_ = bf16[2,64,2240]{2,1,0:T(8,128)(2,1)S(1)} collective-permute-done((bf16[2,64,2240]{2,1,0:T(8,128)(2,1)S(1)}, bf16[2,64,2240]{2,1,0:T(8,128)(2,1)S(1)}, u32[]{:S(2)}, u32[]{:S(2)}) %collective-permute-start.5) | collective-permute-done | bytes 573472 | tf_op jit(solution)/shard_map/ppermute | solution.py:346
  140.7 10.7 %shard_map.97 = (bf16[512,1024]{1,0:T(8,128)(2,1)S(1)}, bf16[512,1024]{1,0:T(8,128)(2,1)S(1)}) custom-call(s32[2]{0:T(128)S(1)} %pad_add_fusion.place_ref, bf16[2,64,2240]{2,1,0:T(8,128)(2,1)S(1)} %shard_map.95.refs_0_, bf16[2,64,2240]{2,1,0:T(8,128)(2,1)S(1)} %collective-permute-done.4.refs_1_, bf16[2,64,2240]{2,1,0:T(8,128)(2,1)S(1)} %collective-permute-done.5.refs_2_, ...), custom_call_target="tpu_custom_call" | custom-call | tf_op jit(solution)/shard_map/pallas_call | solution.py:307
  151.4 3.1 %shard_map.98 = (bf16[4,64,2240]{2,1,0:T(8,128)(2,1)S(1)}, bf16[4,64,2240]{2,1,0:T(8,128)(2,1)S(1)}) custom-call(s32[2]{0:T(128)S(1)} %pad_add_fusion.place_ref, bf16[512,1024]{1,0:T(8,128)(2,1)S(1)} %shard_map.96.refs_10_.now_ref, bf16[512,1024]{1,0:T(8,128)(2,1)S(1)} %get-tuple-element.23.one_ref.now_ref, ...), custom_call_target="tpu_custom_call" | custom-call | tf_op jit(solution)/shard_map/pallas_call | solution.py:369
  154.7 3.0 %shard_map.99 = (bf16[4,64,2240]{2,1,0:T(8,128)(2,1)S(1)}, bf16[4,64,2240]{2,1,0:T(8,128)(2,1)S(1)}) custom-call(s32[2]{0:T(128)S(1)} %pad_add_fusion.place_ref, bf16[512,1024]{1,0:T(8,128)(2,1)S(1)} %get-tuple-element.23.one_ref.now_ref, bf16[512,1024]{1,0:T(8,128)(2,1)S(1)} %collective-permute-done.15.two_ref.one_ref, ...), custom_call_target="tpu_custom_call" | custom-call | tf_op jit(solution)/shard_map/pallas_call | solution.py:369
  158.8 2.6 %collective-permute-start.22 = (bf16[64,2240]{1,0:T(8,128)(2,1)S(1)}, bf16[64,2240]{1,0:T(8,128)(2,1)S(1)}, u32[]{:S(2)}, u32[]{:S(2)}) collective-permute-start(bf16[64,2240]{1,0:T(8,128)(2,1)S(1)} %get-tuple-element.35), channel_id=1, source_target_pairs={{0,4},{1,5},{2,6},{3,7},{4,0},{5,1},{6,2},{7,3},{8,12},{9,13},{10,... | collective-permute-start | bytes 860168 | tf_op jit(solution)/shard_map/ppermute | solution.py:380
  163.8 1.7 collective-permute-start.19
  165.5 10.7 %collective-permute-done.21.refs_3_ = bf16[64,2240]{1,0:T(8,128)(2,1)S(1)} collective-permute-done((bf16[64,2240]{1,0:T(8,128)(2,1)S(1)}, bf16[64,2240]{1,0:T(8,128)(2,1)S(1)}, u32[]{:S(2)}, u32[]{:S(2)}) %collective-permute-start.21) | collective-permute-done | bytes 286752 | tf_op jit(solution)/shard_map/ppermute | solution.py:380
  177.1 10.9 %collective-permute-done.18.refs_0_ = bf16[64,2240]{1,0:T(8,128)(2,1)S(1)} collective-permute-done((bf16[64,2240]{1,0:T(8,128)(2,1)S(1)}, bf16[64,2240]{1,0:T(8,128)(2,1)S(1)}, u32[]{:S(2)}, u32[]{:S(2)}) %collective-permute-start.18) | collective-permute-done | bytes 286752 | tf_op jit(solution)/shard_map/ppermute | solution.py:380
  (66 shorter events, 15.5 us)
Async XLA Ops:
  6.5 76.3 %all-gather.2.cloned.1.call-start = ((), (), s32[]{:S(2)}) async-start(), calls=%async_computation.2 | async-start | bytes 11612160 | tf_op jit(solution)/shard_map/all_gather | solution.py:255
  43.2 26.2 %all-to-all-start.1 = ((bf16[256,8,128]{2,1,0:T(8,128)(2,1)}), bf16[256,8,128]{2,1,0:T(8,128)(2,1)S(1)}, u32[]{:S(2)}, u32[]{:S(2)}) async-start(bf16[256,8,128]{2,1,0:T(8,128)(2,1)} %shard_map.92), calls=%async_computation.1 | async-start | bytes 1048576 | tf_op jit(solution)/shard_map/all_to_all | solution.py:274
  87.4 16.8 %collective-permute-start = (bf16[64,2240]{1,0:T(8,128)(2,1)S(1)}, bf16[64,2240]{1,0:T(8,128)(2,1)S(1)}, u32[]{:S(2)}, u32[]{:S(2)}) collective-permute-start(bf16[64,2240]{1,0:T(8,128)(2,1)S(1)} %get-tuple-element.21.refs_0_.hidden_ref), channel_id=1, source_target_pairs={{0,2},{1,3},{2,4},{3,5},{4,6},{5,7},{6,0},{7,1},{8,10},{9,11},{10,... | collective-permute-start | bytes 860168 | tf_op jit(solution)/shard_map/ppermute | solution.py:346
  88.1 16.2 %collective-permute-start.1 = (bf16[64,2240]{1,0:T(8,128)(2,1)S(1)}, bf16[64,2240]{1,0:T(8,128)(2,1)S(1)}, u32[]{:S(2)}, u32[]{:S(2)}) collective-permute-start(bf16[64,2240]{1,0:T(8,128)(2,1)S(1)} %get-tuple-element.21.refs_0_.hidden_ref), channel_id=1, source_target_pairs={{0,4},{1,5},{2,6},{3,7},{4,0},{5,1},{6,2},{7,3},{8,12},{9,13},{10,... | collective-permute-start | bytes 860168 | tf_op jit(solution)/shard_map/ppermute | solution.py:346
  89.8 15.0 %collective-permute-start.2 = (bf16[64,2240]{1,0:T(8,128)(2,1)S(1)}, bf16[64,2240]{1,0:T(8,128)(2,1)S(1)}, u32[]{:S(2)}, u32[]{:S(2)}) collective-permute-start(bf16[64,2240]{1,0:T(8,128)(2,1)S(1)} %get-tuple-element.21.refs_0_.hidden_ref), channel_id=1, source_target_pairs={{0,6},{1,7},{2,0},{3,1},{4,2},{5,3},{6,4},{7,5},{8,14},{9,15},{10,... | collective-permute-start | bytes 860168 | tf_op jit(solution)/shard_map/ppermute | solution.py:346
  91.9 13.9 %collective-permute-start.3 = (bf16[64,2240]{1,0:T(8,128)(2,1)S(1)}, bf16[64,2240]{1,0:T(8,128)(2,1)S(1)}, u32[]{:S(2)}, u32[]{:S(2)}) collective-permute-start(bf16[64,2240]{1,0:T(8,128)(2,1)S(1)} %get-tuple-element.22.refs_3_.hidden_ref), channel_id=1, source_target_pairs={{0,8},{8,16},{16,24},{24,32},{32,40},{40,48},{48,56},{56,64},{64,7... | collective-permute-start | bytes 860168 | tf_op jit(solution)/shard_map/ppermute | solution.py:349
  94.9 13.6 %collective-permute-start.11 = (bf16[64,2240]{1,0:T(8,128)(2,1)S(1)}, bf16[64,2240]{1,0:T(8,128)(2,1)S(1)}, u32[]{:S(2)}, u32[]{:S(2)}) collective-permute-start(bf16[64,2240]{1,0:T(8,128)(2,1)S(1)} %get-tuple-element.21.refs_0_.hidden_ref), channel_id=1, source_target_pairs={{0,1},{1,0},{2,3},{3,2},{4,5},{5,4},{6,7},{7,6},{8,9},{9,8},{10,11... | collective-permute-start | bytes 860168 | tf_op jit(solution)/shard_map/ppermute | solution.py:360
  104.2 4.3 %collective-permute-start.12 = (bf16[64,2240]{1,0:T(8,128)(2,1)S(1)}, bf16[64,2240]{1,0:T(8,128)(2,1)S(1)}, u32[]{:S(2)}, u32[]{:S(2)}) collective-permute-start(bf16[64,2240]{1,0:T(8,128)(2,1)S(1)} %collective-permute-done.refs_0_.refs_2_), channel_id=1, source_target_pairs={{0,1},{1,0},{2,3},{3,2},{4,5},{5,4},{6,7},{7,6},{8,9},{9,8},{10,11... | collective-permute-start | bytes 860168 | tf_op jit(solution)/shard_map/ppermute | solution.py:360
  104.2 5.9 %collective-permute-start.13 = (bf16[64,2240]{1,0:T(8,128)(2,1)S(1)}, bf16[64,2240]{1,0:T(8,128)(2,1)S(1)}, u32[]{:S(2)}, u32[]{:S(2)}) collective-permute-start(bf16[64,2240]{1,0:T(8,128)(2,1)S(1)} %collective-permute-done.1.refs_1_.refs_4_), channel_id=1, source_target_pairs={{0,1},{1,0},{2,3},{3,2},{4,5},{5,4},{6,7},{7,6},{8,9},{9,8},{10,11... | collective-permute-start | bytes 860168 | tf_op jit(solution)/shard_map/ppermute | solution.py:360
  104.8 5.3 %collective-permute-start.14 = (bf16[64,2240]{1,0:T(8,128)(2,1)S(1)}, bf16[64,2240]{1,0:T(8,128)(2,1)S(1)}, u32[]{:S(2)}, u32[]{:S(2)}) collective-permute-start(bf16[64,2240]{1,0:T(8,128)(2,1)S(1)} %collective-permute-done.2.refs_2_.refs_6_), channel_id=1, source_target_pairs={{0,1},{1,0},{2,3},{3,2},{4,5},{5,4},{6,7},{7,6},{8,9},{9,8},{10,11... | collective-permute-start | bytes 860168 | tf_op jit(solution)/shard_map/ppermute | solution.py:360
  105.8 28.6 %collective-permute-start.9 = (bf16[2,64,2240]{2,1,0:T(8,128)(2,1)S(1)}, bf16[2,64,2240]{2,1,0:T(8,128)(2,1)S(1)}, u32[]{:S(2)}, u32[]{:S(2)}) collective-permute-start(bf16[2,64,2240]{2,1,0:T(8,128)(2,1)S(1)} %shard_map.95.refs_0_), channel_id=1, source_target_pairs={{0,6},{1,7},{2,0},{3,1},{4,2},{5,3},{6,4},{7,5},{8,14},{9,15},{10,... | collective-permute-start | bytes 1720328 | tf_op jit(solution)/shard_map/ppermute | solution.py:346
  108.5 29.3 %collective-permute-start.5 = (bf16[2,64,2240]{2,1,0:T(8,128)(2,1)S(1)}, bf16[2,64,2240]{2,1,0:T(8,128)(2,1)S(1)}, u32[]{:S(2)}, u32[]{:S(2)}) collective-permute-start(bf16[2,64,2240]{2,1,0:T(8,128)(2,1)S(1)} %shard_map.95.refs_0_), channel_id=1, source_target_pairs={{0,2},{1,3},{2,4},{3,5},{4,6},{5,7},{6,0},{7,1},{8,10},{9,11},{10,... | collective-permute-start | bytes 1720328 | tf_op jit(solution)/shard_map/ppermute | solution.py:346
  108.5 29.3 %collective-permute-start.7 = (bf16[2,64,2240]{2,1,0:T(8,128)(2,1)S(1)}, bf16[2,64,2240]{2,1,0:T(8,128)(2,1)S(1)}, u32[]{:S(2)}, u32[]{:S(2)}) collective-permute-start(bf16[2,64,2240]{2,1,0:T(8,128)(2,1)S(1)} %shard_map.95.refs_0_), channel_id=1, source_target_pairs={{0,4},{1,5},{2,6},{3,7},{4,0},{5,1},{6,2},{7,3},{8,12},{9,13},{10,... | collective-permute-start | bytes 1720328 | tf_op jit(solution)/shard_map/ppermute | solution.py:346
  118.5 32.9 %collective-permute-start.15 = (bf16[512,1024]{1,0:T(8,128)(2,1)S(1)}, bf16[512,1024]{1,0:T(8,128)(2,1)S(1)}, u32[]{:S(2)}, u32[]{:S(2)}) collective-permute-start(bf16[512,1024]{1,0:T(8,128)(2,1)S(1)} %shard_map.96.refs_10_.now_ref), channel_id=1, source_target_pairs={{0,8},{8,16},{16,24},{24,32},{32,40},{40,48},{48,56},{56,64},{64,7... | collective-permute-start | bytes 3145736 | tf_op jit(solution)/shard_map/ppermute | solution.py:362
  121.6 16.7 %collective-permute-start.4 = (bf16[2,64,2240]{2,1,0:T(8,128)(2,1)S(1)}, bf16[2,64,2240]{2,1,0:T(8,128)(2,1)S(1)}, u32[]{:S(2)}, u32[]{:S(2)}) collective-permute-start(bf16[2,64,2240]{2,1,0:T(8,128)(2,1)S(1)} %shard_map.95.refs_0_), channel_id=1, source_target_pairs={{0,1},{1,0},{2,3},{3,2},{4,5},{5,4},{6,7},{7,6},{8,9},{9,8},{10,11... | collective-permute-start | bytes 1720328 | tf_op jit(solution)/shard_map/ppermute | solution.py:365
  134.4 3.9 %collective-permute-start.10 = (bf16[2,64,2240]{2,1,0:T(8,128)(2,1)S(1)}, bf16[2,64,2240]{2,1,0:T(8,128)(2,1)S(1)}, u32[]{:S(2)}, u32[]{:S(2)}) collective-permute-start(bf16[2,64,2240]{2,1,0:T(8,128)(2,1)S(1)} %collective-permute-done.9.refs_6_), channel_id=1, source_target_pairs={{0,1},{1,0},{2,3},{3,2},{4,5},{5,4},{6,7},{7,6},{8,9},{9,8},{10,11... | collective-permute-start | bytes 1720328 | tf_op jit(solution)/shard_map/ppermute | solution.py:365
  154.5 3.9 %collective-permute-start.17 = (bf16[4,64,2240]{2,1,0:T(8,128)(2,1)S(1)}, bf16[4,64,2240]{2,1,0:T(8,128)(2,1)S(1)}, u32[]{:S(2)}, u32[]{:S(2)}) collective-permute-start(bf16[4,64,2240]{2,1,0:T(8,128)(2,1)S(1)} %get-tuple-element.29), channel_id=1, source_target_pairs={{0,1},{1,0},{2,3},{3,2},{4,5},{5,4},{6,7},{7,6},{8,9},{9,8},{10,11... | collective-permute-start | bytes 3440648 | tf_op jit(solution)/shard_map/ppermute | solution.py:370
  157.7 4.3 %collective-permute-start.16 = (bf16[4,64,2240]{2,1,0:T(8,128)(2,1)S(1)}, bf16[4,64,2240]{2,1,0:T(8,128)(2,1)S(1)}, u32[]{:S(2)}, u32[]{:S(2)}) collective-permute-start(bf16[4,64,2240]{2,1,0:T(8,128)(2,1)S(1)} %get-tuple-element.27), channel_id=1, source_target_pairs={{0,1},{1,0},{2,3},{3,2},{4,5},{5,4},{6,7},{7,6},{8,9},{9,8},{10,11... | collective-permute-start | bytes 3440648 | tf_op jit(solution)/shard_map/ppermute | solution.py:370
  158.7 17.5 %collective-permute-start.21 = (bf16[64,2240]{1,0:T(8,128)(2,1)S(1)}, bf16[64,2240]{1,0:T(8,128)(2,1)S(1)}, u32[]{:S(2)}, u32[]{:S(2)}) collective-permute-start(bf16[64,2240]{1,0:T(8,128)(2,1)S(1)} %get-tuple-element.34), channel_id=1, source_target_pairs={{0,2},{1,3},{2,4},{3,5},{4,6},{5,7},{6,0},{7,1},{8,10},{9,11},{10,... | collective-permute-start | bytes 860168 | tf_op jit(solution)/shard_map/ppermute | solution.py:380
  158.8 17.4 %collective-permute-start.22 = (bf16[64,2240]{1,0:T(8,128)(2,1)S(1)}, bf16[64,2240]{1,0:T(8,128)(2,1)S(1)}, u32[]{:S(2)}, u32[]{:S(2)}) collective-permute-start(bf16[64,2240]{1,0:T(8,128)(2,1)S(1)} %get-tuple-element.35), channel_id=1, source_target_pairs={{0,4},{1,5},{2,6},{3,7},{4,0},{5,1},{6,2},{7,3},{8,12},{9,13},{10,... | collective-permute-start | bytes 860168 | tf_op jit(solution)/shard_map/ppermute | solution.py:380
  161.4 15.7 %collective-permute-start.23 = (bf16[64,2240]{1,0:T(8,128)(2,1)S(1)}, bf16[64,2240]{1,0:T(8,128)(2,1)S(1)}, u32[]{:S(2)}, u32[]{:S(2)}) collective-permute-start(bf16[64,2240]{1,0:T(8,128)(2,1)S(1)} %get-tuple-element.36), channel_id=1, source_target_pairs={{0,6},{1,7},{2,0},{3,1},{4,2},{5,3},{6,4},{7,5},{8,14},{9,15},{10,... | collective-permute-start | bytes 860168 | tf_op jit(solution)/shard_map/ppermute | solution.py:380
  162.4 25.7 %collective-permute-start.18 = (bf16[64,2240]{1,0:T(8,128)(2,1)S(1)}, bf16[64,2240]{1,0:T(8,128)(2,1)S(1)}, u32[]{:S(2)}, u32[]{:S(2)}) collective-permute-start(bf16[64,2240]{1,0:T(8,128)(2,1)S(1)} %get-tuple-element.31), channel_id=1, source_target_pairs={{0,2},{1,3},{2,4},{3,5},{4,6},{5,7},{6,0},{7,1},{8,10},{9,11},{10,... | collective-permute-start | bytes 860168 | tf_op jit(solution)/shard_map/ppermute | solution.py:380
  163.8 24.2 %collective-permute-start.19 = (bf16[64,2240]{1,0:T(8,128)(2,1)S(1)}, bf16[64,2240]{1,0:T(8,128)(2,1)S(1)}, u32[]{:S(2)}, u32[]{:S(2)}) collective-permute-start(bf16[64,2240]{1,0:T(8,128)(2,1)S(1)} %get-tuple-element.32), channel_id=1, source_target_pairs={{0,4},{1,5},{2,6},{3,7},{4,0},{5,1},{6,2},{7,3},{8,12},{9,13},{10,... | collective-permute-start | bytes 860168 | tf_op jit(solution)/shard_map/ppermute | solution.py:380
  176.2 12.5 %collective-permute-start.20 = (bf16[64,2240]{1,0:T(8,128)(2,1)S(1)}, bf16[64,2240]{1,0:T(8,128)(2,1)S(1)}, u32[]{:S(2)}, u32[]{:S(2)}) collective-permute-start(bf16[64,2240]{1,0:T(8,128)(2,1)S(1)} %get-tuple-element.33), channel_id=1, source_target_pairs={{0,6},{1,7},{2,0},{3,1},{4,2},{5,3},{6,4},{7,5},{8,14},{9,15},{10,... | collective-permute-start | bytes 860168 | tf_op jit(solution)/shard_map/ppermute | solution.py:380
  (11 other events, 151.6 us)
Sparse Core Ops, SparseCore 0:
  9.2 73.5 all-gather.1

commit v10 on v9

--- a/solution.py
+++ b/solution.py
@@ -16,6 +16,8 @@
 SLABS = 18
 SUB = 14
 PIECES = 256
+HALF = 128
+TILE = ("y", "core")
 BF = jnp.bfloat16
 F32 = jnp.float32
 MIB = 1 << 20
@@ -30,7 +32,7 @@
     return first, pair, bound, start, stop, HEAD_DIM * first - start
 
 
-def kv_kernel(k_ref, v_ref, out_ref, last_ref):
+def kv_kernel(place_ref, k_ref, v_ref, mine_ref, other_ref, last_ref, out_ref):
     tokens = k_ref.shape[0]
     key_pos = jnp.maximum(k_ref[...], 0)
     last_ref[...] = jnp.ones((tokens, LANES), BF)
@@ -58,10 +60,17 @@
         out_ref[SUB * c : SUB * (c + 1)] = tile.reshape(SUB, 8, LANES).astype(BF)
     rest = PIECES - SUB * SLABS
     out_ref[SUB * SLABS :] = jnp.zeros((rest, 8, LANES), BF)
+    core = place_ref[1]
+    mine_ref[...] = out_ref[pl.ds(HALF * core, HALF)]
+    other_ref[...] = out_ref[pl.ds(HALF * (1 - core), HALF)]
+
+
+def add_kernel(one_ref, two_ref, out_ref):
+    out_ref[...] = (one_ref[...].astype(F32) + two_ref[...].astype(F32)).astype(BF)
 
 
 def prefix_kernel(in_ref, out_ref):
-    per_block = 16
+    per_block = 8
 
     def block(b, total):
         here = in_ref[pl.ds(b * per_block, per_block)].astype(F32)
@@ -71,10 +80,13 @@
         )
         return total
 
-    lax.fori_loop(0, PIECES // per_block, block, jnp.zeros((8, LANES), F32))
-
-
-def attend_kernel(q_ref, state_ref, att_ref):
+    lax.fori_loop(0, HALF // per_block, block, jnp.zeros((8, LANES), F32))
+
+
+def attend_kernel(place_ref, q_ref, mine_ref, other_ref, att_ref, state_ref):
+    core = place_ref[1]
+    state_ref[pl.ds(HALF * core, HALF)] = mine_ref[...]
+    state_ref[pl.ds(HALF * (1 - core), HALF)] = other_ref[...]
     query_pos = jnp.maximum(q_ref[...], 0)
     lane = lax.broadcasted_iota(jnp.int32, (HEAD_DIM, LANES), 1)
     tile_of = lambda c: state_ref[SUB * c : SUB * (c + 1)].astype(F32).reshape(HEAD_DIM, LANES)
@@ -248,40 +260,46 @@
     tokens = row_count * frames * col_count
     flat = lambda a: a.reshape(tokens, width)
     chan = w_inner.shape[2]
-    peers = lax.axis_size("tile")
-    place = lax.axis_index("tile")
+    peers = lax.axis_size(TILE)
+    place = lax.axis_index(TILE)
     where_am_i = jnp.stack([place // 2, place % 2]).astype(jnp.int32)
 
-    w_out_whole = lax.all_gather(w_output, "tile", axis=0, tiled=True)
+    w_out_whole = lax.all_gather(w_output, TILE, axis=0, tiled=True)
     w_flat = w_inner.reshape(width, 2 * chan)
     taps_s = spatial_taps.reshape(9, 2 * chan)
     taps_t = temporal_taps.reshape(TAPS, 2 * chan)
 
-    pieces = jax.ShapeDtypeStruct((PIECES, 8, LANES), BF)
+    half = jax.ShapeDtypeStruct((HALF, 8, LANES), BF)
+    scalars = pl.BlockSpec(memory_space=pltpu.SMEM)
+    other_core = [(i, i ^ 1) for i in range(peers)]
+    mine, other = pl.pallas_call(
+        kv_kernel,
+        out_shape=[half] * 2,
+        in_specs=[scalars, VMEM, VMEM],
+        out_specs=[VMEM] * 2,
+        scratch_shapes=[pltpu.VMEM((tokens, LANES), BF), pltpu.VMEM((PIECES, 8, LANES), BF)],
+        compiler_params=params(40),
+    )(where_am_i, flat(key_rows), flat(value_rows))
     parts = pl.pallas_call(
-        kv_kernel,
-        out_shape=pieces,
-        in_specs=[VMEM] * 2,
-        out_specs=VMEM,
-        scratch_shapes=[pltpu.VMEM((tokens, LANES), BF)],
-        compiler_params=params(40),
-    )(flat(key_rows), flat(value_rows))
-    everyone = ("blk", "tile")
-    parts = lax.all_to_all(parts, everyone, 0, 0, tiled=True)
+        add_kernel, out_shape=half, in_specs=[VMEM] * 2, out_specs=VMEM, compiler_params=params(20)
+    )(mine, lax.ppermute(other, TILE, other_core))
+    same_core = ("blk", "y")
+    parts = lax.all_to_all(parts, same_core, 0, 0, tiled=True)
     sums = pl.pallas_call(
-        prefix_kernel, out_shape=pieces, in_specs=[VMEM], out_specs=VMEM, compiler_params=params(40)
+        prefix_kernel, out_shape=half, in_specs=[VMEM], out_specs=VMEM, compiler_params=params(40)
     )(parts)
-    state = lax.all_to_all(sums, everyone, 0, 0, tiled=True)
+    state = lax.all_to_all(sums, same_core, 0, 0, tiled=True)
 
     anywhere = pl.BlockSpec(memory_space=pl.ANY)
     frame_rows = row_count * col_count
     attended = pl.pallas_call(
         attend_kernel,
         out_shape=jax.ShapeDtypeStruct((tokens, width), BF),
-        in_specs=[VMEM, VMEM],
+        in_specs=[scalars, VMEM, VMEM, VMEM],
         out_specs=VMEM,
+        scratch_shapes=[pltpu.VMEM((PIECES, 8, LANES), BF)],
         compiler_params=params(40),
-    )(flat(queries), state)
+    )(where_am_i, flat(queries), state, lax.ppermute(state, TILE, other_core))
     one_frame = jax.ShapeDtypeStruct((frame_rows, width), BF)
     early, late = pl.pallas_call(
         hidden_kernel,
@@ -343,7 +361,7 @@
     ahead = [[(i, (i + 2 * k) % peers) for i in range(peers)] for k in range(4)]
 
     def along_of(rows):
-        return [rows] + [lax.ppermute(rows, "tile", ahead[k]) for k in (1, 2, 3)]
+        return [rows] + [lax.ppermute(rows, TILE, ahead[k]) for k in (1, 2, 3)]
 
     late_along = along_of(late)
     before_early = lax.ppermute(early, "blk", next_frames)
@@ -357,17 +375,17 @@
     others_along = along_of(others)
     pieces = []
     for part in late_along:
-        pieces += [part, lax.ppermute(part, "tile", other_core)]
+        pieces += [part, lax.ppermute(part, TILE, other_core)]
     (late_sp,) = pieces_call(pieces_kernel, None, pieces, taps_t)
     before_late_sp = lax.ppermute(late_sp, "blk", next_frames)
     both = []
     for part in others_along:
-        both += [part, lax.ppermute(part, "tile", other_core)]
+        both += [part, lax.ppermute(part, TILE, other_core)]
     early_sp, before_early_sp = pieces_call(both_kernel, 2, both, late_sp)
 
     def core_shares(now, one, two, needed):
         mine, other = point_call(where_am_i, now, one, two, taps_t, w_point, needed)
-        return mine, lax.ppermute(other, "tile", other_core)
+        return mine, lax.ppermute(other, TILE, other_core)
 
     def sums(mine, from_core, rows):
         kept, *sends = pl.pallas_call(
@@ -377,7 +395,7 @@
             out_specs=[VMEM] * 4,
             compiler_params=params(20),
         )(mine, from_core, rows)
-        return kept, [lax.ppermute(part, "tile", ahead[k + 1]) for k, part in enumerate(sends)]
+        return kept, [lax.ppermute(part, TILE, ahead[k + 1]) for k, part in enumerate(sends)]
 
     late_shares = core_shares(late_sp, early_sp, before_late_sp, before_early_sp)
     late_kept, late_back = sums(*late_shares, late)
@@ -394,17 +412,19 @@
 
 def solution(mesh):
     in_specs = (
-        P("tile", "blk", None, None),
-        P("tile", "blk", None, None),
-        P("tile", "blk", None, None),
-        P("tile", "blk", None, None),
-        P("tile", None),
-        P(None, None, "tile"),
-        P("tile", None),
-        P(None, None, None, "tile"),
-        P(None, None, "tile"),
+        P(TILE, "blk", None, None),
+        P(TILE, "blk", None, None),
+        P(TILE, "blk", None, None),
+        P(TILE, "blk", None, None),
+        P(TILE, None),
+        P(None, None, TILE),
+        P(TILE, None),
+        P(None, None, None, TILE),
+        P(None, None, TILE),
     )
-    out_specs = P("tile", "blk", None, None)
+    out_specs = P(TILE, "blk", None, None)
+    sizes = mesh.devices.shape
+    mesh = jax.sharding.Mesh(mesh.devices.reshape(sizes[0], sizes[1] // 2, 2), ("blk", "y", "core"))
     return jax.shard_map(
         on_device, mesh=mesh, in_specs=in_specs, out_specs=out_specs, check_vma=False
     )

time: 197 us -> 190 us (0.964)
  blocking collectives: 33.6 us -> 48.9 us
  waiting for transfers between devices: 77.3 us -> 63 us
  starting transfers between devices: 30.4 us -> 24.8 us
  local copies, waits for them, and re-layouts: 9.81 us -> 6.55 us
    all_to_all x1 -> x2, blocking collectives: 33.6 us -> 48.9 us  [the longest x1 29.1 us: on_device(): parts = lax.all_to_all(parts, same_core, 0, 0, tiled=True)]
    all_to_all x1 -> x0, waiting for transfers between devices: 12.9 us -> none  [on_device(): state = lax.all_to_all(sums, everyone, 0, 0, tiled=True)]
    all_to_all x1 -> x0, starting transfers between devices: 7.13 us -> none  [on_device(): state = lax.all_to_all(sums, everyone, 0, 0, tiled=True)]
    unnamed x22, local copies, waits for them, and re-layouts: 9.81 us -> 6.55 us
    ppermute x22 -> x24, starting transfers between devices: 17.2 us -> 18.1 us  [the longest x6 8.53 us: along_of(): return [rows] + [lax.ppermute(rows, TILE, ahead[k]) for k in (1, 2, 3)]]
    ppermute x22 -> x24, waiting for transfers between devices: 51 us -> 51.4 us  [the longest x6 25.2 us: along_of(): return [rows] + [lax.ppermute(rows, TILE, ahead[k]) for k in (1, 2, 3)]]
  transfers between devices with their start and end apart: 26 -> 27, of which waited for: 12 -> 12; matrix products, arithmetic and copies ran while one was open for 4% -> 3% of each run, Pallas kernels for 12% -> 12%
where the time goes in v10:
time: 190 us; the launch traced here: 189 us
  waiting for transfers between devices  63 us (33%)
  blocking collectives  48.9 us (26%)
  Pallas kernels  32.2 us (17%)
  starting transfers between devices  24.8 us (13%)
  between operations  13.7 us (7%)
  local copies, waits for them, and re-layouts  6.55 us (3%)
    all_to_all x1, blocking collectives, on_device(): parts = lax.all_to_all(parts, same_core, 0, 0, tiled=True)  29.1 us
    ppermute x6, waiting for transfers between devices, along_of(): return [rows] + [lax.ppermute(rows, TILE, ahead[k]) for k in (1, 2, 3)]  25.2 us
    ppermute x6, waiting for transfers between devices, sums(): lax.ppermute(part, TILE, ahead[k + 1])  22.3 us
    all_to_all x1, blocking collectives, on_device(): state = lax.all_to_all(sums, same_core, 0, 0, tiled=True)  19.8 us
    pallas_call x2, Pallas kernels, pieces_call(): pl.pallas_call(kernel, out_shape=[spatial_out] * outs, grid=(2 * chan //...  16.7 us
    all_gather x1, waiting for transfers between devices, on_device(): w_out_whole = lax.all_gather(w_output, TILE, axis=0, tiled=True)  10.8 us
    ppermute x6, starting transfers between devices, along_of(): return [rows] + [lax.ppermute(rows, TILE, ahead[k]) for k in (1, 2, 3)]  8.53 us
    ppermute x6, starting transfers between devices, sums(): lax.ppermute(part, TILE, ahead[k + 1])  7.57 us
  transfers between devices with their start and end apart: 27, of which 12 were waited for; matrix products, arithmetic and copies ran while one was open for 3% of the time, Pallas kernels for 12%

profile of v10, /device:TPU:2, one launch (start us, length us, event | category | flops | bytes accessed | tf_op | source)
XLA Modules:
  0.0 189.2 jit_solution(11894188052078964055)
XLA Ops:
  10.8 29.1 %all_to_all.10.in_ref = bf16[128,8,128]{2,1,0:T(8,128)(2,1)S(1)} all-to-all(bf16[128,8,128]{2,1,0:T(8,128)(2,1)S(1)} %shard_map.92), channel_id=1, replica_groups=mesh['blk'=32,'y'=4,'core'=2] {'blk','y'}, dimensions={0} | all-to-all | bytes 524288 | tf_op jit(solution)/shard_map/all_to_all | solution.py:287
  40.1 19.8 %all_to_all.11.mine_ref = bf16[128,8,128]{2,1,0:T(8,128)(2,1)S(1)} all-to-all(bf16[128,8,128]{2,1,0:T(8,128)(2,1)S(1)} %shard_map.93), channel_id=1, replica_groups=mesh['blk'=32,'y'=4,'core'=2] {'blk','y'}, dimensions={0} | all-to-all | bytes 524288 | tf_op jit(solution)/shard_map/all_to_all | solution.py:291
  59.9 6.1 %copy.10 = bf16[280,8,2,512]{3,1,2,0:T(8,128)(2,1)} copy(bf16[280,8,2,512]{3,2,1,0:T(2,128)(2,1)} %bitcast.31) | data formatting | bytes 9175040
  67.3 10.8 %all-gather.2.cloned.1.call-done.w_hbm = bf16[2240,2240]{1,0:T(8,128)(2,1)} async-done(((bf16[280,2240]{1,0:T(8,128)(2,1)}), bf16[2240,2240]{1,0:T(8,128)(2,1)}) %all-gather.2.cloned.1.call-update) | async-done | bytes 10035216 | tf_op jit(solution)/shard_map/all_gather | solution.py:267
  78.2 4.8 %shard_map.95 = (bf16[64,2240]{1,0:T(8,128)(2,1)S(1)}, bf16[64,2240]{1,0:T(8,128)(2,1)S(1)}) custom-call(bf16[128,2240]{1,0:T(8,128)(2,1)S(1)} %shard_map.94.att_ref, bf16[128,2240]{1,0:T(8,128)(2,1)S(1)} %bitcast.24, bf16[2240,2240]{1,0:T(8,128)(2,1)} %all-gather.2.cloned.1.call-done.w_hbm, bf16[2240,1024]{1,0:T(8,128)(2,1)} %bitcast.15), custom_call_target="tpu_custom_call" | custom-call | tf_op jit(solution)/shard_map/pallas_call | solution.py:304
  83.7 1.8 collective-permute-start.3
  85.5 2.0 %collective-permute-start.4 = (bf16[64,2240]{1,0:T(8,128)(2,1)S(1)}, bf16[64,2240]{1,0:T(8,128)(2,1)S(1)}, u32[]{:S(2)}, u32[]{:S(2)}) collective-permute-start(bf16[64,2240]{1,0:T(8,128)(2,1)S(1)} %get-tuple-element.25.refs_0_.hidden_ref), channel_id=1, source_target_pairs={{0,6},{1,7},{2,0},{3,1},{4,2},{5,3},{6,4},{7,5},{8,14},{9,15},{10,... | collective-permute-start | bytes 860168 | tf_op jit(solution)/shard_map/ppermute | solution.py:364
  87.5 3.3 %collective-permute-start.5 = (bf16[64,2240]{1,0:T(8,128)(2,1)S(1)}, bf16[64,2240]{1,0:T(8,128)(2,1)S(1)}, u32[]{:S(2)}, u32[]{:S(2)}) collective-permute-start(bf16[64,2240]{1,0:T(8,128)(2,1)S(1)} %get-tuple-element.26.refs_3_.hidden_ref), channel_id=1, source_target_pairs={{0,8},{8,16},{16,24},{24,32},{32,40},{40,48},{48,56},{56,64},{64,7... | collective-permute-start | bytes 860168 | tf_op jit(solution)/shard_map/ppermute | solution.py:367
  91.0 8.8 %collective-permute-done.2.refs_0_.refs_2_ = bf16[64,2240]{1,0:T(8,128)(2,1)S(1)} collective-permute-done((bf16[64,2240]{1,0:T(8,128)(2,1)S(1)}, bf16[64,2240]{1,0:T(8,128)(2,1)S(1)}, u32[]{:S(2)}, u32[]{:S(2)}) %collective-permute-start.2) | collective-permute-done | bytes 286752 | tf_op jit(solution)/shard_map/ppermute | solution.py:364
  100.4 1.9 %collective-permute-start.9 = (bf16[2,64,2240]{2,1,0:T(8,128)(2,1)S(1)}, bf16[2,64,2240]{2,1,0:T(8,128)(2,1)S(1)}, u32[]{:S(2)}, u32[]{:S(2)}) collective-permute-start(bf16[2,64,2240]{2,1,0:T(8,128)(2,1)S(1)} %shard_map.96.refs_0_), channel_id=1, source_target_pairs={{0,4},{1,5},{2,6},{3,7},{4,0},{5,1},{6,2},{7,3},{8,12},{9,13},{10,... | collective-permute-start | bytes 1720328 | tf_op jit(solution)/shard_map/ppermute | solution.py:364
  102.3 2.0 %collective-permute-start.11 = (bf16[2,64,2240]{2,1,0:T(8,128)(2,1)S(1)}, bf16[2,64,2240]{2,1,0:T(8,128)(2,1)S(1)}, u32[]{:S(2)}, u32[]{:S(2)}) collective-permute-start(bf16[2,64,2240]{2,1,0:T(8,128)(2,1)S(1)} %shard_map.96.refs_0_), channel_id=1, source_target_pairs={{0,6},{1,7},{2,0},{3,1},{4,2},{5,3},{6,4},{7,5},{8,14},{9,15},{10,... | collective-permute-start | bytes 1720328 | tf_op jit(solution)/shard_map/ppermute | solution.py:364
  104.5 6.0 %shard_map.97.refs_10_.now_ref = bf16[512,1024]{1,0:T(8,128)(2,1)S(1)} custom-call(s32[2]{0:T(128)S(1)} %pad_add_fusion.place_ref, bf16[64,2240]{1,0:T(8,128)(2,1)S(1)} %get-tuple-element.25.refs_0_.hidden_ref, bf16[64,2240]{1,0:T(8,128)(2,1)S(1)} %collective-permute-done.13.refs_1_, bf16[64,2240]{1,0:T(8,128)(2,1)S(1)} %collective-permute-done.2.refs_0_.refs_2_, ...), custom_call_target="tpu_custom_call" | custom-call | tf_op jit(solution)/shard_map/pallas_call | solution.py:325
  110.6 3.4 %collective-permute-start.17 = (bf16[512,1024]{1,0:T(8,128)(2,1)S(1)}, bf16[512,1024]{1,0:T(8,128)(2,1)S(1)}, u32[]{:S(2)}, u32[]{:S(2)}) collective-permute-start(bf16[512,1024]{1,0:T(8,128)(2,1)S(1)} %shard_map.97.refs_10_.now_ref), channel_id=1, source_target_pairs={{0,8},{8,16},{16,24},{24,32},{32,40},{40,48},{48,56},{56,64},{64,7... | collective-permute-start | bytes 3145736 | tf_op jit(solution)/shard_map/ppermute | solution.py:380
  114.0 4.1 %collective-permute-done.9.refs_4_ = bf16[2,64,2240]{2,1,0:T(8,128)(2,1)S(1)} collective-permute-done((bf16[2,64,2240]{2,1,0:T(8,128)(2,1)S(1)}, bf16[2,64,2240]{2,1,0:T(8,128)(2,1)S(1)}, u32[]{:S(2)}, u32[]{:S(2)}) %collective-permute-start.9) | collective-permute-done | bytes 573472 | tf_op jit(solution)/shard_map/ppermute | solution.py:364
  118.2 12.2 %collective-permute-done.11.refs_6_ = bf16[2,64,2240]{2,1,0:T(8,128)(2,1)S(1)} collective-permute-done((bf16[2,64,2240]{2,1,0:T(8,128)(2,1)S(1)}, bf16[2,64,2240]{2,1,0:T(8,128)(2,1)S(1)}, u32[]{:S(2)}, u32[]{:S(2)}) %collective-permute-start.11) | collective-permute-done | bytes 573472 | tf_op jit(solution)/shard_map/ppermute | solution.py:364
  133.2 10.7 %shard_map.98 = (bf16[512,1024]{1,0:T(8,128)(2,1)S(1)}, bf16[512,1024]{1,0:T(8,128)(2,1)S(1)}) custom-call(s32[2]{0:T(128)S(1)} %pad_add_fusion.place_ref, bf16[2,64,2240]{2,1,0:T(8,128)(2,1)S(1)} %shard_map.96.refs_0_, bf16[2,64,2240]{2,1,0:T(8,128)(2,1)S(1)} %collective-permute-done.6.refs_1_, bf16[2,64,2240]{2,1,0:T(8,128)(2,1)S(1)} %collective-permute-done.7.refs_2_, ...), custom_call_target="tpu_custom_call" | custom-call | tf_op jit(solution)/shard_map/pallas_call | solution.py:325
  144.0 3.0 %shard_map.99 = (bf16[4,64,2240]{2,1,0:T(8,128)(2,1)S(1)}, bf16[4,64,2240]{2,1,0:T(8,128)(2,1)S(1)}) custom-call(s32[2]{0:T(128)S(1)} %pad_add_fusion.place_ref, bf16[512,1024]{1,0:T(8,128)(2,1)S(1)} %shard_map.97.refs_10_.now_ref, bf16[512,1024]{1,0:T(8,128)(2,1)S(1)} %get-tuple-element.27.one_ref.now_ref, ...), custom_call_target="tpu_custom_call" | custom-call | tf_op jit(solution)/shard_map/pallas_call | solution.py:387
  147.2 3.0 %shard_map.100 = (bf16[4,64,2240]{2,1,0:T(8,128)(2,1)S(1)}, bf16[4,64,2240]{2,1,0:T(8,128)(2,1)S(1)}) custom-call(s32[2]{0:T(128)S(1)} %pad_add_fusion.place_ref, bf16[512,1024]{1,0:T(8,128)(2,1)S(1)} %get-tuple-element.27.one_ref.now_ref, bf16[512,1024]{1,0:T(8,128)(2,1)S(1)} %collective-permute-done.17.two_ref.one_ref, ...), custom_call_target="tpu_custom_call" | custom-call | tf_op jit(solution)/shard_map/pallas_call | solution.py:387
  152.3 2.9 %collective-permute-start.24 = (bf16[64,2240]{1,0:T(8,128)(2,1)S(1)}, bf16[64,2240]{1,0:T(8,128)(2,1)S(1)}, u32[]{:S(2)}, u32[]{:S(2)}) collective-permute-start(bf16[64,2240]{1,0:T(8,128)(2,1)S(1)} %get-tuple-element.39), channel_id=1, source_target_pairs={{0,4},{1,5},{2,6},{3,7},{4,0},{5,1},{6,2},{7,3},{8,12},{9,13},{10,... | collective-permute-start | bytes 860168 | tf_op jit(solution)/shard_map/ppermute | solution.py:398
  155.9 1.7 collective-permute-start.20
  158.2 4.7 %collective-permute-done.23.refs_3_ = bf16[64,2240]{1,0:T(8,128)(2,1)S(1)} collective-permute-done((bf16[64,2240]{1,0:T(8,128)(2,1)S(1)}, bf16[64,2240]{1,0:T(8,128)(2,1)S(1)}, u32[]{:S(2)}, u32[]{:S(2)}) %collective-permute-start.23) | collective-permute-done | bytes 286752 | tf_op jit(solution)/shard_map/ppermute | solution.py:398
  163.6 5.8 %collective-permute-done.24.refs_4_ = bf16[64,2240]{1,0:T(8,128)(2,1)S(1)} collective-permute-done((bf16[64,2240]{1,0:T(8,128)(2,1)S(1)}, bf16[64,2240]{1,0:T(8,128)(2,1)S(1)}, u32[]{:S(2)}, u32[]{:S(2)}) %collective-permute-start.24) | collective-permute-done | bytes 286752 | tf_op jit(solution)/shard_map/ppermute | solution.py:398
  169.4 4.6 %collective-permute-done.20.refs_0_ = bf16[64,2240]{1,0:T(8,128)(2,1)S(1)} collective-permute-done((bf16[64,2240]{1,0:T(8,128)(2,1)S(1)}, bf16[64,2240]{1,0:T(8,128)(2,1)S(1)}, u32[]{:S(2)}, u32[]{:S(2)}) %collective-permute-start.20) | collective-permute-done | bytes 286752 | tf_op jit(solution)/shard_map/ppermute | solution.py:398
  174.0 7.2 %collective-permute-done.21.refs_1_ = bf16[64,2240]{1,0:T(8,128)(2,1)S(1)} collective-permute-done((bf16[64,2240]{1,0:T(8,128)(2,1)S(1)}, bf16[64,2240]{1,0:T(8,128)(2,1)S(1)}, u32[]{:S(2)}, u32[]{:S(2)}) %collective-permute-start.21) | collective-permute-done | bytes 286752 | tf_op jit(solution)/shard_map/ppermute | solution.py:398
  (70 shorter events, 15.7 us)
Async XLA Ops:
  6.5 71.6 %all-gather.2.cloned.1.call-start = ((), (), s32[]{:S(2)}) async-start(), calls=%async_computation.2 | async-start | bytes 11612160 | tf_op jit(solution)/shard_map/all_gather | solution.py:267
  59.9 6.1 %collective-permute-start.1 = (bf16[128,8,128]{2,1,0:T(8,128)(2,1)S(1)}, bf16[128,8,128]{2,1,0:T(8,128)(2,1)S(1)}, u32[]{:S(2)}, u32[]{:S(2)}) collective-permute-start(bf16[128,8,128]{2,1,0:T(8,128)(2,1)S(1)} %all_to_all.11.mine_ref), channel_id=1, source_target_pairs={{0,1},{1,0},{2,3},{3,2},{4,5},{5,4},{6,7},{7,6},{8,9},{9,8},{10,11... | collective-permute-start | bytes 786440 | tf_op jit(solution)/shard_map/ppermute | solution.py:302
  83.0 16.8 %collective-permute-start.2 = (bf16[64,2240]{1,0:T(8,128)(2,1)S(1)}, bf16[64,2240]{1,0:T(8,128)(2,1)S(1)}, u32[]{:S(2)}, u32[]{:S(2)}) collective-permute-start(bf16[64,2240]{1,0:T(8,128)(2,1)S(1)} %get-tuple-element.25.refs_0_.hidden_ref), channel_id=1, source_target_pairs={{0,2},{1,3},{2,4},{3,5},{4,6},{5,7},{6,0},{7,1},{8,10},{9,11},{10,... | collective-permute-start | bytes 860168 | tf_op jit(solution)/shard_map/ppermute | solution.py:364
  83.7 16.0 %collective-permute-start.3 = (bf16[64,2240]{1,0:T(8,128)(2,1)S(1)}, bf16[64,2240]{1,0:T(8,128)(2,1)S(1)}, u32[]{:S(2)}, u32[]{:S(2)}) collective-permute-start(bf16[64,2240]{1,0:T(8,128)(2,1)S(1)} %get-tuple-element.25.refs_0_.hidden_ref), channel_id=1, source_target_pairs={{0,4},{1,5},{2,6},{3,7},{4,0},{5,1},{6,2},{7,3},{8,12},{9,13},{10,... | collective-permute-start | bytes 860168 | tf_op jit(solution)/shard_map/ppermute | solution.py:364
  85.5 14.9 %collective-permute-start.4 = (bf16[64,2240]{1,0:T(8,128)(2,1)S(1)}, bf16[64,2240]{1,0:T(8,128)(2,1)S(1)}, u32[]{:S(2)}, u32[]{:S(2)}) collective-permute-start(bf16[64,2240]{1,0:T(8,128)(2,1)S(1)} %get-tuple-element.25.refs_0_.hidden_ref), channel_id=1, source_target_pairs={{0,6},{1,7},{2,0},{3,1},{4,2},{5,3},{6,4},{7,5},{8,14},{9,15},{10,... | collective-permute-start | bytes 860168 | tf_op jit(solution)/shard_map/ppermute | solution.py:364
  87.5 12.8 %collective-permute-start.5 = (bf16[64,2240]{1,0:T(8,128)(2,1)S(1)}, bf16[64,2240]{1,0:T(8,128)(2,1)S(1)}, u32[]{:S(2)}, u32[]{:S(2)}) collective-permute-start(bf16[64,2240]{1,0:T(8,128)(2,1)S(1)} %get-tuple-element.26.refs_3_.hidden_ref), channel_id=1, source_target_pairs={{0,8},{8,16},{16,24},{24,32},{32,40},{40,48},{48,56},{56,64},{64,7... | collective-permute-start | bytes 860168 | tf_op jit(solution)/shard_map/ppermute | solution.py:367
  90.9 11.5 %collective-permute-start.13 = (bf16[64,2240]{1,0:T(8,128)(2,1)S(1)}, bf16[64,2240]{1,0:T(8,128)(2,1)S(1)}, u32[]{:S(2)}, u32[]{:S(2)}) collective-permute-start(bf16[64,2240]{1,0:T(8,128)(2,1)S(1)} %get-tuple-element.25.refs_0_.hidden_ref), channel_id=1, source_target_pairs={{0,1},{1,0},{2,3},{3,2},{4,5},{5,4},{6,7},{7,6},{8,9},{9,8},{10,11... | collective-permute-start | bytes 860168 | tf_op jit(solution)/shard_map/ppermute | solution.py:378
  99.7 4.6 %collective-permute-start.14 = (bf16[64,2240]{1,0:T(8,128)(2,1)S(1)}, bf16[64,2240]{1,0:T(8,128)(2,1)S(1)}, u32[]{:S(2)}, u32[]{:S(2)}) collective-permute-start(bf16[64,2240]{1,0:T(8,128)(2,1)S(1)} %collective-permute-done.2.refs_0_.refs_2_), channel_id=1, source_target_pairs={{0,1},{1,0},{2,3},{3,2},{4,5},{5,4},{6,7},{7,6},{8,9},{9,8},{10,11... | collective-permute-start | bytes 860168 | tf_op jit(solution)/shard_map/ppermute | solution.py:378
  99.7 4.7 %collective-permute-start.15 = (bf16[64,2240]{1,0:T(8,128)(2,1)S(1)}, bf16[64,2240]{1,0:T(8,128)(2,1)S(1)}, u32[]{:S(2)}, u32[]{:S(2)}) collective-permute-start(bf16[64,2240]{1,0:T(8,128)(2,1)S(1)} %collective-permute-done.3.refs_1_.refs_4_), channel_id=1, source_target_pairs={{0,1},{1,0},{2,3},{3,2},{4,5},{5,4},{6,7},{7,6},{8,9},{9,8},{10,11... | collective-permute-start | bytes 860168 | tf_op jit(solution)/shard_map/ppermute | solution.py:378
  100.4 4.1 %collective-permute-start.16 = (bf16[64,2240]{1,0:T(8,128)(2,1)S(1)}, bf16[64,2240]{1,0:T(8,128)(2,1)S(1)}, u32[]{:S(2)}, u32[]{:S(2)}) collective-permute-start(bf16[64,2240]{1,0:T(8,128)(2,1)S(1)} %collective-permute-done.4.refs_2_.refs_6_), channel_id=1, source_target_pairs={{0,1},{1,0},{2,3},{3,2},{4,5},{5,4},{6,7},{7,6},{8,9},{9,8},{10,11... | collective-permute-start | bytes 860168 | tf_op jit(solution)/shard_map/ppermute | solution.py:378
  100.4 17.8 %collective-permute-start.9 = (bf16[2,64,2240]{2,1,0:T(8,128)(2,1)S(1)}, bf16[2,64,2240]{2,1,0:T(8,128)(2,1)S(1)}, u32[]{:S(2)}, u32[]{:S(2)}) collective-permute-start(bf16[2,64,2240]{2,1,0:T(8,128)(2,1)S(1)} %shard_map.96.refs_0_), channel_id=1, source_target_pairs={{0,4},{1,5},{2,6},{3,7},{4,0},{5,1},{6,2},{7,3},{8,12},{9,13},{10,... | collective-permute-start | bytes 1720328 | tf_op jit(solution)/shard_map/ppermute | solution.py:364
  102.3 28.0 %collective-permute-start.11 = (bf16[2,64,2240]{2,1,0:T(8,128)(2,1)S(1)}, bf16[2,64,2240]{2,1,0:T(8,128)(2,1)S(1)}, u32[]{:S(2)}, u32[]{:S(2)}) collective-permute-start(bf16[2,64,2240]{2,1,0:T(8,128)(2,1)S(1)} %shard_map.96.refs_0_), channel_id=1, source_target_pairs={{0,6},{1,7},{2,0},{3,1},{4,2},{5,3},{6,4},{7,5},{8,14},{9,15},{10,... | collective-permute-start | bytes 1720328 | tf_op jit(solution)/shard_map/ppermute | solution.py:364
  104.4 26.0 %collective-permute-start.7 = (bf16[2,64,2240]{2,1,0:T(8,128)(2,1)S(1)}, bf16[2,64,2240]{2,1,0:T(8,128)(2,1)S(1)}, u32[]{:S(2)}, u32[]{:S(2)}) collective-permute-start(bf16[2,64,2240]{2,1,0:T(8,128)(2,1)S(1)} %shard_map.96.refs_0_), channel_id=1, source_target_pairs={{0,2},{1,3},{2,4},{3,5},{4,6},{5,7},{6,0},{7,1},{8,10},{9,11},{10,... | collective-permute-start | bytes 1720328 | tf_op jit(solution)/shard_map/ppermute | solution.py:364
  110.6 33.4 %collective-permute-start.17 = (bf16[512,1024]{1,0:T(8,128)(2,1)S(1)}, bf16[512,1024]{1,0:T(8,128)(2,1)S(1)}, u32[]{:S(2)}, u32[]{:S(2)}) collective-permute-start(bf16[512,1024]{1,0:T(8,128)(2,1)S(1)} %shard_map.97.refs_10_.now_ref), channel_id=1, source_target_pairs={{0,8},{8,16},{16,24},{24,32},{32,40},{40,48},{48,56},{56,64},{64,7... | collective-permute-start | bytes 3145736 | tf_op jit(solution)/shard_map/ppermute | solution.py:380
  113.9 17.0 %collective-permute-start.6 = (bf16[2,64,2240]{2,1,0:T(8,128)(2,1)S(1)}, bf16[2,64,2240]{2,1,0:T(8,128)(2,1)S(1)}, u32[]{:S(2)}, u32[]{:S(2)}) collective-permute-start(bf16[2,64,2240]{2,1,0:T(8,128)(2,1)S(1)} %shard_map.96.refs_0_), channel_id=1, source_target_pairs={{0,1},{1,0},{2,3},{3,2},{4,5},{5,4},{6,7},{7,6},{8,9},{9,8},{10,11... | collective-permute-start | bytes 1720328 | tf_op jit(solution)/shard_map/ppermute | solution.py:383
  118.2 12.7 %collective-permute-start.10 = (bf16[2,64,2240]{2,1,0:T(8,128)(2,1)S(1)}, bf16[2,64,2240]{2,1,0:T(8,128)(2,1)S(1)}, u32[]{:S(2)}, u32[]{:S(2)}) collective-permute-start(bf16[2,64,2240]{2,1,0:T(8,128)(2,1)S(1)} %collective-permute-done.9.refs_4_), channel_id=1, source_target_pairs={{0,1},{1,0},{2,3},{3,2},{4,5},{5,4},{6,7},{7,6},{8,9},{9,8},{10,11... | collective-permute-start | bytes 1720328 | tf_op jit(solution)/shard_map/ppermute | solution.py:383
  147.0 3.7 %collective-permute-start.19 = (bf16[4,64,2240]{2,1,0:T(8,128)(2,1)S(1)}, bf16[4,64,2240]{2,1,0:T(8,128)(2,1)S(1)}, u32[]{:S(2)}, u32[]{:S(2)}) collective-permute-start(bf16[4,64,2240]{2,1,0:T(8,128)(2,1)S(1)} %get-tuple-element.33), channel_id=1, source_target_pairs={{0,1},{1,0},{2,3},{3,2},{4,5},{5,4},{6,7},{7,6},{8,9},{9,8},{10,11... | collective-permute-start | bytes 3440648 | tf_op jit(solution)/shard_map/ppermute | solution.py:388
  150.2 5.3 %collective-permute-start.18 = (bf16[4,64,2240]{2,1,0:T(8,128)(2,1)S(1)}, bf16[4,64,2240]{2,1,0:T(8,128)(2,1)S(1)}, u32[]{:S(2)}, u32[]{:S(2)}) collective-permute-start(bf16[4,64,2240]{2,1,0:T(8,128)(2,1)S(1)} %get-tuple-element.31), channel_id=1, source_target_pairs={{0,1},{1,0},{2,3},{3,2},{4,5},{5,4},{6,7},{7,6},{8,9},{9,8},{10,11... | collective-permute-start | bytes 3440648 | tf_op jit(solution)/shard_map/ppermute | solution.py:388
  151.0 11.9 %collective-permute-start.23 = (bf16[64,2240]{1,0:T(8,128)(2,1)S(1)}, bf16[64,2240]{1,0:T(8,128)(2,1)S(1)}, u32[]{:S(2)}, u32[]{:S(2)}) collective-permute-start(bf16[64,2240]{1,0:T(8,128)(2,1)S(1)} %get-tuple-element.38), channel_id=1, source_target_pairs={{0,2},{1,3},{2,4},{3,5},{4,6},{5,7},{6,0},{7,1},{8,10},{9,11},{10,... | collective-permute-start | bytes 860168 | tf_op jit(solution)/shard_map/ppermute | solution.py:398
  152.3 17.1 %collective-permute-start.24 = (bf16[64,2240]{1,0:T(8,128)(2,1)S(1)}, bf16[64,2240]{1,0:T(8,128)(2,1)S(1)}, u32[]{:S(2)}, u32[]{:S(2)}) collective-permute-start(bf16[64,2240]{1,0:T(8,128)(2,1)S(1)} %get-tuple-element.39), channel_id=1, source_target_pairs={{0,4},{1,5},{2,6},{3,7},{4,0},{5,1},{6,2},{7,3},{8,12},{9,13},{10,... | collective-permute-start | bytes 860168 | tf_op jit(solution)/shard_map/ppermute | solution.py:398
  155.2 14.2 %collective-permute-start.25 = (bf16[64,2240]{1,0:T(8,128)(2,1)S(1)}, bf16[64,2240]{1,0:T(8,128)(2,1)S(1)}, u32[]{:S(2)}, u32[]{:S(2)}) collective-permute-start(bf16[64,2240]{1,0:T(8,128)(2,1)S(1)} %get-tuple-element.40), channel_id=1, source_target_pairs={{0,6},{1,7},{2,0},{3,1},{4,2},{5,3},{6,4},{7,5},{8,14},{9,15},{10,... | collective-permute-start | bytes 860168 | tf_op jit(solution)/shard_map/ppermute | solution.py:398
  155.9 18.1 %collective-permute-start.20 = (bf16[64,2240]{1,0:T(8,128)(2,1)S(1)}, bf16[64,2240]{1,0:T(8,128)(2,1)S(1)}, u32[]{:S(2)}, u32[]{:S(2)}) collective-permute-start(bf16[64,2240]{1,0:T(8,128)(2,1)S(1)} %get-tuple-element.35), channel_id=1, source_target_pairs={{0,2},{1,3},{2,4},{3,5},{4,6},{5,7},{6,0},{7,1},{8,10},{9,11},{10,... | collective-permute-start | bytes 860168 | tf_op jit(solution)/shard_map/ppermute | solution.py:398
  157.6 23.6 %collective-permute-start.21 = (bf16[64,2240]{1,0:T(8,128)(2,1)S(1)}, bf16[64,2240]{1,0:T(8,128)(2,1)S(1)}, u32[]{:S(2)}, u32[]{:S(2)}) collective-permute-start(bf16[64,2240]{1,0:T(8,128)(2,1)S(1)} %get-tuple-element.36), channel_id=1, source_target_pairs={{0,4},{1,5},{2,6},{3,7},{4,0},{5,1},{6,2},{7,3},{8,12},{9,13},{10,... | collective-permute-start | bytes 860168 | tf_op jit(solution)/shard_map/ppermute | solution.py:398
  162.9 18.3 %collective-permute-start.22 = (bf16[64,2240]{1,0:T(8,128)(2,1)S(1)}, bf16[64,2240]{1,0:T(8,128)(2,1)S(1)}, u32[]{:S(2)}, u32[]{:S(2)}) collective-permute-start(bf16[64,2240]{1,0:T(8,128)(2,1)S(1)} %get-tuple-element.37), channel_id=1, source_target_pairs={{0,6},{1,7},{2,0},{3,1},{4,2},{5,3},{6,4},{7,5},{8,14},{9,15},{10,... | collective-permute-start | bytes 860168 | tf_op jit(solution)/shard_map/ppermute | solution.py:398
  (12 other events, 133.3 us)
Sparse Core Ops, SparseCore 0:
  9.2 68.9 all-gather.1

commit v11 on v10

--- a/solution.py
+++ b/solution.py
@@ -121,23 +121,23 @@
 
 def hidden_kernel(att_ref, stream_ref, w_hbm, needed_ref, early_ref, late_ref, w_ref, sems):
     tokens = att_ref.shape[0]
-    step = 384
+    step = 512
     spans = [(n, min(n + step, D)) for n in range(0, D, step)]
     copies = []
     for i, (n, stop) in enumerate(spans):
         span = pl.ds(n, stop - n)
-        copies.append(pltpu.make_async_copy(w_hbm.at[:, span], w_ref.at[:, span], sems.at[i]))
+        copies.append(pltpu.make_async_copy(w_hbm.at[span], w_ref.at[span], sems.at[i]))
     for copy in copies:
         copy.start()
+    total = stream_ref[...].astype(F32)
     for copy, (n, stop) in zip(copies, spans):
-        cols = slice(n, stop)
         copy.wait()
-        out = jnp.dot(att_ref[...], w_ref[:, cols], preferred_element_type=F32)
-        out = (out + stream_ref[:, cols].astype(F32)).astype(BF)
-        for r in range(tokens // 32):
-            rows = slice(16 * r, 16 * r + 16)
-            early_ref[rows, cols] = out[32 * r : 32 * r + 16]
-            late_ref[rows, cols] = out[32 * r + 16 : 32 * r + 32]
+        total = total + jnp.dot(att_ref[:, n:stop], w_ref[n:stop], preferred_element_type=F32)
+    out = total.astype(BF)
+    for r in range(tokens // 32):
+        rows = slice(16 * r, 16 * r + 16)
+        early_ref[rows] = out[32 * r : 32 * r + 16]
+        late_ref[rows] = out[32 * r + 16 : 32 * r + 32]
 
 
 def depthwise(hid, w_ref, taps_ref, out_ref, act_ref):
@@ -149,7 +149,7 @@
     act_ref[cols + tokens :] = jnp.zeros((cols, width), F32)
     act_ref[cols : cols + tokens] = act
     taps = taps_ref[...]
-    chunk = 32
+    chunk = 16
     col = lax.broadcasted_iota(jnp.int32, (chunk, width), 0) % cols
     for r in range(0, tokens, chunk):
         near = [act_ref[r + cols * a : r + cols * a + chunk] for a in range(3)]
@@ -306,12 +306,12 @@
         out_shape=[one_frame] * 2,
         in_specs=[VMEM, VMEM, anywhere, anywhere],
         out_specs=[VMEM, VMEM],
-        scratch_shapes=[pltpu.VMEM((width, width), BF), pltpu.SemaphoreType.DMA((6,))],
+        scratch_shapes=[pltpu.VMEM((width, width), BF), pltpu.SemaphoreType.DMA((5,))],
         compiler_params=params(52),
     )(attended, flat(stream_in), w_out_whole, w_flat)
 
     whole_rows = peers * frame_rows
-    block = 256
+    block = 512
 
     spatial_out = jax.ShapeDtypeStruct((whole_rows, 2 * chan), BF)
     weight_specs = [
@@ -335,7 +335,7 @@
                 pltpu.VMEM(lead + (whole_rows + 2 * col_count, block), F32),
                 pltpu.VMEM(lead + (whole_rows, width), BF),
             ],
-            compiler_params=params(24 if frames is None else 32),
+            compiler_params=params(30 if frames is None else 40),
         )(where_am_i, *pieces, w_flat, taps_s, needed)
 
     row_block = 256

time: 190 us -> 189 us (level)
  transfers between devices with their start and end apart: 27 -> 27, of which waited for: 12 -> 12; matrix products, arithmetic and copies ran while one was open for 3% -> 3% of each run, Pallas kernels for 12% -> 11%
where the time goes in v11:
time: 189 us; the launch traced here: 188 us
  waiting for transfers between devices  63.6 us (34%)
  blocking collectives  48.9 us (26%)
  Pallas kernels  30.4 us (16%)
  starting transfers between devices  24.8 us (13%)
  between operations  13.7 us (7%)
  local copies, waits for them, and re-layouts  6.55 us (3%)
    all_to_all x1, blocking collectives, on_device(): parts = lax.all_to_all(parts, same_core, 0, 0, tiled=True)  29.1 us
    ppermute x6, waiting for transfers between devices, along_of(): return [rows] + [lax.ppermute(rows, TILE, ahead[k]) for k in (1, 2, 3)]  25.9 us
    ppermute x6, waiting for transfers between devices, sums(): lax.ppermute(part, TILE, ahead[k + 1])  22.3 us
    all_to_all x1, blocking collectives, on_device(): state = lax.all_to_all(sums, same_core, 0, 0, tiled=True)  19.8 us
    pallas_call x2, Pallas kernels, pieces_call(): pl.pallas_call(kernel, out_shape=[spatial_out] * outs, grid=(2 * chan //...  14.9 us
    all_gather x1, waiting for transfers between devices, on_device(): w_out_whole = lax.all_gather(w_output, TILE, axis=0, tiled=True)  10.8 us
    ppermute x6, starting transfers between devices, along_of(): return [rows] + [lax.ppermute(rows, TILE, ahead[k]) for k in (1, 2, 3)]  8.53 us
    ppermute x6, starting transfers between devices, sums(): lax.ppermute(part, TILE, ahead[k + 1])  7.55 us
  transfers between devices with their start and end apart: 27, of which 12 were waited for; matrix products, arithmetic and copies ran while one was open for 3% of the time, Pallas kernels for 11%

profile of v11, /device:TPU:2, one launch (start us, length us, event | category | flops | bytes accessed | tf_op | source)
XLA Modules:
  0.0 188.0 jit_solution(6760822410044705487)
XLA Ops:
  10.8 29.1 %all_to_all.10.in_ref = bf16[128,8,128]{2,1,0:T(8,128)(2,1)S(1)} all-to-all(bf16[128,8,128]{2,1,0:T(8,128)(2,1)S(1)} %shard_map.92), channel_id=1, replica_groups=mesh['blk'=32,'y'=4,'core'=2] {'blk','y'}, dimensions={0} | all-to-all | bytes 524288 | tf_op jit(solution)/shard_map/all_to_all | solution.py:287
  40.1 19.8 %all_to_all.11.mine_ref = bf16[128,8,128]{2,1,0:T(8,128)(2,1)S(1)} all-to-all(bf16[128,8,128]{2,1,0:T(8,128)(2,1)S(1)} %shard_map.93), channel_id=1, replica_groups=mesh['blk'=32,'y'=4,'core'=2] {'blk','y'}, dimensions={0} | all-to-all | bytes 524288 | tf_op jit(solution)/shard_map/all_to_all | solution.py:291
  59.9 6.1 %copy.10 = bf16[280,8,2,512]{3,1,2,0:T(8,128)(2,1)} copy(bf16[280,8,2,512]{3,2,1,0:T(2,128)(2,1)} %bitcast.31) | data formatting | bytes 9175040
  67.3 10.8 %all-gather.2.cloned.1.call-done.w_hbm = bf16[2240,2240]{1,0:T(8,128)(2,1)} async-done(((bf16[280,2240]{1,0:T(8,128)(2,1)}), bf16[2240,2240]{1,0:T(8,128)(2,1)}) %all-gather.2.cloned.1.call-update) | async-done | bytes 10035216 | tf_op jit(solution)/shard_map/all_gather | solution.py:267
  78.2 4.8 %shard_map.95 = (bf16[64,2240]{1,0:T(8,128)(2,1)S(1)}, bf16[64,2240]{1,0:T(8,128)(2,1)S(1)}) custom-call(bf16[128,2240]{1,0:T(8,128)(2,1)S(1)} %shard_map.94.att_ref, bf16[128,2240]{1,0:T(8,128)(2,1)S(1)} %bitcast.24, bf16[2240,2240]{1,0:T(8,128)(2,1)} %all-gather.2.cloned.1.call-done.w_hbm, bf16[2240,1024]{1,0:T(8,128)(2,1)} %bitcast.15), custom_call_target="tpu_custom_call" | custom-call | tf_op jit(solution)/shard_map/pallas_call | solution.py:304
  83.7 1.8 collective-permute-start.3
  85.5 2.0 %collective-permute-start.4 = (bf16[64,2240]{1,0:T(8,128)(2,1)S(1)}, bf16[64,2240]{1,0:T(8,128)(2,1)S(1)}, u32[]{:S(2)}, u32[]{:S(2)}) collective-permute-start(bf16[64,2240]{1,0:T(8,128)(2,1)S(1)} %get-tuple-element.25.refs_0_.hidden_ref), channel_id=1, source_target_pairs={{0,6},{1,7},{2,0},{3,1},{4,2},{5,3},{6,4},{7,5},{8,14},{9,15},{10,... | collective-permute-start | bytes 860168 | tf_op jit(solution)/shard_map/ppermute | solution.py:364
  87.5 3.3 %collective-permute-start.5 = (bf16[64,2240]{1,0:T(8,128)(2,1)S(1)}, bf16[64,2240]{1,0:T(8,128)(2,1)S(1)}, u32[]{:S(2)}, u32[]{:S(2)}) collective-permute-start(bf16[64,2240]{1,0:T(8,128)(2,1)S(1)} %get-tuple-element.26.refs_3_.hidden_ref), channel_id=1, source_target_pairs={{0,8},{8,16},{16,24},{24,32},{32,40},{40,48},{48,56},{56,64},{64,7... | collective-permute-start | bytes 860168 | tf_op jit(solution)/shard_map/ppermute | solution.py:367
  91.0 8.8 %collective-permute-done.2.refs_0_.refs_2_ = bf16[64,2240]{1,0:T(8,128)(2,1)S(1)} collective-permute-done((bf16[64,2240]{1,0:T(8,128)(2,1)S(1)}, bf16[64,2240]{1,0:T(8,128)(2,1)S(1)}, u32[]{:S(2)}, u32[]{:S(2)}) %collective-permute-start.2) | collective-permute-done | bytes 286752 | tf_op jit(solution)/shard_map/ppermute | solution.py:364
  100.4 1.9 %collective-permute-start.9 = (bf16[2,64,2240]{2,1,0:T(8,128)(2,1)S(1)}, bf16[2,64,2240]{2,1,0:T(8,128)(2,1)S(1)}, u32[]{:S(2)}, u32[]{:S(2)}) collective-permute-start(bf16[2,64,2240]{2,1,0:T(8,128)(2,1)S(1)} %shard_map.96.refs_0_), channel_id=1, source_target_pairs={{0,4},{1,5},{2,6},{3,7},{4,0},{5,1},{6,2},{7,3},{8,12},{9,13},{10,... | collective-permute-start | bytes 1720328 | tf_op jit(solution)/shard_map/ppermute | solution.py:364
  102.3 2.0 %collective-permute-start.11 = (bf16[2,64,2240]{2,1,0:T(8,128)(2,1)S(1)}, bf16[2,64,2240]{2,1,0:T(8,128)(2,1)S(1)}, u32[]{:S(2)}, u32[]{:S(2)}) collective-permute-start(bf16[2,64,2240]{2,1,0:T(8,128)(2,1)S(1)} %shard_map.96.refs_0_), channel_id=1, source_target_pairs={{0,6},{1,7},{2,0},{3,1},{4,2},{5,3},{6,4},{7,5},{8,14},{9,15},{10,... | collective-permute-start | bytes 1720328 | tf_op jit(solution)/shard_map/ppermute | solution.py:364
  104.5 5.4 %shard_map.97.refs_10_.now_ref = bf16[512,1024]{1,0:T(8,128)(2,1)S(1)} custom-call(s32[2]{0:T(128)S(1)} %pad_add_fusion.place_ref, bf16[64,2240]{1,0:T(8,128)(2,1)S(1)} %get-tuple-element.25.refs_0_.hidden_ref, bf16[64,2240]{1,0:T(8,128)(2,1)S(1)} %collective-permute-done.13.refs_1_, bf16[64,2240]{1,0:T(8,128)(2,1)S(1)} %collective-permute-done.2.refs_0_.refs_2_, ...), custom_call_target="tpu_custom_call" | custom-call | tf_op jit(solution)/shard_map/pallas_call | solution.py:325
  109.9 3.4 %collective-permute-start.17 = (bf16[512,1024]{1,0:T(8,128)(2,1)S(1)}, bf16[512,1024]{1,0:T(8,128)(2,1)S(1)}, u32[]{:S(2)}, u32[]{:S(2)}) collective-permute-start(bf16[512,1024]{1,0:T(8,128)(2,1)S(1)} %shard_map.97.refs_10_.now_ref), channel_id=1, source_target_pairs={{0,8},{8,16},{16,24},{24,32},{32,40},{40,48},{48,56},{56,64},{64,7... | collective-permute-start | bytes 3145736 | tf_op jit(solution)/shard_map/ppermute | solution.py:380
  113.4 4.8 %collective-permute-done.9.refs_4_ = bf16[2,64,2240]{2,1,0:T(8,128)(2,1)S(1)} collective-permute-done((bf16[2,64,2240]{2,1,0:T(8,128)(2,1)S(1)}, bf16[2,64,2240]{2,1,0:T(8,128)(2,1)S(1)}, u32[]{:S(2)}, u32[]{:S(2)}) %collective-permute-start.9) | collective-permute-done | bytes 573472 | tf_op jit(solution)/shard_map/ppermute | solution.py:364
  118.2 12.2 %collective-permute-done.11.refs_6_ = bf16[2,64,2240]{2,1,0:T(8,128)(2,1)S(1)} collective-permute-done((bf16[2,64,2240]{2,1,0:T(8,128)(2,1)S(1)}, bf16[2,64,2240]{2,1,0:T(8,128)(2,1)S(1)}, u32[]{:S(2)}, u32[]{:S(2)}) %collective-permute-start.11) | collective-permute-done | bytes 573472 | tf_op jit(solution)/shard_map/ppermute | solution.py:364
  133.2 9.5 %shard_map.98 = (bf16[512,1024]{1,0:T(8,128)(2,1)S(1)}, bf16[512,1024]{1,0:T(8,128)(2,1)S(1)}) custom-call(s32[2]{0:T(128)S(1)} %pad_add_fusion.place_ref, bf16[2,64,2240]{2,1,0:T(8,128)(2,1)S(1)} %shard_map.96.refs_0_, bf16[2,64,2240]{2,1,0:T(8,128)(2,1)S(1)} %collective-permute-done.6.refs_1_, bf16[2,64,2240]{2,1,0:T(8,128)(2,1)S(1)} %collective-permute-done.7.refs_2_, ...), custom_call_target="tpu_custom_call" | custom-call | tf_op jit(solution)/shard_map/pallas_call | solution.py:325
  142.8 3.0 %shard_map.99 = (bf16[4,64,2240]{2,1,0:T(8,128)(2,1)S(1)}, bf16[4,64,2240]{2,1,0:T(8,128)(2,1)S(1)}) custom-call(s32[2]{0:T(128)S(1)} %pad_add_fusion.place_ref, bf16[512,1024]{1,0:T(8,128)(2,1)S(1)} %shard_map.97.refs_10_.now_ref, bf16[512,1024]{1,0:T(8,128)(2,1)S(1)} %get-tuple-element.27.one_ref.now_ref, ...), custom_call_target="tpu_custom_call" | custom-call | tf_op jit(solution)/shard_map/pallas_call | solution.py:387
  146.0 3.0 %shard_map.100 = (bf16[4,64,2240]{2,1,0:T(8,128)(2,1)S(1)}, bf16[4,64,2240]{2,1,0:T(8,128)(2,1)S(1)}) custom-call(s32[2]{0:T(128)S(1)} %pad_add_fusion.place_ref, bf16[512,1024]{1,0:T(8,128)(2,1)S(1)} %get-tuple-element.27.one_ref.now_ref, bf16[512,1024]{1,0:T(8,128)(2,1)S(1)} %collective-permute-done.17.two_ref.one_ref, ...), custom_call_target="tpu_custom_call" | custom-call | tf_op jit(solution)/shard_map/pallas_call | solution.py:387
  151.1 2.9 %collective-permute-start.24 = (bf16[64,2240]{1,0:T(8,128)(2,1)S(1)}, bf16[64,2240]{1,0:T(8,128)(2,1)S(1)}, u32[]{:S(2)}, u32[]{:S(2)}) collective-permute-start(bf16[64,2240]{1,0:T(8,128)(2,1)S(1)} %get-tuple-element.39), channel_id=1, source_target_pairs={{0,4},{1,5},{2,6},{3,7},{4,0},{5,1},{6,2},{7,3},{8,12},{9,13},{10,... | collective-permute-start | bytes 860168 | tf_op jit(solution)/shard_map/ppermute | solution.py:398
  154.7 1.7 collective-permute-start.20
  157.0 4.7 %collective-permute-done.23.refs_3_ = bf16[64,2240]{1,0:T(8,128)(2,1)S(1)} collective-permute-done((bf16[64,2240]{1,0:T(8,128)(2,1)S(1)}, bf16[64,2240]{1,0:T(8,128)(2,1)S(1)}, u32[]{:S(2)}, u32[]{:S(2)}) %collective-permute-start.23) | collective-permute-done | bytes 286752 | tf_op jit(solution)/shard_map/ppermute | solution.py:398
  162.4 5.8 %collective-permute-done.24.refs_4_ = bf16[64,2240]{1,0:T(8,128)(2,1)S(1)} collective-permute-done((bf16[64,2240]{1,0:T(8,128)(2,1)S(1)}, bf16[64,2240]{1,0:T(8,128)(2,1)S(1)}, u32[]{:S(2)}, u32[]{:S(2)}) %collective-permute-start.24) | collective-permute-done | bytes 286752 | tf_op jit(solution)/shard_map/ppermute | solution.py:398
  168.2 4.6 %collective-permute-done.20.refs_0_ = bf16[64,2240]{1,0:T(8,128)(2,1)S(1)} collective-permute-done((bf16[64,2240]{1,0:T(8,128)(2,1)S(1)}, bf16[64,2240]{1,0:T(8,128)(2,1)S(1)}, u32[]{:S(2)}, u32[]{:S(2)}) %collective-permute-start.20) | collective-permute-done | bytes 286752 | tf_op jit(solution)/shard_map/ppermute | solution.py:398
  172.8 7.2 %collective-permute-done.21.refs_1_ = bf16[64,2240]{1,0:T(8,128)(2,1)S(1)} collective-permute-done((bf16[64,2240]{1,0:T(8,128)(2,1)S(1)}, bf16[64,2240]{1,0:T(8,128)(2,1)S(1)}, u32[]{:S(2)}, u32[]{:S(2)}) %collective-permute-start.21) | collective-permute-done | bytes 286752 | tf_op jit(solution)/shard_map/ppermute | solution.py:398
  (70 shorter events, 15.6 us)
Async XLA Ops:
  6.5 71.6 %all-gather.2.cloned.1.call-start = ((), (), s32[]{:S(2)}) async-start(), calls=%async_computation.2 | async-start | bytes 11612160 | tf_op jit(solution)/shard_map/all_gather | solution.py:267
  59.9 6.1 %collective-permute-start.1 = (bf16[128,8,128]{2,1,0:T(8,128)(2,1)S(1)}, bf16[128,8,128]{2,1,0:T(8,128)(2,1)S(1)}, u32[]{:S(2)}, u32[]{:S(2)}) collective-permute-start(bf16[128,8,128]{2,1,0:T(8,128)(2,1)S(1)} %all_to_all.11.mine_ref), channel_id=1, source_target_pairs={{0,1},{1,0},{2,3},{3,2},{4,5},{5,4},{6,7},{7,6},{8,9},{9,8},{10,11... | collective-permute-start | bytes 786440 | tf_op jit(solution)/shard_map/ppermute | solution.py:302
  83.0 16.8 %collective-permute-start.2 = (bf16[64,2240]{1,0:T(8,128)(2,1)S(1)}, bf16[64,2240]{1,0:T(8,128)(2,1)S(1)}, u32[]{:S(2)}, u32[]{:S(2)}) collective-permute-start(bf16[64,2240]{1,0:T(8,128)(2,1)S(1)} %get-tuple-element.25.refs_0_.hidden_ref), channel_id=1, source_target_pairs={{0,2},{1,3},{2,4},{3,5},{4,6},{5,7},{6,0},{7,1},{8,10},{9,11},{10,... | collective-permute-start | bytes 860168 | tf_op jit(solution)/shard_map/ppermute | solution.py:364
  83.7 16.0 %collective-permute-start.3 = (bf16[64,2240]{1,0:T(8,128)(2,1)S(1)}, bf16[64,2240]{1,0:T(8,128)(2,1)S(1)}, u32[]{:S(2)}, u32[]{:S(2)}) collective-permute-start(bf16[64,2240]{1,0:T(8,128)(2,1)S(1)} %get-tuple-element.25.refs_0_.hidden_ref), channel_id=1, source_target_pairs={{0,4},{1,5},{2,6},{3,7},{4,0},{5,1},{6,2},{7,3},{8,12},{9,13},{10,... | collective-permute-start | bytes 860168 | tf_op jit(solution)/shard_map/ppermute | solution.py:364
  85.5 14.9 %collective-permute-start.4 = (bf16[64,2240]{1,0:T(8,128)(2,1)S(1)}, bf16[64,2240]{1,0:T(8,128)(2,1)S(1)}, u32[]{:S(2)}, u32[]{:S(2)}) collective-permute-start(bf16[64,2240]{1,0:T(8,128)(2,1)S(1)} %get-tuple-element.25.refs_0_.hidden_ref), channel_id=1, source_target_pairs={{0,6},{1,7},{2,0},{3,1},{4,2},{5,3},{6,4},{7,5},{8,14},{9,15},{10,... | collective-permute-start | bytes 860168 | tf_op jit(solution)/shard_map/ppermute | solution.py:364
  87.5 12.8 %collective-permute-start.5 = (bf16[64,2240]{1,0:T(8,128)(2,1)S(1)}, bf16[64,2240]{1,0:T(8,128)(2,1)S(1)}, u32[]{:S(2)}, u32[]{:S(2)}) collective-permute-start(bf16[64,2240]{1,0:T(8,128)(2,1)S(1)} %get-tuple-element.26.refs_3_.hidden_ref), channel_id=1, source_target_pairs={{0,8},{8,16},{16,24},{24,32},{32,40},{40,48},{48,56},{56,64},{64,7... | collective-permute-start | bytes 860168 | tf_op jit(solution)/shard_map/ppermute | solution.py:367
  90.9 11.5 %collective-permute-start.13 = (bf16[64,2240]{1,0:T(8,128)(2,1)S(1)}, bf16[64,2240]{1,0:T(8,128)(2,1)S(1)}, u32[]{:S(2)}, u32[]{:S(2)}) collective-permute-start(bf16[64,2240]{1,0:T(8,128)(2,1)S(1)} %get-tuple-element.25.refs_0_.hidden_ref), channel_id=1, source_target_pairs={{0,1},{1,0},{2,3},{3,2},{4,5},{5,4},{6,7},{7,6},{8,9},{9,8},{10,11... | collective-permute-start | bytes 860168 | tf_op jit(solution)/shard_map/ppermute | solution.py:378
  99.7 4.6 %collective-permute-start.14 = (bf16[64,2240]{1,0:T(8,128)(2,1)S(1)}, bf16[64,2240]{1,0:T(8,128)(2,1)S(1)}, u32[]{:S(2)}, u32[]{:S(2)}) collective-permute-start(bf16[64,2240]{1,0:T(8,128)(2,1)S(1)} %collective-permute-done.2.refs_0_.refs_2_), channel_id=1, source_target_pairs={{0,1},{1,0},{2,3},{3,2},{4,5},{5,4},{6,7},{7,6},{8,9},{9,8},{10,11... | collective-permute-start | bytes 860168 | tf_op jit(solution)/shard_map/ppermute | solution.py:378
  99.7 4.7 %collective-permute-start.15 = (bf16[64,2240]{1,0:T(8,128)(2,1)S(1)}, bf16[64,2240]{1,0:T(8,128)(2,1)S(1)}, u32[]{:S(2)}, u32[]{:S(2)}) collective-permute-start(bf16[64,2240]{1,0:T(8,128)(2,1)S(1)} %collective-permute-done.3.refs_1_.refs_4_), channel_id=1, source_target_pairs={{0,1},{1,0},{2,3},{3,2},{4,5},{5,4},{6,7},{7,6},{8,9},{9,8},{10,11... | collective-permute-start | bytes 860168 | tf_op jit(solution)/shard_map/ppermute | solution.py:378
  100.4 4.1 %collective-permute-start.16 = (bf16[64,2240]{1,0:T(8,128)(2,1)S(1)}, bf16[64,2240]{1,0:T(8,128)(2,1)S(1)}, u32[]{:S(2)}, u32[]{:S(2)}) collective-permute-start(bf16[64,2240]{1,0:T(8,128)(2,1)S(1)} %collective-permute-done.4.refs_2_.refs_6_), channel_id=1, source_target_pairs={{0,1},{1,0},{2,3},{3,2},{4,5},{5,4},{6,7},{7,6},{8,9},{9,8},{10,11... | collective-permute-start | bytes 860168 | tf_op jit(solution)/shard_map/ppermute | solution.py:378
  100.4 17.8 %collective-permute-start.9 = (bf16[2,64,2240]{2,1,0:T(8,128)(2,1)S(1)}, bf16[2,64,2240]{2,1,0:T(8,128)(2,1)S(1)}, u32[]{:S(2)}, u32[]{:S(2)}) collective-permute-start(bf16[2,64,2240]{2,1,0:T(8,128)(2,1)S(1)} %shard_map.96.refs_0_), channel_id=1, source_target_pairs={{0,4},{1,5},{2,6},{3,7},{4,0},{5,1},{6,2},{7,3},{8,12},{9,13},{10,... | collective-permute-start | bytes 1720328 | tf_op jit(solution)/shard_map/ppermute | solution.py:364
  102.3 28.0 %collective-permute-start.11 = (bf16[2,64,2240]{2,1,0:T(8,128)(2,1)S(1)}, bf16[2,64,2240]{2,1,0:T(8,128)(2,1)S(1)}, u32[]{:S(2)}, u32[]{:S(2)}) collective-permute-start(bf16[2,64,2240]{2,1,0:T(8,128)(2,1)S(1)} %shard_map.96.refs_0_), channel_id=1, source_target_pairs={{0,6},{1,7},{2,0},{3,1},{4,2},{5,3},{6,4},{7,5},{8,14},{9,15},{10,... | collective-permute-start | bytes 1720328 | tf_op jit(solution)/shard_map/ppermute | solution.py:364
  104.4 26.0 %collective-permute-start.7 = (bf16[2,64,2240]{2,1,0:T(8,128)(2,1)S(1)}, bf16[2,64,2240]{2,1,0:T(8,128)(2,1)S(1)}, u32[]{:S(2)}, u32[]{:S(2)}) collective-permute-start(bf16[2,64,2240]{2,1,0:T(8,128)(2,1)S(1)} %shard_map.96.refs_0_), channel_id=1, source_target_pairs={{0,2},{1,3},{2,4},{3,5},{4,6},{5,7},{6,0},{7,1},{8,10},{9,11},{10,... | collective-permute-start | bytes 1720328 | tf_op jit(solution)/shard_map/ppermute | solution.py:364
  109.9 32.8 %collective-permute-start.17 = (bf16[512,1024]{1,0:T(8,128)(2,1)S(1)}, bf16[512,1024]{1,0:T(8,128)(2,1)S(1)}, u32[]{:S(2)}, u32[]{:S(2)}) collective-permute-start(bf16[512,1024]{1,0:T(8,128)(2,1)S(1)} %shard_map.97.refs_10_.now_ref), channel_id=1, source_target_pairs={{0,8},{8,16},{16,24},{24,32},{32,40},{40,48},{48,56},{56,64},{64,7... | collective-permute-start | bytes 3145736 | tf_op jit(solution)/shard_map/ppermute | solution.py:380
  113.3 17.6 %collective-permute-start.6 = (bf16[2,64,2240]{2,1,0:T(8,128)(2,1)S(1)}, bf16[2,64,2240]{2,1,0:T(8,128)(2,1)S(1)}, u32[]{:S(2)}, u32[]{:S(2)}) collective-permute-start(bf16[2,64,2240]{2,1,0:T(8,128)(2,1)S(1)} %shard_map.96.refs_0_), channel_id=1, source_target_pairs={{0,1},{1,0},{2,3},{3,2},{4,5},{5,4},{6,7},{7,6},{8,9},{9,8},{10,11... | collective-permute-start | bytes 1720328 | tf_op jit(solution)/shard_map/ppermute | solution.py:383
  118.2 12.7 %collective-permute-start.10 = (bf16[2,64,2240]{2,1,0:T(8,128)(2,1)S(1)}, bf16[2,64,2240]{2,1,0:T(8,128)(2,1)S(1)}, u32[]{:S(2)}, u32[]{:S(2)}) collective-permute-start(bf16[2,64,2240]{2,1,0:T(8,128)(2,1)S(1)} %collective-permute-done.9.refs_4_), channel_id=1, source_target_pairs={{0,1},{1,0},{2,3},{3,2},{4,5},{5,4},{6,7},{7,6},{8,9},{9,8},{10,11... | collective-permute-start | bytes 1720328 | tf_op jit(solution)/shard_map/ppermute | solution.py:383
  145.8 3.7 %collective-permute-start.19 = (bf16[4,64,2240]{2,1,0:T(8,128)(2,1)S(1)}, bf16[4,64,2240]{2,1,0:T(8,128)(2,1)S(1)}, u32[]{:S(2)}, u32[]{:S(2)}) collective-permute-start(bf16[4,64,2240]{2,1,0:T(8,128)(2,1)S(1)} %get-tuple-element.33), channel_id=1, source_target_pairs={{0,1},{1,0},{2,3},{3,2},{4,5},{5,4},{6,7},{7,6},{8,9},{9,8},{10,11... | collective-permute-start | bytes 3440648 | tf_op jit(solution)/shard_map/ppermute | solution.py:388
  149.1 5.3 %collective-permute-start.18 = (bf16[4,64,2240]{2,1,0:T(8,128)(2,1)S(1)}, bf16[4,64,2240]{2,1,0:T(8,128)(2,1)S(1)}, u32[]{:S(2)}, u32[]{:S(2)}) collective-permute-start(bf16[4,64,2240]{2,1,0:T(8,128)(2,1)S(1)} %get-tuple-element.31), channel_id=1, source_target_pairs={{0,1},{1,0},{2,3},{3,2},{4,5},{5,4},{6,7},{7,6},{8,9},{9,8},{10,11... | collective-permute-start | bytes 3440648 | tf_op jit(solution)/shard_map/ppermute | solution.py:388
  149.8 11.9 %collective-permute-start.23 = (bf16[64,2240]{1,0:T(8,128)(2,1)S(1)}, bf16[64,2240]{1,0:T(8,128)(2,1)S(1)}, u32[]{:S(2)}, u32[]{:S(2)}) collective-permute-start(bf16[64,2240]{1,0:T(8,128)(2,1)S(1)} %get-tuple-element.38), channel_id=1, source_target_pairs={{0,2},{1,3},{2,4},{3,5},{4,6},{5,7},{6,0},{7,1},{8,10},{9,11},{10,... | collective-permute-start | bytes 860168 | tf_op jit(solution)/shard_map/ppermute | solution.py:398
  151.1 17.1 %collective-permute-start.24 = (bf16[64,2240]{1,0:T(8,128)(2,1)S(1)}, bf16[64,2240]{1,0:T(8,128)(2,1)S(1)}, u32[]{:S(2)}, u32[]{:S(2)}) collective-permute-start(bf16[64,2240]{1,0:T(8,128)(2,1)S(1)} %get-tuple-element.39), channel_id=1, source_target_pairs={{0,4},{1,5},{2,6},{3,7},{4,0},{5,1},{6,2},{7,3},{8,12},{9,13},{10,... | collective-permute-start | bytes 860168 | tf_op jit(solution)/shard_map/ppermute | solution.py:398
  154.0 14.2 %collective-permute-start.25 = (bf16[64,2240]{1,0:T(8,128)(2,1)S(1)}, bf16[64,2240]{1,0:T(8,128)(2,1)S(1)}, u32[]{:S(2)}, u32[]{:S(2)}) collective-permute-start(bf16[64,2240]{1,0:T(8,128)(2,1)S(1)} %get-tuple-element.40), channel_id=1, source_target_pairs={{0,6},{1,7},{2,0},{3,1},{4,2},{5,3},{6,4},{7,5},{8,14},{9,15},{10,... | collective-permute-start | bytes 860168 | tf_op jit(solution)/shard_map/ppermute | solution.py:398
  154.7 18.1 %collective-permute-start.20 = (bf16[64,2240]{1,0:T(8,128)(2,1)S(1)}, bf16[64,2240]{1,0:T(8,128)(2,1)S(1)}, u32[]{:S(2)}, u32[]{:S(2)}) collective-permute-start(bf16[64,2240]{1,0:T(8,128)(2,1)S(1)} %get-tuple-element.35), channel_id=1, source_target_pairs={{0,2},{1,3},{2,4},{3,5},{4,6},{5,7},{6,0},{7,1},{8,10},{9,11},{10,... | collective-permute-start | bytes 860168 | tf_op jit(solution)/shard_map/ppermute | solution.py:398
  156.4 23.6 %collective-permute-start.21 = (bf16[64,2240]{1,0:T(8,128)(2,1)S(1)}, bf16[64,2240]{1,0:T(8,128)(2,1)S(1)}, u32[]{:S(2)}, u32[]{:S(2)}) collective-permute-start(bf16[64,2240]{1,0:T(8,128)(2,1)S(1)} %get-tuple-element.36), channel_id=1, source_target_pairs={{0,4},{1,5},{2,6},{3,7},{4,0},{5,1},{6,2},{7,3},{8,12},{9,13},{10,... | collective-permute-start | bytes 860168 | tf_op jit(solution)/shard_map/ppermute | solution.py:398
  161.7 18.3 %collective-permute-start.22 = (bf16[64,2240]{1,0:T(8,128)(2,1)S(1)}, bf16[64,2240]{1,0:T(8,128)(2,1)S(1)}, u32[]{:S(2)}, u32[]{:S(2)}) collective-permute-start(bf16[64,2240]{1,0:T(8,128)(2,1)S(1)} %get-tuple-element.37), channel_id=1, source_target_pairs={{0,6},{1,7},{2,0},{3,1},{4,2},{5,3},{6,4},{7,5},{8,14},{9,15},{10,... | collective-permute-start | bytes 860168 | tf_op jit(solution)/shard_map/ppermute | solution.py:398
  (12 other events, 132.2 us)
Sparse Core Ops, SparseCore 0:
  9.2 68.9 all-gather.1

commit v12 on v11

--- a/solution.py
+++ b/solution.py
@@ -208,9 +208,10 @@
     out = lax.dot_general(gated, w_ref[...], over_channels, preferred_element_type=F32).astype(BF)
     y, core = place_ref[0], place_ref[1]
     i = pl.program_id(0)
-    rows = out.shape[0] // 4
-    for k in range(4):
-        target = 4 * i + k
+    rows = mine_ref.shape[1]
+    count = out.shape[0] // rows
+    for k in range(count):
+        target = count * i + k
         slot = (target // 2 - y + 4) % 4
 
         @pl.when(core == k % 2)
@@ -338,7 +339,7 @@
             compiler_params=params(30 if frames is None else 40),
         )(where_am_i, *pieces, w_flat, taps_s, needed)
 
-    row_block = 256
+    row_block = 512
     point_call = pl.pallas_call(
         point_kernel,
         out_shape=[jax.ShapeDtypeStruct((4, frame_rows, width), BF)] * 2,

time: 189 us -> 188 us (level)
  no operation moved by 1% of the time
where the time goes in v12:
time: 188 us
  waiting for transfers between devices  63.7 us (34%)
  blocking collectives  48.9 us (26%)
  Pallas kernels  29.9 us (16%)
  starting transfers between devices  24.8 us (13%)
  between operations  13.7 us (7%)
  local copies, waits for them, and re-layouts  6.55 us (3%)
    all_to_all x1, blocking collectives, on_device(): parts = lax.all_to_all(parts, same_core, 0, 0, tiled=True)  29.1 us
    ppermute x6, waiting for transfers between devices, along_of(): return [rows] + [lax.ppermute(rows, TILE, ahead[k]) for k in (1, 2, 3)]  25.9 us
    ppermute x6, waiting for transfers between devices, sums(): lax.ppermute(part, TILE, ahead[k + 1])  22.3 us
    all_to_all x1, blocking collectives, on_device(): state = lax.all_to_all(sums, same_core, 0, 0, tiled=True)  19.8 us
    pallas_call x2, Pallas kernels, pieces_call(): pl.pallas_call(kernel, out_shape=[spatial_out] * outs, grid=(2 * chan //...  14.9 us
    all_gather x1, waiting for transfers between devices, on_device(): w_out_whole = lax.all_gather(w_output, TILE, axis=0, tiled=True)  10.8 us
    ppermute x6, starting transfers between devices, along_of(): return [rows] + [lax.ppermute(rows, TILE, ahead[k]) for k in (1, 2, 3)]  8.53 us
    ppermute x6, starting transfers between devices, sums(): lax.ppermute(part, TILE, ahead[k + 1])  7.53 us
  transfers between devices with their start and end apart: 27, of which 12 were waited for; matrix products, arithmetic and copies ran while one was open for 3% of the time, Pallas kernels for 11%

profile of v12, /device:TPU:2, one launch (start us, length us, event | category | flops | bytes accessed | tf_op | source)
XLA Modules:
  0.0 187.5 jit_solution(15930772538468209384)
XLA Ops:
  10.8 29.1 %all_to_all.10.in_ref = bf16[128,8,128]{2,1,0:T(8,128)(2,1)S(1)} all-to-all(bf16[128,8,128]{2,1,0:T(8,128)(2,1)S(1)} %shard_map.92), channel_id=1, replica_groups=mesh['blk'=32,'y'=4,'core'=2] {'blk','y'}, dimensions={0} | all-to-all | bytes 524288 | tf_op jit(solution)/shard_map/all_to_all | solution.py:288
  40.1 19.8 %all_to_all.11.mine_ref = bf16[128,8,128]{2,1,0:T(8,128)(2,1)S(1)} all-to-all(bf16[128,8,128]{2,1,0:T(8,128)(2,1)S(1)} %shard_map.93), channel_id=1, replica_groups=mesh['blk'=32,'y'=4,'core'=2] {'blk','y'}, dimensions={0} | all-to-all | bytes 524288 | tf_op jit(solution)/shard_map/all_to_all | solution.py:292
  59.9 6.1 %copy.10 = bf16[280,8,2,512]{3,1,2,0:T(8,128)(2,1)} copy(bf16[280,8,2,512]{3,2,1,0:T(2,128)(2,1)} %bitcast.31) | data formatting | bytes 9175040
  67.3 10.8 %all-gather.2.cloned.1.call-done.w_hbm = bf16[2240,2240]{1,0:T(8,128)(2,1)} async-done(((bf16[280,2240]{1,0:T(8,128)(2,1)}), bf16[2240,2240]{1,0:T(8,128)(2,1)}) %all-gather.2.cloned.1.call-update) | async-done | bytes 10035216 | tf_op jit(solution)/shard_map/all_gather | solution.py:268
  78.2 4.8 %shard_map.95 = (bf16[64,2240]{1,0:T(8,128)(2,1)S(1)}, bf16[64,2240]{1,0:T(8,128)(2,1)S(1)}) custom-call(bf16[128,2240]{1,0:T(8,128)(2,1)S(1)} %shard_map.94.att_ref, bf16[128,2240]{1,0:T(8,128)(2,1)S(1)} %bitcast.24, bf16[2240,2240]{1,0:T(8,128)(2,1)} %all-gather.2.cloned.1.call-done.w_hbm, bf16[2240,1024]{1,0:T(8,128)(2,1)} %bitcast.15), custom_call_target="tpu_custom_call" | custom-call | tf_op jit(solution)/shard_map/pallas_call | solution.py:305
  83.7 1.8 collective-permute-start.3
  85.5 2.0 %collective-permute-start.4 = (bf16[64,2240]{1,0:T(8,128)(2,1)S(1)}, bf16[64,2240]{1,0:T(8,128)(2,1)S(1)}, u32[]{:S(2)}, u32[]{:S(2)}) collective-permute-start(bf16[64,2240]{1,0:T(8,128)(2,1)S(1)} %get-tuple-element.25.refs_0_.hidden_ref), channel_id=1, source_target_pairs={{0,6},{1,7},{2,0},{3,1},{4,2},{5,3},{6,4},{7,5},{8,14},{9,15},{10,... | collective-permute-start | bytes 860168 | tf_op jit(solution)/shard_map/ppermute | solution.py:365
  87.5 3.3 %collective-permute-start.5 = (bf16[64,2240]{1,0:T(8,128)(2,1)S(1)}, bf16[64,2240]{1,0:T(8,128)(2,1)S(1)}, u32[]{:S(2)}, u32[]{:S(2)}) collective-permute-start(bf16[64,2240]{1,0:T(8,128)(2,1)S(1)} %get-tuple-element.26.refs_3_.hidden_ref), channel_id=1, source_target_pairs={{0,8},{8,16},{16,24},{24,32},{32,40},{40,48},{48,56},{56,64},{64,7... | collective-permute-start | bytes 860168 | tf_op jit(solution)/shard_map/ppermute | solution.py:368
  91.0 8.8 %collective-permute-done.2.refs_0_.refs_2_ = bf16[64,2240]{1,0:T(8,128)(2,1)S(1)} collective-permute-done((bf16[64,2240]{1,0:T(8,128)(2,1)S(1)}, bf16[64,2240]{1,0:T(8,128)(2,1)S(1)}, u32[]{:S(2)}, u32[]{:S(2)}) %collective-permute-start.2) | collective-permute-done | bytes 286752 | tf_op jit(solution)/shard_map/ppermute | solution.py:365
  100.4 1.9 %collective-permute-start.9 = (bf16[2,64,2240]{2,1,0:T(8,128)(2,1)S(1)}, bf16[2,64,2240]{2,1,0:T(8,128)(2,1)S(1)}, u32[]{:S(2)}, u32[]{:S(2)}) collective-permute-start(bf16[2,64,2240]{2,1,0:T(8,128)(2,1)S(1)} %shard_map.96.refs_0_), channel_id=1, source_target_pairs={{0,4},{1,5},{2,6},{3,7},{4,0},{5,1},{6,2},{7,3},{8,12},{9,13},{10,... | collective-permute-start | bytes 1720328 | tf_op jit(solution)/shard_map/ppermute | solution.py:365
  102.3 2.0 %collective-permute-start.11 = (bf16[2,64,2240]{2,1,0:T(8,128)(2,1)S(1)}, bf16[2,64,2240]{2,1,0:T(8,128)(2,1)S(1)}, u32[]{:S(2)}, u32[]{:S(2)}) collective-permute-start(bf16[2,64,2240]{2,1,0:T(8,128)(2,1)S(1)} %shard_map.96.refs_0_), channel_id=1, source_target_pairs={{0,6},{1,7},{2,0},{3,1},{4,2},{5,3},{6,4},{7,5},{8,14},{9,15},{10,... | collective-permute-start | bytes 1720328 | tf_op jit(solution)/shard_map/ppermute | solution.py:365
  104.5 5.4 %shard_map.97.refs_10_.now_ref = bf16[512,1024]{1,0:T(8,128)(2,1)S(1)} custom-call(s32[2]{0:T(128)S(1)} %pad_add_fusion.place_ref, bf16[64,2240]{1,0:T(8,128)(2,1)S(1)} %get-tuple-element.25.refs_0_.hidden_ref, bf16[64,2240]{1,0:T(8,128)(2,1)S(1)} %collective-permute-done.13.refs_1_, bf16[64,2240]{1,0:T(8,128)(2,1)S(1)} %collective-permute-done.2.refs_0_.refs_2_, ...), custom_call_target="tpu_custom_call" | custom-call | tf_op jit(solution)/shard_map/pallas_call | solution.py:326
  109.9 3.4 %collective-permute-start.17 = (bf16[512,1024]{1,0:T(8,128)(2,1)S(1)}, bf16[512,1024]{1,0:T(8,128)(2,1)S(1)}, u32[]{:S(2)}, u32[]{:S(2)}) collective-permute-start(bf16[512,1024]{1,0:T(8,128)(2,1)S(1)} %shard_map.97.refs_10_.now_ref), channel_id=1, source_target_pairs={{0,8},{8,16},{16,24},{24,32},{32,40},{40,48},{48,56},{56,64},{64,7... | collective-permute-start | bytes 3145736 | tf_op jit(solution)/shard_map/ppermute | solution.py:381
  113.4 4.8 %collective-permute-done.9.refs_4_ = bf16[2,64,2240]{2,1,0:T(8,128)(2,1)S(1)} collective-permute-done((bf16[2,64,2240]{2,1,0:T(8,128)(2,1)S(1)}, bf16[2,64,2240]{2,1,0:T(8,128)(2,1)S(1)}, u32[]{:S(2)}, u32[]{:S(2)}) %collective-permute-start.9) | collective-permute-done | bytes 573472 | tf_op jit(solution)/shard_map/ppermute | solution.py:365
  118.2 12.2 %collective-permute-done.11.refs_6_ = bf16[2,64,2240]{2,1,0:T(8,128)(2,1)S(1)} collective-permute-done((bf16[2,64,2240]{2,1,0:T(8,128)(2,1)S(1)}, bf16[2,64,2240]{2,1,0:T(8,128)(2,1)S(1)}, u32[]{:S(2)}, u32[]{:S(2)}) %collective-permute-start.11) | collective-permute-done | bytes 573472 | tf_op jit(solution)/shard_map/ppermute | solution.py:365
  133.2 9.5 %shard_map.98 = (bf16[512,1024]{1,0:T(8,128)(2,1)S(1)}, bf16[512,1024]{1,0:T(8,128)(2,1)S(1)}) custom-call(s32[2]{0:T(128)S(1)} %pad_add_fusion.place_ref, bf16[2,64,2240]{2,1,0:T(8,128)(2,1)S(1)} %shard_map.96.refs_0_, bf16[2,64,2240]{2,1,0:T(8,128)(2,1)S(1)} %collective-permute-done.6.refs_1_, bf16[2,64,2240]{2,1,0:T(8,128)(2,1)S(1)} %collective-permute-done.7.refs_2_, ...), custom_call_target="tpu_custom_call" | custom-call | tf_op jit(solution)/shard_map/pallas_call | solution.py:326
  142.8 2.8 %shard_map.99 = (bf16[4,64,2240]{2,1,0:T(8,128)(2,1)S(1)}, bf16[4,64,2240]{2,1,0:T(8,128)(2,1)S(1)}) custom-call(s32[2]{0:T(128)S(1)} %pad_add_fusion.place_ref, bf16[512,1024]{1,0:T(8,128)(2,1)S(1)} %shard_map.97.refs_10_.now_ref, bf16[512,1024]{1,0:T(8,128)(2,1)S(1)} %get-tuple-element.27.one_ref.now_ref, ...), custom_call_target="tpu_custom_call" | custom-call | tf_op jit(solution)/shard_map/pallas_call | solution.py:388
  145.8 2.8 %shard_map.100 = (bf16[4,64,2240]{2,1,0:T(8,128)(2,1)S(1)}, bf16[4,64,2240]{2,1,0:T(8,128)(2,1)S(1)}) custom-call(s32[2]{0:T(128)S(1)} %pad_add_fusion.place_ref, bf16[512,1024]{1,0:T(8,128)(2,1)S(1)} %get-tuple-element.27.one_ref.now_ref, bf16[512,1024]{1,0:T(8,128)(2,1)S(1)} %collective-permute-done.17.two_ref.one_ref, ...), custom_call_target="tpu_custom_call" | custom-call | tf_op jit(solution)/shard_map/pallas_call | solution.py:388
  150.7 2.9 %collective-permute-start.24 = (bf16[64,2240]{1,0:T(8,128)(2,1)S(1)}, bf16[64,2240]{1,0:T(8,128)(2,1)S(1)}, u32[]{:S(2)}, u32[]{:S(2)}) collective-permute-start(bf16[64,2240]{1,0:T(8,128)(2,1)S(1)} %get-tuple-element.39), channel_id=1, source_target_pairs={{0,4},{1,5},{2,6},{3,7},{4,0},{5,1},{6,2},{7,3},{8,12},{9,13},{10,... | collective-permute-start | bytes 860168 | tf_op jit(solution)/shard_map/ppermute | solution.py:399
  154.3 1.7 collective-permute-start.20
  156.6 4.7 %collective-permute-done.23.refs_3_ = bf16[64,2240]{1,0:T(8,128)(2,1)S(1)} collective-permute-done((bf16[64,2240]{1,0:T(8,128)(2,1)S(1)}, bf16[64,2240]{1,0:T(8,128)(2,1)S(1)}, u32[]{:S(2)}, u32[]{:S(2)}) %collective-permute-start.23) | collective-permute-done | bytes 286752 | tf_op jit(solution)/shard_map/ppermute | solution.py:399
  162.0 5.8 %collective-permute-done.24.refs_4_ = bf16[64,2240]{1,0:T(8,128)(2,1)S(1)} collective-permute-done((bf16[64,2240]{1,0:T(8,128)(2,1)S(1)}, bf16[64,2240]{1,0:T(8,128)(2,1)S(1)}, u32[]{:S(2)}, u32[]{:S(2)}) %collective-permute-start.24) | collective-permute-done | bytes 286752 | tf_op jit(solution)/shard_map/ppermute | solution.py:399
  167.8 4.6 %collective-permute-done.20.refs_0_ = bf16[64,2240]{1,0:T(8,128)(2,1)S(1)} collective-permute-done((bf16[64,2240]{1,0:T(8,128)(2,1)S(1)}, bf16[64,2240]{1,0:T(8,128)(2,1)S(1)}, u32[]{:S(2)}, u32[]{:S(2)}) %collective-permute-start.20) | collective-permute-done | bytes 286752 | tf_op jit(solution)/shard_map/ppermute | solution.py:399
  172.4 7.2 %collective-permute-done.21.refs_1_ = bf16[64,2240]{1,0:T(8,128)(2,1)S(1)} collective-permute-done((bf16[64,2240]{1,0:T(8,128)(2,1)S(1)}, bf16[64,2240]{1,0:T(8,128)(2,1)S(1)}, u32[]{:S(2)}, u32[]{:S(2)}) %collective-permute-start.21) | collective-permute-done | bytes 286752 | tf_op jit(solution)/shard_map/ppermute | solution.py:399
  (70 shorter events, 15.7 us)
Async XLA Ops:
  6.5 71.6 %all-gather.2.cloned.1.call-start = ((), (), s32[]{:S(2)}) async-start(), calls=%async_computation.2 | async-start | bytes 11612160 | tf_op jit(solution)/shard_map/all_gather | solution.py:268
  59.9 6.1 %collective-permute-start.1 = (bf16[128,8,128]{2,1,0:T(8,128)(2,1)S(1)}, bf16[128,8,128]{2,1,0:T(8,128)(2,1)S(1)}, u32[]{:S(2)}, u32[]{:S(2)}) collective-permute-start(bf16[128,8,128]{2,1,0:T(8,128)(2,1)S(1)} %all_to_all.11.mine_ref), channel_id=1, source_target_pairs={{0,1},{1,0},{2,3},{3,2},{4,5},{5,4},{6,7},{7,6},{8,9},{9,8},{10,11... | collective-permute-start | bytes 786440 | tf_op jit(solution)/shard_map/ppermute | solution.py:303
  83.0 16.8 %collective-permute-start.2 = (bf16[64,2240]{1,0:T(8,128)(2,1)S(1)}, bf16[64,2240]{1,0:T(8,128)(2,1)S(1)}, u32[]{:S(2)}, u32[]{:S(2)}) collective-permute-start(bf16[64,2240]{1,0:T(8,128)(2,1)S(1)} %get-tuple-element.25.refs_0_.hidden_ref), channel_id=1, source_target_pairs={{0,2},{1,3},{2,4},{3,5},{4,6},{5,7},{6,0},{7,1},{8,10},{9,11},{10,... | collective-permute-start | bytes 860168 | tf_op jit(solution)/shard_map/ppermute | solution.py:365
  83.7 16.0 %collective-permute-start.3 = (bf16[64,2240]{1,0:T(8,128)(2,1)S(1)}, bf16[64,2240]{1,0:T(8,128)(2,1)S(1)}, u32[]{:S(2)}, u32[]{:S(2)}) collective-permute-start(bf16[64,2240]{1,0:T(8,128)(2,1)S(1)} %get-tuple-element.25.refs_0_.hidden_ref), channel_id=1, source_target_pairs={{0,4},{1,5},{2,6},{3,7},{4,0},{5,1},{6,2},{7,3},{8,12},{9,13},{10,... | collective-permute-start | bytes 860168 | tf_op jit(solution)/shard_map/ppermute | solution.py:365
  85.5 14.9 %collective-permute-start.4 = (bf16[64,2240]{1,0:T(8,128)(2,1)S(1)}, bf16[64,2240]{1,0:T(8,128)(2,1)S(1)}, u32[]{:S(2)}, u32[]{:S(2)}) collective-permute-start(bf16[64,2240]{1,0:T(8,128)(2,1)S(1)} %get-tuple-element.25.refs_0_.hidden_ref), channel_id=1, source_target_pairs={{0,6},{1,7},{2,0},{3,1},{4,2},{5,3},{6,4},{7,5},{8,14},{9,15},{10,... | collective-permute-start | bytes 860168 | tf_op jit(solution)/shard_map/ppermute | solution.py:365
  87.5 12.8 %collective-permute-start.5 = (bf16[64,2240]{1,0:T(8,128)(2,1)S(1)}, bf16[64,2240]{1,0:T(8,128)(2,1)S(1)}, u32[]{:S(2)}, u32[]{:S(2)}) collective-permute-start(bf16[64,2240]{1,0:T(8,128)(2,1)S(1)} %get-tuple-element.26.refs_3_.hidden_ref), channel_id=1, source_target_pairs={{0,8},{8,16},{16,24},{24,32},{32,40},{40,48},{48,56},{56,64},{64,7... | collective-permute-start | bytes 860168 | tf_op jit(solution)/shard_map/ppermute | solution.py:368
  90.9 11.5 %collective-permute-start.13 = (bf16[64,2240]{1,0:T(8,128)(2,1)S(1)}, bf16[64,2240]{1,0:T(8,128)(2,1)S(1)}, u32[]{:S(2)}, u32[]{:S(2)}) collective-permute-start(bf16[64,2240]{1,0:T(8,128)(2,1)S(1)} %get-tuple-element.25.refs_0_.hidden_ref), channel_id=1, source_target_pairs={{0,1},{1,0},{2,3},{3,2},{4,5},{5,4},{6,7},{7,6},{8,9},{9,8},{10,11... | collective-permute-start | bytes 860168 | tf_op jit(solution)/shard_map/ppermute | solution.py:379
  99.7 4.6 %collective-permute-start.14 = (bf16[64,2240]{1,0:T(8,128)(2,1)S(1)}, bf16[64,2240]{1,0:T(8,128)(2,1)S(1)}, u32[]{:S(2)}, u32[]{:S(2)}) collective-permute-start(bf16[64,2240]{1,0:T(8,128)(2,1)S(1)} %collective-permute-done.2.refs_0_.refs_2_), channel_id=1, source_target_pairs={{0,1},{1,0},{2,3},{3,2},{4,5},{5,4},{6,7},{7,6},{8,9},{9,8},{10,11... | collective-permute-start | bytes 860168 | tf_op jit(solution)/shard_map/ppermute | solution.py:379
  99.7 4.7 %collective-permute-start.15 = (bf16[64,2240]{1,0:T(8,128)(2,1)S(1)}, bf16[64,2240]{1,0:T(8,128)(2,1)S(1)}, u32[]{:S(2)}, u32[]{:S(2)}) collective-permute-start(bf16[64,2240]{1,0:T(8,128)(2,1)S(1)} %collective-permute-done.3.refs_1_.refs_4_), channel_id=1, source_target_pairs={{0,1},{1,0},{2,3},{3,2},{4,5},{5,4},{6,7},{7,6},{8,9},{9,8},{10,11... | collective-permute-start | bytes 860168 | tf_op jit(solution)/shard_map/ppermute | solution.py:379
  100.4 4.1 %collective-permute-start.16 = (bf16[64,2240]{1,0:T(8,128)(2,1)S(1)}, bf16[64,2240]{1,0:T(8,128)(2,1)S(1)}, u32[]{:S(2)}, u32[]{:S(2)}) collective-permute-start(bf16[64,2240]{1,0:T(8,128)(2,1)S(1)} %collective-permute-done.4.refs_2_.refs_6_), channel_id=1, source_target_pairs={{0,1},{1,0},{2,3},{3,2},{4,5},{5,4},{6,7},{7,6},{8,9},{9,8},{10,11... | collective-permute-start | bytes 860168 | tf_op jit(solution)/shard_map/ppermute | solution.py:379
  100.4 17.8 %collective-permute-start.9 = (bf16[2,64,2240]{2,1,0:T(8,128)(2,1)S(1)}, bf16[2,64,2240]{2,1,0:T(8,128)(2,1)S(1)}, u32[]{:S(2)}, u32[]{:S(2)}) collective-permute-start(bf16[2,64,2240]{2,1,0:T(8,128)(2,1)S(1)} %shard_map.96.refs_0_), channel_id=1, source_target_pairs={{0,4},{1,5},{2,6},{3,7},{4,0},{5,1},{6,2},{7,3},{8,12},{9,13},{10,... | collective-permute-start | bytes 1720328 | tf_op jit(solution)/shard_map/ppermute | solution.py:365
  102.3 28.0 %collective-permute-start.11 = (bf16[2,64,2240]{2,1,0:T(8,128)(2,1)S(1)}, bf16[2,64,2240]{2,1,0:T(8,128)(2,1)S(1)}, u32[]{:S(2)}, u32[]{:S(2)}) collective-permute-start(bf16[2,64,2240]{2,1,0:T(8,128)(2,1)S(1)} %shard_map.96.refs_0_), channel_id=1, source_target_pairs={{0,6},{1,7},{2,0},{3,1},{4,2},{5,3},{6,4},{7,5},{8,14},{9,15},{10,... | collective-permute-start | bytes 1720328 | tf_op jit(solution)/shard_map/ppermute | solution.py:365
  104.4 26.0 %collective-permute-start.7 = (bf16[2,64,2240]{2,1,0:T(8,128)(2,1)S(1)}, bf16[2,64,2240]{2,1,0:T(8,128)(2,1)S(1)}, u32[]{:S(2)}, u32[]{:S(2)}) collective-permute-start(bf16[2,64,2240]{2,1,0:T(8,128)(2,1)S(1)} %shard_map.96.refs_0_), channel_id=1, source_target_pairs={{0,2},{1,3},{2,4},{3,5},{4,6},{5,7},{6,0},{7,1},{8,10},{9,11},{10,... | collective-permute-start | bytes 1720328 | tf_op jit(solution)/shard_map/ppermute | solution.py:365
  109.9 32.8 %collective-permute-start.17 = (bf16[512,1024]{1,0:T(8,128)(2,1)S(1)}, bf16[512,1024]{1,0:T(8,128)(2,1)S(1)}, u32[]{:S(2)}, u32[]{:S(2)}) collective-permute-start(bf16[512,1024]{1,0:T(8,128)(2,1)S(1)} %shard_map.97.refs_10_.now_ref), channel_id=1, source_target_pairs={{0,8},{8,16},{16,24},{24,32},{32,40},{40,48},{48,56},{56,64},{64,7... | collective-permute-start | bytes 3145736 | tf_op jit(solution)/shard_map/ppermute | solution.py:381
  113.3 17.6 %collective-permute-start.6 = (bf16[2,64,2240]{2,1,0:T(8,128)(2,1)S(1)}, bf16[2,64,2240]{2,1,0:T(8,128)(2,1)S(1)}, u32[]{:S(2)}, u32[]{:S(2)}) collective-permute-start(bf16[2,64,2240]{2,1,0:T(8,128)(2,1)S(1)} %shard_map.96.refs_0_), channel_id=1, source_target_pairs={{0,1},{1,0},{2,3},{3,2},{4,5},{5,4},{6,7},{7,6},{8,9},{9,8},{10,11... | collective-permute-start | bytes 1720328 | tf_op jit(solution)/shard_map/ppermute | solution.py:384
  118.2 12.7 %collective-permute-start.10 = (bf16[2,64,2240]{2,1,0:T(8,128)(2,1)S(1)}, bf16[2,64,2240]{2,1,0:T(8,128)(2,1)S(1)}, u32[]{:S(2)}, u32[]{:S(2)}) collective-permute-start(bf16[2,64,2240]{2,1,0:T(8,128)(2,1)S(1)} %collective-permute-done.9.refs_4_), channel_id=1, source_target_pairs={{0,1},{1,0},{2,3},{3,2},{4,5},{5,4},{6,7},{7,6},{8,9},{9,8},{10,11... | collective-permute-start | bytes 1720328 | tf_op jit(solution)/shard_map/ppermute | solution.py:384
  145.6 3.5 %collective-permute-start.19 = (bf16[4,64,2240]{2,1,0:T(8,128)(2,1)S(1)}, bf16[4,64,2240]{2,1,0:T(8,128)(2,1)S(1)}, u32[]{:S(2)}, u32[]{:S(2)}) collective-permute-start(bf16[4,64,2240]{2,1,0:T(8,128)(2,1)S(1)} %get-tuple-element.33), channel_id=1, source_target_pairs={{0,1},{1,0},{2,3},{3,2},{4,5},{5,4},{6,7},{7,6},{8,9},{9,8},{10,11... | collective-permute-start | bytes 3440648 | tf_op jit(solution)/shard_map/ppermute | solution.py:389
  148.6 5.3 %collective-permute-start.18 = (bf16[4,64,2240]{2,1,0:T(8,128)(2,1)S(1)}, bf16[4,64,2240]{2,1,0:T(8,128)(2,1)S(1)}, u32[]{:S(2)}, u32[]{:S(2)}) collective-permute-start(bf16[4,64,2240]{2,1,0:T(8,128)(2,1)S(1)} %get-tuple-element.31), channel_id=1, source_target_pairs={{0,1},{1,0},{2,3},{3,2},{4,5},{5,4},{6,7},{7,6},{8,9},{9,8},{10,11... | collective-permute-start | bytes 3440648 | tf_op jit(solution)/shard_map/ppermute | solution.py:389
  149.4 11.9 %collective-permute-start.23 = (bf16[64,2240]{1,0:T(8,128)(2,1)S(1)}, bf16[64,2240]{1,0:T(8,128)(2,1)S(1)}, u32[]{:S(2)}, u32[]{:S(2)}) collective-permute-start(bf16[64,2240]{1,0:T(8,128)(2,1)S(1)} %get-tuple-element.38), channel_id=1, source_target_pairs={{0,2},{1,3},{2,4},{3,5},{4,6},{5,7},{6,0},{7,1},{8,10},{9,11},{10,... | collective-permute-start | bytes 860168 | tf_op jit(solution)/shard_map/ppermute | solution.py:399
  150.7 17.1 %collective-permute-start.24 = (bf16[64,2240]{1,0:T(8,128)(2,1)S(1)}, bf16[64,2240]{1,0:T(8,128)(2,1)S(1)}, u32[]{:S(2)}, u32[]{:S(2)}) collective-permute-start(bf16[64,2240]{1,0:T(8,128)(2,1)S(1)} %get-tuple-element.39), channel_id=1, source_target_pairs={{0,4},{1,5},{2,6},{3,7},{4,0},{5,1},{6,2},{7,3},{8,12},{9,13},{10,... | collective-permute-start | bytes 860168 | tf_op jit(solution)/shard_map/ppermute | solution.py:399
  153.6 14.2 %collective-permute-start.25 = (bf16[64,2240]{1,0:T(8,128)(2,1)S(1)}, bf16[64,2240]{1,0:T(8,128)(2,1)S(1)}, u32[]{:S(2)}, u32[]{:S(2)}) collective-permute-start(bf16[64,2240]{1,0:T(8,128)(2,1)S(1)} %get-tuple-element.40), channel_id=1, source_target_pairs={{0,6},{1,7},{2,0},{3,1},{4,2},{5,3},{6,4},{7,5},{8,14},{9,15},{10,... | collective-permute-start | bytes 860168 | tf_op jit(solution)/shard_map/ppermute | solution.py:399
  154.3 18.1 %collective-permute-start.20 = (bf16[64,2240]{1,0:T(8,128)(2,1)S(1)}, bf16[64,2240]{1,0:T(8,128)(2,1)S(1)}, u32[]{:S(2)}, u32[]{:S(2)}) collective-permute-start(bf16[64,2240]{1,0:T(8,128)(2,1)S(1)} %get-tuple-element.35), channel_id=1, source_target_pairs={{0,2},{1,3},{2,4},{3,5},{4,6},{5,7},{6,0},{7,1},{8,10},{9,11},{10,... | collective-permute-start | bytes 860168 | tf_op jit(solution)/shard_map/ppermute | solution.py:399
  156.0 23.6 %collective-permute-start.21 = (bf16[64,2240]{1,0:T(8,128)(2,1)S(1)}, bf16[64,2240]{1,0:T(8,128)(2,1)S(1)}, u32[]{:S(2)}, u32[]{:S(2)}) collective-permute-start(bf16[64,2240]{1,0:T(8,128)(2,1)S(1)} %get-tuple-element.36), channel_id=1, source_target_pairs={{0,4},{1,5},{2,6},{3,7},{4,0},{5,1},{6,2},{7,3},{8,12},{9,13},{10,... | collective-permute-start | bytes 860168 | tf_op jit(solution)/shard_map/ppermute | solution.py:399
  161.3 18.3 %collective-permute-start.22 = (bf16[64,2240]{1,0:T(8,128)(2,1)S(1)}, bf16[64,2240]{1,0:T(8,128)(2,1)S(1)}, u32[]{:S(2)}, u32[]{:S(2)}) collective-permute-start(bf16[64,2240]{1,0:T(8,128)(2,1)S(1)} %get-tuple-element.37), channel_id=1, source_target_pairs={{0,6},{1,7},{2,0},{3,1},{4,2},{5,3},{6,4},{7,5},{8,14},{9,15},{10,... | collective-permute-start | bytes 860168 | tf_op jit(solution)/shard_map/ppermute | solution.py:399
  (12 other events, 132.2 us)
Sparse Core Ops, SparseCore 0:
  9.2 68.9 all-gather.1
